TPU v7x, 32 devices: a whole 2x2x4 slice. The times are simulated.
32 devices in a mesh: chan: 4 (over z), tm: 8 (over y, x, core).
Axes of the slice: x: 2, y: 2, z: 4, core: 2. Of those that a mesh axis runs over, the one named last changes fastest.
Arguments:
- recording: bfloat16 [4096, 120000], P('chan', 'tm'), may hold values from -6 to 6
- offsets: int32 [16], replicated, may hold values from 0 to 3749, as said below
- band_bins: int32 [20], replicated, may hold values from 61 to 300
- dead_flags: int32 [4096], P('chan'), may hold values 0 or 1
Outputs:
- stacks: bfloat16 [2, 20, 4096, 4096], P(None, None, 'tm', 'chan')
Inputs may be any that keep to these rules, and one draw needn't show every extreme that they name: `offsets`: every window's offset is drawn afresh; the last window of some block of 2 consecutive windows has the largest offset.
All inputs are finite; a program needn't handle non-finite values. No bound on the sum of `dead_flags` on one device may be relied on, other than what follows from the above.
Results may differ from a plain program's by a relative error of at most 0.0063.
Values may be sent and summed in bfloat16 or wider, within the bound.
No kernel may reach another device: no remote copies, remote signals or barrier semaphores. Data moves between devices by JAX's collectives and lax.ppermute only.
A program may use at most 192 MiB of HBM per device.

v0:
```python
import math

import jax
import jax.numpy as jnp
from jax import lax
from jax.sharding import PartitionSpec as P

L = 15000
NB = 20


TWO_PI = 2.0 * math.pi
FLOOR = 0.7


def shifted(block, axis, distance):
    devices = range(lax.axis_size(axis))
    route = [(i - distance, i) for i in devices if i - distance in devices]
    return lax.ppermute(block, axis, route)


def phase_table(band_bins, shifts, span_len, length):
    position = (
        lax.broadcasted_iota(jnp.int32, (shifts.shape[0], 1, span_len), 2) - shifts[:, None, None]
    )
    inside = (position >= 0) & (position < length)
    lag_index = jnp.where(inside, position, 0)
    turn_index = band_bins[None, :, None] * lag_index % length
    angles = turn_index.astype(jnp.float32) * (TWO_PI / length)
    norm_scale = 1.0 / math.sqrt(length)
    cosine = jnp.where(inside, jnp.cos(angles) * norm_scale, 0.0)
    sine_part = jnp.where(inside, -jnp.sin(angles) * norm_scale, 0.0)
    dft_table = jnp.concatenate([cosine, sine_part], axis=1).astype(jnp.bfloat16)
    weights = inside[:, 0, :].astype(jnp.float32)
    return (dft_table, weights)


def partial_spectra(samples, dft_table, weights):
    raw_spectra = jnp.einsum("wks,cs->wkc", dft_table, samples, preferred_element_type=jnp.float32)
    squares = samples.astype(jnp.float32)
    squares = squares * squares
    energy = jnp.einsum("ws,cs->wc", weights, squares, precision=lax.Precision.HIGHEST)
    return (raw_spectra, energy)


def shards(recording, offsets, band_bins, dead_flags):
    channels, block_len = recording.shape
    length = L
    hop_size = length // 2
    rim_width = hop_size + hop_size // 2
    windows = block_len // hop_size
    tm_count = lax.axis_size("tm")
    tm_index = lax.axis_index("tm")
    own_offsets = lax.dynamic_slice_in_dim(offsets, tm_index * windows, windows)
    starts = jnp.arange(windows, dtype=jnp.int32) * hop_size + own_offsets
    dft_table, weights = phase_table(band_bins, starts, block_len, length)
    raw_spectra, energy = partial_spectra(recording, dft_table, weights)
    before = lax.dynamic_slice_in_dim(offsets, jnp.maximum(tm_index - 1, 0) * windows, windows)
    back_starts = jnp.arange(windows, dtype=jnp.int32) * hop_size + before - block_len
    back_table, back_weights = phase_table(band_bins, back_starts, rim_width, length)
    back_raw, back_energy = partial_spectra(recording[:, :rim_width], back_table, back_weights)
    more_raw, more_energy = shifted((back_raw, back_energy), "tm", -1)
    raw_spectra = raw_spectra + more_raw
    energy = energy + more_energy
    spectra = raw_spectra / jnp.sqrt(energy / length + 1e-06)[:, None, :]
    level = jnp.mean(spectra * spectra, axis=1) * 2.0
    alive = (1 - dead_flags).astype(jnp.float32)
    factor = alive[None, :] / jnp.sqrt(jnp.maximum(level, FLOOR))
    white = (spectra * factor[:, None, :]).astype(jnp.bfloat16).reshape(windows, 2, NB, channels)
    rows_all = lax.all_gather(white, "tm", axis=0, tiled=True)
    every_chan = lax.all_gather(white, "chan", axis=3, tiled=True)
    cols_all = lax.all_to_all(every_chan, "tm", split_axis=3, concat_axis=0, tiled=True)
    flipped = jnp.stack([-cols_all[:, 1], cols_all[:, 0]], axis=1)
    both_cols = jnp.stack([cols_all, flipped], axis=0)
    stacked = jnp.einsum(
        "swpbj,wpbi->sbji", both_cols, rows_all, preferred_element_type=jnp.float32
    )
    stack_scale = 1.0 / math.sqrt(windows * tm_count)
    return (stacked * stack_scale).astype(jnp.bfloat16)


def solution(mesh):
    placed = (P("chan", "tm"), P(), P(), P("chan"))
    return jax.shard_map(
        shards, mesh=mesh, in_specs=placed, out_specs=P(None, None, "tm", "chan"), check_vma=False
    )
```

profile of v0, /device:TPU:0, one launch (start us, length us, event | category | flops | bytes accessed | tf_op | source)
XLA Modules:
  0.0 256.0 jit_solution(18303234041970334680)
XLA Ops:
  6.5 0.8 dynamic-slice_add_fusion
  7.3 21.0 %fusion.4 = f32[2,1024]{1,0:T(2,128)S(1)} fusion(bf16[1024,15000]{0,1:T(8,128)(2,1)} %param.4, s32[2]{0:T(128)S(1)} %get-tuple-element.12), kind=kOutput, calls=%fused_computation.5 | convolution fusion | flops 299609984 | bytes 23060488 | tf_op jit(solution)/shard_map/ws,cs->wc/dot_general | solution.py:42
  28.3 1.3 collective-permute-start.1
  29.6 0.2 compare_and_fusion.1
  29.9 9.4 %select_convert_fusion.3 = (bf16[2,20,11250]{2,1,0:T(8,128)(2,1)S(1)}, bf16[2,20,11250]{2,1,0:T(8,128)(2,1)S(1)}) fusion(s32[2,11250]{1,0:T(2,128)S(1)} %fusion.57, s32[20]{0:T(128)S(1)} %copy-done.1, pred[2,11250]{1,0:T(4,128)(4,1)S(1)} %compare_and_fusion.1), kind=kLoop, calls=%fused_computation.31 | loop fusion | flops 7200000 | bytes 1912580 | tf_op jit(solution)/shard_map/convert
  39.4 9.7 %fusion.10 = f32[2,40,1024]{2,1,0:T(8,128)S(1)} fusion(bf16[1024,15000]{0,1:T(8,128)(2,1)} %param.4, bf16[2,20,11250]{2,1,0:T(8,128)(2,1)S(1)} %get-tuple-element.10, bf16[2,20,11250]{2,1,0:T(8,128)(2,1)S(1)} %get-tuple-element.9), kind=kOutput, calls=%fused_computation.11 | convolution fusion | flops 1846800000 | bytes 25179968 | tf_op jit(solution)/shard_map/wks,cs->wkc/dot_general | solution.py:39
  49.1 1.5 collective-permute-start
  50.6 0.2 compare_and_fusion
  50.9 12.5 %select_convert_fusion.1 = (bf16[2,20,15000]{2,1,0:T(8,128)(2,1)S(1)}, bf16[2,20,15000]{2,1,0:T(8,128)(2,1)S(1)}) fusion(s32[2,15000]{1,0:T(2,128)S(1)} %fusion.56, s32[20]{0:T(128)S(1)} %copy-done.1, pred[2,15000]{1,0:T(4,128)(4,1)S(1)} %compare_and_fusion), kind=kLoop, calls=%fused_computation.20 | loop fusion | flops 9600000 | bytes 2550080 | tf_op jit(solution)/shard_map/convert.2
  63.5 28.0 %fusion.53 = f32[2,1024]{1,0:T(2,128)S(1)} fusion(f32[2,1024]{1,0:T(2,128)S(1)} %collective-permute-done.1, bf16[1024,15000]{0,1:T(8,128)(2,1)} %param.4, s32[2]{0:T(128)S(1)} %get-tuple-element.11), kind=kOutput, calls=%fused_computation.48 | convolution fusion | flops 399486144 | bytes 30736392 | tf_op jit(solution)/shard_map/ws,cs->wc/dot_general | solution.py:42
  91.5 12.5 %multiply_reduce_fusion = (f32[2,1024]{1,0:T(2,128)S(1)}, f32[2,40,1024]{2,1,0:T(8,128)S(1)}) fusion(f32[2,1024]{1,0:T(2,128)S(1)} %fusion.53, f32[2,40,1024]{2,1,0:T(8,128)S(1)} %collective-permute-done, bf16[1024,15000]{0,1:T(8,128)(2,1)} %param.4, bf16[2,20,15000]{2,1,0:T(8,128)(2,1)S(1)} %get-tuple-element.8, bf16[2,20,15000]{2,1,0:T(8,128)(2,1)S(1)} %get-tuple-element.7), kind=kOutput, calls=%fused_computation.52 | convolution fusion | flops 2462725632 | bytes 33791744 | tf_op jit(solution)/shard_map/wks,cs->wkc/dot_general | solution.py:39
  104.0 0.2 copy.22
  104.2 0.8 copy.23
  105.1 19.3 %all_gather.7 = bf16[2,2,20,4096]{3,0,2,1:T(2,128)(2,1)S(1)} all-gather(bf16[2,2,20,1024]{3,0,2,1:T(2,128)(2,1)S(1)} %bitcast.37), channel_id=1, replica_groups=mesh['chan'=4,'tm'=8] {'chan'}, dimensions={3}, use_global_device_ids=true | all-gather | bytes 819200 | tf_op jit(solution)/shard_map/all_gather | solution.py:71
  124.4 7.6 %copy.24 = bf16[2,2,20,4096]{2,1,0,3:T(2,128)(2,1)} copy(bf16[2,2,20,4096]{3,0,2,1:T(2,128)(2,1)S(1)} %all_gather.7) | data formatting | bytes 1310720 | tf_op jit(solution)/shard_map/all_gather | solution.py:71
  132.0 9.4 %reshape.108 = bf16[8,2,20480]{2,1,0:T(2,128)(2,1)S(1)} reshape(bf16[4096,2,2,20]{3,2,1,0:T(2,128)(2,1)} %bitcast.33) | data formatting | bytes 1310720
  141.4 16.9 %all_to_all.18 = bf16[8,2,20480]{2,1,0:T(2,128)(2,1)S(1)} all-to-all(bf16[8,2,20480]{2,1,0:T(2,128)(2,1)S(1)} %reshape.108), channel_id=1, replica_groups=mesh['chan'=4,'tm'=8] {'tm'}, dimensions={0} | all-to-all | bytes 1310720 | tf_op jit(solution)/shard_map/all_to_all | solution.py:72
  158.3 11.3 %reshape.109 = bf16[4096,2,2,20]{3,2,1,0:T(2,128)(2,1)} reshape(bf16[8,2,20480]{2,1,0:T(2,128)(2,1)S(1)} %all_to_all.18) | data formatting | bytes 1310720
  169.6 6.2 %copy.34 = bf16[2,2,20,8,512]{4,3,1,2,0:T(8,128)(2,1)S(1)} copy(bf16[2,2,20,8,512]{2,1,0,4,3:T(2,128)(2,1)} %bitcast.34) | data formatting | bytes 1310720 | tf_op jit(solution)/shard_map/all_to_all | solution.py:72
  175.8 0.7 copy.26
  176.5 0.2 all_to_all.16
  176.7 0.2 stack.13
  177.1 18.5 %fusion.7 = bf16[2,20,512,1024]{2,3,0,1:T(8,128)(2,1)} fusion(bf16[1,16,2,20,512]{4,1,2,0,3:T(8,128)(2,1)S(1)} %maximum_bitcast_fusion, bf16[1,16,2,20,512]{4,1,2,0,3:T(8,128)(2,1)S(1)} %stack.13, bf16[16,2,20,1024,1]{3,1,2,0,4:T(2,128)(2,1)} %bitcast.38), kind=kOutput, calls=%fused_computation.8 | convolution fusion | flops 1386741760 | bytes 44564480 | tf_op jit(solution)/shard_map/swpbj,wpbi->sbji/dot_general | solution.py:75
  195.6 53.5 %copy.29 = bf16[2,20,512,1024]{3,2,1,0:T(8,128)(2,1)} copy(bf16[2,20,512,1024]{2,3,0,1:T(8,128)(2,1)} %fusion.7) | data formatting | bytes 83886080 | tf_op jit(solution)/shard_map/convert_element_type | solution.py:79
  (16 shorter events, 0.5 us)
Async XLA Ops:
  6.5 170.6 %all-gather.2.cloned.1.call-start = ((), (), s32[]{:S(2)}) async-start(), calls=%async_computation.1 | async-start | bytes 1474560 | tf_op jit(solution)/shard_map/all_gather | solution.py:70
  7.3 22.6 %copy-start.1 = (s32[20]{0:T(128)S(1)}, s32[20]{0:T(128)}, u32[]{:S(2)}) copy-start(s32[20]{0:T(128)} %param.6) | copy-start | bytes 244
  28.3 35.1 %collective-permute-start.1 = (f32[2,1024]{1,0:T(2,128)S(1)}, f32[2,1024]{1,0:T(2,128)S(1)}, u32[]{:S(2)}, u32[]{:S(2)}) collective-permute-start(f32[2,1024]{1,0:T(2,128)S(1)} %fusion.4), channel_id=1, source_target_pairs={{1,0},{2,1},{3,2},{4,3},{5,4},{6,5},{7,6},{9,8},{10,9},{11,10},{12... | collective-permute-start | bytes 24584 | tf_op jit(solution)/shard_map/ppermute | solution.py:19
  49.1 14.4 %copy-start = (s32[1024]{0:T(1024)S(1)}, s32[1024]{0:T(1024)}, u32[]{:S(2)}) copy-start(s32[1024]{0:T(1024)} %param.7) | copy-start | bytes 12292
  49.1 42.4 %collective-permute-start = (f32[2,40,1024]{2,1,0:T(8,128)S(1)}, f32[2,40,1024]{2,1,0:T(8,128)S(1)}, u32[]{:S(2)}, u32[]{:S(2)}) collective-permute-start(f32[2,40,1024]{2,1,0:T(8,128)S(1)} %fusion.10), channel_id=1, source_target_pairs={{1,0},{2,1},{3,2},{4,3},{5,4},{6,5},{7,6},{9,8},{10,9},{11,10},{12... | collective-permute-start | bytes 983048 | tf_op jit(solution)/shard_map/ppermute | solution.py:19
Sparse Core Ops, SparseCore 0:
  105.2 29.1 all-gather.1
where the time goes:
time: 258 us; the launch traced here: 256 us
  local copies, waits for them, and re-layouts  90.1 us (35%)
  matrix products  89.7 us (35%)
  blocking collectives  36.2 us (14%)
  other arithmetic  23.5 us (9%)
  between operations  13.6 us (5%)
  starting transfers between devices  2.76 us (1%)
    convert_element_type x1, local copies, waits for them, and re-layouts, shards(): return (stacked * stack_scale).astype(jnp.bfloat16)  53.5 us
    dot_general x2, matrix products, partial_spectra(): jnp.einsum('ws,cs->wc', weights, squares, precision=lax.Precision.HIGHEST)  49 us
    dot_general x2, matrix products, partial_spectra(): jnp.einsum('wks,cs->wkc', dft_table, samples, preferred_element_type=jnp....  22.2 us
    another operation x2, other arithmetic  22 us
    unnamed x6, local copies, waits for them, and re-layouts  20.7 us
    all_gather x1, blocking collectives, shards(): every_chan = lax.all_gather(white, 'chan', axis=3, tiled=True)  19.3 us
    dot_general x1, matrix products, shards(): jnp.einsum('swpbj,wpbi->sbji', both_cols, rows_all, preferred_element_typ...  18.5 us
    all_to_all x1, blocking collectives, shards(): lax.all_to_all(every_chan, 'tm', split_axis=3, concat_axis=0, tiled=True)  16.9 us
  transfers between devices with their start and end apart: 3, of which 0 were waited for; matrix products, arithmetic and copies ran while one was open for 37% of the time, Pallas kernels for 0%

commit v1 on v0

v1 whole, which is shorter than its diff:
```python
import functools
import math

import jax
import jax.numpy as jnp
from jax import lax
from jax.experimental import pallas as pl
from jax.experimental.pallas import tpu as pltpu
from jax.sharding import PartitionSpec as P

L = 15000
FLOOR = 0.7
F32 = jnp.float32
BF16 = jnp.bfloat16
LANE = 128
DEPTH = 256
STEP = 2048
ROW_TILE = 16


def shifted(block, axis, distance):
    devices = range(lax.axis_size(axis))
    route = [(i - distance, i) for i in devices if i - distance in devices]
    return lax.ppermute(block, axis, route)


def cos_sin(turns, length):
    quarter = jnp.floor(turns * (4.0 / length) + 0.5)
    angle = (turns * 4.0 - quarter * length) * (math.pi / (2.0 * length))
    square = angle * angle
    sine = angle * (
        1.0 + square * (-1.0 / 6 + square * (1.0 / 120 + square * (-1.0 / 5040 + square * (1.0 / 362880))))
    )
    cosine = 1.0 + square * (
        -0.5 + square * (1.0 / 24 + square * (-1.0 / 720 + square * (1.0 / 40320)))
    )
    quadrant = quarter - 4.0 * jnp.floor(quarter * 0.25)
    odd = (quadrant == 1.0) | (quadrant == 3.0)
    cos_sign = jnp.where((quadrant == 1.0) | (quadrant == 2.0), -1.0, 1.0)
    sin_sign = jnp.where(quadrant >= 2.0, -1.0, 1.0)
    return cos_sign * jnp.where(odd, sine, cosine), sin_sign * jnp.where(odd, cosine, sine)


def spectra_kernel(
    bins, windows, block_len, steps,
    offsets, band_bins, x_ref, own_ref, back_ref,
    acc, seg, cos_now, sin_now, cos_turn, sin_turn, place, even, odd,
):
    channels = x_ref.shape[1]
    length, hop = L, L // 2
    rows = bins * windows * 2
    half_tile = ROW_TILE // 2
    per_group = half_tile // windows
    groups = rows // ROW_TILE
    states = groups * half_tile
    step = pl.program_id(0)
    half = STEP // 2
    tiles = STEP // ROW_TILE
    tm = lax.axis_index("tm")
    ahead = [offsets[tm * windows + w] + w * hop for w in range(windows)]
    before = jnp.maximum(tm - 1, 0) * windows
    behind = [offsets[before + w] + w * hop + length - block_len for w in range(windows)]
    ends = []
    for w in range(windows):
        ends += [jnp.minimum(ahead[w], behind[w]), jnp.maximum(ahead[w], behind[w])]
    segments = len(ends) + 1
    trash = segments

    def make_table(table, first, count):
        for j in range(count):
            moved = ((first + j) * DEPTH).astype(F32)
            for side in range(2):
                limit = moved if side else -moved
                for g in range(groups):
                    at = slice(side * states + g * half_tile, side * states + (g + 1) * half_tile)
                    to = side * rows + g * ROW_TILE
                    c, s = cos_now[at, :], sin_now[at, :]
                    inside = place[at, :] >= limit
                    wave = jnp.concatenate([jnp.where(inside, c, 0.0), jnp.where(inside, s, 0.0)], axis=0)
                    table[to:to + ROW_TILE, j * DEPTH:(j + 1) * DEPTH] = wave.astype(BF16)
                    ct, st = cos_turn[at, :], sin_turn[at, :]
                    cos_now[at, :] = c * ct + s * st
                    sin_now[at, :] = s * ct - c * st

    @pl.when(step == 0)
    def _():
        shape = (half_tile, DEPTH)
        row = lax.broadcasted_iota(jnp.int32, shape, 0)
        lane = lax.broadcasted_iota(jnp.int32, shape, 1).astype(F32)
        norm = 1.0 / math.sqrt(length)
        for side in range(2):
            for g in range(groups):
                at = slice(side * states + g * half_tile, side * states + (g + 1) * half_tile)
                tone = jnp.zeros(shape, jnp.int32)
                start = jnp.zeros(shape, jnp.int32)
                for i in range(per_group):
                    tone = jnp.where(row // windows == i, band_bins[g * per_group + i], tone)
                for w in range(windows):
                    here = behind[w] - length if side else ahead[w]
                    start = jnp.where(row % windows == w, here, start)
                tone, start = tone.astype(F32), start.astype(F32)
                cosine, sine = cos_sin((lane - start) * tone, length)
                cos_now[at, :] = cosine * norm
                sin_now[at, :] = -sine * norm
                cos_turn[at, :], sin_turn[at, :] = cos_sin(tone * DEPTH, length)
                place[at, :] = start + (length - 1) - lane if side else lane - start
        make_table(even, jnp.int32(0), half // DEPTH)
        acc[...] = jnp.zeros_like(acc)
        seg[...] = jnp.zeros_like(seg)

    base = step * STEP

    def segment_of(position):
        index = jnp.int32(0)
        for end in ends:
            index += (end <= position).astype(jnp.int32)
        return index

    def body(kind):
        used = STEP if kind != "last" else block_len - (steps - 1) * STEP
        first = step * (STEP // DEPTH)

        def piece(low):
            full = max(0, min(half, used - low)) // LANE * LANE
            rest = max(0, min(half, used - low)) - full
            table = even if low == 0 else odd
            if full:
                acc[...] += jnp.dot(table[:, :full], x_ref[low:low + full, :], preferred_element_type=F32)
            if rest:
                cut = x_ref[low + full:low + full + LANE, :]
                inside = lax.broadcasted_iota(jnp.int32, cut.shape, 0) < rest
                cut = jnp.where(inside, cut.astype(F32), 0.0).astype(BF16)
                acc[...] += jnp.dot(table[:, full:full + LANE], cut, preferred_element_type=F32)

        def energy(low, high):
            total = None
            for t in range(low, high):
                if t * ROW_TILE >= used:
                    continue
                x = x_ref[t * ROW_TILE:(t + 1) * ROW_TILE, :].astype(F32)
                if (t + 1) * ROW_TILE > used:
                    inside = lax.broadcasted_iota(jnp.int32, x.shape, 0) < used - t * ROW_TILE
                    x = jnp.where(inside, x, 0.0)
                square = x * x
                square = square[:half_tile] + square[half_tile:]
                if kind == "edge":
                    seg[targets[t]] += square
                else:
                    total = square if total is None else total + square
            if total is not None:
                seg[target] += total

        if kind == "edge":
            targets = []
            for t in range(tiles):
                cut = functools.reduce(
                    jnp.logical_or, [end // ROW_TILE == step * tiles + t for end in ends]
                )
                targets.append(jnp.where(cut, trash, segment_of(base + t * ROW_TILE)))
        else:
            target = segment_of(base)
        piece(0)
        energy(0, tiles // 2)
        if used > half:
            make_table(odd, first + half // DEPTH, pl.cdiv(min(used - half, half), DEPTH))
        piece(half)
        energy(tiles // 2, tiles)
        if kind != "last":
            make_table(even, first + STEP // DEPTH, half // DEPTH)

    last = steps - 1
    cut_here = functools.reduce(jnp.logical_or, [end // STEP == step for end in ends])

    @pl.when(jnp.logical_and(step < last, jnp.logical_not(cut_here)))
    def _():
        body("plain")

    @pl.when(jnp.logical_and(step < last, cut_here))
    def _():
        body("edge")
        for i, end in enumerate(ends):
            low = ends[i - 1] if i else jnp.int32(0)
            high = ends[i + 1] if i + 1 < len(ends) else jnp.int32(block_len)

            @pl.when(end // STEP == step)
            def _():
                tile = end // ROW_TILE
                at = pl.ds(pl.multiple_of((tile - step * tiles) * ROW_TILE, ROW_TILE), ROW_TILE)
                x = x_ref[at, :].astype(F32)
                spot = lax.broadcasted_iota(jnp.int32, x.shape, 0) + tile * ROW_TILE
                under = jnp.logical_and(spot >= low, spot < end)
                over = jnp.logical_and(spot >= end, spot < high)
                over = jnp.logical_and(over, high // ROW_TILE != tile)
                square = x * x
                for where, index in ((under, i), (over, i + 1)):
                    kept = jnp.where(where, square, 0.0)
                    seg[index] += kept[:half_tile] + kept[half_tile:]

    @pl.when(step == last)
    def _():
        body("last")
        own_ref[:rows, :] = acc[:rows, :]
        back_ref[:rows, :] = acc[rows:, :]
        parts = [seg[i] for i in range(segments)]
        own_energy, back_energy = [], []
        for w in range(windows):
            turn = parts[2 * w + 1]
            early = ahead[w] <= behind[w]
            after = sum(parts[2 * w + 2:]) + jnp.where(early, turn, 0.0)
            until = sum(parts[:2 * w + 1]) + jnp.where(early, turn, 0.0)
            own_energy.append(jnp.sum(after, axis=0, keepdims=True))
            back_energy.append(jnp.sum(until, axis=0, keepdims=True))
        row = lax.broadcasted_iota(jnp.int32, (half_tile, channels), 0)
        for ref, found in ((own_ref, own_energy), (back_ref, back_energy)):
            block = jnp.zeros((half_tile, channels), F32)
            for w in range(windows):
                block = jnp.where(row == w, found[w], block)
            ref[rows:, :] = block


def spectra_of(recording, offsets, band_bins, windows):
    channels, block_len = recording.shape
    bins = band_bins.shape[0]
    rows = bins * windows * 2
    kept = rows + ROW_TILE // 2
    steps = pl.cdiv(block_len, STEP)
    out = jax.ShapeDtypeStruct((kept, channels), F32)
    state = pltpu.VMEM((rows, DEPTH), F32)
    table = pltpu.VMEM((2 * rows, STEP // 2), BF16)
    return pl.pallas_call(
        functools.partial(spectra_kernel, bins, windows, block_len, steps),
        out_shape=(out, out),
        grid=(steps,),
        in_specs=[
            pl.BlockSpec(memory_space=pltpu.SMEM),
            pl.BlockSpec(memory_space=pltpu.SMEM),
            pl.BlockSpec((STEP, channels), lambda i: (i, 0)),
        ],
        out_specs=(
            pl.BlockSpec((kept, channels), lambda i: (0, 0)),
            pl.BlockSpec((kept, channels), lambda i: (0, 0)),
        ),
        scratch_shapes=[
            pltpu.VMEM((2 * rows, channels), F32),
            pltpu.VMEM((2 * windows + 2, ROW_TILE // 2, channels), F32),
            state, state, state, state, state, table, table,
        ],
        compiler_params=pltpu.CompilerParams(
            dimension_semantics=("arbitrary",), vmem_limit_bytes=40 * 2**20
        ),
        cost_estimate=pl.CostEstimate(
            flops=2 * channels * block_len * 2 * rows,
            bytes_accessed=channels * block_len * 2,
            transcendentals=0,
        ),
        name="band_spectra",
    )(offsets, band_bins, recording.T)


def whiten_kernel(bins, windows, own_ref, more_ref, dead_ref, white_ref):
    rows = bins * windows * 2
    raw = own_ref[:rows, :] + more_ref[:rows, :]
    energy = own_ref[rows:rows + 8, :] + more_ref[rows:rows + 8, :]
    inverse = 1.0 / jnp.sqrt(energy / L + 1e-06)
    which = lax.broadcasted_iota(jnp.int32, (rows, 1), 0) % windows
    scale = inverse[windows - 1:windows, :]
    for w in range(windows - 1):
        scale = jnp.where(which == w, inverse[w:w + 1, :], scale)
    spectra = raw * scale
    power = spectra * spectra
    alive = (1 - dead_ref[...]).astype(F32)
    factor = None
    for w in reversed(range(windows)):
        level = jnp.sum(jnp.where(which == w, power, 0.0), axis=0, keepdims=True) * (1.0 / bins)
        one = alive / jnp.sqrt(jnp.maximum(level, FLOOR))
        factor = one if factor is None else jnp.where(which == w, one, factor)
    white = (spectra * factor).astype(BF16)
    width = white_ref.shape[2]
    for h in range(white_ref.shape[0]):
        white_ref[h] = white[:, h * width:(h + 1) * width]


def whiten(own, more, dead, bins, windows, halves):
    channels = own.shape[1]
    rows = bins * windows * 2
    return pl.pallas_call(
        functools.partial(whiten_kernel, bins, windows),
        out_shape=jax.ShapeDtypeStruct((halves, rows, channels // halves), BF16),
        name="whiten",
    )(own, more, dead.reshape(1, channels))


def stack_kernel(windows, scale, cols_ref, rows_ref, out_ref, lhs):
    bin_index = pl.program_id(0)
    per_group = ROW_TILE // (2 * windows)
    devices = cols_ref.shape[0]
    depth = devices * ROW_TILE
    width = cols_ref.shape[2]
    slot = bin_index % per_group
    exact = math.frexp(scale)[0] == 0.5

    @pl.when(slot == 0)
    def _():
        cols = cols_ref[...].astype(F32)
        if exact:
            cols = cols * scale
        head, tail = cols[:, :ROW_TILE // 2], cols[:, ROW_TILE // 2:]
        straight = cols.reshape(depth, width)
        turned = jnp.concatenate([-tail, head], axis=1).reshape(depth, width)
        lhs[:width, :] = straight.T.astype(BF16)
        lhs[width:, :] = turned.T.astype(BF16)

    which = lax.broadcasted_iota(jnp.int32, (depth, 1), 0) % (ROW_TILE // 2) // windows
    for h in range(rows_ref.shape[1]):
        span = rows_ref.shape[3]
        block = rows_ref[:, h].reshape(depth, span).astype(F32)
        rhs = jnp.where(which == slot, block, 0.0).astype(BF16)
        for part in range(2):
            product = jnp.dot(
                lhs[part * width:(part + 1) * width, :], rhs, preferred_element_type=F32
            )
            if not exact:
                product = product * scale
            out_ref[part, 0, :, h * span:(h + 1) * span] = product.astype(BF16)


def stacks_of(cols_all, rows_all, bins, windows):
    devices, halves, _, span = rows_all.shape
    width = cols_all.shape[2]
    per_group = ROW_TILE // (2 * windows)
    scale = 1.0 / math.sqrt(windows * devices)
    channels = halves * span
    return pl.pallas_call(
        functools.partial(stack_kernel, windows, scale),
        out_shape=jax.ShapeDtypeStruct((2, bins, width, channels), BF16),
        grid=(bins,),
        in_specs=[
            pl.BlockSpec((devices, ROW_TILE, width), lambda b: (0, b // per_group, 0)),
            pl.BlockSpec((devices, halves, ROW_TILE, span), lambda b: (0, 0, b // per_group, 0)),
        ],
        out_specs=pl.BlockSpec((2, 1, width, channels), lambda b: (0, b, 0, 0)),
        scratch_shapes=[pltpu.VMEM((2 * width, devices * ROW_TILE), BF16)],
        compiler_params=pltpu.CompilerParams(
            dimension_semantics=("arbitrary",), vmem_limit_bytes=40 * 2**20
        ),
        cost_estimate=pl.CostEstimate(
            flops=2 * 2 * bins * width * channels * devices * ROW_TILE,
            bytes_accessed=2 * bins * width * channels * 2,
            transcendentals=0,
        ),
        name="stack_products",
    )(cols_all, rows_all)


def shards(recording, offsets, band_bins, dead_flags):
    channels, block_len = recording.shape
    windows = block_len // (L // 2)
    bins = band_bins.shape[0]
    rows = bins * windows * 2
    chan_count, tm_count = lax.axis_size("chan"), lax.axis_size("tm")
    halves = tm_count // chan_count
    own, back = spectra_of(recording, offsets, band_bins, windows)
    more = shifted(back, "tm", -1)
    white = whiten(own, more, dead_flags, bins, windows, halves)
    rows_all = lax.all_gather(white, "tm", axis=0)
    every_chan = lax.all_gather(white, "chan", axis=0)
    every_chan = every_chan.reshape(tm_count, rows, channels // halves)
    cols_all = lax.all_to_all(every_chan, "tm", split_axis=0, concat_axis=0, tiled=True)
    return stacks_of(cols_all, rows_all, bins, windows)


def solution(mesh):
    placed = (P("chan", "tm"), P(), P(), P("chan"))
    return jax.shard_map(
        shards, mesh=mesh, in_specs=placed, out_specs=P(None, None, "tm", "chan"), check_vma=False
    )
```

time: 258 us -> 102 us (0.40)
  matrix products: 89.7 us -> 0 us
  local copies, waits for them, and re-layouts: 90.1 us -> 4.09 us
  Pallas kernels: 0 us -> 41.3 us
  other arithmetic: 23.5 us -> 0 us
  waiting for transfers between devices: 0.04 us -> 2.9 us
    dot_general x5 -> x0, matrix products: 89.7 us -> none  [the longest x2 49 us: partial_spectra(): jnp.einsum('ws,cs->wc', weights, squares, precision=lax.Precision.HIGHEST)]
    convert_element_type x2 -> x0, local copies, waits for them, and re-layouts: 53.6 us -> none  [the longest x1 53.5 us: shards(): return (stacked * stack_scale).astype(jnp.bfloat16)]
    pallas_call x0 -> x3, Pallas kernels: none -> 41.3 us  [the longest x1 21.7 us: stacks_of(): pl.pallas_call(functools.partial(stack_kernel, windows, scale), out_shape...]
    another operation x3 -> x0, other arithmetic: 22 us -> none
    unnamed x6 -> x10, local copies, waits for them, and re-layouts: 20.7 us -> 4.09 us
    all_gather x1 -> x0, local copies, waits for them, and re-layouts: 7.58 us -> none  [shards(): every_chan = lax.all_gather(white, 'chan', axis=3, tiled=True)]
    all_to_all x3 -> x0, local copies, waits for them, and re-layouts: 7.12 us -> none  [shards(): lax.all_to_all(every_chan, 'tm', split_axis=3, concat_axis=0, tiled=True)]
    all_to_all x1, blocking collectives: 16.9 us -> 20.9 us  [shards(): lax.all_to_all(every_chan, 'tm', split_axis=0, concat_axis=0, tiled=True)]
  transfers between devices with their start and end apart: 3 -> 2, of which waited for: 0 -> 1; matrix products, arithmetic and copies ran while one was open for 37% -> 0% of each run, Pallas kernels for 0% -> 0%
where the time goes in v1:
time: 102 us; the launch traced here: 101 us
  Pallas kernels  41.3 us (40%)
  blocking collectives  38.4 us (38%)
  between operations  13.4 us (13%)
  local copies, waits for them, and re-layouts  4.09 us (4%)
  waiting for transfers between devices  2.9 us (3%)
  starting transfers between devices  1.28 us (1%)
    pallas_call x1, Pallas kernels, stacks_of(): pl.pallas_call(functools.partial(stack_kernel, windows, scale), out_shape...  21.7 us
    all_to_all x1, blocking collectives, shards(): lax.all_to_all(every_chan, 'tm', split_axis=0, concat_axis=0, tiled=True)  20.9 us
    pallas_call x1, Pallas kernels, spectra_of(): pl.pallas_call(functools.partial(spectra_kernel, bins, windows, block_len...  17.6 us
    all_gather x1, blocking collectives, shards(): every_chan = lax.all_gather(white, 'chan', axis=0)  17.5 us
    unnamed x10, local copies, waits for them, and re-layouts  4.09 us
    ppermute x1, waiting for transfers between devices, shifted(): return lax.ppermute(block, axis, route)  2.88 us
  transfers between devices with their start and end apart: 2, of which 1 were waited for; matrix products, arithmetic and copies ran while one was open for 0% of the time, Pallas kernels for 0%

profile of v1, /device:TPU:0, one launch (start us, length us, event | category | flops | bytes accessed | tf_op | source)
XLA Modules:
  0.0 101.3 jit_solution(11183145839678025418)
XLA Ops:
  6.5 0.0 all-gather.4.cloned.1.call-start
  6.5 0.0 copy-start.2
  6.5 0.7 copy-done.2
  7.2 0.0 copy-start.3
  7.2 0.7 copy-done.3
  7.8 17.6 %band_spectra.1 = (f32[88,1024]{1,0:T(8,128)S(1)}, f32[88,1024]{1,0:T(8,128)S(1)}) custom-call(s32[16]{0:T(128)S(1)} %copy-done.2, s32[20]{0:T(128)S(1)} %copy-done.3, bf16[15000,1024]{1,0:T(8,128)(2,1)} %bitcast.4), custom_call_target="tpu_custom_call" | custom-call | flops 4915200000 | bytes 30720000 | tf_op jit(solution)/shard_map/band_spectra/pallas_call | solution.py:230
  25.4 0.0 copy-start.1
  25.4 0.7 copy-done.1
  26.2 1.3 %collective-permute-start = (f32[88,1024]{1,0:T(8,128)S(1)}, f32[88,1024]{1,0:T(8,128)S(1)}, u32[]{:S(2)}, u32[]{:S(2)}) collective-permute-start(f32[88,1024]{1,0:T(8,128)S(1)} %get-tuple-element.8), channel_id=1, source_target_pairs={{1,0},{2,1},{3,2},{4,3},{5,4},{6,5},{7,6},{9,8},{10,9},{11,10},{12... | collective-permute-start | bytes 1081352 | tf_op jit(solution)/shard_map/ppermute | solution.py:24
  27.4 2.9 %collective-permute-done.more_ref = f32[88,1024]{1,0:T(8,128)S(1)} collective-permute-done((f32[88,1024]{1,0:T(8,128)S(1)}, f32[88,1024]{1,0:T(8,128)S(1)}, u32[]{:S(2)}, u32[]{:S(2)}) %collective-permute-start) | collective-permute-done | bytes 360480 | tf_op jit(solution)/shard_map/ppermute | solution.py:24
  30.3 0.0 copy-start.4
  30.3 0.7 copy-done.4
  31.1 2.0 %whiten.1 = bf16[2,80,512]{2,1,0:T(8,128)(2,1)} custom-call(f32[88,1024]{1,0:T(8,128)} %copy-done.1, f32[88,1024]{1,0:T(8,128)} %copy-done.4, s32[1,1024]{1,0:T(1,128)} %bitcast.5), custom_call_target="tpu_custom_call" | custom-call | tf_op jit(solution)/shard_map/whiten/pallas_call | solution.py:286
  33.1 0.0 all-gather.4.cloned.1.call-update
  33.1 17.5 %all-gather = bf16[8,80,512]{2,1,0:T(8,128)(2,1)S(1)} all-gather(bf16[2,80,512]{2,1,0:T(8,128)(2,1)} %whiten.1), channel_id=2, replica_groups=mesh['chan'=4,'tm'=8] {'chan'}, dimensions={0}, use_global_device_ids=true | all-gather | bytes 819200 | tf_op jit(solution)/shard_map/all_gather | solution.py:366
  50.6 20.9 %all_to_all.5.cols_ref = bf16[8,80,512]{2,1,0:T(8,128)(2,1)S(1)} all-to-all(bf16[8,80,512]{2,1,0:T(8,128)(2,1)S(1)} %all-gather), channel_id=1, replica_groups=mesh['chan'=4,'tm'=8] {'tm'}, dimensions={0} | all-to-all | bytes 1310720 | tf_op jit(solution)/shard_map/all_to_all | solution.py:368
  71.5 0.0 all-gather.4.cloned.1.call-done
  71.5 0.0 copy-start
  71.5 1.3 %copy-done = bf16[16,80,512]{2,1,0:T(8,128)(2,1)S(1)} copy-done((bf16[16,80,512]{2,1,0:T(8,128)(2,1)S(1)}, bf16[16,80,512]{2,1,0:T(8,128)(2,1)}, u32[]{:S(2)}) %copy-start) | copy-done | bytes 1310744
  72.8 21.7 %stack_products.1 = bf16[2,20,512,1024]{3,2,1,0:T(8,128)(2,1)} custom-call(bf16[8,80,512]{2,1,0:T(8,128)(2,1)S(1)} %all_to_all.5.cols_ref, bf16[8,2,80,512]{3,2,1,0:T(8,128)(2,1)S(1)} %bitcast.3), custom_call_target="tpu_custom_call" | custom-call | flops 5368709120 | bytes 41943040 | tf_op jit(solution)/shard_map/stack_products/pallas_call | solution.py:333
Async XLA Ops:
  6.5 65.0 %all-gather.4.cloned.1.call-start = ((), (), s32[]{:S(2)}) async-start(), calls=%async_computation.1 | async-start | bytes 1474560 | tf_op jit(solution)/shard_map/all_gather | solution.py:365
  6.5 0.7 copy-start.2
  7.2 0.7 copy-start.3
  25.4 0.7 copy-start.1
  26.2 4.2 %collective-permute-start = (f32[88,1024]{1,0:T(8,128)S(1)}, f32[88,1024]{1,0:T(8,128)S(1)}, u32[]{:S(2)}, u32[]{:S(2)}) collective-permute-start(f32[88,1024]{1,0:T(8,128)S(1)} %get-tuple-element.8), channel_id=1, source_target_pairs={{1,0},{2,1},{3,2},{4,3},{5,4},{6,5},{7,6},{9,8},{10,9},{11,10},{12... | collective-permute-start | bytes 1081352 | tf_op jit(solution)/shard_map/ppermute | solution.py:24
  30.3 0.7 copy-start.4
  71.5 1.3 %copy-start = (bf16[16,80,512]{2,1,0:T(8,128)(2,1)S(1)}, bf16[16,80,512]{2,1,0:T(8,128)(2,1)}, u32[]{:S(2)}) copy-start(bf16[16,80,512]{2,1,0:T(8,128)(2,1)} %all-gather.4.cloned.1.call-done) | copy-start | bytes 3932164
Sparse Core Ops, SparseCore 0:
  33.2 32.3 all-gather.3

commit v2 on v0

v2 whole, which is shorter than its diff:
```python
import functools
import math

import jax
import jax.numpy as jnp
from jax import lax
from jax.experimental import pallas as pl
from jax.experimental.pallas import tpu as pltpu
from jax.sharding import PartitionSpec as P

L = 15000
FLOOR = 0.7
F32 = jnp.float32
BF16 = jnp.bfloat16
LANE = 128
DEPTH = 256
PIECE = 512
STEP = 2 * PIECE
ROW_TILE = 16


def shifted(block, axis, distance):
    devices = range(lax.axis_size(axis))
    route = [(i - distance, i) for i in devices if i - distance in devices]
    return lax.ppermute(block, axis, route)


def cos_sin(turns, length):
    quarter = jnp.floor(turns * (4.0 / length) + 0.5)
    angle = (turns * 4.0 - quarter * length) * (math.pi / (2.0 * length))
    square = angle * angle
    sine = angle * (
        1.0 + square * (-1.0 / 6 + square * (1.0 / 120 + square * (-1.0 / 5040 + square * (1.0 / 362880))))
    )
    cosine = 1.0 + square * (
        -0.5 + square * (1.0 / 24 + square * (-1.0 / 720 + square * (1.0 / 40320)))
    )
    quadrant = quarter - 4.0 * jnp.floor(quarter * 0.25)
    odd = (quadrant == 1.0) | (quadrant == 3.0)
    cos_sign = jnp.where((quadrant == 1.0) | (quadrant == 2.0), -1.0, 1.0)
    sin_sign = jnp.where(quadrant >= 2.0, -1.0, 1.0)
    return cos_sign * jnp.where(odd, sine, cosine), sin_sign * jnp.where(odd, cosine, sine)


def spectra_kernel(
    bins, windows, block_len,
    offsets_hbm, bins_hbm, dead_hbm, x_hbm, tail_ref, own_ref, back_ref,
    offsets, band_bins, dead, x_ref, acc, seg, cos_now, sin_now, cos_turn, sin_turn, place, even, odd,
    small_sems, x_sems,
):
    channels = x_ref.shape[1]
    length, hop = L, L // 2
    rows = bins * windows * 2
    half_tile = ROW_TILE // 2
    per_group = half_tile // windows
    groups = rows // ROW_TILE
    states = groups * half_tile
    bulk = block_len // ROW_TILE * ROW_TILE
    padded = x_ref.shape[0]
    steps = padded // STEP
    columns = [slice(n, min(n + DEPTH, channels)) for n in range(0, channels, DEPTH)]

    def x_copy(i):
        size = min(STEP, bulk - i * STEP)
        at = pl.ds(i * STEP, size)
        return pltpu.make_async_copy(x_hbm.at[at], x_ref.at[at], x_sems.at[i])

    small = [
        pltpu.make_async_copy(offsets_hbm, offsets, small_sems.at[0]),
        pltpu.make_async_copy(bins_hbm, band_bins, small_sems.at[1]),
        pltpu.make_async_copy(dead_hbm, dead, small_sems.at[2]),
    ]
    for copy in small:
        copy.start()
    for i in range(pl.cdiv(bulk, STEP)):
        x_copy(i).start()
    for copy in small:
        copy.wait()

    tm = lax.axis_index("tm")
    ahead = [offsets[tm * windows + w] + w * hop for w in range(windows)]
    before = jnp.maximum(tm - 1, 0) * windows
    behind = [offsets[before + w] + w * hop + length - block_len for w in range(windows)]
    ends = []
    for w in range(windows):
        ends += [jnp.minimum(ahead[w], behind[w]), jnp.maximum(ahead[w], behind[w])]
    segments = len(ends) + 1
    trash = segments

    def make_table(table, first, count):
        for j in range(count):
            moved = jnp.asarray((first + j) * DEPTH, jnp.int32).astype(F32)
            for side in range(2):
                limit = moved if side else -moved
                for g in range(groups):
                    at = slice(side * states + g * half_tile, side * states + (g + 1) * half_tile)
                    to = side * rows + g * ROW_TILE
                    c, s = cos_now[at, :], sin_now[at, :]
                    inside = place[at, :] >= limit
                    wave = jnp.concatenate([jnp.where(inside, c, 0.0), jnp.where(inside, s, 0.0)], axis=0)
                    table[to:to + ROW_TILE, j * DEPTH:(j + 1) * DEPTH] = wave.astype(BF16)
                    ct, st = cos_turn[at, :], sin_turn[at, :]
                    cos_now[at, :] = c * ct + s * st
                    sin_now[at, :] = s * ct - c * st

    shape = (half_tile, DEPTH)
    row = lax.broadcasted_iota(jnp.int32, shape, 0)
    lane = lax.broadcasted_iota(jnp.int32, shape, 1).astype(F32)
    norm = 1.0 / math.sqrt(length)
    for side in range(2):
        for g in range(groups):
            at = slice(side * states + g * half_tile, side * states + (g + 1) * half_tile)
            tone = jnp.zeros(shape, jnp.int32)
            start = jnp.zeros(shape, jnp.int32)
            for i in range(per_group):
                tone = jnp.where(row // windows == i, band_bins[g * per_group + i], tone)
            for w in range(windows):
                here = behind[w] - length if side else ahead[w]
                start = jnp.where(row % windows == w, here, start)
            tone, start = tone.astype(F32), start.astype(F32)
            cosine, sine = cos_sin((lane - start) * tone, length)
            cos_now[at, :] = cosine * norm
            sin_now[at, :] = -sine * norm
            cos_turn[at, :], sin_turn[at, :] = cos_sin(tone * DEPTH, length)
            place[at, :] = start + (length - 1) - lane if side else lane - start
    make_table(even, 0, PIECE // DEPTH)
    acc[...] = jnp.zeros_like(acc)
    seg[...] = jnp.zeros_like(seg)
    x_ref[bulk:, :] = jnp.zeros((padded - bulk, channels), BF16)
    if block_len > bulk:
        inside = lax.broadcasted_iota(jnp.int32, (ROW_TILE, channels), 0) < block_len - bulk
        x_ref[bulk:bulk + ROW_TILE, :] = jnp.where(inside, tail_ref[...].astype(F32), 0.0).astype(BF16)

    def segment_of(position):
        index = jnp.int32(0)
        for end in ends:
            index += (end <= position).astype(jnp.int32)
        return index

    def has_end(first, size):
        return functools.reduce(
            jnp.logical_or, [jnp.logical_and(end >= first, end < first + size) for end in ends]
        )

    def piece(base, size, table, edge):
        tiles = size // ROW_TILE
        if edge:
            targets = [
                jnp.where(has_end(base + t * ROW_TILE, ROW_TILE), trash, segment_of(base + t * ROW_TILE))
                for t in range(tiles)
            ]
        else:
            target = segment_of(base)
        for at in columns:
            block = x_ref[pl.ds(base, size), at]
            acc[:, at] += jnp.dot(table[:, :size], block, preferred_element_type=F32)
            total = None
            for t in range(tiles):
                x = x_ref[pl.ds(base + t * ROW_TILE, ROW_TILE), at].astype(F32)
                square = x * x
                square = square[:half_tile] + square[half_tile:]
                if edge:
                    seg[targets[t], :, at] += square
                else:
                    total = square if total is None else total + square
            if not edge:
                seg[target, :, at] += total

    def body(i, edge):
        base = pl.multiple_of(i * STEP, STEP)
        make_table(odd, i * (STEP // DEPTH) + PIECE // DEPTH, PIECE // DEPTH)
        piece(base, PIECE, even, edge)
        make_table(even, (i + 1) * (STEP // DEPTH), PIECE // DEPTH)
        piece(base + PIECE, PIECE, odd, edge)

    @pl.loop(0, steps)
    def _(i):
        at = pl.ds(pl.multiple_of(i * STEP, STEP), STEP)
        pltpu.make_async_copy(x_hbm.at[at], x_ref.at[at], x_sems.at[i]).wait()
        cut = has_end(i * STEP, STEP)

        @pl.when(jnp.logical_not(cut))
        def _():
            body(i, False)

        @pl.when(cut)
        def _():
            body(i, True)

    done = steps * STEP
    if done < padded:
        if done < bulk:
            x_copy(steps).wait()
        first = min(PIECE, padded - done)
        if padded - done > first:
            make_table(odd, (done + first) // DEPTH, (padded - done - first) // DEPTH)
        piece(done, first, even, False)
        if padded - done > first:
            piece(done + first, padded - done - first, odd, False)

    for i, end in enumerate(ends):
        low = ends[i - 1] if i else jnp.int32(0)
        high = ends[i + 1] if i + 1 < len(ends) else jnp.int32(block_len)
        tile = end // ROW_TILE
        x = x_ref[pl.ds(pl.multiple_of(tile * ROW_TILE, ROW_TILE), ROW_TILE), :].astype(F32)
        spot = lax.broadcasted_iota(jnp.int32, x.shape, 0) + tile * ROW_TILE
        under = jnp.logical_and(spot >= low, spot < end)
        over = jnp.logical_and(spot >= end, spot < high)
        over = jnp.logical_and(over, high // ROW_TILE != tile)
        square = x * x
        for where, index in ((under, i), (over, i + 1)):
            kept = jnp.where(where, square, 0.0)
            seg[index] += kept[:half_tile] + kept[half_tile:]

    own_ref[:rows, :] = acc[:rows, :]
    back_ref[:rows, :] = acc[rows:, :].astype(BF16)
    parts = [seg[i] for i in range(segments)]
    row = lax.broadcasted_iota(jnp.int32, (half_tile, channels), 0)
    own_block = jnp.where(row == windows, (1 - dead[...]).astype(F32), 0.0)
    back_block = jnp.zeros((ROW_TILE, channels), F32)
    back_row = lax.broadcasted_iota(jnp.int32, (ROW_TILE, channels), 0)
    for w in range(windows):
        turn = parts[2 * w + 1]
        early = ahead[w] <= behind[w]
        after = sum(parts[2 * w + 2:]) + jnp.where(early, turn, 0.0)
        until = sum(parts[:2 * w + 1]) + jnp.where(early, turn, 0.0)
        own_block = jnp.where(row == w, jnp.sum(after, axis=0, keepdims=True), own_block)
        rest = jnp.sum(until, axis=0, keepdims=True)
        for term in range(3):
            piece_of = rest.astype(BF16).astype(F32)
            rest = rest - piece_of
            back_block = jnp.where(back_row == term * windows + w, piece_of, back_block)
    own_ref[rows:, :] = own_block
    back_ref[rows:, :] = back_block.astype(BF16)


def spectra_of(recording, offsets, band_bins, dead, windows):
    channels, block_len = recording.shape
    bins = band_bins.shape[0]
    rows = bins * windows * 2
    padded = pl.cdiv(block_len, DEPTH) * DEPTH
    bulk = block_len // ROW_TILE * ROW_TILE
    samples = recording.T
    hbm = pl.BlockSpec(memory_space=pltpu.HBM)
    whole = pl.BlockSpec(memory_space=pltpu.VMEM)
    state = pltpu.VMEM((rows, DEPTH), F32)
    table = pltpu.VMEM((2 * rows, PIECE), BF16)
    return pl.pallas_call(
        functools.partial(spectra_kernel, bins, windows, block_len),
        out_shape=(
            jax.ShapeDtypeStruct((rows + ROW_TILE // 2, channels), F32),
            jax.ShapeDtypeStruct((rows + ROW_TILE, channels), BF16),
        ),
        grid=(1,),
        in_specs=[
            hbm, hbm, hbm, hbm,
            pl.BlockSpec((ROW_TILE, channels), lambda i: (min(bulk, block_len - 1) // ROW_TILE, 0)),
        ],
        out_specs=(whole, whole),
        scratch_shapes=[
            pltpu.SMEM(offsets.shape, jnp.int32),
            pltpu.SMEM(band_bins.shape, jnp.int32),
            pltpu.VMEM((1, channels), jnp.int32),
            pltpu.VMEM((padded, channels), BF16),
            pltpu.VMEM((2 * rows, channels), F32),
            pltpu.VMEM((2 * windows + 2, ROW_TILE // 2, channels), F32),
            state, state, state, state, state, table, table,
            pltpu.SemaphoreType.DMA((3,)),
            pltpu.SemaphoreType.DMA((pl.cdiv(padded, STEP),)),
        ],
        compiler_params=pltpu.CompilerParams(vmem_limit_bytes=48 * 2**20),
        cost_estimate=pl.CostEstimate(
            flops=2 * channels * block_len * 2 * rows,
            bytes_accessed=channels * block_len * 2,
            transcendentals=0,
        ),
        name="band_spectra",
    )(offsets, band_bins, dead.reshape(1, channels), samples, samples)


def whiten_kernel(bins, windows, own_ref, more_ref, white_ref):
    rows = bins * windows * 2
    raw = own_ref[:rows, :] + more_ref[:rows, :].astype(F32)
    extra = more_ref[rows:, :].astype(F32)
    which = lax.broadcasted_iota(jnp.int32, (rows, 1), 0) % windows
    alive = own_ref[rows + windows:rows + windows + 1, :]
    scale = factor = None
    for w in range(windows):
        energy = own_ref[rows + w:rows + w + 1, :]
        for term in range(3):
            energy = energy + extra[term * windows + w:term * windows + w + 1, :]
        inverse = 1.0 / jnp.sqrt(energy / L + 1e-06)
        scale = inverse if w == 0 else jnp.where(which == w, inverse, scale)
    spectra = raw * scale
    power = spectra * spectra
    for w in range(windows):
        level = jnp.sum(jnp.where(which == w, power, 0.0), axis=0, keepdims=True) * (1.0 / bins)
        one = alive / jnp.sqrt(jnp.maximum(level, FLOOR))
        factor = one if w == 0 else jnp.where(which == w, one, factor)
    white = (spectra * factor).astype(BF16)
    width = white_ref.shape[2]
    for h in range(white_ref.shape[0]):
        white_ref[h] = white[:, h * width:(h + 1) * width]


def whiten(own, more, bins, windows, halves):
    channels = own.shape[1]
    rows = bins * windows * 2
    return pl.pallas_call(
        functools.partial(whiten_kernel, bins, windows),
        out_shape=jax.ShapeDtypeStruct((halves, rows, channels // halves), BF16),
        name="whiten",
    )(own, more)


def order_kernel(*refs):
    blocks, out_ref = refs[:-1], refs[-1]
    mine = lax.axis_index("chan")
    halves = blocks[0].shape[0]
    for away, block in enumerate(blocks):
        out_ref[pl.ds(jnp.bitwise_xor(mine, away) * halves, halves)] = block[...]


def in_order(blocks):
    halves, rows, width = blocks[0].shape
    return pl.pallas_call(
        order_kernel,
        out_shape=jax.ShapeDtypeStruct((len(blocks) * halves, rows, width), BF16),
        name="order_blocks",
    )(*blocks)


BINS_A_STEP = 2


def stack_kernel(windows, scale, devices, cols_ref, *refs):
    row_refs, out_ref, lhs, held = refs[:devices], refs[devices], refs[devices + 1], refs[devices + 2]
    per_group = ROW_TILE // (2 * windows)
    per_step = out_ref.shape[1]
    step = pl.program_id(0)
    width = cols_ref.shape[2]
    depth = devices * ROW_TILE
    halves, _, span = row_refs[0].shape
    first = step * per_step % per_group
    exact = math.frexp(scale)[0] == 0.5
    tm = lax.axis_index("tm")

    @pl.when(first == 0)
    def _():
        cols = cols_ref[...].astype(F32)
        if exact:
            cols = cols * scale
        head, tail = cols[:, :ROW_TILE // 2], cols[:, ROW_TILE // 2:]
        straight = cols.reshape(depth, width)
        turned = jnp.concatenate([-tail, head], axis=1).reshape(depth, width)
        lhs[:width, :] = straight.T.astype(BF16)
        lhs[width:, :] = turned.T.astype(BF16)
        for away in range(devices):
            to = pl.multiple_of(jnp.bitwise_xor(tm, away) * ROW_TILE, ROW_TILE)
            for h in range(halves):
                held[pl.ds(to, ROW_TILE), h * span:(h + 1) * span] = row_refs[away][h].astype(F32)

    channels = halves * span
    which = lax.broadcasted_iota(jnp.int32, (depth, 1), 0) % (ROW_TILE // 2) // windows
    for b in range(per_step):
        for n in range(0, channels, DEPTH):
            at = slice(n, min(n + DEPTH, channels))
            rhs = jnp.where(which == first + b, held[:, at], 0.0).astype(BF16)
            for part in range(2):
                product = jnp.dot(
                    lhs[part * width:(part + 1) * width, :], rhs, preferred_element_type=F32
                )
                if not exact:
                    product = product * scale
                out_ref[part, b, :, at] = product.astype(BF16)


def stacks_of(cols_all, row_blocks, bins, windows):
    devices = len(row_blocks)
    halves, _, span = row_blocks[0].shape
    width = cols_all.shape[2]
    per_group = ROW_TILE // (2 * windows)
    scale = 1.0 / math.sqrt(windows * devices)
    channels = halves * span
    group = lambda i: i * BINS_A_STEP // per_group
    return pl.pallas_call(
        functools.partial(stack_kernel, windows, scale, devices),
        out_shape=jax.ShapeDtypeStruct((2, bins, width, channels), BF16),
        grid=(bins // BINS_A_STEP,),
        in_specs=[pl.BlockSpec((devices, ROW_TILE, width), lambda i: (0, group(i), 0))]
        + [pl.BlockSpec((halves, ROW_TILE, span), lambda i: (0, group(i), 0))] * devices,
        out_specs=pl.BlockSpec((2, BINS_A_STEP, width, channels), lambda i: (0, i, 0, 0)),
        scratch_shapes=[
            pltpu.VMEM((2 * width, devices * ROW_TILE), BF16),
            pltpu.VMEM((devices * ROW_TILE, channels), F32),
        ],
        compiler_params=pltpu.CompilerParams(
            dimension_semantics=("arbitrary",), vmem_limit_bytes=40 * 2**20
        ),
        cost_estimate=pl.CostEstimate(
            flops=2 * 2 * bins * width * channels * devices * ROW_TILE,
            bytes_accessed=2 * bins * width * channels * 2,
            transcendentals=0,
        ),
        name="stack_products",
    )(cols_all, *row_blocks)


def from_partners(block, axis):
    count = lax.axis_size(axis)
    blocks = [block]
    for away in range(1, count):
        blocks.append(lax.ppermute(block, axis, [(i, i ^ away) for i in range(count)]))
    return blocks


def shards(recording, offsets, band_bins, dead_flags):
    channels, block_len = recording.shape
    windows = block_len // (L // 2)
    bins = band_bins.shape[0]
    halves = lax.axis_size("tm") // lax.axis_size("chan")
    own, back = spectra_of(recording, offsets, band_bins, dead_flags, windows)
    more = shifted(back, "tm", -1)
    white = whiten(own, more, bins, windows, halves)
    every_chan = in_order(from_partners(white, "chan"))
    row_blocks = from_partners(white, "tm")
    cols_all = lax.all_to_all(every_chan, "tm", split_axis=0, concat_axis=0, tiled=True)
    return stacks_of(cols_all, row_blocks, bins, windows)


def solution(mesh):
    placed = (P("chan", "tm"), P(), P(), P("chan"))
    return jax.shard_map(
        shards, mesh=mesh, in_specs=placed, out_specs=P(None, None, "tm", "chan"), check_vma=False
    )
```

time: 258 us -> 102 us (0.40)
  matrix products: 89.7 us -> 0 us
  local copies, waits for them, and re-layouts: 90.1 us -> 5.63 us
  Pallas kernels: 0 us -> 41.6 us
  blocking collectives: 36.2 us -> 0 us
  waiting for transfers between devices: 0.04 us -> 34.2 us
  other arithmetic: 23.5 us -> 0 us
  starting transfers between devices: 2.76 us -> 19.8 us
  between operations: 13.6 us -> 0.06 us
    dot_general x5 -> x0, matrix products: 89.7 us -> none  [the longest x2 49 us: partial_spectra(): jnp.einsum('ws,cs->wc', weights, squares, precision=lax.Precision.HIGHEST)]
    convert_element_type x2 -> x0, local copies, waits for them, and re-layouts: 53.6 us -> none  [the longest x1 53.5 us: shards(): return (stacked * stack_scale).astype(jnp.bfloat16)]
    pallas_call x0 -> x4, Pallas kernels: none -> 41.6 us  [the longest x1 19 us: spectra_of(): pl.pallas_call(functools.partial(spectra_kernel, bins, windows, block_len...]
    ppermute x0 -> x10, waiting for transfers between devices: none -> 31.4 us  [from_partners(): lax.ppermute(block, axis, [(i, i ^ away) for i in range(count)])]
    another operation x3 -> x0, other arithmetic: 22 us -> none
    all_gather x1 -> x0, blocking collectives: 19.3 us -> none  [shards(): every_chan = lax.all_gather(white, 'chan', axis=3, tiled=True)]
    all_to_all x1 -> x0, blocking collectives: 16.9 us -> none  [shards(): lax.all_to_all(every_chan, 'tm', split_axis=3, concat_axis=0, tiled=True)]
    unnamed x6 -> x18, local copies, waits for them, and re-layouts: 20.7 us -> 5.63 us
  transfers between devices with their start and end apart: 3 -> 12, of which waited for: 0 -> 7; matrix products, arithmetic and copies ran while one was open for 37% -> 0% of each run, Pallas kernels for 0% -> 0%
where the time goes in v2:
time: 102 us; the launch traced here: 101 us
  Pallas kernels  41.6 us (41%)
  waiting for transfers between devices  34.2 us (34%)
  starting transfers between devices  19.8 us (19%)
  local copies, waits for them, and re-layouts  5.63 us (6%)
    ppermute x10, waiting for transfers between devices, from_partners(): lax.ppermute(block, axis, [(i, i ^ away) for i in range(count)])  31.4 us
    pallas_call x1, Pallas kernels, spectra_of(): pl.pallas_call(functools.partial(spectra_kernel, bins, windows, block_len...  19 us
    pallas_call x1, Pallas kernels, stacks_of(): pl.pallas_call(functools.partial(stack_kernel, windows, scale, devices),...  18.5 us
    ppermute x10, starting transfers between devices, from_partners(): lax.ppermute(block, axis, [(i, i ^ away) for i in range(count)])  11.7 us
    all_to_all x1, starting transfers between devices, shards(): lax.all_to_all(every_chan, 'tm', split_axis=0, concat_axis=0, tiled=True)  6.85 us
    unnamed x18, local copies, waits for them, and re-layouts  5.63 us
    ppermute x1, waiting for transfers between devices, shifted(): return lax.ppermute(block, axis, route)  2.76 us
  transfers between devices with their start and end apart: 12, of which 7 were waited for; matrix products, arithmetic and copies ran while one was open for 0% of the time, Pallas kernels for 0%

profile of v2, /device:TPU:0, one launch (start us, length us, event | category | flops | bytes accessed | tf_op | source)
XLA Modules:
  0.0 101.2 jit_solution(9025194042320069789)
XLA Ops:
  0.0 0.7 copy-done.2
  0.7 0.7 copy-done.3
  1.3 0.7 copy-done.4
  2.0 19.0 %band_spectra.1 = (f32[88,1024]{1,0:T(8,128)S(1)}, bf16[96,1024]{1,0:T(8,128)(2,1)S(1)}) custom-call(s32[16]{0:T(128)S(1)} %copy-done.3, s32[20]{0:T(128)S(1)} %copy-done.4, s32[1,1024]{1,0:T(1,128)S(1)} %bitcast.2, bf16[15000,1024]{1,0:T(8,128)(2,1)} %bitcast.3, bf16[15000,1024]{1,0:T(8,128)(2,1)} %bitcast.4), custom_call_target="tpu_custom_call" | custom-call | flops 4915200000 | bytes 30720000 | tf_op jit(solution)/shard_map/band_spectra/pallas_call | solution.py:248
  21.1 0.7 copy-done.1
  21.8 1.3 %collective-permute-start = (bf16[96,1024]{1,0:T(8,128)(2,1)S(1)}, bf16[96,1024]{1,0:T(8,128)(2,1)S(1)}, u32[]{:S(2)}, u32[]{:S(2)}) collective-permute-start(bf16[96,1024]{1,0:T(8,128)(2,1)S(1)} %get-tuple-element.8), channel_id=1, source_target_pairs={{1,0},{2,1},{3,2},{4,3},{5,4},{6,5},{7,6},{9,8},{10,9},{11,10},{12... | collective-permute-start | bytes 589832 | tf_op jit(solution)/shard_map/ppermute | solution.py:25
  23.1 2.8 %collective-permute-done.more_ref = bf16[96,1024]{1,0:T(8,128)(2,1)S(1)} collective-permute-done((bf16[96,1024]{1,0:T(8,128)(2,1)S(1)}, bf16[96,1024]{1,0:T(8,128)(2,1)S(1)}, u32[]{:S(2)}, u32[]{:S(2)}) %collective-permute-start) | collective-permute-done | bytes 196640 | tf_op jit(solution)/shard_map/ppermute | solution.py:25
  25.8 0.7 copy-done.5
  26.5 1.9 %whiten.1.refs_0_ = bf16[2,80,512]{2,1,0:T(8,128)(2,1)} custom-call(f32[88,1024]{1,0:T(8,128)} %copy-done.1, bf16[96,1024]{1,0:T(8,128)(2,1)} %copy-done.5), custom_call_target="tpu_custom_call" | custom-call | tf_op jit(solution)/shard_map/whiten/pallas_call | solution.py:309
  28.5 4.4 %collective-permute-start.3 = (bf16[2,80,512]{2,1,0:T(8,128)(2,1)}, bf16[2,80,512]{2,1,0:T(8,128)(2,1)S(1)}, u32[]{:S(2)}, u32[]{:S(2)}) collective-permute-start(bf16[2,80,512]{2,1,0:T(8,128)(2,1)} %whiten.1.refs_0_), channel_id=1, source_target_pairs={{0,24},{8,16},{16,8},{24,0},{1,25},{9,17},{17,9},{25,1},{2,26},{10... | collective-permute-start | bytes 491528 | tf_op jit(solution)/shard_map/ppermute | solution.py:413
  33.5 3.0 %collective-permute-done.3.refs_3_ = bf16[2,80,512]{2,1,0:T(8,128)(2,1)S(1)} collective-permute-done((bf16[2,80,512]{2,1,0:T(8,128)(2,1)}, bf16[2,80,512]{2,1,0:T(8,128)(2,1)S(1)}, u32[]{:S(2)}, u32[]{:S(2)}) %collective-permute-start.3) | collective-permute-done | bytes 163872 | tf_op jit(solution)/shard_map/ppermute | solution.py:413
  36.5 10.8 %collective-permute-done.2.refs_2_ = bf16[2,80,512]{2,1,0:T(8,128)(2,1)S(1)} collective-permute-done((bf16[2,80,512]{2,1,0:T(8,128)(2,1)}, bf16[2,80,512]{2,1,0:T(8,128)(2,1)S(1)}, u32[]{:S(2)}, u32[]{:S(2)}) %collective-permute-start.2) | collective-permute-done | bytes 163872 | tf_op jit(solution)/shard_map/ppermute | solution.py:413
  47.9 0.7 copy-done.8
  48.6 2.0 %order_blocks.1 = bf16[8,80,512]{2,1,0:T(8,128)(2,1)} custom-call(bf16[2,80,512]{2,1,0:T(8,128)(2,1)} %whiten.1.refs_0_, bf16[2,80,512]{2,1,0:T(8,128)(2,1)} %copy-done.8, bf16[2,80,512]{2,1,0:T(8,128)(2,1)} %copy-done.7, bf16[2,80,512]{2,1,0:T(8,128)(2,1)} %copy-done.6), custom_call_target="tpu_custom_call" | custom-call | tf_op jit(solution)/shard_map/order_blocks/pallas_call | solution.py:326
  50.6 6.8 %all-to-all-start = ((bf16[8,80,512]{2,1,0:T(8,128)(2,1)}), bf16[8,80,512]{2,1,0:T(8,128)(2,1)S(1)}, u32[]{:S(2)}, u32[]{:S(2)}) async-start(bf16[8,80,512]{2,1,0:T(8,128)(2,1)} %order_blocks.1), calls=%async_computation | async-start | bytes 1310720 | tf_op jit(solution)/shard_map/all_to_all | solution.py:427
  57.5 2.7 %collective-permute-start.10 = (bf16[2,80,512]{2,1,0:T(8,128)(2,1)}, bf16[2,80,512]{2,1,0:T(8,128)(2,1)S(1)}, u32[]{:S(2)}, u32[]{:S(2)}) collective-permute-start(bf16[2,80,512]{2,1,0:T(8,128)(2,1)} %whiten.1.refs_0_), channel_id=1, source_target_pairs={{0,7},{1,6},{2,5},{3,4},{4,3},{5,2},{6,1},{7,0},{8,15},{9,14},{10,... | collective-permute-start | bytes 491528 | tf_op jit(solution)/shard_map/ppermute | solution.py:413
  60.5 1.6 %collective-permute-start.8 = (bf16[2,80,512]{2,1,0:T(8,128)(2,1)}, bf16[2,80,512]{2,1,0:T(8,128)(2,1)S(1)}, u32[]{:S(2)}, u32[]{:S(2)}) collective-permute-start(bf16[2,80,512]{2,1,0:T(8,128)(2,1)} %whiten.1.refs_0_), channel_id=1, source_target_pairs={{0,5},{1,4},{2,7},{3,6},{4,1},{5,0},{6,3},{7,2},{8,13},{9,12},{10,... | collective-permute-start | bytes 491528 | tf_op jit(solution)/shard_map/ppermute | solution.py:413
  62.3 1.3 %collective-permute-start.6 = (bf16[2,80,512]{2,1,0:T(8,128)(2,1)}, bf16[2,80,512]{2,1,0:T(8,128)(2,1)S(1)}, u32[]{:S(2)}, u32[]{:S(2)}) collective-permute-start(bf16[2,80,512]{2,1,0:T(8,128)(2,1)} %whiten.1.refs_0_), channel_id=1, source_target_pairs={{0,3},{1,2},{2,1},{3,0},{4,7},{5,6},{6,5},{7,4},{8,11},{9,10},{10,... | collective-permute-start | bytes 491528 | tf_op jit(solution)/shard_map/ppermute | solution.py:413
  63.6 8.1 %collective-permute-done.10.refs_7_ = bf16[2,80,512]{2,1,0:T(8,128)(2,1)S(1)} collective-permute-done((bf16[2,80,512]{2,1,0:T(8,128)(2,1)}, bf16[2,80,512]{2,1,0:T(8,128)(2,1)S(1)}, u32[]{:S(2)}, u32[]{:S(2)}) %collective-permute-start.10) | collective-permute-done | bytes 163872 | tf_op jit(solution)/shard_map/ppermute | solution.py:413
  72.3 3.9 %collective-permute-done.9.refs_6_ = bf16[2,80,512]{2,1,0:T(8,128)(2,1)S(1)} collective-permute-done((bf16[2,80,512]{2,1,0:T(8,128)(2,1)}, bf16[2,80,512]{2,1,0:T(8,128)(2,1)S(1)}, u32[]{:S(2)}, u32[]{:S(2)}) %collective-permute-start.9) | collective-permute-done | bytes 163872 | tf_op jit(solution)/shard_map/ppermute | solution.py:413
  76.2 1.5 %collective-permute-done.8.refs_5_ = bf16[2,80,512]{2,1,0:T(8,128)(2,1)S(1)} collective-permute-done((bf16[2,80,512]{2,1,0:T(8,128)(2,1)}, bf16[2,80,512]{2,1,0:T(8,128)(2,1)S(1)}, u32[]{:S(2)}, u32[]{:S(2)}) %collective-permute-start.8) | collective-permute-done | bytes 163872 | tf_op jit(solution)/shard_map/ppermute | solution.py:413
  77.6 4.2 %collective-permute-done.7.refs_4_ = bf16[2,80,512]{2,1,0:T(8,128)(2,1)S(1)} collective-permute-done((bf16[2,80,512]{2,1,0:T(8,128)(2,1)}, bf16[2,80,512]{2,1,0:T(8,128)(2,1)S(1)}, u32[]{:S(2)}, u32[]{:S(2)}) %collective-permute-start.7) | collective-permute-done | bytes 163872 | tf_op jit(solution)/shard_map/ppermute | solution.py:413
  81.8 0.9 copy-done
  82.7 18.5 %stack_products.1 = bf16[2,20,512,1024]{3,2,1,0:T(8,128)(2,1)} custom-call(bf16[8,80,512]{2,1,0:T(8,128)(2,1)S(1)} %all-to-all-done.cols_ref, bf16[2,80,512]{2,1,0:T(8,128)(2,1)S(1)} %copy-done, bf16[2,80,512]{2,1,0:T(8,128)(2,1)S(1)} %collective-permute-done.4.refs_1_, bf16[2,80,512]{2,1,0:T(8,128)(2,1)S(1)} %collective-permute-done.5.refs_2_, ...), custom_call_target="tpu_custom_call" | custom-call | flops 5368709120 | bytes 41943040 | tf_op jit(solution)/shard_map/stack_products/pallas_call | solution.py:386
  (22 shorter events, 2.4 us)
Async XLA Ops:
  0.0 0.7 copy-start.2
  0.7 0.7 copy-start.3
  1.3 0.7 copy-start.4
  21.1 0.7 copy-start.1
  21.8 4.1 %collective-permute-start = (bf16[96,1024]{1,0:T(8,128)(2,1)S(1)}, bf16[96,1024]{1,0:T(8,128)(2,1)S(1)}, u32[]{:S(2)}, u32[]{:S(2)}) collective-permute-start(bf16[96,1024]{1,0:T(8,128)(2,1)S(1)} %get-tuple-element.8), channel_id=1, source_target_pairs={{1,0},{2,1},{3,2},{4,3},{5,4},{6,5},{7,6},{9,8},{10,9},{11,10},{12... | collective-permute-start | bytes 589832 | tf_op jit(solution)/shard_map/ppermute | solution.py:25
  25.8 0.7 copy-start.5
  28.5 8.0 %collective-permute-start.3 = (bf16[2,80,512]{2,1,0:T(8,128)(2,1)}, bf16[2,80,512]{2,1,0:T(8,128)(2,1)S(1)}, u32[]{:S(2)}, u32[]{:S(2)}) collective-permute-start(bf16[2,80,512]{2,1,0:T(8,128)(2,1)} %whiten.1.refs_0_), channel_id=1, source_target_pairs={{0,24},{8,16},{16,8},{24,0},{1,25},{9,17},{17,9},{25,1},{2,26},{10... | collective-permute-start | bytes 491528 | tf_op jit(solution)/shard_map/ppermute | solution.py:413
  32.9 14.4 %collective-permute-start.2 = (bf16[2,80,512]{2,1,0:T(8,128)(2,1)}, bf16[2,80,512]{2,1,0:T(8,128)(2,1)S(1)}, u32[]{:S(2)}, u32[]{:S(2)}) collective-permute-start(bf16[2,80,512]{2,1,0:T(8,128)(2,1)} %whiten.1.refs_0_), channel_id=1, source_target_pairs={{0,16},{8,24},{16,0},{24,8},{1,17},{9,25},{17,1},{25,9},{2,18},{10... | collective-permute-start | bytes 491528 | tf_op jit(solution)/shard_map/ppermute | solution.py:413
  32.9 14.4 %collective-permute-start.1 = (bf16[2,80,512]{2,1,0:T(8,128)(2,1)}, bf16[2,80,512]{2,1,0:T(8,128)(2,1)S(1)}, u32[]{:S(2)}, u32[]{:S(2)}) collective-permute-start(bf16[2,80,512]{2,1,0:T(8,128)(2,1)} %whiten.1.refs_0_), channel_id=1, source_target_pairs={{0,8},{8,0},{16,24},{24,16},{1,9},{9,1},{17,25},{25,17},{2,10},{10... | collective-permute-start | bytes 491528 | tf_op jit(solution)/shard_map/ppermute | solution.py:413
  36.5 10.8 %copy-start.6 = (bf16[2,80,512]{2,1,0:T(8,128)(2,1)}, bf16[2,80,512]{2,1,0:T(8,128)(2,1)S(1)}, u32[]{:S(2)}) copy-start(bf16[2,80,512]{2,1,0:T(8,128)(2,1)S(1)} %collective-permute-done.3.refs_3_) | copy-start | bytes 491524
  47.3 0.7 copy-start.7
  47.9 0.7 copy-start.8
  50.6 31.2 %all-to-all-start = ((bf16[8,80,512]{2,1,0:T(8,128)(2,1)}), bf16[8,80,512]{2,1,0:T(8,128)(2,1)S(1)}, u32[]{:S(2)}, u32[]{:S(2)}) async-start(bf16[8,80,512]{2,1,0:T(8,128)(2,1)} %order_blocks.1), calls=%async_computation | async-start | bytes 1310720 | tf_op jit(solution)/shard_map/all_to_all | solution.py:427
  57.5 14.3 %collective-permute-start.10 = (bf16[2,80,512]{2,1,0:T(8,128)(2,1)}, bf16[2,80,512]{2,1,0:T(8,128)(2,1)S(1)}, u32[]{:S(2)}, u32[]{:S(2)}) collective-permute-start(bf16[2,80,512]{2,1,0:T(8,128)(2,1)} %whiten.1.refs_0_), channel_id=1, source_target_pairs={{0,7},{1,6},{2,5},{3,4},{4,3},{5,2},{6,1},{7,0},{8,15},{9,14},{10,... | collective-permute-start | bytes 491528 | tf_op jit(solution)/shard_map/ppermute | solution.py:413
  60.1 16.0 %collective-permute-start.9 = (bf16[2,80,512]{2,1,0:T(8,128)(2,1)}, bf16[2,80,512]{2,1,0:T(8,128)(2,1)S(1)}, u32[]{:S(2)}, u32[]{:S(2)}) collective-permute-start(bf16[2,80,512]{2,1,0:T(8,128)(2,1)} %whiten.1.refs_0_), channel_id=1, source_target_pairs={{0,6},{1,7},{2,4},{3,5},{4,2},{5,3},{6,0},{7,1},{8,14},{9,15},{10,... | collective-permute-start | bytes 491528 | tf_op jit(solution)/shard_map/ppermute | solution.py:413
  60.5 17.1 %collective-permute-start.8 = (bf16[2,80,512]{2,1,0:T(8,128)(2,1)}, bf16[2,80,512]{2,1,0:T(8,128)(2,1)S(1)}, u32[]{:S(2)}, u32[]{:S(2)}) collective-permute-start(bf16[2,80,512]{2,1,0:T(8,128)(2,1)} %whiten.1.refs_0_), channel_id=1, source_target_pairs={{0,5},{1,4},{2,7},{3,6},{4,1},{5,0},{6,3},{7,2},{8,13},{9,12},{10,... | collective-permute-start | bytes 491528 | tf_op jit(solution)/shard_map/ppermute | solution.py:413
  62.1 19.7 %collective-permute-start.7 = (bf16[2,80,512]{2,1,0:T(8,128)(2,1)}, bf16[2,80,512]{2,1,0:T(8,128)(2,1)S(1)}, u32[]{:S(2)}, u32[]{:S(2)}) collective-permute-start(bf16[2,80,512]{2,1,0:T(8,128)(2,1)} %whiten.1.refs_0_), channel_id=1, source_target_pairs={{0,4},{1,5},{2,6},{3,7},{4,0},{5,1},{6,2},{7,3},{8,12},{9,13},{10,... | collective-permute-start | bytes 491528 | tf_op jit(solution)/shard_map/ppermute | solution.py:413
  62.3 19.5 %collective-permute-start.6 = (bf16[2,80,512]{2,1,0:T(8,128)(2,1)}, bf16[2,80,512]{2,1,0:T(8,128)(2,1)S(1)}, u32[]{:S(2)}, u32[]{:S(2)}) collective-permute-start(bf16[2,80,512]{2,1,0:T(8,128)(2,1)} %whiten.1.refs_0_), channel_id=1, source_target_pairs={{0,3},{1,2},{2,1},{3,0},{4,7},{5,6},{6,5},{7,4},{8,11},{9,10},{10,... | collective-permute-start | bytes 491528 | tf_op jit(solution)/shard_map/ppermute | solution.py:413
  71.7 10.1 %collective-permute-start.5 = (bf16[2,80,512]{2,1,0:T(8,128)(2,1)}, bf16[2,80,512]{2,1,0:T(8,128)(2,1)S(1)}, u32[]{:S(2)}, u32[]{:S(2)}) collective-permute-start(bf16[2,80,512]{2,1,0:T(8,128)(2,1)} %whiten.1.refs_0_), channel_id=1, source_target_pairs={{0,2},{1,3},{2,0},{3,1},{4,6},{5,7},{6,4},{7,5},{8,10},{9,11},{10,... | collective-permute-start | bytes 491528 | tf_op jit(solution)/shard_map/ppermute | solution.py:413
  76.2 5.7 %collective-permute-start.4 = (bf16[2,80,512]{2,1,0:T(8,128)(2,1)}, bf16[2,80,512]{2,1,0:T(8,128)(2,1)S(1)}, u32[]{:S(2)}, u32[]{:S(2)}) collective-permute-start(bf16[2,80,512]{2,1,0:T(8,128)(2,1)} %whiten.1.refs_0_), channel_id=1, source_target_pairs={{0,1},{1,0},{2,3},{3,2},{4,5},{5,4},{6,7},{7,6},{8,9},{9,8},{10,11... | collective-permute-start | bytes 491528 | tf_op jit(solution)/shard_map/ppermute | solution.py:413
  81.8 0.9 copy-start

commit v3 on v2

--- a/solution.py
+++ b/solution.py
@@ -85,23 +85,21 @@
     for w in range(windows):
         ends += [jnp.minimum(ahead[w], behind[w]), jnp.maximum(ahead[w], behind[w])]
     segments = len(ends) + 1
-    trash = segments
-
-    def make_table(table, first, count):
-        for j in range(count):
-            moved = jnp.asarray((first + j) * DEPTH, jnp.int32).astype(F32)
-            for side in range(2):
-                limit = moved if side else -moved
-                for g in range(groups):
-                    at = slice(side * states + g * half_tile, side * states + (g + 1) * half_tile)
-                    to = side * rows + g * ROW_TILE
-                    c, s = cos_now[at, :], sin_now[at, :]
-                    inside = place[at, :] >= limit
-                    wave = jnp.concatenate([jnp.where(inside, c, 0.0), jnp.where(inside, s, 0.0)], axis=0)
-                    table[to:to + ROW_TILE, j * DEPTH:(j + 1) * DEPTH] = wave.astype(BF16)
-                    ct, st = cos_turn[at, :], sin_turn[at, :]
-                    cos_now[at, :] = c * ct + s * st
-                    sin_now[at, :] = s * ct - c * st
+
+    def make_table(table, j, index):
+        moved = jnp.asarray(index * DEPTH, jnp.int32).astype(F32)
+        for side in range(2):
+            limit = moved if side else -moved
+            for g in range(groups):
+                at = slice(side * states + g * half_tile, side * states + (g + 1) * half_tile)
+                to = side * rows + g * ROW_TILE
+                c, s = cos_now[at, :], sin_now[at, :]
+                inside = place[at, :] >= limit
+                wave = jnp.concatenate([jnp.where(inside, c, 0.0), jnp.where(inside, s, 0.0)], axis=0)
+                table[to:to + ROW_TILE, j * DEPTH:(j + 1) * DEPTH] = wave.astype(BF16)
+                ct, st = cos_turn[at, :], sin_turn[at, :]
+                cos_now[at, :] = c * ct + s * st
+                sin_now[at, :] = s * ct - c * st
 
     shape = (half_tile, DEPTH)
     row = lax.broadcasted_iota(jnp.int32, shape, 0)
@@ -123,7 +121,8 @@
             sin_now[at, :] = -sine * norm
             cos_turn[at, :], sin_turn[at, :] = cos_sin(tone * DEPTH, length)
             place[at, :] = start + (length - 1) - lane if side else lane - start
-    make_table(even, 0, PIECE // DEPTH)
+    for j in range(PIECE // DEPTH):
+        make_table(even, j, j)
     acc[...] = jnp.zeros_like(acc)
     seg[...] = jnp.zeros_like(seg)
     x_ref[bulk:, :] = jnp.zeros((padded - bulk, channels), BF16)
@@ -142,36 +141,61 @@
             jnp.logical_or, [jnp.logical_and(end >= first, end < first + size) for end in ends]
         )
 
-    def piece(base, size, table, edge):
-        tiles = size // ROW_TILE
-        if edge:
-            targets = [
-                jnp.where(has_end(base + t * ROW_TILE, ROW_TILE), trash, segment_of(base + t * ROW_TILE))
-                for t in range(tiles)
-            ]
-        else:
+    def weights_of(base, tiles, first):
+        kept = []
+        for t in range(tiles):
+            at = base + t * ROW_TILE
+            whole = jnp.logical_not(has_end(at, ROW_TILE))
+            index = segment_of(at) - first
+            kept.append([
+                jnp.where(jnp.logical_and(whole, index == k), 1.0, 0.0).astype(F32) for k in range(3)
+            ])
+        return kept
+
+    def energy(base, size, at, weights):
+        totals = [None] * (3 if weights else 1)
+        for t in range(size // ROW_TILE):
+            x = x_ref[pl.ds(base + t * ROW_TILE, ROW_TILE), at].astype(F32)
+            square = x * x
+            square = square[:half_tile] + square[half_tile:]
+            for k in range(len(totals)):
+                term = square * weights[t][k] if weights else square
+                totals[k] = term if t == 0 else totals[k] + term
+        return totals
+
+    def store(found):
+        if found is None:
+            return
+        at, product, totals, target = found
+        acc[:, at] += product
+        for k, total in enumerate(totals):
+            seg[target + k, :, at] += total
+
+    def pieces(parts, edge):
+        held = None
+        for base, size, table, later, tile, count in parts:
             target = segment_of(base)
-        for at in columns:
-            block = x_ref[pl.ds(base, size), at]
-            acc[:, at] += jnp.dot(table[:, :size], block, preferred_element_type=F32)
-            total = None
-            for t in range(tiles):
-                x = x_ref[pl.ds(base + t * ROW_TILE, ROW_TILE), at].astype(F32)
-                square = x * x
-                square = square[:half_tile] + square[half_tile:]
-                if edge:
-                    seg[targets[t], :, at] += square
-                else:
-                    total = square if total is None else total + square
-            if not edge:
-                seg[target, :, at] += total
+            weights = weights_of(base, size // ROW_TILE, target) if edge else None
+            for n, at in enumerate(columns):
+                product = jnp.dot(table[:, :size], x_ref[pl.ds(base, size), at], preferred_element_type=F32)
+                totals = energy(base, size, at, weights)
+                store(held)
+                held = at, product, totals, target
+                if later is not None and n < count:
+                    make_table(later, n, tile + n)
+            if later is not None:
+                for n in range(len(columns), count):
+                    make_table(later, n, tile + n)
+        store(held)
 
     def body(i, edge):
         base = pl.multiple_of(i * STEP, STEP)
-        make_table(odd, i * (STEP // DEPTH) + PIECE // DEPTH, PIECE // DEPTH)
-        piece(base, PIECE, even, edge)
-        make_table(even, (i + 1) * (STEP // DEPTH), PIECE // DEPTH)
-        piece(base + PIECE, PIECE, odd, edge)
+        tile = i * (STEP // DEPTH)
+        per_piece = PIECE // DEPTH
+        pieces([
+            (base, PIECE, even, odd, tile + per_piece, per_piece),
+            (base + PIECE, PIECE, odd, even, tile + 2 * per_piece, per_piece),
+        ], edge)
 
     @pl.loop(0, steps)
     def _(i):
@@ -192,11 +216,12 @@
         if done < bulk:
             x_copy(steps).wait()
         first = min(PIECE, padded - done)
-        if padded - done > first:
-            make_table(odd, (done + first) // DEPTH, (padded - done - first) // DEPTH)
-        piece(done, first, even, False)
-        if padded - done > first:
-            piece(done + first, padded - done - first, odd, False)
+        rest = padded - done - first
+        tile = (done + first) // DEPTH
+        parts = [(done, first, even, odd if rest else None, tile, rest // DEPTH)]
+        if rest:
+            parts.append((done + first, rest, odd, None, 0, 0))
+        pieces(parts, False)
 
     for i, end in enumerate(ends):
         low = ends[i - 1] if i else jnp.int32(0)
@@ -263,12 +288,12 @@
             pltpu.VMEM((1, channels), jnp.int32),
             pltpu.VMEM((padded, channels), BF16),
             pltpu.VMEM((2 * rows, channels), F32),
-            pltpu.VMEM((2 * windows + 2, ROW_TILE // 2, channels), F32),
+            pltpu.VMEM((2 * windows + 3, ROW_TILE // 2, channels), F32),
             state, state, state, state, state, table, table,
             pltpu.SemaphoreType.DMA((3,)),
             pltpu.SemaphoreType.DMA((pl.cdiv(padded, STEP),)),
         ],
-        compiler_params=pltpu.CompilerParams(vmem_limit_bytes=48 * 2**20),
+        compiler_params=pltpu.CompilerParams(vmem_limit_bytes=60 * 2**20),
         cost_estimate=pl.CostEstimate(
             flops=2 * channels * block_len * 2 * rows,
             bytes_accessed=channels * block_len * 2,
@@ -278,7 +303,7 @@
     )(offsets, band_bins, dead.reshape(1, channels), samples, samples)
 
 
-def whiten_kernel(bins, windows, own_ref, more_ref, white_ref):
+def whiten_kernel(bins, windows, own_ref, more_ref, *white_refs):
     rows = bins * windows * 2
     raw = own_ref[:rows, :] + more_ref[:rows, :].astype(F32)
     extra = more_ref[rows:, :].astype(F32)
@@ -298,52 +323,40 @@
         one = alive / jnp.sqrt(jnp.maximum(level, FLOOR))
         factor = one if w == 0 else jnp.where(which == w, one, factor)
     white = (spectra * factor).astype(BF16)
-    width = white_ref.shape[2]
-    for h in range(white_ref.shape[0]):
-        white_ref[h] = white[:, h * width:(h + 1) * width]
-
-
-def whiten(own, more, bins, windows, halves):
+    for white_ref in white_refs:
+        copies, halves, _, width = white_ref.shape
+        for h in range(halves):
+            for copy in range(copies):
+                white_ref[copy, h] = white[:, h * width:(h + 1) * width]
+
+
+def whiten(own, more, bins, windows, halves, copies):
     channels = own.shape[1]
     rows = bins * windows * 2
     return pl.pallas_call(
         functools.partial(whiten_kernel, bins, windows),
-        out_shape=jax.ShapeDtypeStruct((halves, rows, channels // halves), BF16),
+        out_shape=[
+            jax.ShapeDtypeStruct((count, halves, rows, channels // halves), BF16) for count in copies
+        ],
+        compiler_params=pltpu.CompilerParams(vmem_limit_bytes=12 * 2**20),
         name="whiten",
     )(own, more)
 
 
-def order_kernel(*refs):
-    blocks, out_ref = refs[:-1], refs[-1]
-    mine = lax.axis_index("chan")
-    halves = blocks[0].shape[0]
-    for away, block in enumerate(blocks):
-        out_ref[pl.ds(jnp.bitwise_xor(mine, away) * halves, halves)] = block[...]
-
-
-def in_order(blocks):
-    halves, rows, width = blocks[0].shape
-    return pl.pallas_call(
-        order_kernel,
-        out_shape=jax.ShapeDtypeStruct((len(blocks) * halves, rows, width), BF16),
-        name="order_blocks",
-    )(*blocks)
-
-
 BINS_A_STEP = 2
 
 
 def stack_kernel(windows, scale, devices, cols_ref, *refs):
-    row_refs, out_ref, lhs, held = refs[:devices], refs[devices], refs[devices + 1], refs[devices + 2]
+    row_refs, (out_ref, lhs, held) = refs[:devices], refs[devices:]
     per_group = ROW_TILE // (2 * windows)
     per_step = out_ref.shape[1]
     step = pl.program_id(0)
     width = cols_ref.shape[2]
     depth = devices * ROW_TILE
     halves, _, span = row_refs[0].shape
+    tm = lax.axis_index("tm")
     first = step * per_step % per_group
     exact = math.frexp(scale)[0] == 0.5
-    tm = lax.axis_index("tm")
 
     @pl.when(first == 0)
     def _():
@@ -362,17 +375,23 @@
 
     channels = halves * span
     which = lax.broadcasted_iota(jnp.int32, (depth, 1), 0) % (ROW_TILE // 2) // windows
+    tall = min(DEPTH, width)
+    late = None
     for b in range(per_step):
         for n in range(0, channels, DEPTH):
             at = slice(n, min(n + DEPTH, channels))
             rhs = jnp.where(which == first + b, held[:, at], 0.0).astype(BF16)
             for part in range(2):
-                product = jnp.dot(
-                    lhs[part * width:(part + 1) * width, :], rhs, preferred_element_type=F32
-                )
-                if not exact:
-                    product = product * scale
-                out_ref[part, b, :, at] = product.astype(BF16)
+                for m in range(0, width, tall):
+                    low = part * width + m
+                    product = jnp.dot(lhs[low:low + tall, :], rhs, preferred_element_type=F32)
+                    if not exact:
+                        product = product * scale
+                    product = product.astype(BF16)
+                    if late is not None:
+                        out_ref[late[0]] = late[1]
+                    late = (part, b, slice(m, m + tall), at), product
+    out_ref[late[0]] = late[1]
 
 
 def stacks_of(cols_all, row_blocks, bins, windows):
@@ -406,26 +425,32 @@
     )(cols_all, *row_blocks)
 
 
-def from_partners(block, axis):
-    count = lax.axis_size(axis)
-    blocks = [block]
-    for away in range(1, count):
-        blocks.append(lax.ppermute(block, axis, [(i, i ^ away) for i in range(count)]))
-    return blocks
+def exchanged(blocks, axis):
+    return lax.all_to_all(blocks, axis, split_axis=0, concat_axis=0, tiled=True)
+
+
+def from_partner(block, axis, away):
+    return lax.ppermute(block, axis, [(i, i ^ away) for i in range(lax.axis_size(axis))])
 
 
 def shards(recording, offsets, band_bins, dead_flags):
     channels, block_len = recording.shape
     windows = block_len // (L // 2)
     bins = band_bins.shape[0]
-    halves = lax.axis_size("tm") // lax.axis_size("chan")
+    chan_count, tm_count = lax.axis_size("chan"), lax.axis_size("tm")
+    halves = tm_count // chan_count
     own, back = spectra_of(recording, offsets, band_bins, dead_flags, windows)
     more = shifted(back, "tm", -1)
-    white = whiten(own, more, bins, windows, halves)
-    every_chan = in_order(from_partners(white, "chan"))
-    row_blocks = from_partners(white, "tm")
-    cols_all = lax.all_to_all(every_chan, "tm", split_axis=0, concat_axis=0, tiled=True)
-    return stacks_of(cols_all, row_blocks, bins, windows)
+    white, for_chan = whiten(own, more, bins, windows, halves, (1, chan_count))
+    white = white[0]
+    row_blocks = {0: white}
+    for away in [*range(2, tm_count, 2), 1]:
+        row_blocks[away] = from_partner(white, "tm", away)
+    every_chan = exchanged(for_chan, "chan").reshape(tm_count, *for_chan.shape[2:])
+    for away in range(2, tm_count, 2):
+        row_blocks[away + 1] = from_partner(row_blocks[away], "tm", 1)
+    cols_all = exchanged(every_chan, "tm")
+    return stacks_of(cols_all, [row_blocks[i] for i in range(tm_count)], bins, windows)
 
 
 def solution(mesh):

time: 102 us -> 103 us (level)
  blocking collectives: 0 us -> 22.6 us
  waiting for transfers between devices: 34.2 us -> 19.1 us
  starting transfers between devices: 19.8 us -> 13 us
  Pallas kernels: 41.6 us -> 47.2 us
  local copies, waits for them, and re-layouts: 5.63 us -> 0.98 us
    all_to_all x0 -> x1, blocking collectives: none -> 22.6 us  [exchanged(): return lax.all_to_all(blocks, axis, split_axis=0, concat_axis=0, tiled=True)]
    ppermute x10 -> x7, waiting for transfers between devices: 31.4 us -> 14.7 us  [from_partner(): lax.ppermute(block, axis, [(i, i ^ away) for i in range(lax.axis_size(axi...]
    pallas_call x1, Pallas kernels: 19 us -> 28.4 us  [spectra_of(): pl.pallas_call(functools.partial(spectra_kernel, bins, windows, block_len...]
    ppermute x10 -> x7, starting transfers between devices: 11.7 us -> 4.23 us  [from_partner(): lax.ppermute(block, axis, [(i, i ^ away) for i in range(lax.axis_size(axi...]
    unnamed x18 -> x2, local copies, waits for them, and re-layouts: 5.63 us -> 0.98 us
    pallas_call x1 -> x0, Pallas kernels: 2.04 us -> none  [in_order(): pl.pallas_call(order_kernel, out_shape=jax.ShapeDtypeStruct((len(blocks)...]
    ppermute x1, waiting for transfers between devices: 2.76 us -> 4.44 us  [shifted(): return lax.ppermute(block, axis, route)]
    pallas_call x1, Pallas kernels: 1.94 us -> 0.28 us  [whiten(): pl.pallas_call(functools.partial(whiten_kernel, bins, windows), out_shape...]
  transfers between devices with their start and end apart: 12 -> 9, of which waited for: 7 -> 5; matrix products, arithmetic and copies ran while one was open for 0% -> 0% of each run, Pallas kernels for 0% -> 0%
where the time goes in v3:
time: 103 us
  Pallas kernels  47.2 us (46%)
  blocking collectives  22.6 us (22%)
  waiting for transfers between devices  19.1 us (19%)
  starting transfers between devices  13 us (13%)
    pallas_call x1, Pallas kernels, spectra_of(): pl.pallas_call(functools.partial(spectra_kernel, bins, windows, block_len...  28.4 us
    all_to_all x1, blocking collectives, exchanged(): return lax.all_to_all(blocks, axis, split_axis=0, concat_axis=0, tiled=True)  22.6 us
    pallas_call x1, Pallas kernels, stacks_of(): pl.pallas_call(functools.partial(stack_kernel, windows, scale, devices),...  18.5 us
    ppermute x7, waiting for transfers between devices, from_partner(): lax.ppermute(block, axis, [(i, i ^ away) for i in range(lax.axis_size(axi...  14.7 us
    all_to_all x1, starting transfers between devices, exchanged(): return lax.all_to_all(blocks, axis, split_axis=0, concat_axis=0, tiled=True)  7.43 us
    ppermute x1, waiting for transfers between devices, shifted(): return lax.ppermute(block, axis, route)  4.44 us
    ppermute x7, starting transfers between devices, from_partner(): lax.ppermute(block, axis, [(i, i ^ away) for i in range(lax.axis_size(axi...  4.23 us
  transfers between devices with their start and end apart: 9, of which 5 were waited for; matrix products, arithmetic and copies ran while one was open for 0% of the time, Pallas kernels for 0%

profile of v3, /device:TPU:0, one launch (start us, length us, event | category | flops | bytes accessed | tf_op | source)
XLA Modules:
  0.0 102.9 jit_solution(8728433907969388339)
XLA Ops:
  0.0 28.4 %band_spectra.1 = (f32[88,1024]{1,0:T(8,128)}, bf16[96,1024]{1,0:T(8,128)(2,1)}) custom-call(s32[16]{0:T(128)} %offsets_hbm.1, s32[20]{0:T(128)} %bins_hbm.1, s32[1,1024]{1,0:T(1,128)} %bitcast.11, bf16[15000,1024]{1,0:T(8,128)(2,1)} %bitcast.9, bf16[15000,1024]{1,0:T(8,128)(2,1)} %bitcast.10), custom_call_target="tpu_custom_call" | custom-call | flops 4915200000 | bytes 30720000 | tf_op jit(solution)/shard_map/band_spectra/pallas_call | solution.py:273
  28.4 1.3 %collective-permute-start = (bf16[96,1024]{1,0:T(8,128)(2,1)}, bf16[96,1024]{1,0:T(8,128)(2,1)S(1)}, u32[]{:S(2)}, u32[]{:S(2)}) collective-permute-start(bf16[96,1024]{1,0:T(8,128)(2,1)} %get-tuple-element.10), channel_id=1, source_target_pairs={{1,0},{2,1},{3,2},{4,3},{5,4},{6,5},{7,6},{9,8},{10,9},{11,10},{12... | collective-permute-start | bytes 589832 | tf_op jit(solution)/shard_map/ppermute | solution.py:25
  29.7 4.4 %collective-permute-done.more_ref = bf16[96,1024]{1,0:T(8,128)(2,1)S(1)} collective-permute-done((bf16[96,1024]{1,0:T(8,128)(2,1)}, bf16[96,1024]{1,0:T(8,128)(2,1)S(1)}, u32[]{:S(2)}, u32[]{:S(2)}) %collective-permute-start) | collective-permute-done | bytes 196640 | tf_op jit(solution)/shard_map/ppermute | solution.py:25
  34.1 0.0 copy-start
  34.1 1.0 copy-done
  35.1 0.3 whiten.1
  35.4 22.6 %all_to_all.10 = bf16[4,2,80,512]{3,2,1,0:T(8,128)(2,1)} all-to-all(bf16[4,2,80,512]{3,2,1,0:T(8,128)(2,1)S(1)} %get-tuple-element.11), channel_id=1, replica_groups=mesh['chan'=4,'tm'=8] {'chan'}, dimensions={0} | all-to-all | bytes 1310720 | tf_op jit(solution)/shard_map/all_to_all | solution.py:429
  58.0 7.4 %all-to-all-start.1 = ((bf16[8,80,512]{2,1,0:T(8,128)(2,1)}), bf16[8,80,512]{2,1,0:T(8,128)(2,1)S(1)}, u32[]{:S(2)}, u32[]{:S(2)}) async-start(bf16[8,80,512]{2,1,0:T(8,128)(2,1)} %bitcast.2), calls=%async_computation.1 | async-start | bytes 1310720 | tf_op jit(solution)/shard_map/all_to_all | solution.py:429
  65.5 2.9 %collective-permute-start.6 = (bf16[2,80,512]{2,1,0:T(8,128)(2,1)S(1)}, bf16[2,80,512]{2,1,0:T(8,128)(2,1)S(1)}, u32[]{:S(2)}, u32[]{:S(2)}) collective-permute-start(bf16[2,80,512]{2,1,0:T(8,128)(2,1)S(1)} %bitcast.4), channel_id=1, source_target_pairs={{0,6},{1,7},{2,4},{3,5},{4,2},{5,3},{6,0},{7,1},{8,14},{9,15},{10,... | collective-permute-start | bytes 491528 | tf_op jit(solution)/shard_map/ppermute | solution.py:433
  68.4 0.6 collective-permute-start.4
  69.0 0.3 collective-permute-start.2
  69.2 0.0 collective-permute-start.1
  69.2 11.4 %collective-permute-done.6.refs_6_ = bf16[2,80,512]{2,1,0:T(8,128)(2,1)S(1)} collective-permute-done((bf16[2,80,512]{2,1,0:T(8,128)(2,1)S(1)}, bf16[2,80,512]{2,1,0:T(8,128)(2,1)S(1)}, u32[]{:S(2)}, u32[]{:S(2)}) %collective-permute-start.6) | collective-permute-done | bytes 163872 | tf_op jit(solution)/shard_map/ppermute | solution.py:433
  80.7 0.0 collective-permute-start.7
  80.7 2.1 %collective-permute-done.4.refs_4_ = bf16[2,80,512]{2,1,0:T(8,128)(2,1)S(1)} collective-permute-done((bf16[2,80,512]{2,1,0:T(8,128)(2,1)S(1)}, bf16[2,80,512]{2,1,0:T(8,128)(2,1)S(1)}, u32[]{:S(2)}, u32[]{:S(2)}) %collective-permute-start.4) | collective-permute-done | bytes 163872 | tf_op jit(solution)/shard_map/ppermute | solution.py:433
  82.7 0.0 collective-permute-start.5
  82.7 0.0 collective-permute-done.2.refs_2_
  82.8 0.5 collective-permute-start.3
  83.3 0.0 collective-permute-done.1.refs_1_
  83.3 0.0 collective-permute-done.7.refs_7_
  83.3 0.9 collective-permute-done.5.refs_5_
  84.1 0.2 collective-permute-done.3.refs_3_
  84.4 0.0 all-to-all-done.1.cols_ref
  84.4 18.5 %stack_products.1 = bf16[2,20,512,1024]{3,2,1,0:T(8,128)(2,1)} custom-call(bf16[8,80,512]{2,1,0:T(8,128)(2,1)S(1)} %all-to-all-done.1.cols_ref, bf16[2,80,512]{2,1,0:T(8,128)(2,1)S(1)} %bitcast.8, bf16[2,80,512]{2,1,0:T(8,128)(2,1)S(1)} %collective-permute-done.1.refs_1_, bf16[2,80,512]{2,1,0:T(8,128)(2,1)S(1)} %collective-permute-done.2.refs_2_, ...), custom_call_target="tpu_custom_call" | custom-call | flops 5368709120 | bytes 41943040 | tf_op jit(solution)/shard_map/stack_products/pallas_call | solution.py:405
Async XLA Ops:
  28.4 5.7 %collective-permute-start = (bf16[96,1024]{1,0:T(8,128)(2,1)}, bf16[96,1024]{1,0:T(8,128)(2,1)S(1)}, u32[]{:S(2)}, u32[]{:S(2)}) collective-permute-start(bf16[96,1024]{1,0:T(8,128)(2,1)} %get-tuple-element.10), channel_id=1, source_target_pairs={{1,0},{2,1},{3,2},{4,3},{5,4},{6,5},{7,6},{9,8},{10,9},{11,10},{12... | collective-permute-start | bytes 589832 | tf_op jit(solution)/shard_map/ppermute | solution.py:25
  34.1 1.0 copy-start
  58.0 26.3 %all-to-all-start.1 = ((bf16[8,80,512]{2,1,0:T(8,128)(2,1)}), bf16[8,80,512]{2,1,0:T(8,128)(2,1)S(1)}, u32[]{:S(2)}, u32[]{:S(2)}) async-start(bf16[8,80,512]{2,1,0:T(8,128)(2,1)} %bitcast.2), calls=%async_computation.1 | async-start | bytes 1310720 | tf_op jit(solution)/shard_map/all_to_all | solution.py:429
  65.5 15.2 %collective-permute-start.6 = (bf16[2,80,512]{2,1,0:T(8,128)(2,1)S(1)}, bf16[2,80,512]{2,1,0:T(8,128)(2,1)S(1)}, u32[]{:S(2)}, u32[]{:S(2)}) collective-permute-start(bf16[2,80,512]{2,1,0:T(8,128)(2,1)S(1)} %bitcast.4), channel_id=1, source_target_pairs={{0,6},{1,7},{2,4},{3,5},{4,2},{5,3},{6,0},{7,1},{8,14},{9,15},{10,... | collective-permute-start | bytes 491528 | tf_op jit(solution)/shard_map/ppermute | solution.py:433
  68.4 14.3 %collective-permute-start.4 = (bf16[2,80,512]{2,1,0:T(8,128)(2,1)S(1)}, bf16[2,80,512]{2,1,0:T(8,128)(2,1)S(1)}, u32[]{:S(2)}, u32[]{:S(2)}) collective-permute-start(bf16[2,80,512]{2,1,0:T(8,128)(2,1)S(1)} %bitcast.5), channel_id=1, source_target_pairs={{0,4},{1,5},{2,6},{3,7},{4,0},{5,1},{6,2},{7,3},{8,12},{9,13},{10,... | collective-permute-start | bytes 491528 | tf_op jit(solution)/shard_map/ppermute | solution.py:433
  69.0 13.8 %collective-permute-start.2 = (bf16[2,80,512]{2,1,0:T(8,128)(2,1)S(1)}, bf16[2,80,512]{2,1,0:T(8,128)(2,1)S(1)}, u32[]{:S(2)}, u32[]{:S(2)}) collective-permute-start(bf16[2,80,512]{2,1,0:T(8,128)(2,1)S(1)} %bitcast.6), channel_id=1, source_target_pairs={{0,2},{1,3},{2,0},{3,1},{4,6},{5,7},{6,4},{7,5},{8,10},{9,11},{10,... | collective-permute-start | bytes 491528 | tf_op jit(solution)/shard_map/ppermute | solution.py:433
  69.2 14.0 %collective-permute-start.1 = (bf16[2,80,512]{2,1,0:T(8,128)(2,1)S(1)}, bf16[2,80,512]{2,1,0:T(8,128)(2,1)S(1)}, u32[]{:S(2)}, u32[]{:S(2)}) collective-permute-start(bf16[2,80,512]{2,1,0:T(8,128)(2,1)S(1)} %bitcast.7), channel_id=1, source_target_pairs={{0,1},{1,0},{2,3},{3,2},{4,5},{5,4},{6,7},{7,6},{8,9},{9,8},{10,11... | collective-permute-start | bytes 491528 | tf_op jit(solution)/shard_map/ppermute | solution.py:433
  80.7 2.6 %collective-permute-start.7 = (bf16[2,80,512]{2,1,0:T(8,128)(2,1)S(1)}, bf16[2,80,512]{2,1,0:T(8,128)(2,1)S(1)}, u32[]{:S(2)}, u32[]{:S(2)}) collective-permute-start(bf16[2,80,512]{2,1,0:T(8,128)(2,1)S(1)} %collective-permute-done.6.refs_6_), channel_id=1, source_target_pairs={{0,1},{1,0},{2,3},{3,2},{4,5},{5,4},{6,7},{7,6},{8,9},{9,8},{10,11... | collective-permute-start | bytes 491528 | tf_op jit(solution)/shard_map/ppermute | solution.py:433
  82.7 1.4 %collective-permute-start.5 = (bf16[2,80,512]{2,1,0:T(8,128)(2,1)S(1)}, bf16[2,80,512]{2,1,0:T(8,128)(2,1)S(1)}, u32[]{:S(2)}, u32[]{:S(2)}) collective-permute-start(bf16[2,80,512]{2,1,0:T(8,128)(2,1)S(1)} %collective-permute-done.4.refs_4_), channel_id=1, source_target_pairs={{0,1},{1,0},{2,3},{3,2},{4,5},{5,4},{6,7},{7,6},{8,9},{9,8},{10,11... | collective-permute-start | bytes 491528 | tf_op jit(solution)/shard_map/ppermute | solution.py:433
  82.8 1.6 %collective-permute-start.3 = (bf16[2,80,512]{2,1,0:T(8,128)(2,1)S(1)}, bf16[2,80,512]{2,1,0:T(8,128)(2,1)S(1)}, u32[]{:S(2)}, u32[]{:S(2)}) collective-permute-start(bf16[2,80,512]{2,1,0:T(8,128)(2,1)S(1)} %collective-permute-done.2.refs_2_), channel_id=1, source_target_pairs={{0,1},{1,0},{2,3},{3,2},{4,5},{5,4},{6,7},{7,6},{8,9},{9,8},{10,11... | collective-permute-start | bytes 491528 | tf_op jit(solution)/shard_map/ppermute | solution.py:433

commit v4 on v2

--- a/solution.py
+++ b/solution.py
@@ -14,7 +14,7 @@
 BF16 = jnp.bfloat16
 LANE = 128
 DEPTH = 256
-PIECE = 512
+PIECE = 1024
 STEP = 2 * PIECE
 ROW_TILE = 16
 
@@ -58,7 +58,6 @@
     bulk = block_len // ROW_TILE * ROW_TILE
     padded = x_ref.shape[0]
     steps = padded // STEP
-    columns = [slice(n, min(n + DEPTH, channels)) for n in range(0, channels, DEPTH)]
 
     def x_copy(i):
         size = min(STEP, bulk - i * STEP)
@@ -151,27 +150,25 @@
             ]
         else:
             target = segment_of(base)
-        for at in columns:
-            block = x_ref[pl.ds(base, size), at]
-            acc[:, at] += jnp.dot(table[:, :size], block, preferred_element_type=F32)
-            total = None
-            for t in range(tiles):
-                x = x_ref[pl.ds(base + t * ROW_TILE, ROW_TILE), at].astype(F32)
-                square = x * x
-                square = square[:half_tile] + square[half_tile:]
-                if edge:
-                    seg[targets[t], :, at] += square
-                else:
-                    total = square if total is None else total + square
-            if not edge:
-                seg[target, :, at] += total
+        acc[...] += jnp.dot(table[:, :size], x_ref[pl.ds(base, size), :], preferred_element_type=F32)
+        total = None
+        for t in range(tiles):
+            x = x_ref[pl.ds(base + t * ROW_TILE, ROW_TILE), :].astype(F32)
+            square = x * x
+            square = square[:half_tile] + square[half_tile:]
+            if edge:
+                seg[targets[t]] += square
+            else:
+                total = square if total is None else total + square
+        if not edge:
+            seg[target] += total
 
     def body(i, edge):
         base = pl.multiple_of(i * STEP, STEP)
+        piece(base, PIECE, even, edge)
         make_table(odd, i * (STEP // DEPTH) + PIECE // DEPTH, PIECE // DEPTH)
-        piece(base, PIECE, even, edge)
+        piece(base + PIECE, PIECE, odd, edge)
         make_table(even, (i + 1) * (STEP // DEPTH), PIECE // DEPTH)
-        piece(base + PIECE, PIECE, odd, edge)
 
     @pl.loop(0, steps)
     def _(i):
@@ -268,7 +265,7 @@
             pltpu.SemaphoreType.DMA((3,)),
             pltpu.SemaphoreType.DMA((pl.cdiv(padded, STEP),)),
         ],
-        compiler_params=pltpu.CompilerParams(vmem_limit_bytes=48 * 2**20),
+        compiler_params=pltpu.CompilerParams(vmem_limit_bytes=60 * 2**20),
         cost_estimate=pl.CostEstimate(
             flops=2 * channels * block_len * 2 * rows,
             bytes_accessed=channels * block_len * 2,
@@ -278,7 +275,7 @@
     )(offsets, band_bins, dead.reshape(1, channels), samples, samples)
 
 
-def whiten_kernel(bins, windows, own_ref, more_ref, white_ref):
+def whiten_kernel(bins, windows, own_ref, more_ref, *white_refs):
     rows = bins * windows * 2
     raw = own_ref[:rows, :] + more_ref[:rows, :].astype(F32)
     extra = more_ref[rows:, :].astype(F32)
@@ -298,81 +295,80 @@
         one = alive / jnp.sqrt(jnp.maximum(level, FLOOR))
         factor = one if w == 0 else jnp.where(which == w, one, factor)
     white = (spectra * factor).astype(BF16)
-    width = white_ref.shape[2]
-    for h in range(white_ref.shape[0]):
-        white_ref[h] = white[:, h * width:(h + 1) * width]
-
-
-def whiten(own, more, bins, windows, halves):
+    for white_ref in white_refs:
+        copies, halves, _, width = white_ref.shape
+        for h in range(halves):
+            for copy in range(copies):
+                white_ref[copy, h] = white[:, h * width:(h + 1) * width]
+
+
+def whiten(own, more, bins, windows, halves, copies):
     channels = own.shape[1]
     rows = bins * windows * 2
     return pl.pallas_call(
         functools.partial(whiten_kernel, bins, windows),
-        out_shape=jax.ShapeDtypeStruct((halves, rows, channels // halves), BF16),
+        out_shape=[
+            jax.ShapeDtypeStruct((count, halves, rows, channels // halves), BF16) for count in copies
+        ],
+        compiler_params=pltpu.CompilerParams(vmem_limit_bytes=12 * 2**20),
         name="whiten",
     )(own, more)
 
 
-def order_kernel(*refs):
-    blocks, out_ref = refs[:-1], refs[-1]
-    mine = lax.axis_index("chan")
-    halves = blocks[0].shape[0]
-    for away, block in enumerate(blocks):
-        out_ref[pl.ds(jnp.bitwise_xor(mine, away) * halves, halves)] = block[...]
-
-
-def in_order(blocks):
-    halves, rows, width = blocks[0].shape
-    return pl.pallas_call(
-        order_kernel,
-        out_shape=jax.ShapeDtypeStruct((len(blocks) * halves, rows, width), BF16),
-        name="order_blocks",
-    )(*blocks)
-
-
-BINS_A_STEP = 2
-
-
 def stack_kernel(windows, scale, devices, cols_ref, *refs):
-    row_refs, out_ref, lhs, held = refs[:devices], refs[devices], refs[devices + 1], refs[devices + 2]
+    row_refs, (out_hbm, lhs, held, made, sems) = refs[:devices], refs[devices:]
     per_group = ROW_TILE // (2 * windows)
-    per_step = out_ref.shape[1]
     step = pl.program_id(0)
     width = cols_ref.shape[2]
     depth = devices * ROW_TILE
     halves, _, span = row_refs[0].shape
-    first = step * per_step % per_group
+    channels = halves * span
     exact = math.frexp(scale)[0] == 0.5
     tm = lax.axis_index("tm")
 
-    @pl.when(first == 0)
-    def _():
-        cols = cols_ref[...].astype(F32)
-        if exact:
-            cols = cols * scale
-        head, tail = cols[:, :ROW_TILE // 2], cols[:, ROW_TILE // 2:]
-        straight = cols.reshape(depth, width)
-        turned = jnp.concatenate([-tail, head], axis=1).reshape(depth, width)
-        lhs[:width, :] = straight.T.astype(BF16)
-        lhs[width:, :] = turned.T.astype(BF16)
-        for away in range(devices):
-            to = pl.multiple_of(jnp.bitwise_xor(tm, away) * ROW_TILE, ROW_TILE)
-            for h in range(halves):
-                held[pl.ds(to, ROW_TILE), h * span:(h + 1) * span] = row_refs[away][h].astype(F32)
-
-    channels = halves * span
+    cols = cols_ref[...].astype(F32)
+    if exact:
+        cols = cols * scale
+    head, tail = cols[:, :ROW_TILE // 2], cols[:, ROW_TILE // 2:]
+    straight = cols.reshape(depth, width)
+    turned = jnp.concatenate([-tail, head], axis=1).reshape(depth, width)
+    lhs[:width, :] = straight.T.astype(BF16)
+    lhs[width:, :] = turned.T.astype(BF16)
+    for away in range(devices):
+        to = pl.multiple_of(jnp.bitwise_xor(tm, away) * ROW_TILE, ROW_TILE)
+        for h in range(halves):
+            held[pl.ds(to, ROW_TILE), h * span:(h + 1) * span] = row_refs[away][h].astype(F32)
+
+    def out_copy(slot, part, bin_index):
+        return pltpu.make_async_copy(made.at[slot], out_hbm.at[part, bin_index], sems.at[slot])
+
     which = lax.broadcasted_iota(jnp.int32, (depth, 1), 0) % (ROW_TILE // 2) // windows
-    for b in range(per_step):
+    for b in range(per_group):
+        for part in range(2):
+            slot = 2 * b + part
+
+            @pl.when(step > 0)
+            def _():
+                out_copy(slot, part, (step - 1) * per_group + b).wait()
+
         for n in range(0, channels, DEPTH):
             at = slice(n, min(n + DEPTH, channels))
-            rhs = jnp.where(which == first + b, held[:, at], 0.0).astype(BF16)
+            rhs = jnp.where(which == b, held[:, at], 0.0).astype(BF16)
             for part in range(2):
                 product = jnp.dot(
                     lhs[part * width:(part + 1) * width, :], rhs, preferred_element_type=F32
                 )
                 if not exact:
                     product = product * scale
-                out_ref[part, b, :, at] = product.astype(BF16)
+                made[2 * b + part, :, at] = product.astype(BF16)
+        for part in range(2):
+            out_copy(2 * b + part, part, step * per_group + b).start()
+
+    @pl.when(step == pl.num_programs(0) - 1)
+    def _():
+        for b in range(per_group):
+            for part in range(2):
+                out_copy(2 * b + part, part, step * per_group + b).wait()
 
 
 def stacks_of(cols_all, row_blocks, bins, windows):
@@ -382,17 +378,18 @@
     per_group = ROW_TILE // (2 * windows)
     scale = 1.0 / math.sqrt(windows * devices)
     channels = halves * span
-    group = lambda i: i * BINS_A_STEP // per_group
     return pl.pallas_call(
         functools.partial(stack_kernel, windows, scale, devices),
         out_shape=jax.ShapeDtypeStruct((2, bins, width, channels), BF16),
-        grid=(bins // BINS_A_STEP,),
-        in_specs=[pl.BlockSpec((devices, ROW_TILE, width), lambda i: (0, group(i), 0))]
-        + [pl.BlockSpec((halves, ROW_TILE, span), lambda i: (0, group(i), 0))] * devices,
-        out_specs=pl.BlockSpec((2, BINS_A_STEP, width, channels), lambda i: (0, i, 0, 0)),
+        grid=(bins // per_group,),
+        in_specs=[pl.BlockSpec((devices, ROW_TILE, width), lambda i: (0, i, 0))]
+        + [pl.BlockSpec((halves, ROW_TILE, span), lambda i: (0, i, 0))] * devices,
+        out_specs=pl.BlockSpec(memory_space=pltpu.HBM),
         scratch_shapes=[
             pltpu.VMEM((2 * width, devices * ROW_TILE), BF16),
             pltpu.VMEM((devices * ROW_TILE, channels), F32),
+            pltpu.VMEM((2 * per_group, width, channels), BF16),
+            pltpu.SemaphoreType.DMA((2 * per_group,)),
         ],
         compiler_params=pltpu.CompilerParams(
             dimension_semantics=("arbitrary",), vmem_limit_bytes=40 * 2**20
@@ -406,26 +403,44 @@
     )(cols_all, *row_blocks)
 
 
-def from_partners(block, axis):
-    count = lax.axis_size(axis)
-    blocks = [block]
-    for away in range(1, count):
-        blocks.append(lax.ppermute(block, axis, [(i, i ^ away) for i in range(count)]))
-    return blocks
+def after(block, *others):
+    return pl.pallas_call(
+        lambda *refs: None,
+        out_shape=jax.ShapeDtypeStruct(block.shape, block.dtype),
+        in_specs=[pl.BlockSpec(memory_space=pl.ANY)] * (1 + len(others)),
+        out_specs=pl.BlockSpec(memory_space=pl.ANY),
+        input_output_aliases={0: 0},
+        name="after",
+    )(block, *others)
+
+
+def exchanged(blocks, axis):
+    return lax.all_to_all(blocks, axis, split_axis=0, concat_axis=0, tiled=True)
+
+
+def from_partner(block, axis, away):
+    return lax.ppermute(block, axis, [(i, i ^ away) for i in range(lax.axis_size(axis))])
 
 
 def shards(recording, offsets, band_bins, dead_flags):
     channels, block_len = recording.shape
     windows = block_len // (L // 2)
     bins = band_bins.shape[0]
-    halves = lax.axis_size("tm") // lax.axis_size("chan")
+    chan_count, tm_count = lax.axis_size("chan"), lax.axis_size("tm")
+    halves = tm_count // chan_count
     own, back = spectra_of(recording, offsets, band_bins, dead_flags, windows)
     more = shifted(back, "tm", -1)
-    white = whiten(own, more, bins, windows, halves)
-    every_chan = in_order(from_partners(white, "chan"))
-    row_blocks = from_partners(white, "tm")
-    cols_all = lax.all_to_all(every_chan, "tm", split_axis=0, concat_axis=0, tiled=True)
-    return stacks_of(cols_all, row_blocks, bins, windows)
+    white, for_chan = whiten(own, more, bins, windows, halves, (1, chan_count))
+    white = white[0]
+    row_blocks = {0: white}
+    for away in [*range(2, tm_count, 2), 1]:
+        row_blocks[away] = from_partner(white, "tm", away)
+    every_chan = exchanged(for_chan, "chan").reshape(tm_count, *for_chan.shape[2:])
+    every_chan = after(every_chan, *[row_blocks[away] for away in range(2, tm_count, 2)])
+    for away in range(2, tm_count, 2):
+        row_blocks[away + 1] = from_partner(row_blocks[away], "tm", 1)
+    cols_all = exchanged(every_chan, "tm")
+    return stacks_of(cols_all, [row_blocks[i] for i in range(tm_count)], bins, windows)
 
 
 def solution(mesh):

time: 102 us -> 94.7 us (0.928)
  waiting for transfers between devices: 34.2 us -> 23.2 us
  starting transfers between devices: 19.8 us -> 22.4 us
  Pallas kernels: 41.6 us -> 43.7 us
  local copies, waits for them, and re-layouts: 5.63 us -> 4.57 us
    ppermute x10 -> x7, waiting for transfers between devices: 31.4 us -> 9.86 us  [from_partner(): lax.ppermute(block, axis, [(i, i ^ away) for i in range(lax.axis_size(axi...]
    all_to_all x1 -> x2, waiting for transfers between devices: 0.01 us -> 11.1 us  [exchanged(): return lax.all_to_all(blocks, axis, split_axis=0, concat_axis=0, tiled=True)]
    pallas_call x1, Pallas kernels: 19 us -> 26.1 us  [spectra_of(): pl.pallas_call(functools.partial(spectra_kernel, bins, windows, block_len...]
    all_to_all x1 -> x2, starting transfers between devices: 6.85 us -> 13.6 us  [exchanged(): return lax.all_to_all(blocks, axis, split_axis=0, concat_axis=0, tiled=True)]
    ppermute x10 -> x7, starting transfers between devices: 11.7 us -> 7.49 us  [from_partner(): lax.ppermute(block, axis, [(i, i ^ away) for i in range(lax.axis_size(axi...]
    pallas_call x1, Pallas kernels: 18.5 us -> 16.5 us  [stacks_of(): pl.pallas_call(functools.partial(stack_kernel, windows, scale, devices),...]
    pallas_call x1, Pallas kernels: 2.04 us -> 0.01 us  [after(): pl.pallas_call(lambda *refs: None, out_shape=jax.ShapeDtypeStruct(block.s...]
    unnamed x18 -> x16, local copies, waits for them, and re-layouts: 5.63 us -> 4.57 us
  transfers between devices with their start and end apart: 12 -> 10, of which waited for: 7 -> 10; matrix products, arithmetic and copies ran while one was open for 0% -> 0% of each run, Pallas kernels for 0% -> 0%
where the time goes in v4:
time: 94.7 us; the launch traced here: 94 us
  Pallas kernels  43.7 us (46%)
  waiting for transfers between devices  23.2 us (24%)
  starting transfers between devices  22.4 us (24%)
  local copies, waits for them, and re-layouts  4.57 us (5%)
    pallas_call x1, Pallas kernels, spectra_of(): pl.pallas_call(functools.partial(spectra_kernel, bins, windows, block_len...  26.1 us
    pallas_call x1, Pallas kernels, stacks_of(): pl.pallas_call(functools.partial(stack_kernel, windows, scale, devices),...  16.5 us
    all_to_all x2, starting transfers between devices, exchanged(): return lax.all_to_all(blocks, axis, split_axis=0, concat_axis=0, tiled=True)  13.6 us
    all_to_all x2, waiting for transfers between devices, exchanged(): return lax.all_to_all(blocks, axis, split_axis=0, concat_axis=0, tiled=True)  11.1 us
    ppermute x7, waiting for transfers between devices, from_partner(): lax.ppermute(block, axis, [(i, i ^ away) for i in range(lax.axis_size(axi...  9.86 us
    ppermute x7, starting transfers between devices, from_partner(): lax.ppermute(block, axis, [(i, i ^ away) for i in range(lax.axis_size(axi...  7.49 us
    unnamed x16, local copies, waits for them, and re-layouts  4.57 us
    ppermute x1, waiting for transfers between devices, shifted(): return lax.ppermute(block, axis, route)  2.25 us
  transfers between devices with their start and end apart: 10, of which 10 were waited for; matrix products, arithmetic and copies ran while one was open for 0% of the time, Pallas kernels for 0%

profile of v4, /device:TPU:0, one launch (start us, length us, event | category | flops | bytes accessed | tf_op | source)
XLA Modules:
  0.0 94.0 jit_solution(15639628780965515866)
XLA Ops:
  0.0 26.1 %band_spectra.1 = (f32[88,1024]{1,0:T(8,128)}, bf16[96,1024]{1,0:T(8,128)(2,1)}) custom-call(s32[16]{0:T(128)} %offsets_hbm.1, s32[20]{0:T(128)} %bins_hbm.1, s32[1,1024]{1,0:T(1,128)} %bitcast.12, bf16[15000,1024]{1,0:T(8,128)(2,1)} %bitcast.9, bf16[15000,1024]{1,0:T(8,128)(2,1)} %bitcast.10), custom_call_target="tpu_custom_call" | custom-call | flops 4915200000 | bytes 30720000 | tf_op jit(solution)/shard_map/band_spectra/pallas_call | solution.py:245
  26.1 1.3 %collective-permute-start = (bf16[96,1024]{1,0:T(8,128)(2,1)}, bf16[96,1024]{1,0:T(8,128)(2,1)S(1)}, u32[]{:S(2)}, u32[]{:S(2)}) collective-permute-start(bf16[96,1024]{1,0:T(8,128)(2,1)} %get-tuple-element.10), channel_id=1, source_target_pairs={{1,0},{2,1},{3,2},{4,3},{5,4},{6,5},{7,6},{9,8},{10,9},{11,10},{12... | collective-permute-start | bytes 589832 | tf_op jit(solution)/shard_map/ppermute | solution.py:25
  27.4 2.2 %collective-permute-done.more_ref = bf16[96,1024]{1,0:T(8,128)(2,1)S(1)} collective-permute-done((bf16[96,1024]{1,0:T(8,128)(2,1)}, bf16[96,1024]{1,0:T(8,128)(2,1)S(1)}, u32[]{:S(2)}, u32[]{:S(2)}) %collective-permute-start) | collective-permute-done | bytes 196640 | tf_op jit(solution)/shard_map/ppermute | solution.py:25
  29.7 1.0 %copy-done.6 = f32[88,1024]{1,0:T(8,128)S(1)} copy-done((f32[88,1024]{1,0:T(8,128)S(1)}, f32[88,1024]{1,0:T(8,128)}, u32[]{:S(2)}) %copy-start.6) | copy-done | bytes 360472
  30.6 1.1 %whiten.1 = (bf16[1,2,80,512]{3,2,1,0:T(8,128)(2,1)S(1)}, bf16[4,2,80,512]{3,2,1,0:T(8,128)(2,1)}) custom-call(f32[88,1024]{1,0:T(8,128)S(1)} %copy-done.6, bf16[96,1024]{1,0:T(8,128)(2,1)S(1)} %collective-permute-done.more_ref), custom_call_target="tpu_custom_call" | custom-call | tf_op jit(solution)/shard_map/whiten/pallas_call | solution.py:308
  31.8 6.3 %all-to-all-start = ((bf16[4,2,80,512]{3,2,1,0:T(8,128)(2,1)}), bf16[4,2,80,512]{3,2,1,0:T(8,128)(2,1)S(1)}, u32[]{:S(2)}, u32[]{:S(2)}) async-start(bf16[4,2,80,512]{3,2,1,0:T(8,128)(2,1)} %get-tuple-element.11), calls=%async_computation | async-start | bytes 1310720 | tf_op jit(solution)/shard_map/all_to_all | solution.py:418
  38.1 5.9 %collective-permute-start.3 = (bf16[2,80,512]{2,1,0:T(8,128)(2,1)S(1)}, bf16[2,80,512]{2,1,0:T(8,128)(2,1)S(1)}, u32[]{:S(2)}, u32[]{:S(2)}) collective-permute-start(bf16[2,80,512]{2,1,0:T(8,128)(2,1)S(1)} %bitcast.4), channel_id=1, source_target_pairs={{0,6},{1,7},{2,4},{3,5},{4,2},{5,3},{6,0},{7,1},{8,14},{9,15},{10,... | collective-permute-start | bytes 491528 | tf_op jit(solution)/shard_map/ppermute | solution.py:422
  43.9 0.6 collective-permute-start.1
  44.6 4.4 %collective-permute-done.3.refs_3_.refs_6_ = bf16[2,80,512]{2,1,0:T(8,128)(2,1)S(1)} collective-permute-done((bf16[2,80,512]{2,1,0:T(8,128)(2,1)S(1)}, bf16[2,80,512]{2,1,0:T(8,128)(2,1)S(1)}, u32[]{:S(2)}, u32[]{:S(2)}) %collective-permute-start.3) | collective-permute-done | bytes 163872 | tf_op jit(solution)/shard_map/ppermute | solution.py:422
  49.0 3.5 %collective-permute-done.2.refs_2_.refs_4_ = bf16[2,80,512]{2,1,0:T(8,128)(2,1)S(1)} collective-permute-done((bf16[2,80,512]{2,1,0:T(8,128)(2,1)S(1)}, bf16[2,80,512]{2,1,0:T(8,128)(2,1)S(1)}, u32[]{:S(2)}, u32[]{:S(2)}) %collective-permute-start.2) | collective-permute-done | bytes 163872 | tf_op jit(solution)/shard_map/ppermute | solution.py:422
  52.5 0.3 collective-permute-done.1.refs_1_.refs_2_
  52.8 2.6 %all-to-all-done = bf16[4,2,80,512]{3,2,1,0:T(8,128)(2,1)S(1)} async-done(((bf16[4,2,80,512]{3,2,1,0:T(8,128)(2,1)}), bf16[4,2,80,512]{3,2,1,0:T(8,128)(2,1)S(1)}, u32[]{:S(2)}, u32[]{:S(2)}) %all-to-all-start) | async-done | bytes 655392 | tf_op jit(solution)/shard_map/all_to_all | solution.py:418
  55.5 0.8 copy-done.7
  56.3 7.3 %all-to-all-start.1 = ((bf16[8,80,512]{2,1,0:T(8,128)(2,1)}), bf16[8,80,512]{2,1,0:T(8,128)(2,1)S(1)}, u32[]{:S(2)}, u32[]{:S(2)}) async-start(bf16[8,80,512]{2,1,0:T(8,128)(2,1)} %after.1), calls=%async_computation.1 | async-start | bytes 1310720 | tf_op jit(solution)/shard_map/all_to_all | solution.py:418
  63.6 0.5 collective-permute-start.4
  64.1 0.5 collective-permute-start.6
  64.6 0.7 collective-permute-done.4.refs_1_
  65.3 0.4 collective-permute-done.7.refs_7_
  65.9 0.3 collective-permute-done.5.refs_3_
  66.2 8.5 %all-to-all-done.1.cols_ref = bf16[8,80,512]{2,1,0:T(8,128)(2,1)S(1)} async-done(((bf16[8,80,512]{2,1,0:T(8,128)(2,1)}), bf16[8,80,512]{2,1,0:T(8,128)(2,1)S(1)}, u32[]{:S(2)}, u32[]{:S(2)}) %all-to-all-start.1) | async-done | bytes 655392 | tf_op jit(solution)/shard_map/all_to_all | solution.py:418
  74.7 0.9 copy-done.1
  75.7 0.9 copy-done.3
  76.6 0.9 copy-done.5
  77.5 16.5 %stack_products.1 = bf16[2,20,512,1024]{3,2,1,0:T(8,128)(2,1)} custom-call(bf16[8,80,512]{2,1,0:T(8,128)(2,1)S(1)} %all-to-all-done.1.cols_ref, bf16[2,80,512]{2,1,0:T(8,128)(2,1)S(1)} %bitcast.8, bf16[2,80,512]{2,1,0:T(8,128)(2,1)S(1)} %collective-permute-done.4.refs_1_, bf16[2,80,512]{2,1,0:T(8,128)(2,1)S(1)} %copy-done.5, ...), custom_call_target="tpu_custom_call" | custom-call | flops 5368709120 | bytes 41943040 | tf_op jit(solution)/shard_map/stack_products/pallas_call | solution.py:381
  (16 shorter events, 0.3 us)
Async XLA Ops:
  26.1 3.5 %collective-permute-start = (bf16[96,1024]{1,0:T(8,128)(2,1)}, bf16[96,1024]{1,0:T(8,128)(2,1)S(1)}, u32[]{:S(2)}, u32[]{:S(2)}) collective-permute-start(bf16[96,1024]{1,0:T(8,128)(2,1)} %get-tuple-element.10), channel_id=1, source_target_pairs={{1,0},{2,1},{3,2},{4,3},{5,4},{6,5},{7,6},{9,8},{10,9},{11,10},{12... | collective-permute-start | bytes 589832 | tf_op jit(solution)/shard_map/ppermute | solution.py:25
  29.7 1.0 %copy-start.6 = (f32[88,1024]{1,0:T(8,128)S(1)}, f32[88,1024]{1,0:T(8,128)}, u32[]{:S(2)}) copy-start(f32[88,1024]{1,0:T(8,128)} %get-tuple-element.9.own_ref) | copy-start | bytes 1081348
  31.8 23.7 %all-to-all-start = ((bf16[4,2,80,512]{3,2,1,0:T(8,128)(2,1)}), bf16[4,2,80,512]{3,2,1,0:T(8,128)(2,1)S(1)}, u32[]{:S(2)}, u32[]{:S(2)}) async-start(bf16[4,2,80,512]{3,2,1,0:T(8,128)(2,1)} %get-tuple-element.11), calls=%async_computation | async-start | bytes 1310720 | tf_op jit(solution)/shard_map/all_to_all | solution.py:418
  38.1 10.9 %collective-permute-start.3 = (bf16[2,80,512]{2,1,0:T(8,128)(2,1)S(1)}, bf16[2,80,512]{2,1,0:T(8,128)(2,1)S(1)}, u32[]{:S(2)}, u32[]{:S(2)}) collective-permute-start(bf16[2,80,512]{2,1,0:T(8,128)(2,1)S(1)} %bitcast.4), channel_id=1, source_target_pairs={{0,6},{1,7},{2,4},{3,5},{4,2},{5,3},{6,0},{7,1},{8,14},{9,15},{10,... | collective-permute-start | bytes 491528 | tf_op jit(solution)/shard_map/ppermute | solution.py:422
  43.9 8.6 %collective-permute-start.2 = (bf16[2,80,512]{2,1,0:T(8,128)(2,1)S(1)}, bf16[2,80,512]{2,1,0:T(8,128)(2,1)S(1)}, u32[]{:S(2)}, u32[]{:S(2)}) collective-permute-start(bf16[2,80,512]{2,1,0:T(8,128)(2,1)S(1)} %bitcast.5), channel_id=1, source_target_pairs={{0,4},{1,5},{2,6},{3,7},{4,0},{5,1},{6,2},{7,3},{8,12},{9,13},{10,... | collective-permute-start | bytes 491528 | tf_op jit(solution)/shard_map/ppermute | solution.py:422
  43.9 8.9 %collective-permute-start.1 = (bf16[2,80,512]{2,1,0:T(8,128)(2,1)S(1)}, bf16[2,80,512]{2,1,0:T(8,128)(2,1)S(1)}, u32[]{:S(2)}, u32[]{:S(2)}) collective-permute-start(bf16[2,80,512]{2,1,0:T(8,128)(2,1)S(1)} %bitcast.6), channel_id=1, source_target_pairs={{0,2},{1,3},{2,0},{3,1},{4,6},{5,7},{6,4},{7,5},{8,10},{9,11},{10,... | collective-permute-start | bytes 491528 | tf_op jit(solution)/shard_map/ppermute | solution.py:422
  49.0 6.5 %copy-start = (bf16[2,80,512]{2,1,0:T(8,128)(2,1)}, bf16[2,80,512]{2,1,0:T(8,128)(2,1)S(1)}, u32[]{:S(2)}) copy-start(bf16[2,80,512]{2,1,0:T(8,128)(2,1)S(1)} %collective-permute-done.3.refs_3_.refs_6_) | copy-start | bytes 491524
  52.5 3.0 %copy-start.2 = (bf16[2,80,512]{2,1,0:T(8,128)(2,1)}, bf16[2,80,512]{2,1,0:T(8,128)(2,1)S(1)}, u32[]{:S(2)}) copy-start(bf16[2,80,512]{2,1,0:T(8,128)(2,1)S(1)} %collective-permute-done.2.refs_2_.refs_4_) | copy-start | bytes 491524
  52.8 2.6 %copy-start.4 = (bf16[2,80,512]{2,1,0:T(8,128)(2,1)}, bf16[2,80,512]{2,1,0:T(8,128)(2,1)S(1)}, u32[]{:S(2)}) copy-start(bf16[2,80,512]{2,1,0:T(8,128)(2,1)S(1)} %collective-permute-done.1.refs_1_.refs_2_) | copy-start | bytes 491524
  55.4 0.8 copy-start.7
  56.3 18.5 %all-to-all-start.1 = ((bf16[8,80,512]{2,1,0:T(8,128)(2,1)}), bf16[8,80,512]{2,1,0:T(8,128)(2,1)S(1)}, u32[]{:S(2)}, u32[]{:S(2)}) async-start(bf16[8,80,512]{2,1,0:T(8,128)(2,1)} %after.1), calls=%async_computation.1 | async-start | bytes 1310720 | tf_op jit(solution)/shard_map/all_to_all | solution.py:418
  63.6 1.7 %collective-permute-start.4 = (bf16[2,80,512]{2,1,0:T(8,128)(2,1)S(1)}, bf16[2,80,512]{2,1,0:T(8,128)(2,1)S(1)}, u32[]{:S(2)}, u32[]{:S(2)}) collective-permute-start(bf16[2,80,512]{2,1,0:T(8,128)(2,1)S(1)} %bitcast.7), channel_id=1, source_target_pairs={{0,1},{1,0},{2,3},{3,2},{4,5},{5,4},{6,7},{7,6},{8,9},{9,8},{10,11... | collective-permute-start | bytes 491528 | tf_op jit(solution)/shard_map/ppermute | solution.py:422
  64.1 1.6 %collective-permute-start.7 = (bf16[2,80,512]{2,1,0:T(8,128)(2,1)}, bf16[2,80,512]{2,1,0:T(8,128)(2,1)S(1)}, u32[]{:S(2)}, u32[]{:S(2)}) collective-permute-start(bf16[2,80,512]{2,1,0:T(8,128)(2,1)} %copy-done), channel_id=1, source_target_pairs={{0,1},{1,0},{2,3},{3,2},{4,5},{5,4},{6,7},{7,6},{8,9},{9,8},{10,11... | collective-permute-start | bytes 491528 | tf_op jit(solution)/shard_map/ppermute | solution.py:422
  64.1 1.8 %collective-permute-start.6 = (bf16[2,80,512]{2,1,0:T(8,128)(2,1)}, bf16[2,80,512]{2,1,0:T(8,128)(2,1)S(1)}, u32[]{:S(2)}, u32[]{:S(2)}) collective-permute-start(bf16[2,80,512]{2,1,0:T(8,128)(2,1)} %copy-done.2), channel_id=1, source_target_pairs={{0,1},{1,0},{2,3},{3,2},{4,5},{5,4},{6,7},{7,6},{8,9},{9,8},{10,11... | collective-permute-start | bytes 491528 | tf_op jit(solution)/shard_map/ppermute | solution.py:422
  64.6 1.6 %collective-permute-start.5 = (bf16[2,80,512]{2,1,0:T(8,128)(2,1)}, bf16[2,80,512]{2,1,0:T(8,128)(2,1)S(1)}, u32[]{:S(2)}, u32[]{:S(2)}) collective-permute-start(bf16[2,80,512]{2,1,0:T(8,128)(2,1)} %copy-done.4), channel_id=1, source_target_pairs={{0,1},{1,0},{2,3},{3,2},{4,5},{5,4},{6,7},{7,6},{8,9},{9,8},{10,11... | collective-permute-start | bytes 491528 | tf_op jit(solution)/shard_map/ppermute | solution.py:422
  74.7 0.9 copy-start.1
  75.7 0.9 copy-start.3
  76.6 0.9 copy-start.5

commit v5 on v4

--- a/solution.py
+++ b/solution.py
@@ -14,7 +14,7 @@
 BF16 = jnp.bfloat16
 LANE = 128
 DEPTH = 256
-PIECE = 1024
+PIECE = 512
 STEP = 2 * PIECE
 ROW_TILE = 16
 
@@ -58,6 +58,7 @@
     bulk = block_len // ROW_TILE * ROW_TILE
     padded = x_ref.shape[0]
     steps = padded // STEP
+    columns = [slice(n, min(n + DEPTH, channels)) for n in range(0, channels, DEPTH)]
 
     def x_copy(i):
         size = min(STEP, bulk - i * STEP)
@@ -141,7 +142,7 @@
             jnp.logical_or, [jnp.logical_and(end >= first, end < first + size) for end in ends]
         )
 
-    def piece(base, size, table, edge):
+    def piece(view, low, base, size, table, edge):
         tiles = size // ROW_TILE
         if edge:
             targets = [
@@ -150,25 +151,28 @@
             ]
         else:
             target = segment_of(base)
-        acc[...] += jnp.dot(table[:, :size], x_ref[pl.ds(base, size), :], preferred_element_type=F32)
-        total = None
-        for t in range(tiles):
-            x = x_ref[pl.ds(base + t * ROW_TILE, ROW_TILE), :].astype(F32)
-            square = x * x
-            square = square[:half_tile] + square[half_tile:]
-            if edge:
-                seg[targets[t]] += square
-            else:
-                total = square if total is None else total + square
-        if not edge:
-            seg[target] += total
+        for at in columns:
+            block = view[low:low + size, at]
+            acc[:, at] += jnp.dot(table[:, :size], block, preferred_element_type=F32)
+            total = None
+            for t in range(tiles):
+                x = view[low + t * ROW_TILE:low + (t + 1) * ROW_TILE, at].astype(F32)
+                square = x * x
+                square = square[:half_tile] + square[half_tile:]
+                if edge:
+                    seg[targets[t], :, at] += square
+                else:
+                    total = square if total is None else total + square
+            if not edge:
+                seg[target, :, at] += total
 
     def body(i, edge):
         base = pl.multiple_of(i * STEP, STEP)
-        piece(base, PIECE, even, edge)
+        view = x_ref.at[pl.ds(base, STEP)]
         make_table(odd, i * (STEP // DEPTH) + PIECE // DEPTH, PIECE // DEPTH)
-        piece(base + PIECE, PIECE, odd, edge)
+        piece(view, 0, base, PIECE, even, edge)
         make_table(even, (i + 1) * (STEP // DEPTH), PIECE // DEPTH)
+        piece(view, PIECE, base + PIECE, PIECE, odd, edge)
 
     @pl.loop(0, steps)
     def _(i):
@@ -191,9 +195,9 @@
         first = min(PIECE, padded - done)
         if padded - done > first:
             make_table(odd, (done + first) // DEPTH, (padded - done - first) // DEPTH)
-        piece(done, first, even, False)
+        piece(x_ref, done, done, first, even, False)
         if padded - done > first:
-            piece(done + first, padded - done - first, odd, False)
+            piece(x_ref, done + first, done + first, padded - done - first, odd, False)
 
     for i, end in enumerate(ends):
         low = ends[i - 1] if i else jnp.int32(0)
@@ -275,7 +279,7 @@
     )(offsets, band_bins, dead.reshape(1, channels), samples, samples)
 
 
-def whiten_kernel(bins, windows, own_ref, more_ref, *white_refs):
+def whiten_kernel(bins, windows, firsts, own_ref, more_ref, *white_refs):
     rows = bins * windows * 2
     raw = own_ref[:rows, :] + more_ref[:rows, :].astype(F32)
     extra = more_ref[rows:, :].astype(F32)
@@ -295,28 +299,28 @@
         one = alive / jnp.sqrt(jnp.maximum(level, FLOOR))
         factor = one if w == 0 else jnp.where(which == w, one, factor)
     white = (spectra * factor).astype(BF16)
-    for white_ref in white_refs:
-        copies, halves, _, width = white_ref.shape
+    for first, white_ref in zip(firsts, white_refs):
+        copies, halves, count, width = white_ref.shape
         for h in range(halves):
             for copy in range(copies):
-                white_ref[copy, h] = white[:, h * width:(h + 1) * width]
-
-
-def whiten(own, more, bins, windows, halves, copies):
+                white_ref[copy, h] = white[first:first + count, h * width:(h + 1) * width]
+
+
+def whiten(own, more, bins, windows, halves, wanted):
     channels = own.shape[1]
-    rows = bins * windows * 2
     return pl.pallas_call(
-        functools.partial(whiten_kernel, bins, windows),
+        functools.partial(whiten_kernel, bins, windows, [first for _, first, _ in wanted]),
         out_shape=[
-            jax.ShapeDtypeStruct((count, halves, rows, channels // halves), BF16) for count in copies
+            jax.ShapeDtypeStruct((copies, halves, count, channels // halves), BF16)
+            for copies, _, count in wanted
         ],
         compiler_params=pltpu.CompilerParams(vmem_limit_bytes=12 * 2**20),
         name="whiten",
     )(own, more)
 
 
-def stack_kernel(windows, scale, devices, cols_ref, *refs):
-    row_refs, (out_hbm, lhs, held, made, sems) = refs[:devices], refs[devices:]
+def stack_kernel(windows, scale, devices, first_group, cols_ref, *refs):
+    row_refs, (out_hbm, lhs, held, made, sems) = refs[:devices], refs[-5:]
     per_group = ROW_TILE // (2 * windows)
     step = pl.program_id(0)
     width = cols_ref.shape[2]
@@ -340,7 +344,8 @@
             held[pl.ds(to, ROW_TILE), h * span:(h + 1) * span] = row_refs[away][h].astype(F32)
 
     def out_copy(slot, part, bin_index):
-        return pltpu.make_async_copy(made.at[slot], out_hbm.at[part, bin_index], sems.at[slot])
+        to = out_hbm.at[part, first_group * per_group + bin_index]
+        return pltpu.make_async_copy(made.at[slot], to, sems.at[slot])
 
     which = lax.broadcasted_iota(jnp.int32, (depth, 1), 0) % (ROW_TILE // 2) // windows
     for b in range(per_group):
@@ -371,20 +376,24 @@
                 out_copy(2 * b + part, part, step * per_group + b).wait()
 
 
-def stacks_of(cols_all, row_blocks, bins, windows):
+def stacks_of(cols_all, row_blocks, first_group, bins, windows, before=None):
     devices = len(row_blocks)
     halves, _, span = row_blocks[0].shape
-    width = cols_all.shape[2]
+    _, rows, width = cols_all.shape
     per_group = ROW_TILE // (2 * windows)
+    groups = rows // ROW_TILE
     scale = 1.0 / math.sqrt(windows * devices)
     channels = halves * span
+    hbm = pl.BlockSpec(memory_space=pltpu.HBM)
     return pl.pallas_call(
-        functools.partial(stack_kernel, windows, scale, devices),
+        functools.partial(stack_kernel, windows, scale, devices, first_group),
         out_shape=jax.ShapeDtypeStruct((2, bins, width, channels), BF16),
-        grid=(bins // per_group,),
+        grid=(groups,),
         in_specs=[pl.BlockSpec((devices, ROW_TILE, width), lambda i: (0, i, 0))]
-        + [pl.BlockSpec((halves, ROW_TILE, span), lambda i: (0, i, 0))] * devices,
-        out_specs=pl.BlockSpec(memory_space=pltpu.HBM),
+        + [pl.BlockSpec((halves, ROW_TILE, span), lambda i: (0, first_group + i, 0))] * devices
+        + ([] if before is None else [hbm]),
+        out_specs=hbm,
+        input_output_aliases={} if before is None else {1 + devices: 0},
         scratch_shapes=[
             pltpu.VMEM((2 * width, devices * ROW_TILE), BF16),
             pltpu.VMEM((devices * ROW_TILE, channels), F32),
@@ -392,15 +401,15 @@
             pltpu.SemaphoreType.DMA((2 * per_group,)),
         ],
         compiler_params=pltpu.CompilerParams(
-            dimension_semantics=("arbitrary",), vmem_limit_bytes=40 * 2**20
+            dimension_semantics=("arbitrary",), vmem_limit_bytes=24 * 2**20
         ),
         cost_estimate=pl.CostEstimate(
-            flops=2 * 2 * bins * width * channels * devices * ROW_TILE,
-            bytes_accessed=2 * bins * width * channels * 2,
+            flops=2 * 2 * groups * per_group * width * channels * devices * ROW_TILE,
+            bytes_accessed=2 * groups * per_group * width * channels * 2,
             transcendentals=0,
         ),
         name="stack_products",
-    )(cols_all, *row_blocks)
+    )(cols_all, *row_blocks, *([] if before is None else [before]))
 
 
 def after(block, *others):
@@ -410,6 +419,7 @@
         in_specs=[pl.BlockSpec(memory_space=pl.ANY)] * (1 + len(others)),
         out_specs=pl.BlockSpec(memory_space=pl.ANY),
         input_output_aliases={0: 0},
+        compiler_params=pltpu.CompilerParams(vmem_limit_bytes=2**20),
         name="after",
     )(block, *others)
 
@@ -430,17 +440,31 @@
     halves = tm_count // chan_count
     own, back = spectra_of(recording, offsets, band_bins, dead_flags, windows)
     more = shifted(back, "tm", -1)
-    white, for_chan = whiten(own, more, bins, windows, halves, (1, chan_count))
+    rows = bins * windows * 2
+    groups = rows // ROW_TILE
+    cut = (groups + 1) // 2
+    spans = [(0, cut), (cut, groups - cut)]
+    white, *for_chan = whiten(
+        own, more, bins, windows, halves,
+        [(1, 0, rows)] + [(chan_count, first * ROW_TILE, count * ROW_TILE) for first, count in spans],
+    )
     white = white[0]
     row_blocks = {0: white}
     for away in [*range(2, tm_count, 2), 1]:
         row_blocks[away] = from_partner(white, "tm", away)
-    every_chan = exchanged(for_chan, "chan").reshape(tm_count, *for_chan.shape[2:])
-    every_chan = after(every_chan, *[row_blocks[away] for away in range(2, tm_count, 2)])
+    every_chan = [
+        exchanged(block, "chan").reshape(tm_count, *block.shape[2:]) for block in for_chan
+    ]
+    every_chan[0] = after(every_chan[0], *[row_blocks[away] for away in range(2, tm_count, 2)])
     for away in range(2, tm_count, 2):
         row_blocks[away + 1] = from_partner(row_blocks[away], "tm", 1)
-    cols_all = exchanged(every_chan, "tm")
-    return stacks_of(cols_all, [row_blocks[i] for i in range(tm_count)], bins, windows)
+    cols = [exchanged(every_chan[0], "tm")]
+    cols.append(exchanged(after(every_chan[1], cols[0]), "tm"))
+    in_order = [row_blocks[i] for i in range(tm_count)]
+    stacks = None
+    for (first, _), part in zip(spans, cols):
+        stacks = stacks_of(part, in_order, first, bins, windows, stacks)
+    return stacks
 
 
 def solution(mesh):

time: 94.7 us -> 101 us (1.067)
  blocking collectives: 0 us -> 16.2 us
  waiting for transfers between devices: 23.2 us -> 16.7 us
  local copies, waits for them, and re-layouts: 4.57 us -> 0.98 us
  Pallas kernels: 43.7 us -> 45.1 us
    all_to_all x0 -> x1, blocking collectives: none -> 16.2 us  [exchanged(): return lax.all_to_all(blocks, axis, split_axis=0, concat_axis=0, tiled=True)]
    all_to_all x2 -> x3, waiting for transfers between devices: 11.1 us -> 7.19 us  [exchanged(): return lax.all_to_all(blocks, axis, split_axis=0, concat_axis=0, tiled=True)]
    unnamed x16 -> x2, local copies, waits for them, and re-layouts: 4.57 us -> 0.98 us
    ppermute x7, waiting for transfers between devices: 9.86 us -> 6.9 us  [from_partner(): lax.ppermute(block, axis, [(i, i ^ away) for i in range(lax.axis_size(axi...]
    all_to_all x2 -> x3, starting transfers between devices: 13.6 us -> 11.2 us  [exchanged(): return lax.all_to_all(blocks, axis, split_axis=0, concat_axis=0, tiled=True)]
    ppermute x7, starting transfers between devices: 7.49 us -> 9.01 us  [from_partner(): lax.ppermute(block, axis, [(i, i ^ away) for i in range(lax.axis_size(axi...]
    pallas_call x2 -> x3, Pallas kernels: 17.6 us -> 18.8 us  [the longest x2 17.8 us: stacks_of(): pl.pallas_call(functools.partial(stack_kernel, windows, scale, devices, f...]
  transfers between devices with their start and end apart: 10 -> 11, of which waited for: 10 -> 5; matrix products, arithmetic and copies ran while one was open for 0% -> 0% of each run, Pallas kernels for 0% -> 10%
where the time goes in v5:
time: 101 us
  Pallas kernels  45.1 us (45%)
  starting transfers between devices  21.5 us (21%)
  waiting for transfers between devices  16.7 us (17%)
  blocking collectives  16.2 us (16%)
    pallas_call x1, Pallas kernels, spectra_of(): pl.pallas_call(functools.partial(spectra_kernel, bins, windows, block_len...  26.4 us
    pallas_call x2, Pallas kernels, stacks_of(): pl.pallas_call(functools.partial(stack_kernel, windows, scale, devices, f...  17.8 us
    all_to_all x1, blocking collectives, exchanged(): return lax.all_to_all(blocks, axis, split_axis=0, concat_axis=0, tiled=True)  16.2 us
    all_to_all x3, starting transfers between devices, exchanged(): return lax.all_to_all(blocks, axis, split_axis=0, concat_axis=0, tiled=True)  11.2 us
    ppermute x7, starting transfers between devices, from_partner(): lax.ppermute(block, axis, [(i, i ^ away) for i in range(lax.axis_size(axi...  9.01 us
    all_to_all x3, waiting for transfers between devices, exchanged(): return lax.all_to_all(blocks, axis, split_axis=0, concat_axis=0, tiled=True)  7.19 us
    ppermute x7, waiting for transfers between devices, from_partner(): lax.ppermute(block, axis, [(i, i ^ away) for i in range(lax.axis_size(axi...  6.9 us
    ppermute x1, waiting for transfers between devices, shifted(): return lax.ppermute(block, axis, route)  2.59 us
  transfers between devices with their start and end apart: 11, of which 5 were waited for; matrix products, arithmetic and copies ran while one was open for 0% of the time, Pallas kernels for 10%

profile of v5, /device:TPU:0, one launch (start us, length us, event | category | flops | bytes accessed | tf_op | source)
XLA Modules:
  0.0 100.7 jit_solution(8090096834842471150)
XLA Ops:
  0.0 26.4 %band_spectra.1 = (f32[88,1024]{1,0:T(8,128)}, bf16[96,1024]{1,0:T(8,128)(2,1)}) custom-call(s32[16]{0:T(128)} %offsets_hbm.1, s32[20]{0:T(128)} %bins_hbm.1, s32[1,1024]{1,0:T(1,128)} %bitcast.13, bf16[15000,1024]{1,0:T(8,128)(2,1)} %bitcast.11, bf16[15000,1024]{1,0:T(8,128)(2,1)} %bitcast.12), custom_call_target="tpu_custom_call" | custom-call | flops 4915200000 | bytes 30720000 | tf_op jit(solution)/shard_map/band_spectra/pallas_call | solution.py:249
  26.4 1.3 %collective-permute-start = (bf16[96,1024]{1,0:T(8,128)(2,1)}, bf16[96,1024]{1,0:T(8,128)(2,1)S(1)}, u32[]{:S(2)}, u32[]{:S(2)}) collective-permute-start(bf16[96,1024]{1,0:T(8,128)(2,1)} %get-tuple-element.11), channel_id=1, source_target_pairs={{1,0},{2,1},{3,2},{4,3},{5,4},{6,5},{7,6},{9,8},{10,9},{11,10},{12... | collective-permute-start | bytes 589832 | tf_op jit(solution)/shard_map/ppermute | solution.py:25
  27.7 2.6 %collective-permute-done.more_ref = bf16[96,1024]{1,0:T(8,128)(2,1)S(1)} collective-permute-done((bf16[96,1024]{1,0:T(8,128)(2,1)}, bf16[96,1024]{1,0:T(8,128)(2,1)S(1)}, u32[]{:S(2)}, u32[]{:S(2)}) %collective-permute-start) | collective-permute-done | bytes 196640 | tf_op jit(solution)/shard_map/ppermute | solution.py:25
  30.3 1.0 copy-done
  31.3 0.9 whiten.1
  32.2 16.2 %all_to_all.20 = bf16[4,2,48,512]{3,2,1,0:T(8,128)(2,1)} all-to-all(bf16[4,2,48,512]{3,2,1,0:T(8,128)(2,1)S(1)} %get-tuple-element.13), channel_id=1, replica_groups=mesh['chan'=4,'tm'=8] {'chan'}, dimensions={0} | all-to-all | bytes 786432 | tf_op jit(solution)/shard_map/all_to_all | solution.py:428
  48.4 4.4 %all-to-all-start = ((bf16[4,2,32,512]{3,2,1,0:T(8,128)(2,1)}), bf16[4,2,32,512]{3,2,1,0:T(8,128)(2,1)}, u32[]{:S(2)}, u32[]{:S(2)}) async-start(bf16[4,2,32,512]{3,2,1,0:T(8,128)(2,1)} %get-tuple-element.12), calls=%async_computation | async-start | bytes 524288 | tf_op jit(solution)/shard_map/all_to_all | solution.py:428
  52.8 4.0 %collective-permute-start.3 = (bf16[2,80,512]{2,1,0:T(8,128)(2,1)S(1)}, bf16[2,80,512]{2,1,0:T(8,128)(2,1)S(1)}, u32[]{:S(2)}, u32[]{:S(2)}) collective-permute-start(bf16[2,80,512]{2,1,0:T(8,128)(2,1)S(1)} %bitcast.5), channel_id=1, source_target_pairs={{0,6},{1,7},{2,4},{3,5},{4,2},{5,3},{6,0},{7,1},{8,14},{9,15},{10,... | collective-permute-start | bytes 491528 | tf_op jit(solution)/shard_map/ppermute | solution.py:432
  56.8 2.6 %collective-permute-start.2 = (bf16[2,80,512]{2,1,0:T(8,128)(2,1)S(1)}, bf16[2,80,512]{2,1,0:T(8,128)(2,1)S(1)}, u32[]{:S(2)}, u32[]{:S(2)}) collective-permute-start(bf16[2,80,512]{2,1,0:T(8,128)(2,1)S(1)} %bitcast.6), channel_id=1, source_target_pairs={{0,4},{1,5},{2,6},{3,7},{4,0},{5,1},{6,2},{7,3},{8,12},{9,13},{10,... | collective-permute-start | bytes 491528 | tf_op jit(solution)/shard_map/ppermute | solution.py:432
  59.5 1.3 %collective-permute-start.1 = (bf16[2,80,512]{2,1,0:T(8,128)(2,1)S(1)}, bf16[2,80,512]{2,1,0:T(8,128)(2,1)S(1)}, u32[]{:S(2)}, u32[]{:S(2)}) collective-permute-start(bf16[2,80,512]{2,1,0:T(8,128)(2,1)S(1)} %bitcast.7), channel_id=1, source_target_pairs={{0,2},{1,3},{2,0},{3,1},{4,6},{5,7},{6,4},{7,5},{8,10},{9,11},{10,... | collective-permute-start | bytes 491528 | tf_op jit(solution)/shard_map/ppermute | solution.py:432
  60.7 1.0 collective-permute-done.3.refs_3_.refs_6_
  61.7 4.9 %collective-permute-done.2.refs_2_.refs_4_ = bf16[2,80,512]{2,1,0:T(8,128)(2,1)S(1)} collective-permute-done((bf16[2,80,512]{2,1,0:T(8,128)(2,1)S(1)}, bf16[2,80,512]{2,1,0:T(8,128)(2,1)S(1)}, u32[]{:S(2)}, u32[]{:S(2)}) %collective-permute-start.2) | collective-permute-done | bytes 163872 | tf_op jit(solution)/shard_map/ppermute | solution.py:432
  66.6 1.0 collective-permute-done.1.refs_1_.refs_2_
  67.6 0.0 all-to-all-done
  67.6 3.5 %all-to-all-start.2 = ((bf16[8,48,512]{2,1,0:T(8,128)(2,1)}), bf16[8,48,512]{2,1,0:T(8,128)(2,1)S(1)}, u32[]{:S(2)}, u32[]{:S(2)}) async-start(bf16[8,48,512]{2,1,0:T(8,128)(2,1)} %after.2), calls=%async_computation.2 | async-start | bytes 786432 | tf_op jit(solution)/shard_map/all_to_all | solution.py:428
  71.1 0.4 collective-permute-start.4
  71.5 0.2 collective-permute-start.7
  71.7 0.3 collective-permute-start.6
  72.0 0.2 collective-permute-start.5
  72.2 7.2 %all-to-all-done.2.refs_1_.cols_ref = bf16[8,48,512]{2,1,0:T(8,128)(2,1)S(1)} async-done(((bf16[8,48,512]{2,1,0:T(8,128)(2,1)}), bf16[8,48,512]{2,1,0:T(8,128)(2,1)S(1)}, u32[]{:S(2)}, u32[]{:S(2)}) %all-to-all-start.2) | async-done | bytes 393248 | tf_op jit(solution)/shard_map/all_to_all | solution.py:428
  79.4 3.4 %all-to-all-start.3 = ((bf16[8,32,512]{2,1,0:T(8,128)(2,1)}), bf16[8,32,512]{2,1,0:T(8,128)(2,1)S(1)}, u32[]{:S(2)}, u32[]{:S(2)}) async-start(bf16[8,32,512]{2,1,0:T(8,128)(2,1)} %after.3), calls=%async_computation.3 | async-start | bytes 524288 | tf_op jit(solution)/shard_map/all_to_all | solution.py:428
  82.8 0.0 collective-permute-done.6.refs_5_
  82.8 10.4 %stack_products.2.refs_8_ = bf16[2,20,512,1024]{3,2,1,0:T(8,128)(2,1)} custom-call(bf16[8,48,512]{2,1,0:T(8,128)(2,1)S(1)} %all-to-all-done.2.refs_1_.cols_ref, bf16[2,80,512]{2,1,0:T(8,128)(2,1)S(1)} %bitcast.9, bf16[2,80,512]{2,1,0:T(8,128)(2,1)S(1)} %collective-permute-done.4.refs_1_, bf16[2,80,512]{2,1,0:T(8,128)(2,1)S(1)} %collective-permute-done.1.refs_1_.refs_2_, ...), custom_call_target="tpu_custom_call" | custom-call | flops 3221225472 | bytes 25165824 | tf_op jit(solution)/shard_map/stack_products/pallas_call | solution.py:388
  93.3 7.4 %stack_products.3 = bf16[2,20,512,1024]{3,2,1,0:T(8,128)(2,1)} custom-call(bf16[8,32,512]{2,1,0:T(8,128)(2,1)S(1)} %all-to-all-done.3.cols_ref, bf16[2,80,512]{2,1,0:T(8,128)(2,1)S(1)} %bitcast.10, bf16[2,80,512]{2,1,0:T(8,128)(2,1)S(1)} %collective-permute-done.4.refs_1_, ...), custom_call_target="tpu_custom_call", output_to_operand_aliasing={{}: (9, {})} | custom-call | flops 2147483648 | bytes 16777216 | tf_op jit(solution)/shard_map/stack_products/pallas_call | solution.py:388
  (7 shorter events, 0.0 us)
Async XLA Ops:
  26.4 3.9 %collective-permute-start = (bf16[96,1024]{1,0:T(8,128)(2,1)}, bf16[96,1024]{1,0:T(8,128)(2,1)S(1)}, u32[]{:S(2)}, u32[]{:S(2)}) collective-permute-start(bf16[96,1024]{1,0:T(8,128)(2,1)} %get-tuple-element.11), channel_id=1, source_target_pairs={{1,0},{2,1},{3,2},{4,3},{5,4},{6,5},{7,6},{9,8},{10,9},{11,10},{12... | collective-permute-start | bytes 589832 | tf_op jit(solution)/shard_map/ppermute | solution.py:25
  30.3 1.0 copy-start
  48.4 19.2 %all-to-all-start = ((bf16[4,2,32,512]{3,2,1,0:T(8,128)(2,1)}), bf16[4,2,32,512]{3,2,1,0:T(8,128)(2,1)}, u32[]{:S(2)}, u32[]{:S(2)}) async-start(bf16[4,2,32,512]{3,2,1,0:T(8,128)(2,1)} %get-tuple-element.12), calls=%async_computation | async-start | bytes 524288 | tf_op jit(solution)/shard_map/all_to_all | solution.py:428
  52.8 8.9 %collective-permute-start.3 = (bf16[2,80,512]{2,1,0:T(8,128)(2,1)S(1)}, bf16[2,80,512]{2,1,0:T(8,128)(2,1)S(1)}, u32[]{:S(2)}, u32[]{:S(2)}) collective-permute-start(bf16[2,80,512]{2,1,0:T(8,128)(2,1)S(1)} %bitcast.5), channel_id=1, source_target_pairs={{0,6},{1,7},{2,4},{3,5},{4,2},{5,3},{6,0},{7,1},{8,14},{9,15},{10,... | collective-permute-start | bytes 491528 | tf_op jit(solution)/shard_map/ppermute | solution.py:432
  56.8 9.8 %collective-permute-start.2 = (bf16[2,80,512]{2,1,0:T(8,128)(2,1)S(1)}, bf16[2,80,512]{2,1,0:T(8,128)(2,1)S(1)}, u32[]{:S(2)}, u32[]{:S(2)}) collective-permute-start(bf16[2,80,512]{2,1,0:T(8,128)(2,1)S(1)} %bitcast.6), channel_id=1, source_target_pairs={{0,4},{1,5},{2,6},{3,7},{4,0},{5,1},{6,2},{7,3},{8,12},{9,13},{10,... | collective-permute-start | bytes 491528 | tf_op jit(solution)/shard_map/ppermute | solution.py:432
  59.5 8.2 %collective-permute-start.1 = (bf16[2,80,512]{2,1,0:T(8,128)(2,1)S(1)}, bf16[2,80,512]{2,1,0:T(8,128)(2,1)S(1)}, u32[]{:S(2)}, u32[]{:S(2)}) collective-permute-start(bf16[2,80,512]{2,1,0:T(8,128)(2,1)S(1)} %bitcast.7), channel_id=1, source_target_pairs={{0,2},{1,3},{2,0},{3,1},{4,6},{5,7},{6,4},{7,5},{8,10},{9,11},{10,... | collective-permute-start | bytes 491528 | tf_op jit(solution)/shard_map/ppermute | solution.py:432
  67.6 11.7 %all-to-all-start.2 = ((bf16[8,48,512]{2,1,0:T(8,128)(2,1)}), bf16[8,48,512]{2,1,0:T(8,128)(2,1)S(1)}, u32[]{:S(2)}, u32[]{:S(2)}) async-start(bf16[8,48,512]{2,1,0:T(8,128)(2,1)} %after.2), calls=%async_computation.2 | async-start | bytes 786432 | tf_op jit(solution)/shard_map/all_to_all | solution.py:428
  71.1 11.7 %collective-permute-start.4 = (bf16[2,80,512]{2,1,0:T(8,128)(2,1)S(1)}, bf16[2,80,512]{2,1,0:T(8,128)(2,1)S(1)}, u32[]{:S(2)}, u32[]{:S(2)}) collective-permute-start(bf16[2,80,512]{2,1,0:T(8,128)(2,1)S(1)} %bitcast.8), channel_id=1, source_target_pairs={{0,1},{1,0},{2,3},{3,2},{4,5},{5,4},{6,7},{7,6},{8,9},{9,8},{10,11... | collective-permute-start | bytes 491528 | tf_op jit(solution)/shard_map/ppermute | solution.py:432
  71.5 11.3 %collective-permute-start.7 = (bf16[2,80,512]{2,1,0:T(8,128)(2,1)S(1)}, bf16[2,80,512]{2,1,0:T(8,128)(2,1)S(1)}, u32[]{:S(2)}, u32[]{:S(2)}) collective-permute-start(bf16[2,80,512]{2,1,0:T(8,128)(2,1)S(1)} %collective-permute-done.3.refs_3_.refs_6_), channel_id=1, source_target_pairs={{0,1},{1,0},{2,3},{3,2},{4,5},{5,4},{6,7},{7,6},{8,9},{9,8},{10,11... | collective-permute-start | bytes 491528 | tf_op jit(solution)/shard_map/ppermute | solution.py:432
  71.7 11.1 %collective-permute-start.6 = (bf16[2,80,512]{2,1,0:T(8,128)(2,1)S(1)}, bf16[2,80,512]{2,1,0:T(8,128)(2,1)S(1)}, u32[]{:S(2)}, u32[]{:S(2)}) collective-permute-start(bf16[2,80,512]{2,1,0:T(8,128)(2,1)S(1)} %collective-permute-done.2.refs_2_.refs_4_), channel_id=1, source_target_pairs={{0,1},{1,0},{2,3},{3,2},{4,5},{5,4},{6,7},{7,6},{8,9},{9,8},{10,11... | collective-permute-start | bytes 491528 | tf_op jit(solution)/shard_map/ppermute | solution.py:432
  72.0 10.8 %collective-permute-start.5 = (bf16[2,80,512]{2,1,0:T(8,128)(2,1)S(1)}, bf16[2,80,512]{2,1,0:T(8,128)(2,1)S(1)}, u32[]{:S(2)}, u32[]{:S(2)}) collective-permute-start(bf16[2,80,512]{2,1,0:T(8,128)(2,1)S(1)} %collective-permute-done.1.refs_1_.refs_2_), channel_id=1, source_target_pairs={{0,1},{1,0},{2,3},{3,2},{4,5},{5,4},{6,7},{7,6},{8,9},{9,8},{10,11... | collective-permute-start | bytes 491528 | tf_op jit(solution)/shard_map/ppermute | solution.py:432
  79.4 13.9 %all-to-all-start.3 = ((bf16[8,32,512]{2,1,0:T(8,128)(2,1)}), bf16[8,32,512]{2,1,0:T(8,128)(2,1)S(1)}, u32[]{:S(2)}, u32[]{:S(2)}) async-start(bf16[8,32,512]{2,1,0:T(8,128)(2,1)} %after.3), calls=%async_computation.3 | async-start | bytes 524288 | tf_op jit(solution)/shard_map/all_to_all | solution.py:428

commit v6 on v4

--- a/solution.py
+++ b/solution.py
@@ -14,8 +14,7 @@
 BF16 = jnp.bfloat16
 LANE = 128
 DEPTH = 256
-PIECE = 1024
-STEP = 2 * PIECE
+STEP = 1024
 ROW_TILE = 16
 
 
@@ -45,7 +44,7 @@
 def spectra_kernel(
     bins, windows, block_len,
     offsets_hbm, bins_hbm, dead_hbm, x_hbm, tail_ref, own_ref, back_ref,
-    offsets, band_bins, dead, x_ref, acc, seg, cos_now, sin_now, cos_turn, sin_turn, place, even, odd,
+    offsets, band_bins, dead, x_ref, acc, seg, part_seg, cos_now, sin_now, cos_turn, sin_turn, place, table,
     small_sems, x_sems,
 ):
     channels = x_ref.shape[1]
@@ -58,6 +57,7 @@
     bulk = block_len // ROW_TILE * ROW_TILE
     padded = x_ref.shape[0]
     steps = padded // STEP
+    columns = [slice(n, min(n + DEPTH, channels)) for n in range(0, channels, DEPTH)]
 
     def x_copy(i):
         size = min(STEP, bulk - i * STEP)
@@ -71,10 +71,10 @@
     ]
     for copy in small:
         copy.start()
+    for copy in small:
+        copy.wait()
     for i in range(pl.cdiv(bulk, STEP)):
         x_copy(i).start()
-    for copy in small:
-        copy.wait()
 
     tm = lax.axis_index("tm")
     ahead = [offsets[tm * windows + w] + w * hop for w in range(windows)]
@@ -86,21 +86,21 @@
     segments = len(ends) + 1
     trash = segments
 
-    def make_table(table, first, count):
-        for j in range(count):
-            moved = jnp.asarray((first + j) * DEPTH, jnp.int32).astype(F32)
-            for side in range(2):
-                limit = moved if side else -moved
-                for g in range(groups):
-                    at = slice(side * states + g * half_tile, side * states + (g + 1) * half_tile)
-                    to = side * rows + g * ROW_TILE
-                    c, s = cos_now[at, :], sin_now[at, :]
-                    inside = place[at, :] >= limit
-                    wave = jnp.concatenate([jnp.where(inside, c, 0.0), jnp.where(inside, s, 0.0)], axis=0)
-                    table[to:to + ROW_TILE, j * DEPTH:(j + 1) * DEPTH] = wave.astype(BF16)
-                    ct, st = cos_turn[at, :], sin_turn[at, :]
-                    cos_now[at, :] = c * ct + s * st
-                    sin_now[at, :] = s * ct - c * st
+    def make_table(index):
+        moved = (index * DEPTH).astype(F32)
+        to_lanes = pl.ds(pl.multiple_of(index * DEPTH, DEPTH), DEPTH)
+        for side in range(2):
+            limit = moved if side else -moved
+            for g in range(groups):
+                at = slice(side * states + g * half_tile, side * states + (g + 1) * half_tile)
+                to = side * rows + g * ROW_TILE
+                c, s = cos_now[at, :], sin_now[at, :]
+                inside = place[at, :] >= limit
+                wave = jnp.concatenate([jnp.where(inside, c, 0.0), jnp.where(inside, s, 0.0)], axis=0)
+                table[to:to + ROW_TILE, to_lanes] = wave.astype(BF16)
+                ct, st = cos_turn[at, :], sin_turn[at, :]
+                cos_now[at, :] = c * ct + s * st
+                sin_now[at, :] = s * ct - c * st
 
     shape = (half_tile, DEPTH)
     row = lax.broadcasted_iota(jnp.int32, shape, 0)
@@ -122,7 +122,11 @@
             sin_now[at, :] = -sine * norm
             cos_turn[at, :], sin_turn[at, :] = cos_sin(tone * DEPTH, length)
             place[at, :] = start + (length - 1) - lane if side else lane - start
-    make_table(even, 0, PIECE // DEPTH)
+
+    @pl.loop(0, padded // DEPTH)
+    def _(index):
+        make_table(index)
+
     acc[...] = jnp.zeros_like(acc)
     seg[...] = jnp.zeros_like(seg)
     x_ref[bulk:, :] = jnp.zeros((padded - bulk, channels), BF16)
@@ -141,34 +145,33 @@
             jnp.logical_or, [jnp.logical_and(end >= first, end < first + size) for end in ends]
         )
 
-    def piece(base, size, table, edge):
+    def body(base, size, edge):
+        view = x_ref.at[pl.ds(base, size)]
+        waves = table.at[:, pl.ds(base, size)]
         tiles = size // ROW_TILE
+
+        def squares(t, at):
+            x = view[t * ROW_TILE:(t + 1) * ROW_TILE, at].astype(F32)
+            square = x * x
+            return square[:half_tile] + square[half_tile:]
+
+        for at in columns:
+            if not edge:
+                total = squares(0, at)
+                for t in range(1, tiles):
+                    total = total + squares(t, at)
+            product = jnp.dot(waves[...], view[:, at], preferred_element_type=F32)
+            acc[:, at] += product
+            if not edge:
+                part_seg[:, at] = total
         if edge:
-            targets = [
-                jnp.where(has_end(base + t * ROW_TILE, ROW_TILE), trash, segment_of(base + t * ROW_TILE))
-                for t in range(tiles)
-            ]
+            for t in range(tiles):
+                first = base + t * ROW_TILE
+                target = jnp.where(has_end(first, ROW_TILE), trash, segment_of(first))
+                for at in columns:
+                    seg[target, :, at] += squares(t, at)
         else:
-            target = segment_of(base)
-        acc[...] += jnp.dot(table[:, :size], x_ref[pl.ds(base, size), :], preferred_element_type=F32)
-        total = None
-        for t in range(tiles):
-            x = x_ref[pl.ds(base + t * ROW_TILE, ROW_TILE), :].astype(F32)
-            square = x * x
-            square = square[:half_tile] + square[half_tile:]
-            if edge:
-                seg[targets[t]] += square
-            else:
-                total = square if total is None else total + square
-        if not edge:
-            seg[target] += total
-
-    def body(i, edge):
-        base = pl.multiple_of(i * STEP, STEP)
-        piece(base, PIECE, even, edge)
-        make_table(odd, i * (STEP // DEPTH) + PIECE // DEPTH, PIECE // DEPTH)
-        piece(base + PIECE, PIECE, odd, edge)
-        make_table(even, (i + 1) * (STEP // DEPTH), PIECE // DEPTH)
+            seg[segment_of(base)] += part_seg[...]
 
     @pl.loop(0, steps)
     def _(i):
@@ -178,22 +181,17 @@
 
         @pl.when(jnp.logical_not(cut))
         def _():
-            body(i, False)
+            body(pl.multiple_of(i * STEP, STEP), STEP, False)
 
         @pl.when(cut)
         def _():
-            body(i, True)
+            body(pl.multiple_of(i * STEP, STEP), STEP, True)
 
     done = steps * STEP
     if done < padded:
         if done < bulk:
             x_copy(steps).wait()
-        first = min(PIECE, padded - done)
-        if padded - done > first:
-            make_table(odd, (done + first) // DEPTH, (padded - done - first) // DEPTH)
-        piece(done, first, even, False)
-        if padded - done > first:
-            piece(done + first, padded - done - first, odd, False)
+        body(done, padded - done, False)
 
     for i, end in enumerate(ends):
         low = ends[i - 1] if i else jnp.int32(0)
@@ -241,7 +239,6 @@
     hbm = pl.BlockSpec(memory_space=pltpu.HBM)
     whole = pl.BlockSpec(memory_space=pltpu.VMEM)
     state = pltpu.VMEM((rows, DEPTH), F32)
-    table = pltpu.VMEM((2 * rows, PIECE), BF16)
     return pl.pallas_call(
         functools.partial(spectra_kernel, bins, windows, block_len),
         out_shape=(
@@ -261,7 +258,9 @@
             pltpu.VMEM((padded, channels), BF16),
             pltpu.VMEM((2 * rows, channels), F32),
             pltpu.VMEM((2 * windows + 2, ROW_TILE // 2, channels), F32),
-            state, state, state, state, state, table, table,
+            pltpu.VMEM((ROW_TILE // 2, channels), F32),
+            state, state, state, state, state,
+            pltpu.VMEM((2 * rows, padded), BF16),
             pltpu.SemaphoreType.DMA((3,)),
             pltpu.SemaphoreType.DMA((pl.cdiv(padded, STEP),)),
         ],
@@ -275,7 +274,7 @@
     )(offsets, band_bins, dead.reshape(1, channels), samples, samples)
 
 
-def whiten_kernel(bins, windows, own_ref, more_ref, *white_refs):
+def whiten_kernel(bins, windows, firsts, own_ref, more_ref, *white_refs):
     rows = bins * windows * 2
     raw = own_ref[:rows, :] + more_ref[:rows, :].astype(F32)
     extra = more_ref[rows:, :].astype(F32)
@@ -295,38 +294,38 @@
         one = alive / jnp.sqrt(jnp.maximum(level, FLOOR))
         factor = one if w == 0 else jnp.where(which == w, one, factor)
     white = (spectra * factor).astype(BF16)
-    for white_ref in white_refs:
-        copies, halves, _, width = white_ref.shape
+    for first, white_ref in zip(firsts, white_refs):
+        copies, halves, count, width = white_ref.shape
         for h in range(halves):
             for copy in range(copies):
-                white_ref[copy, h] = white[:, h * width:(h + 1) * width]
-
-
-def whiten(own, more, bins, windows, halves, copies):
+                white_ref[copy, h] = white[first:first + count, h * width:(h + 1) * width]
+
+
+def whiten(own, more, bins, windows, halves, wanted):
     channels = own.shape[1]
-    rows = bins * windows * 2
     return pl.pallas_call(
-        functools.partial(whiten_kernel, bins, windows),
+        functools.partial(whiten_kernel, bins, windows, [first for _, first, _ in wanted]),
         out_shape=[
-            jax.ShapeDtypeStruct((count, halves, rows, channels // halves), BF16) for count in copies
+            jax.ShapeDtypeStruct((copies, halves, count, channels // halves), BF16)
+            for copies, _, count in wanted
         ],
         compiler_params=pltpu.CompilerParams(vmem_limit_bytes=12 * 2**20),
         name="whiten",
     )(own, more)
 
 
-def stack_kernel(windows, scale, devices, cols_ref, *refs):
-    row_refs, (out_hbm, lhs, held, made, sems) = refs[:devices], refs[devices:]
+def stack_kernel(windows, scale, devices, *refs):
+    col_refs, row_refs = refs[:devices], refs[devices:2 * devices]
+    out_hbm, lhs, held, made, sems = refs[2 * devices:]
     per_group = ROW_TILE // (2 * windows)
     step = pl.program_id(0)
-    width = cols_ref.shape[2]
+    width = col_refs[0].shape[1]
     depth = devices * ROW_TILE
     halves, _, span = row_refs[0].shape
     channels = halves * span
     exact = math.frexp(scale)[0] == 0.5
-    tm = lax.axis_index("tm")
-
-    cols = cols_ref[...].astype(F32)
+
+    cols = jnp.stack([ref[...].astype(F32) for ref in col_refs])
     if exact:
         cols = cols * scale
     head, tail = cols[:, :ROW_TILE // 2], cols[:, ROW_TILE // 2:]
@@ -335,12 +334,13 @@
     lhs[:width, :] = straight.T.astype(BF16)
     lhs[width:, :] = turned.T.astype(BF16)
     for away in range(devices):
-        to = pl.multiple_of(jnp.bitwise_xor(tm, away) * ROW_TILE, ROW_TILE)
+        to = slice(away * ROW_TILE, (away + 1) * ROW_TILE)
         for h in range(halves):
-            held[pl.ds(to, ROW_TILE), h * span:(h + 1) * span] = row_refs[away][h].astype(F32)
+            held[to, h * span:(h + 1) * span] = row_refs[away][h].astype(F32)
 
     def out_copy(slot, part, bin_index):
-        return pltpu.make_async_copy(made.at[slot], out_hbm.at[part, bin_index], sems.at[slot])
+        to = out_hbm.at[part, bin_index]
+        return pltpu.make_async_copy(made.at[slot], to, sems.at[slot])
 
     which = lax.broadcasted_iota(jnp.int32, (depth, 1), 0) % (ROW_TILE // 2) // windows
     for b in range(per_group):
@@ -371,10 +371,10 @@
                 out_copy(2 * b + part, part, step * per_group + b).wait()
 
 
-def stacks_of(cols_all, row_blocks, bins, windows):
+def stacks_of(col_blocks, row_blocks, bins, windows):
     devices = len(row_blocks)
     halves, _, span = row_blocks[0].shape
-    width = cols_all.shape[2]
+    width = col_blocks[0].shape[1]
     per_group = ROW_TILE // (2 * windows)
     scale = 1.0 / math.sqrt(windows * devices)
     channels = halves * span
@@ -382,7 +382,7 @@
         functools.partial(stack_kernel, windows, scale, devices),
         out_shape=jax.ShapeDtypeStruct((2, bins, width, channels), BF16),
         grid=(bins // per_group,),
-        in_specs=[pl.BlockSpec((devices, ROW_TILE, width), lambda i: (0, i, 0))]
+        in_specs=[pl.BlockSpec((ROW_TILE, width), lambda i: (i, 0))] * devices
         + [pl.BlockSpec((halves, ROW_TILE, span), lambda i: (0, i, 0))] * devices,
         out_specs=pl.BlockSpec(memory_space=pltpu.HBM),
         scratch_shapes=[
@@ -392,7 +392,7 @@
             pltpu.SemaphoreType.DMA((2 * per_group,)),
         ],
         compiler_params=pltpu.CompilerParams(
-            dimension_semantics=("arbitrary",), vmem_limit_bytes=40 * 2**20
+            dimension_semantics=("arbitrary",), vmem_limit_bytes=24 * 2**20
         ),
         cost_estimate=pl.CostEstimate(
             flops=2 * 2 * bins * width * channels * devices * ROW_TILE,
@@ -400,18 +400,26 @@
             transcendentals=0,
         ),
         name="stack_products",
-    )(cols_all, *row_blocks)
-
-
-def after(block, *others):
+    )(*col_blocks, *row_blocks)
+
+
+def pick_kernel(count, blocks_ref, *refs):
+    tm = lax.axis_index("tm")
+    for away, out_ref in enumerate(refs[-count:]):
+        out_ref[...] = blocks_ref[jnp.bitwise_xor(tm, away)]
+
+
+def picked(blocks, *others):
+    count, rows, width = blocks.shape
     return pl.pallas_call(
-        lambda *refs: None,
-        out_shape=jax.ShapeDtypeStruct(block.shape, block.dtype),
-        in_specs=[pl.BlockSpec(memory_space=pl.ANY)] * (1 + len(others)),
-        out_specs=pl.BlockSpec(memory_space=pl.ANY),
-        input_output_aliases={0: 0},
-        name="after",
-    )(block, *others)
+        functools.partial(pick_kernel, count),
+        out_shape=[jax.ShapeDtypeStruct((rows, width), blocks.dtype)] * count,
+        in_specs=[pl.BlockSpec(memory_space=pltpu.VMEM)]
+        + [pl.BlockSpec(memory_space=pl.ANY)] * len(others),
+        out_specs=[pl.BlockSpec(memory_space=pltpu.VMEM)] * count,
+        compiler_params=pltpu.CompilerParams(vmem_limit_bytes=8 * 2**20),
+        name="pick_blocks",
+    )(blocks, *others)
 
 
 def exchanged(blocks, axis):
@@ -430,17 +438,19 @@
     halves = tm_count // chan_count
     own, back = spectra_of(recording, offsets, band_bins, dead_flags, windows)
     more = shifted(back, "tm", -1)
-    white, for_chan = whiten(own, more, bins, windows, halves, (1, chan_count))
+    rows = bins * windows * 2
+    white, for_chan = whiten(own, more, bins, windows, halves, [(1, 0, rows), (chan_count, 0, rows)])
     white = white[0]
     row_blocks = {0: white}
     for away in [*range(2, tm_count, 2), 1]:
         row_blocks[away] = from_partner(white, "tm", away)
-    every_chan = exchanged(for_chan, "chan").reshape(tm_count, *for_chan.shape[2:])
-    every_chan = after(every_chan, *[row_blocks[away] for away in range(2, tm_count, 2)])
+    every_chan = exchanged(for_chan, "chan").reshape(tm_count, rows, channels // halves)
+    col_blocks = list(picked(every_chan, *[row_blocks[away] for away in range(2, tm_count, 2)]))
+    for away in range(1, tm_count):
+        col_blocks[away] = from_partner(col_blocks[away], "tm", away)
     for away in range(2, tm_count, 2):
         row_blocks[away + 1] = from_partner(row_blocks[away], "tm", 1)
-    cols_all = exchanged(every_chan, "tm")
-    return stacks_of(cols_all, [row_blocks[i] for i in range(tm_count)], bins, windows)
+    return stacks_of(col_blocks, [row_blocks[i] for i in range(tm_count)], bins, windows)
 
 
 def solution(mesh):

time: 94.7 us -> 77.2 us (0.82)
  Pallas kernels: 43.7 us -> 33.5 us
  waiting for transfers between devices: 23.2 us -> 18.1 us
  local copies, waits for them, and re-layouts: 4.57 us -> 0.98 us
  starting transfers between devices: 22.4 us -> 24.3 us
    pallas_call x1, Pallas kernels: 26.1 us -> 16 us  [spectra_of(): pl.pallas_call(functools.partial(spectra_kernel, bins, windows, block_len...]
    ppermute x7 -> x14, starting transfers between devices: 7.49 us -> 16.7 us  [from_partner(): lax.ppermute(block, axis, [(i, i ^ away) for i in range(lax.axis_size(axi...]
    all_to_all x2 -> x1, waiting for transfers between devices: 11.1 us -> 3.75 us  [exchanged(): return lax.all_to_all(blocks, axis, split_axis=0, concat_axis=0, tiled=True)]
    all_to_all x2 -> x1, starting transfers between devices: 13.6 us -> 6.29 us  [exchanged(): return lax.all_to_all(blocks, axis, split_axis=0, concat_axis=0, tiled=True)]
    unnamed x16 -> x2, local copies, waits for them, and re-layouts: 4.57 us -> 0.98 us
    ppermute x7 -> x14, waiting for transfers between devices: 9.86 us -> 12.1 us  [from_partner(): lax.ppermute(block, axis, [(i, i ^ away) for i in range(lax.axis_size(axi...]
  transfers between devices with their start and end apart: 10 -> 16, of which waited for: 10 -> 7; matrix products, arithmetic and copies ran while one was open for 0% -> 0% of each run, Pallas kernels for 0% -> 0%
where the time goes in v6:
time: 77.2 us; the launch traced here: 76.9 us
  Pallas kernels  33.5 us (43%)
  starting transfers between devices  24.3 us (31%)
  waiting for transfers between devices  18.1 us (23%)
  local copies, waits for them, and re-layouts  0.98 us (1%)
    ppermute x14, starting transfers between devices, from_partner(): lax.ppermute(block, axis, [(i, i ^ away) for i in range(lax.axis_size(axi...  16.7 us
    pallas_call x1, Pallas kernels, stacks_of(): pl.pallas_call(functools.partial(stack_kernel, windows, scale, devices),...  16.3 us
    pallas_call x1, Pallas kernels, spectra_of(): pl.pallas_call(functools.partial(spectra_kernel, bins, windows, block_len...  16 us
    ppermute x14, waiting for transfers between devices, from_partner(): lax.ppermute(block, axis, [(i, i ^ away) for i in range(lax.axis_size(axi...  12.1 us
    all_to_all x1, starting transfers between devices, exchanged(): return lax.all_to_all(blocks, axis, split_axis=0, concat_axis=0, tiled=True)  6.29 us
    all_to_all x1, waiting for transfers between devices, exchanged(): return lax.all_to_all(blocks, axis, split_axis=0, concat_axis=0, tiled=True)  3.75 us
    ppermute x1, waiting for transfers between devices, shifted(): return lax.ppermute(block, axis, route)  2.27 us
  transfers between devices with their start and end apart: 16, of which 7 were waited for; matrix products, arithmetic and copies ran while one was open for 0% of the time, Pallas kernels for 0%

profile of v6, /device:TPU:0, one launch (start us, length us, event | category | flops | bytes accessed | tf_op | source)
XLA Modules:
  0.0 76.9 jit_solution(533063645091396857)
XLA Ops:
  0.0 16.0 %band_spectra.1 = (f32[88,1024]{1,0:T(8,128)}, bf16[96,1024]{1,0:T(8,128)(2,1)}) custom-call(s32[16]{0:T(128)} %offsets_hbm.1, s32[20]{0:T(128)} %bins_hbm.1, s32[1,1024]{1,0:T(1,128)} %bitcast.12, bf16[15000,1024]{1,0:T(8,128)(2,1)} %bitcast.10, bf16[15000,1024]{1,0:T(8,128)(2,1)} %bitcast.11), custom_call_target="tpu_custom_call" | custom-call | flops 4915200000 | bytes 30720000 | tf_op jit(solution)/shard_map/band_spectra/pallas_call | solution.py:242
  16.0 1.3 %collective-permute-start = (bf16[96,1024]{1,0:T(8,128)(2,1)}, bf16[96,1024]{1,0:T(8,128)(2,1)S(1)}, u32[]{:S(2)}, u32[]{:S(2)}) collective-permute-start(bf16[96,1024]{1,0:T(8,128)(2,1)} %get-tuple-element.18), channel_id=1, source_target_pairs={{1,0},{2,1},{3,2},{4,3},{5,4},{6,5},{7,6},{9,8},{10,9},{11,10},{12... | collective-permute-start | bytes 589832 | tf_op jit(solution)/shard_map/ppermute | solution.py:24
  17.3 2.3 %collective-permute-done.more_ref = bf16[96,1024]{1,0:T(8,128)(2,1)S(1)} collective-permute-done((bf16[96,1024]{1,0:T(8,128)(2,1)}, bf16[96,1024]{1,0:T(8,128)(2,1)S(1)}, u32[]{:S(2)}, u32[]{:S(2)}) %collective-permute-start) | collective-permute-done | bytes 196640 | tf_op jit(solution)/shard_map/ppermute | solution.py:24
  19.6 1.0 %copy-done = f32[88,1024]{1,0:T(8,128)S(1)} copy-done((f32[88,1024]{1,0:T(8,128)S(1)}, f32[88,1024]{1,0:T(8,128)}, u32[]{:S(2)}) %copy-start) | copy-done | bytes 360472
  20.6 1.1 %whiten.1 = (bf16[1,2,80,512]{3,2,1,0:T(8,128)(2,1)S(1)}, bf16[4,2,80,512]{3,2,1,0:T(8,128)(2,1)}) custom-call(f32[88,1024]{1,0:T(8,128)S(1)} %copy-done, bf16[96,1024]{1,0:T(8,128)(2,1)S(1)} %collective-permute-done.more_ref), custom_call_target="tpu_custom_call" | custom-call | tf_op jit(solution)/shard_map/whiten/pallas_call | solution.py:306
  21.7 6.3 %all-to-all-start = ((bf16[4,2,80,512]{3,2,1,0:T(8,128)(2,1)}), bf16[4,2,80,512]{3,2,1,0:T(8,128)(2,1)S(1)}, u32[]{:S(2)}, u32[]{:S(2)}) async-start(bf16[4,2,80,512]{3,2,1,0:T(8,128)(2,1)} %get-tuple-element.19), calls=%async_computation | async-start | bytes 1310720 | tf_op jit(solution)/shard_map/all_to_all | solution.py:426
  28.0 4.3 %collective-permute-start.3 = (bf16[2,80,512]{2,1,0:T(8,128)(2,1)S(1)}, bf16[2,80,512]{2,1,0:T(8,128)(2,1)S(1)}, u32[]{:S(2)}, u32[]{:S(2)}) collective-permute-start(bf16[2,80,512]{2,1,0:T(8,128)(2,1)S(1)} %bitcast.5), channel_id=1, source_target_pairs={{0,6},{1,7},{2,4},{3,5},{4,2},{5,3},{6,0},{7,1},{8,14},{9,15},{10,... | collective-permute-start | bytes 491528 | tf_op jit(solution)/shard_map/ppermute | solution.py:430
  32.4 0.5 collective-permute-start.2
  32.9 0.9 %collective-permute-start.1 = (bf16[2,80,512]{2,1,0:T(8,128)(2,1)S(1)}, bf16[2,80,512]{2,1,0:T(8,128)(2,1)S(1)}, u32[]{:S(2)}, u32[]{:S(2)}) collective-permute-start(bf16[2,80,512]{2,1,0:T(8,128)(2,1)S(1)} %bitcast.7), channel_id=1, source_target_pairs={{0,2},{1,3},{2,0},{3,1},{4,6},{5,7},{6,4},{7,5},{8,10},{9,11},{10,... | collective-permute-start | bytes 491528 | tf_op jit(solution)/shard_map/ppermute | solution.py:430
  33.8 0.8 %collective-permute-start.11 = (bf16[2,80,512]{2,1,0:T(8,128)(2,1)S(1)}, bf16[2,80,512]{2,1,0:T(8,128)(2,1)S(1)}, u32[]{:S(2)}, u32[]{:S(2)}) collective-permute-start(bf16[2,80,512]{2,1,0:T(8,128)(2,1)S(1)} %bitcast.8), channel_id=1, source_target_pairs={{0,1},{1,0},{2,3},{3,2},{4,5},{5,4},{6,7},{7,6},{8,9},{9,8},{10,11... | collective-permute-start | bytes 491528 | tf_op jit(solution)/shard_map/ppermute | solution.py:430
  34.6 2.0 %collective-permute-done.3.refs_2_.refs_14_ = bf16[2,80,512]{2,1,0:T(8,128)(2,1)S(1)} collective-permute-done((bf16[2,80,512]{2,1,0:T(8,128)(2,1)S(1)}, bf16[2,80,512]{2,1,0:T(8,128)(2,1)S(1)}, u32[]{:S(2)}, u32[]{:S(2)}) %collective-permute-start.3) | collective-permute-done | bytes 163872 | tf_op jit(solution)/shard_map/ppermute | solution.py:430
  36.6 0.7 collective-permute-start.14
  37.3 3.6 %collective-permute-done.2.refs_1_.refs_12_ = bf16[2,80,512]{2,1,0:T(8,128)(2,1)S(1)} collective-permute-done((bf16[2,80,512]{2,1,0:T(8,128)(2,1)S(1)}, bf16[2,80,512]{2,1,0:T(8,128)(2,1)S(1)}, u32[]{:S(2)}, u32[]{:S(2)}) %collective-permute-start.2) | collective-permute-done | bytes 163872 | tf_op jit(solution)/shard_map/ppermute | solution.py:430
  40.9 0.1 collective-permute-start.13
  41.1 0.9 %collective-permute-done.1.refs_0_.refs_10_ = bf16[2,80,512]{2,1,0:T(8,128)(2,1)S(1)} collective-permute-done((bf16[2,80,512]{2,1,0:T(8,128)(2,1)S(1)}, bf16[2,80,512]{2,1,0:T(8,128)(2,1)S(1)}, u32[]{:S(2)}, u32[]{:S(2)}) %collective-permute-start.1) | collective-permute-done | bytes 163872 | tf_op jit(solution)/shard_map/ppermute | solution.py:430
  41.9 3.7 %all-to-all-done = bf16[4,2,80,512]{3,2,1,0:T(8,128)(2,1)S(1)} async-done(((bf16[4,2,80,512]{3,2,1,0:T(8,128)(2,1)}), bf16[4,2,80,512]{3,2,1,0:T(8,128)(2,1)S(1)}, u32[]{:S(2)}, u32[]{:S(2)}) %all-to-all-start) | async-done | bytes 655392 | tf_op jit(solution)/shard_map/all_to_all | solution.py:426
  45.7 1.0 %collective-permute-start.4 = (bf16[80,512]{1,0:T(8,128)(2,1)S(1)}, bf16[80,512]{1,0:T(8,128)(2,1)S(1)}, u32[]{:S(2)}, u32[]{:S(2)}) collective-permute-start(bf16[80,512]{1,0:T(8,128)(2,1)S(1)} %get-tuple-element.22), channel_id=1, source_target_pairs={{0,1},{1,0},{2,3},{3,2},{4,5},{5,4},{6,7},{7,6},{8,9},{9,8},{10,11... | collective-permute-start | bytes 245768 | tf_op jit(solution)/shard_map/ppermute | solution.py:430
  46.7 3.4 %collective-permute-start.5 = (bf16[80,512]{1,0:T(8,128)(2,1)S(1)}, bf16[80,512]{1,0:T(8,128)(2,1)S(1)}, u32[]{:S(2)}, u32[]{:S(2)}) collective-permute-start(bf16[80,512]{1,0:T(8,128)(2,1)S(1)} %get-tuple-element.23), channel_id=1, source_target_pairs={{0,2},{1,3},{2,0},{3,1},{4,6},{5,7},{6,4},{7,5},{8,10},{9,11},{10,... | collective-permute-start | bytes 245768 | tf_op jit(solution)/shard_map/ppermute | solution.py:430
  50.1 2.5 %collective-permute-start.7 = (bf16[80,512]{1,0:T(8,128)(2,1)S(1)}, bf16[80,512]{1,0:T(8,128)(2,1)S(1)}, u32[]{:S(2)}, u32[]{:S(2)}) collective-permute-start(bf16[80,512]{1,0:T(8,128)(2,1)S(1)} %get-tuple-element.25), channel_id=1, source_target_pairs={{0,4},{1,5},{2,6},{3,7},{4,0},{5,1},{6,2},{7,3},{8,12},{9,13},{10,... | collective-permute-start | bytes 245768 | tf_op jit(solution)/shard_map/ppermute | solution.py:430
  52.6 1.2 %collective-permute-start.9 = (bf16[80,512]{1,0:T(8,128)(2,1)S(1)}, bf16[80,512]{1,0:T(8,128)(2,1)S(1)}, u32[]{:S(2)}, u32[]{:S(2)}) collective-permute-start(bf16[80,512]{1,0:T(8,128)(2,1)S(1)} %get-tuple-element.27), channel_id=1, source_target_pairs={{0,6},{1,7},{2,4},{3,5},{4,2},{5,3},{6,0},{7,1},{8,14},{9,15},{10,... | collective-permute-start | bytes 245768 | tf_op jit(solution)/shard_map/ppermute | solution.py:430
  53.8 1.2 %collective-permute-start.10 = (bf16[80,512]{1,0:T(8,128)(2,1)S(1)}, bf16[80,512]{1,0:T(8,128)(2,1)S(1)}, u32[]{:S(2)}, u32[]{:S(2)}) collective-permute-start(bf16[80,512]{1,0:T(8,128)(2,1)S(1)} %get-tuple-element.28), channel_id=1, source_target_pairs={{0,7},{1,6},{2,5},{3,4},{4,3},{5,2},{6,1},{7,0},{8,15},{9,14},{10,... | collective-permute-start | bytes 245768 | tf_op jit(solution)/shard_map/ppermute | solution.py:430
  55.0 0.5 collective-permute-done.7.refs_4_
  55.5 5.0 %collective-permute-done.8.refs_5_ = bf16[80,512]{1,0:T(8,128)(2,1)S(1)} collective-permute-done((bf16[80,512]{1,0:T(8,128)(2,1)S(1)}, bf16[80,512]{1,0:T(8,128)(2,1)S(1)}, u32[]{:S(2)}, u32[]{:S(2)}) %collective-permute-start.8) | collective-permute-done | bytes 81952 | tf_op jit(solution)/shard_map/ppermute | solution.py:430
  60.6 16.3 %stack_products.1 = bf16[2,20,512,1024]{3,2,1,0:T(8,128)(2,1)} custom-call(bf16[80,512]{1,0:T(8,128)(2,1)S(1)} %get-tuple-element.21.refs_0_, bf16[80,512]{1,0:T(8,128)(2,1)S(1)} %collective-permute-done.4.refs_1_, bf16[80,512]{1,0:T(8,128)(2,1)S(1)} %collective-permute-done.5.refs_2_, bf16[80,512]{1,0:T(8,128)(2,1)S(1)} %collective-permute-done.6.refs_3_, ...), custom_call_target="tpu_custom_call" | custom-call | flops 5368709120 | bytes 41943040 | tf_op jit(solution)/shard_map/stack_products/pallas_call | solution.py:381
  (14 shorter events, 0.1 us)
Async XLA Ops:
  16.0 3.6 %collective-permute-start = (bf16[96,1024]{1,0:T(8,128)(2,1)}, bf16[96,1024]{1,0:T(8,128)(2,1)S(1)}, u32[]{:S(2)}, u32[]{:S(2)}) collective-permute-start(bf16[96,1024]{1,0:T(8,128)(2,1)} %get-tuple-element.18), channel_id=1, source_target_pairs={{1,0},{2,1},{3,2},{4,3},{5,4},{6,5},{7,6},{9,8},{10,9},{11,10},{12... | collective-permute-start | bytes 589832 | tf_op jit(solution)/shard_map/ppermute | solution.py:24
  19.6 1.0 %copy-start = (f32[88,1024]{1,0:T(8,128)S(1)}, f32[88,1024]{1,0:T(8,128)}, u32[]{:S(2)}) copy-start(f32[88,1024]{1,0:T(8,128)} %get-tuple-element.17.own_ref) | copy-start | bytes 1081348
  21.7 23.9 %all-to-all-start = ((bf16[4,2,80,512]{3,2,1,0:T(8,128)(2,1)}), bf16[4,2,80,512]{3,2,1,0:T(8,128)(2,1)S(1)}, u32[]{:S(2)}, u32[]{:S(2)}) async-start(bf16[4,2,80,512]{3,2,1,0:T(8,128)(2,1)} %get-tuple-element.19), calls=%async_computation | async-start | bytes 1310720 | tf_op jit(solution)/shard_map/all_to_all | solution.py:426
  28.0 8.6 %collective-permute-start.3 = (bf16[2,80,512]{2,1,0:T(8,128)(2,1)S(1)}, bf16[2,80,512]{2,1,0:T(8,128)(2,1)S(1)}, u32[]{:S(2)}, u32[]{:S(2)}) collective-permute-start(bf16[2,80,512]{2,1,0:T(8,128)(2,1)S(1)} %bitcast.5), channel_id=1, source_target_pairs={{0,6},{1,7},{2,4},{3,5},{4,2},{5,3},{6,0},{7,1},{8,14},{9,15},{10,... | collective-permute-start | bytes 491528 | tf_op jit(solution)/shard_map/ppermute | solution.py:430
  32.4 8.6 %collective-permute-start.2 = (bf16[2,80,512]{2,1,0:T(8,128)(2,1)S(1)}, bf16[2,80,512]{2,1,0:T(8,128)(2,1)S(1)}, u32[]{:S(2)}, u32[]{:S(2)}) collective-permute-start(bf16[2,80,512]{2,1,0:T(8,128)(2,1)S(1)} %bitcast.6), channel_id=1, source_target_pairs={{0,4},{1,5},{2,6},{3,7},{4,0},{5,1},{6,2},{7,3},{8,12},{9,13},{10,... | collective-permute-start | bytes 491528 | tf_op jit(solution)/shard_map/ppermute | solution.py:430
  32.9 9.1 %collective-permute-start.1 = (bf16[2,80,512]{2,1,0:T(8,128)(2,1)S(1)}, bf16[2,80,512]{2,1,0:T(8,128)(2,1)S(1)}, u32[]{:S(2)}, u32[]{:S(2)}) collective-permute-start(bf16[2,80,512]{2,1,0:T(8,128)(2,1)S(1)} %bitcast.7), channel_id=1, source_target_pairs={{0,2},{1,3},{2,0},{3,1},{4,6},{5,7},{6,4},{7,5},{8,10},{9,11},{10,... | collective-permute-start | bytes 491528 | tf_op jit(solution)/shard_map/ppermute | solution.py:430
  33.8 12.9 %collective-permute-start.11 = (bf16[2,80,512]{2,1,0:T(8,128)(2,1)S(1)}, bf16[2,80,512]{2,1,0:T(8,128)(2,1)S(1)}, u32[]{:S(2)}, u32[]{:S(2)}) collective-permute-start(bf16[2,80,512]{2,1,0:T(8,128)(2,1)S(1)} %bitcast.8), channel_id=1, source_target_pairs={{0,1},{1,0},{2,3},{3,2},{4,5},{5,4},{6,7},{7,6},{8,9},{9,8},{10,11... | collective-permute-start | bytes 491528 | tf_op jit(solution)/shard_map/ppermute | solution.py:430
  36.6 13.4 %collective-permute-start.14 = (bf16[2,80,512]{2,1,0:T(8,128)(2,1)S(1)}, bf16[2,80,512]{2,1,0:T(8,128)(2,1)S(1)}, u32[]{:S(2)}, u32[]{:S(2)}) collective-permute-start(bf16[2,80,512]{2,1,0:T(8,128)(2,1)S(1)} %collective-permute-done.3.refs_2_.refs_14_), channel_id=1, source_target_pairs={{0,1},{1,0},{2,3},{3,2},{4,5},{5,4},{6,7},{7,6},{8,9},{9,8},{10,11... | collective-permute-start | bytes 491528 | tf_op jit(solution)/shard_map/ppermute | solution.py:430
  40.9 9.1 %collective-permute-start.13 = (bf16[2,80,512]{2,1,0:T(8,128)(2,1)S(1)}, bf16[2,80,512]{2,1,0:T(8,128)(2,1)S(1)}, u32[]{:S(2)}, u32[]{:S(2)}) collective-permute-start(bf16[2,80,512]{2,1,0:T(8,128)(2,1)S(1)} %collective-permute-done.2.refs_1_.refs_12_), channel_id=1, source_target_pairs={{0,1},{1,0},{2,3},{3,2},{4,5},{5,4},{6,7},{7,6},{8,9},{9,8},{10,11... | collective-permute-start | bytes 491528 | tf_op jit(solution)/shard_map/ppermute | solution.py:430
  41.9 10.7 %collective-permute-start.12 = (bf16[2,80,512]{2,1,0:T(8,128)(2,1)S(1)}, bf16[2,80,512]{2,1,0:T(8,128)(2,1)S(1)}, u32[]{:S(2)}, u32[]{:S(2)}) collective-permute-start(bf16[2,80,512]{2,1,0:T(8,128)(2,1)S(1)} %collective-permute-done.1.refs_0_.refs_10_), channel_id=1, source_target_pairs={{0,1},{1,0},{2,3},{3,2},{4,5},{5,4},{6,7},{7,6},{8,9},{9,8},{10,11... | collective-permute-start | bytes 491528 | tf_op jit(solution)/shard_map/ppermute | solution.py:430
  45.7 6.9 %collective-permute-start.4 = (bf16[80,512]{1,0:T(8,128)(2,1)S(1)}, bf16[80,512]{1,0:T(8,128)(2,1)S(1)}, u32[]{:S(2)}, u32[]{:S(2)}) collective-permute-start(bf16[80,512]{1,0:T(8,128)(2,1)S(1)} %get-tuple-element.22), channel_id=1, source_target_pairs={{0,1},{1,0},{2,3},{3,2},{4,5},{5,4},{6,7},{7,6},{8,9},{9,8},{10,11... | collective-permute-start | bytes 245768 | tf_op jit(solution)/shard_map/ppermute | solution.py:430
  46.7 7.2 %collective-permute-start.5 = (bf16[80,512]{1,0:T(8,128)(2,1)S(1)}, bf16[80,512]{1,0:T(8,128)(2,1)S(1)}, u32[]{:S(2)}, u32[]{:S(2)}) collective-permute-start(bf16[80,512]{1,0:T(8,128)(2,1)S(1)} %get-tuple-element.23), channel_id=1, source_target_pairs={{0,2},{1,3},{2,0},{3,1},{4,6},{5,7},{6,4},{7,5},{8,10},{9,11},{10,... | collective-permute-start | bytes 245768 | tf_op jit(solution)/shard_map/ppermute | solution.py:430
  50.0 5.0 %collective-permute-start.6 = (bf16[80,512]{1,0:T(8,128)(2,1)S(1)}, bf16[80,512]{1,0:T(8,128)(2,1)S(1)}, u32[]{:S(2)}, u32[]{:S(2)}) collective-permute-start(bf16[80,512]{1,0:T(8,128)(2,1)S(1)} %get-tuple-element.24), channel_id=1, source_target_pairs={{0,3},{1,2},{2,1},{3,0},{4,7},{5,6},{6,5},{7,4},{8,11},{9,10},{10,... | collective-permute-start | bytes 245768 | tf_op jit(solution)/shard_map/ppermute | solution.py:430
  50.1 5.5 %collective-permute-start.7 = (bf16[80,512]{1,0:T(8,128)(2,1)S(1)}, bf16[80,512]{1,0:T(8,128)(2,1)S(1)}, u32[]{:S(2)}, u32[]{:S(2)}) collective-permute-start(bf16[80,512]{1,0:T(8,128)(2,1)S(1)} %get-tuple-element.25), channel_id=1, source_target_pairs={{0,4},{1,5},{2,6},{3,7},{4,0},{5,1},{6,2},{7,3},{8,12},{9,13},{10,... | collective-permute-start | bytes 245768 | tf_op jit(solution)/shard_map/ppermute | solution.py:430
  52.6 8.0 %collective-permute-start.8 = (bf16[80,512]{1,0:T(8,128)(2,1)S(1)}, bf16[80,512]{1,0:T(8,128)(2,1)S(1)}, u32[]{:S(2)}, u32[]{:S(2)}) collective-permute-start(bf16[80,512]{1,0:T(8,128)(2,1)S(1)} %get-tuple-element.26), channel_id=1, source_target_pairs={{0,5},{1,4},{2,7},{3,6},{4,1},{5,0},{6,3},{7,2},{8,13},{9,12},{10,... | collective-permute-start | bytes 245768 | tf_op jit(solution)/shard_map/ppermute | solution.py:430
  52.6 8.0 %collective-permute-start.9 = (bf16[80,512]{1,0:T(8,128)(2,1)S(1)}, bf16[80,512]{1,0:T(8,128)(2,1)S(1)}, u32[]{:S(2)}, u32[]{:S(2)}) collective-permute-start(bf16[80,512]{1,0:T(8,128)(2,1)S(1)} %get-tuple-element.27), channel_id=1, source_target_pairs={{0,6},{1,7},{2,4},{3,5},{4,2},{5,3},{6,0},{7,1},{8,14},{9,15},{10,... | collective-permute-start | bytes 245768 | tf_op jit(solution)/shard_map/ppermute | solution.py:430
  53.8 6.8 %collective-permute-start.10 = (bf16[80,512]{1,0:T(8,128)(2,1)S(1)}, bf16[80,512]{1,0:T(8,128)(2,1)S(1)}, u32[]{:S(2)}, u32[]{:S(2)}) collective-permute-start(bf16[80,512]{1,0:T(8,128)(2,1)S(1)} %get-tuple-element.28), channel_id=1, source_target_pairs={{0,7},{1,6},{2,5},{3,4},{4,3},{5,2},{6,1},{7,0},{8,15},{9,14},{10,... | collective-permute-start | bytes 245768 | tf_op jit(solution)/shard_map/ppermute | solution.py:430

commit v7 on v6

--- a/solution.py
+++ b/solution.py
@@ -16,12 +16,6 @@
 DEPTH = 256
 STEP = 1024
 ROW_TILE = 16
-
-
-def shifted(block, axis, distance):
-    devices = range(lax.axis_size(axis))
-    route = [(i - distance, i) for i in devices if i - distance in devices]
-    return lax.ppermute(block, axis, route)
 
 
 def cos_sin(turns, length):
@@ -42,11 +36,12 @@
 
 
 def spectra_kernel(
-    bins, windows, block_len,
-    offsets_hbm, bins_hbm, dead_hbm, x_hbm, tail_ref, own_ref, back_ref,
-    offsets, band_bins, dead, x_ref, acc, seg, part_seg, cos_now, sin_now, cos_turn, sin_turn, place, table,
-    small_sems, x_sems,
+    bins, windows, block_len, low_end, high_end, sides,
+    offsets_hbm, bins_hbm, dead_hbm, x_hbm, tail_ref, own_ref, *refs,
 ):
+    back_ref = refs[0] if sides == 2 else None
+    offsets, band_bins, dead, x_ref, acc, seg, part_seg, cos_now, sin_now, cos_turn, sin_turn, place, table = refs[-15:-2]
+    small_sems, x_sems = refs[-2:]
     channels = x_ref.shape[1]
     length, hop = L, L // 2
     rows = bins * windows * 2
@@ -54,15 +49,16 @@
     per_group = half_tile // windows
     groups = rows // ROW_TILE
     states = groups * half_tile
-    bulk = block_len // ROW_TILE * ROW_TILE
+    bulk = (high_end - low_end) // ROW_TILE * ROW_TILE
     padded = x_ref.shape[0]
     steps = padded // STEP
     columns = [slice(n, min(n + DEPTH, channels)) for n in range(0, channels, DEPTH)]
 
     def x_copy(i):
         size = min(STEP, bulk - i * STEP)
-        at = pl.ds(i * STEP, size)
-        return pltpu.make_async_copy(x_hbm.at[at], x_ref.at[at], x_sems.at[i])
+        return pltpu.make_async_copy(
+            x_hbm.at[pl.ds(low_end + i * STEP, size)], x_ref.at[pl.ds(i * STEP, size)], x_sems.at[i]
+        )
 
     small = [
         pltpu.make_async_copy(offsets_hbm, offsets, small_sems.at[0]),
@@ -81,7 +77,7 @@
     before = jnp.maximum(tm - 1, 0) * windows
     behind = [offsets[before + w] + w * hop + length - block_len for w in range(windows)]
     ends = []
-    for w in range(windows):
+    for w in range(windows if sides == 2 else 0):
         ends += [jnp.minimum(ahead[w], behind[w]), jnp.maximum(ahead[w], behind[w])]
     segments = len(ends) + 1
     trash = segments
@@ -89,7 +85,7 @@
     def make_table(index):
         moved = (index * DEPTH).astype(F32)
         to_lanes = pl.ds(pl.multiple_of(index * DEPTH, DEPTH), DEPTH)
-        for side in range(2):
+        for side in range(sides):
             limit = moved if side else -moved
             for g in range(groups):
                 at = slice(side * states + g * half_tile, side * states + (g + 1) * half_tile)
@@ -104,9 +100,9 @@
 
     shape = (half_tile, DEPTH)
     row = lax.broadcasted_iota(jnp.int32, shape, 0)
-    lane = lax.broadcasted_iota(jnp.int32, shape, 1).astype(F32)
+    lane = (lax.broadcasted_iota(jnp.int32, shape, 1) + low_end).astype(F32)
     norm = 1.0 / math.sqrt(length)
-    for side in range(2):
+    for side in range(sides):
         for g in range(groups):
             at = slice(side * states + g * half_tile, side * states + (g + 1) * half_tile)
             tone = jnp.zeros(shape, jnp.int32)
@@ -129,9 +125,10 @@
 
     acc[...] = jnp.zeros_like(acc)
     seg[...] = jnp.zeros_like(seg)
-    x_ref[bulk:, :] = jnp.zeros((padded - bulk, channels), BF16)
-    if block_len > bulk:
-        inside = lax.broadcasted_iota(jnp.int32, (ROW_TILE, channels), 0) < block_len - bulk
+    if padded > bulk:
+        x_ref[bulk:, :] = jnp.zeros((padded - bulk, channels), BF16)
+    if high_end - low_end > bulk:
+        inside = lax.broadcasted_iota(jnp.int32, (ROW_TILE, channels), 0) < high_end - low_end - bulk
         x_ref[bulk:bulk + ROW_TILE, :] = jnp.where(inside, tail_ref[...].astype(F32), 0.0).astype(BF16)
 
     def segment_of(position):
@@ -141,9 +138,10 @@
         return index
 
     def has_end(first, size):
-        return functools.reduce(
-            jnp.logical_or, [jnp.logical_and(end >= first, end < first + size) for end in ends]
-        )
+        found = jnp.bool_(False)
+        for end in ends:
+            found = jnp.logical_or(found, jnp.logical_and(end >= first, end < first + size))
+        return found
 
     def body(base, size, edge):
         view = x_ref.at[pl.ds(base, size)]
@@ -175,17 +173,22 @@
 
     @pl.loop(0, steps)
     def _(i):
-        at = pl.ds(pl.multiple_of(i * STEP, STEP), STEP)
-        pltpu.make_async_copy(x_hbm.at[at], x_ref.at[at], x_sems.at[i]).wait()
-        cut = has_end(i * STEP, STEP)
+        base = pl.multiple_of(i * STEP, STEP)
+        pltpu.make_async_copy(
+            x_hbm.at[pl.ds(low_end + base, STEP)], x_ref.at[pl.ds(base, STEP)], x_sems.at[i]
+        ).wait()
+        if not ends:
+            body(base, STEP, False)
+            return
+        cut = has_end(base, STEP)
 
         @pl.when(jnp.logical_not(cut))
         def _():
-            body(pl.multiple_of(i * STEP, STEP), STEP, False)
+            body(base, STEP, False)
 
         @pl.when(cut)
         def _():
-            body(pl.multiple_of(i * STEP, STEP), STEP, True)
+            body(base, STEP, True)
 
     done = steps * STEP
     if done < padded:
@@ -195,7 +198,7 @@
 
     for i, end in enumerate(ends):
         low = ends[i - 1] if i else jnp.int32(0)
-        high = ends[i + 1] if i + 1 < len(ends) else jnp.int32(block_len)
+        high = ends[i + 1] if i + 1 < len(ends) else jnp.int32(high_end)
         tile = end // ROW_TILE
         x = x_ref[pl.ds(pl.multiple_of(tile * ROW_TILE, ROW_TILE), ROW_TILE), :].astype(F32)
         spot = lax.broadcasted_iota(jnp.int32, x.shape, 0) + tile * ROW_TILE
@@ -208,81 +211,86 @@
             seg[index] += kept[:half_tile] + kept[half_tile:]
 
     own_ref[:rows, :] = acc[:rows, :]
-    back_ref[:rows, :] = acc[rows:, :].astype(BF16)
     parts = [seg[i] for i in range(segments)]
     row = lax.broadcasted_iota(jnp.int32, (half_tile, channels), 0)
     own_block = jnp.where(row == windows, (1 - dead[...]).astype(F32), 0.0)
+    for w in range(windows):
+        after = sum(parts[2 * w + 2:]) if ends else parts[0]
+        if ends:
+            after = after + jnp.where(ahead[w] <= behind[w], parts[2 * w + 1], 0.0)
+        own_block = jnp.where(row == w, jnp.sum(after, axis=0, keepdims=True), own_block)
+    own_ref[rows:, :] = own_block
+    if sides == 1:
+        return
+    back_ref[:rows, :] = acc[rows:, :].astype(BF16)
     back_block = jnp.zeros((ROW_TILE, channels), F32)
     back_row = lax.broadcasted_iota(jnp.int32, (ROW_TILE, channels), 0)
     for w in range(windows):
-        turn = parts[2 * w + 1]
-        early = ahead[w] <= behind[w]
-        after = sum(parts[2 * w + 2:]) + jnp.where(early, turn, 0.0)
-        until = sum(parts[:2 * w + 1]) + jnp.where(early, turn, 0.0)
-        own_block = jnp.where(row == w, jnp.sum(after, axis=0, keepdims=True), own_block)
+        until = sum(parts[:2 * w + 1]) + jnp.where(ahead[w] <= behind[w], parts[2 * w + 1], 0.0)
         rest = jnp.sum(until, axis=0, keepdims=True)
         for term in range(3):
             piece_of = rest.astype(BF16).astype(F32)
             rest = rest - piece_of
             back_block = jnp.where(back_row == term * windows + w, piece_of, back_block)
-    own_ref[rows:, :] = own_block
     back_ref[rows:, :] = back_block.astype(BF16)
 
 
-def spectra_of(recording, offsets, band_bins, dead, windows):
+def spectra_of(recording, offsets, band_bins, dead, windows, low_end, high_end, sides):
     channels, block_len = recording.shape
     bins = band_bins.shape[0]
     rows = bins * windows * 2
-    padded = pl.cdiv(block_len, DEPTH) * DEPTH
-    bulk = block_len // ROW_TILE * ROW_TILE
+    padded = pl.cdiv(high_end - low_end, DEPTH) * DEPTH
+    bulk = (high_end - low_end) // ROW_TILE * ROW_TILE
+    tail = min(low_end + bulk, block_len - 1) // ROW_TILE
     samples = recording.T
     hbm = pl.BlockSpec(memory_space=pltpu.HBM)
     whole = pl.BlockSpec(memory_space=pltpu.VMEM)
-    state = pltpu.VMEM((rows, DEPTH), F32)
+    state = pltpu.VMEM((rows // 2 * sides, DEPTH), F32)
+    out_shape = [
+        jax.ShapeDtypeStruct((rows + ROW_TILE // 2, channels), F32),
+        jax.ShapeDtypeStruct((rows + ROW_TILE, channels), BF16),
+    ][:sides]
     return pl.pallas_call(
-        functools.partial(spectra_kernel, bins, windows, block_len),
-        out_shape=(
-            jax.ShapeDtypeStruct((rows + ROW_TILE // 2, channels), F32),
-            jax.ShapeDtypeStruct((rows + ROW_TILE, channels), BF16),
-        ),
+        functools.partial(spectra_kernel, bins, windows, block_len, low_end, high_end, sides),
+        out_shape=out_shape,
         grid=(1,),
         in_specs=[
             hbm, hbm, hbm, hbm,
-            pl.BlockSpec((ROW_TILE, channels), lambda i: (min(bulk, block_len - 1) // ROW_TILE, 0)),
+            pl.BlockSpec((ROW_TILE, channels), lambda i: (tail, 0)),
         ],
-        out_specs=(whole, whole),
+        out_specs=[whole] * sides,
         scratch_shapes=[
             pltpu.SMEM(offsets.shape, jnp.int32),
             pltpu.SMEM(band_bins.shape, jnp.int32),
             pltpu.VMEM((1, channels), jnp.int32),
             pltpu.VMEM((padded, channels), BF16),
-            pltpu.VMEM((2 * rows, channels), F32),
+            pltpu.VMEM((sides * rows, channels), F32),
             pltpu.VMEM((2 * windows + 2, ROW_TILE // 2, channels), F32),
             pltpu.VMEM((ROW_TILE // 2, channels), F32),
             state, state, state, state, state,
-            pltpu.VMEM((2 * rows, padded), BF16),
+            pltpu.VMEM((sides * rows, padded), BF16),
             pltpu.SemaphoreType.DMA((3,)),
             pltpu.SemaphoreType.DMA((pl.cdiv(padded, STEP),)),
         ],
         compiler_params=pltpu.CompilerParams(vmem_limit_bytes=60 * 2**20),
         cost_estimate=pl.CostEstimate(
-            flops=2 * channels * block_len * 2 * rows,
-            bytes_accessed=channels * block_len * 2,
+            flops=2 * channels * (high_end - low_end) * sides * rows,
+            bytes_accessed=channels * (high_end - low_end) * 2,
             transcendentals=0,
         ),
-        name="band_spectra",
+        name="band_spectra" if sides == 2 else "band_spectra_rest",
     )(offsets, band_bins, dead.reshape(1, channels), samples, samples)
 
 
-def whiten_kernel(bins, windows, firsts, own_ref, more_ref, *white_refs):
+def whiten_kernel(bins, windows, own_ref, rest_ref, more_ref, white_ref):
     rows = bins * windows * 2
-    raw = own_ref[:rows, :] + more_ref[:rows, :].astype(F32)
+    raw = own_ref[:rows, :] + rest_ref[:rows, :] + more_ref[:rows, :].astype(F32)
     extra = more_ref[rows:, :].astype(F32)
     which = lax.broadcasted_iota(jnp.int32, (rows, 1), 0) % windows
     alive = own_ref[rows + windows:rows + windows + 1, :]
     scale = factor = None
     for w in range(windows):
-        energy = own_ref[rows + w:rows + w + 1, :]
+        energy = own_ref[rows + w:rows + w + 1, :] + rest_ref[rows + w:rows + w + 1, :]
         for term in range(3):
             energy = energy + extra[term * windows + w:term * windows + w + 1, :]
         inverse = 1.0 / jnp.sqrt(energy / L + 1e-06)
@@ -294,34 +302,29 @@
         one = alive / jnp.sqrt(jnp.maximum(level, FLOOR))
         factor = one if w == 0 else jnp.where(which == w, one, factor)
     white = (spectra * factor).astype(BF16)
-    for first, white_ref in zip(firsts, white_refs):
-        copies, halves, count, width = white_ref.shape
-        for h in range(halves):
-            for copy in range(copies):
-                white_ref[copy, h] = white[first:first + count, h * width:(h + 1) * width]
-
-
-def whiten(own, more, bins, windows, halves, wanted):
+    width = white_ref.shape[2]
+    for h in range(white_ref.shape[0]):
+        white_ref[h] = white[:, h * width:(h + 1) * width]
+
+
+def whiten(own, rest, more, bins, windows, halves):
     channels = own.shape[1]
     return pl.pallas_call(
-        functools.partial(whiten_kernel, bins, windows, [first for _, first, _ in wanted]),
-        out_shape=[
-            jax.ShapeDtypeStruct((copies, halves, count, channels // halves), BF16)
-            for copies, _, count in wanted
-        ],
+        functools.partial(whiten_kernel, bins, windows),
+        out_shape=jax.ShapeDtypeStruct((halves, bins * windows * 2, channels // halves), BF16),
         compiler_params=pltpu.CompilerParams(vmem_limit_bytes=12 * 2**20),
         name="whiten",
-    )(own, more)
+    )(own, rest, more)
 
 
 def stack_kernel(windows, scale, devices, *refs):
-    col_refs, row_refs = refs[:devices], refs[devices:2 * devices]
-    out_hbm, lhs, held, made, sems = refs[2 * devices:]
+    col_refs, row_refs = refs[:devices], refs[devices:devices + 2]
+    out_hbm, lhs, held, made, sems = refs[devices + 2:]
     per_group = ROW_TILE // (2 * windows)
     step = pl.program_id(0)
     width = col_refs[0].shape[1]
     depth = devices * ROW_TILE
-    halves, _, span = row_refs[0].shape
+    _, halves, _, span = row_refs[0].shape
     channels = halves * span
     exact = math.frexp(scale)[0] == 0.5
 
@@ -336,7 +339,7 @@
     for away in range(devices):
         to = slice(away * ROW_TILE, (away + 1) * ROW_TILE)
         for h in range(halves):
-            held[to, h * span:(h + 1) * span] = row_refs[away][h].astype(F32)
+            held[to, h * span:(h + 1) * span] = row_refs[away % 2][away // 2, h].astype(F32)
 
     def out_copy(slot, part, bin_index):
         to = out_hbm.at[part, bin_index]
@@ -372,8 +375,8 @@
 
 
 def stacks_of(col_blocks, row_blocks, bins, windows):
-    devices = len(row_blocks)
-    halves, _, span = row_blocks[0].shape
+    devices = len(col_blocks)
+    chips, halves, _, span = row_blocks[0].shape
     width = col_blocks[0].shape[1]
     per_group = ROW_TILE // (2 * windows)
     scale = 1.0 / math.sqrt(windows * devices)
@@ -383,7 +386,7 @@
         out_shape=jax.ShapeDtypeStruct((2, bins, width, channels), BF16),
         grid=(bins // per_group,),
         in_specs=[pl.BlockSpec((ROW_TILE, width), lambda i: (i, 0))] * devices
-        + [pl.BlockSpec((halves, ROW_TILE, span), lambda i: (0, i, 0))] * devices,
+        + [pl.BlockSpec((chips, halves, ROW_TILE, span), lambda i: (0, 0, i, 0))] * 2,
         out_specs=pl.BlockSpec(memory_space=pltpu.HBM),
         scratch_shapes=[
             pltpu.VMEM((2 * width, devices * ROW_TILE), BF16),
@@ -403,27 +406,55 @@
     )(*col_blocks, *row_blocks)
 
 
-def pick_kernel(count, blocks_ref, *refs):
-    tm = lax.axis_index("tm")
-    for away, out_ref in enumerate(refs[-count:]):
-        out_ref[...] = blocks_ref[jnp.bitwise_xor(tm, away)]
-
-
-def picked(blocks, *others):
-    count, rows, width = blocks.shape
-    return pl.pallas_call(
-        functools.partial(pick_kernel, count),
-        out_shape=[jax.ShapeDtypeStruct((rows, width), blocks.dtype)] * count,
-        in_specs=[pl.BlockSpec(memory_space=pltpu.VMEM)]
-        + [pl.BlockSpec(memory_space=pl.ANY)] * len(others),
-        out_specs=[pl.BlockSpec(memory_space=pltpu.VMEM)] * count,
-        compiler_params=pltpu.CompilerParams(vmem_limit_bytes=8 * 2**20),
+def pick_kernel(count, reach, row_count, *refs):
+    chan_refs, row_refs = refs[:len(reach)], refs[len(reach):len(reach) + row_count]
+    joined_ref, out_refs, held = refs[len(reach) + row_count], refs[-1 - count:-1], refs[-1]
+    tm, mine = lax.axis_index("tm"), lax.axis_index("chan")
+    size = held.shape[0]
+    halves = chan_refs[0].shape[0]
+    for far, ref in zip(reach, chan_refs):
+        @pl.when(jnp.logical_and(mine + far >= 0, mine + far < size))
+        def _():
+            held[mine + far] = ref[...]
+    for i, ref in enumerate(row_refs):
+        joined_ref[i] = ref[...]
+    for away, out_ref in enumerate(out_refs):
+        wanted = jnp.bitwise_xor(tm, away)
+        out_ref[...] = held[wanted // halves, wanted % halves]
+
+
+def picked(blocks, row_blocks, count, chan_count):
+    reach = list(blocks)
+    block = blocks[0]
+    _, rows, width = block.shape
+    whole = pl.BlockSpec(memory_space=pltpu.VMEM)
+    joined, *picks = pl.pallas_call(
+        functools.partial(pick_kernel, count, reach, len(row_blocks)),
+        out_shape=[jax.ShapeDtypeStruct((len(row_blocks), *block.shape), block.dtype)]
+        + [jax.ShapeDtypeStruct((rows, width), block.dtype)] * count,
+        in_specs=[whole] * (len(blocks) + len(row_blocks)),
+        out_specs=[whole] * (1 + count),
+        scratch_shapes=[pltpu.VMEM((chan_count, *block.shape), block.dtype)],
+        compiler_params=pltpu.CompilerParams(vmem_limit_bytes=16 * 2**20),
         name="pick_blocks",
-    )(blocks, *others)
-
-
-def exchanged(blocks, axis):
-    return lax.all_to_all(blocks, axis, split_axis=0, concat_axis=0, tiled=True)
+    )(*blocks.values(), *row_blocks)
+    return joined, picks
+
+
+def moved(block, axis, far):
+    count = lax.axis_size(axis)
+    return lax.ppermute(block, axis, [(i + far, i) for i in range(count) if 0 <= i + far < count])
+
+
+def chan_blocks(block):
+    blocks = {0: block}
+    for far in range(1, lax.axis_size("chan")):
+        for sign in (-1, 1):
+            if far < 3:
+                blocks[sign * far] = moved(block, "chan", sign * far)
+            else:
+                blocks[sign * far] = moved(blocks[sign * (far - 1)], "chan", sign)
+    return blocks
 
 
 def from_partner(block, axis, away):
@@ -436,21 +467,18 @@
     bins = band_bins.shape[0]
     chan_count, tm_count = lax.axis_size("chan"), lax.axis_size("tm")
     halves = tm_count // chan_count
-    own, back = spectra_of(recording, offsets, band_bins, dead_flags, windows)
-    more = shifted(back, "tm", -1)
-    rows = bins * windows * 2
-    white, for_chan = whiten(own, more, bins, windows, halves, [(1, 0, rows), (chan_count, 0, rows)])
-    white = white[0]
-    row_blocks = {0: white}
-    for away in [*range(2, tm_count, 2), 1]:
-        row_blocks[away] = from_partner(white, "tm", away)
-    every_chan = exchanged(for_chan, "chan").reshape(tm_count, rows, channels // halves)
-    col_blocks = list(picked(every_chan, *[row_blocks[away] for away in range(2, tm_count, 2)]))
+    rim = L // 2 + L // 4
+    cut = min(pl.cdiv(rim, STEP) * STEP, block_len)
+    own, back = spectra_of(recording, offsets, band_bins, dead_flags, windows, 0, cut, 2)
+    more = moved(back, "tm", 1)
+    rest, = spectra_of(recording, offsets, band_bins, dead_flags, windows, cut, block_len, 1)
+    white = whiten(own, rest, more, bins, windows, halves)
+    blocks = chan_blocks(white)
+    row_blocks = [white] + [from_partner(white, "tm", away) for away in range(2, tm_count, 2)]
+    joined, col_blocks = picked(blocks, row_blocks, tm_count, chan_count)
     for away in range(1, tm_count):
         col_blocks[away] = from_partner(col_blocks[away], "tm", away)
-    for away in range(2, tm_count, 2):
-        row_blocks[away + 1] = from_partner(row_blocks[away], "tm", 1)
-    return stacks_of(col_blocks, [row_blocks[i] for i in range(tm_count)], bins, windows)
+    return stacks_of(col_blocks, [joined, from_partner(joined, "tm", 1)], bins, windows)
 
 
 def solution(mesh):

time: 77.2 us -> 78.5 us (1.017)
  waiting for transfers between devices: 18.1 us -> 7.98 us
  starting transfers between devices: 24.3 us -> 33.6 us
  Pallas kernels: 33.5 us -> 35.3 us
    ppermute x1 -> x7, starting transfers between devices: 1.29 us -> 19.8 us  [moved(): lax.ppermute(block, axis, [(i + far, i) for i in range(count) if 0 <= i +...]
    ppermute x14 -> x11, waiting for transfers between devices: 12.1 us -> 5.19 us  [from_partner(): lax.ppermute(block, axis, [(i, i ^ away) for i in range(lax.axis_size(axi...]
    all_to_all x1 -> x0, starting transfers between devices: 6.29 us -> none  [exchanged(): return lax.all_to_all(blocks, axis, split_axis=0, concat_axis=0, tiled=True)]
    all_to_all x1 -> x0, waiting for transfers between devices: 3.75 us -> none  [exchanged(): return lax.all_to_all(blocks, axis, split_axis=0, concat_axis=0, tiled=True)]
    ppermute x14 -> x11, starting transfers between devices: 16.7 us -> 13.8 us  [from_partner(): lax.ppermute(block, axis, [(i, i ^ away) for i in range(lax.axis_size(axi...]
    pallas_call x1 -> x2, Pallas kernels: 16 us -> 18.7 us  [spectra_of(): pl.pallas_call(functools.partial(spectra_kernel, bins, windows, block_len...]
    ppermute x1 -> x7, waiting for transfers between devices: 2.27 us -> 2.79 us  [moved(): lax.ppermute(block, axis, [(i + far, i) for i in range(count) if 0 <= i +...]
  transfers between devices with their start and end apart: 16 -> 18, of which waited for: 7 -> 6; matrix products, arithmetic and copies ran while one was open for 0% -> 0% of each run, Pallas kernels for 0% -> 8%
where the time goes in v7:
time: 78.5 us; the launch traced here: 78.1 us
  Pallas kernels  35.3 us (45%)
  starting transfers between devices  33.6 us (43%)
  waiting for transfers between devices  7.98 us (10%)
  local copies, waits for them, and re-layouts  0.98 us (1%)
    ppermute x7, starting transfers between devices, moved(): lax.ppermute(block, axis, [(i + far, i) for i in range(count) if 0 <= i +...  19.8 us
    pallas_call x2, Pallas kernels, spectra_of(): pl.pallas_call(functools.partial(spectra_kernel, bins, windows, block_len...  18.7 us
    pallas_call x1, Pallas kernels, stacks_of(): pl.pallas_call(functools.partial(stack_kernel, windows, scale, devices),...  16.2 us
    ppermute x11, starting transfers between devices, from_partner(): lax.ppermute(block, axis, [(i, i ^ away) for i in range(lax.axis_size(axi...  13.8 us
    ppermute x11, waiting for transfers between devices, from_partner(): lax.ppermute(block, axis, [(i, i ^ away) for i in range(lax.axis_size(axi...  5.19 us
    ppermute x7, waiting for transfers between devices, moved(): lax.ppermute(block, axis, [(i + far, i) for i in range(count) if 0 <= i +...  2.79 us
  transfers between devices with their start and end apart: 18, of which 6 were waited for; matrix products, arithmetic and copies ran while one was open for 0% of the time, Pallas kernels for 8%

profile of v7, /device:TPU:0, one launch (start us, length us, event | category | flops | bytes accessed | tf_op | source)
XLA Modules:
  0.0 78.1 jit_solution(18118520713996629605)
XLA Ops:
  0.0 12.2 %band_spectra.1 = (f32[88,1024]{1,0:T(8,128)}, bf16[96,1024]{1,0:T(8,128)(2,1)}) custom-call(s32[16]{0:T(128)} %offsets_hbm.3, s32[20]{0:T(128)} %bins_hbm.3, s32[1,1024]{1,0:T(1,128)} %bitcast.6, bf16[15000,1024]{1,0:T(8,128)(2,1)} %bitcast.2, bf16[15000,1024]{1,0:T(8,128)(2,1)} %bitcast.3), custom_call_target="tpu_custom_call" | custom-call | flops 3690987520 | bytes 23068672 | tf_op jit(solution)/shard_map/band_spectra/pallas_call | solution.py:253
  12.2 1.4 %collective-permute-start = (bf16[96,1024]{1,0:T(8,128)(2,1)}, bf16[96,1024]{1,0:T(8,128)(2,1)S(1)}, u32[]{:S(2)}, u32[]{:S(2)}) collective-permute-start(bf16[96,1024]{1,0:T(8,128)(2,1)} %get-tuple-element.17), channel_id=1, source_target_pairs={{1,0},{2,1},{3,2},{4,3},{5,4},{6,5},{7,6},{9,8},{10,9},{11,10},{12... | collective-permute-start | bytes 589832 | tf_op jit(solution)/shard_map/ppermute | solution.py:446
  13.6 6.5 %band_spectra_rest.1.rest_ref = f32[88,1024]{1,0:T(8,128)} custom-call(s32[16]{0:T(128)} %offsets_hbm.3, s32[20]{0:T(128)} %bins_hbm.3, s32[1,1024]{1,0:T(1,128)} %bitcast.7, bf16[15000,1024]{1,0:T(8,128)(2,1)} %bitcast.4, bf16[15000,1024]{1,0:T(8,128)(2,1)} %bitcast.5), custom_call_target="tpu_custom_call" | custom-call | flops 612106240 | bytes 7651328 | tf_op jit(solution)/shard_map/band_spectra_rest/pallas_call | solution.py:253
  20.2 1.0 %copy-done = f32[88,1024]{1,0:T(8,128)S(1)} copy-done((f32[88,1024]{1,0:T(8,128)S(1)}, f32[88,1024]{1,0:T(8,128)}, u32[]{:S(2)}) %copy-start) | copy-done | bytes 360472
  21.4 4.8 %collective-permute-start.9 = (bf16[2,80,512]{2,1,0:T(8,128)(2,1)S(1)}, bf16[2,80,512]{2,1,0:T(8,128)(2,1)S(1)}, u32[]{:S(2)}, u32[]{:S(2)}) collective-permute-start(bf16[2,80,512]{2,1,0:T(8,128)(2,1)S(1)} %whiten.1.refs_0_.refs_7_), channel_id=1, source_target_pairs={{0,6},{1,7},{2,4},{3,5},{4,2},{5,3},{6,0},{7,1},{8,14},{9,15},{10,... | collective-permute-start | bytes 491528 | tf_op jit(solution)/shard_map/ppermute | solution.py:461
  26.2 0.5 collective-permute-start.8
  26.7 1.3 %collective-permute-start.4 = (bf16[2,80,512]{2,1,0:T(8,128)(2,1)S(1)}, bf16[2,80,512]{2,1,0:T(8,128)(2,1)S(1)}, u32[]{:S(2)}, u32[]{:S(2)}) collective-permute-start(bf16[2,80,512]{2,1,0:T(8,128)(2,1)S(1)} %whiten.1.refs_0_.refs_7_), channel_id=1, source_target_pairs={{16,0},{24,8},{17,1},{25,9},{18,2},{26,10},{19,3},{27,11},{20,4},{... | collective-permute-start | bytes 491528 | tf_op jit(solution)/shard_map/ppermute | solution.py:446
  28.0 5.5 %collective-permute-start.3 = (bf16[2,80,512]{2,1,0:T(8,128)(2,1)S(1)}, bf16[2,80,512]{2,1,0:T(8,128)(2,1)S(1)}, u32[]{:S(2)}, u32[]{:S(2)}) collective-permute-start(bf16[2,80,512]{2,1,0:T(8,128)(2,1)S(1)} %whiten.1.refs_0_.refs_7_), channel_id=1, source_target_pairs={{0,16},{8,24},{1,17},{9,25},{2,18},{10,26},{3,19},{11,27},{4,20},{... | collective-permute-start | bytes 491528 | tf_op jit(solution)/shard_map/ppermute | solution.py:446
  33.5 1.0 %collective-permute-start.7 = (bf16[2,80,512]{2,1,0:T(8,128)(2,1)S(1)}, bf16[2,80,512]{2,1,0:T(8,128)(2,1)S(1)}, u32[]{:S(2)}, u32[]{:S(2)}) collective-permute-start(bf16[2,80,512]{2,1,0:T(8,128)(2,1)S(1)} %whiten.1.refs_0_.refs_7_), channel_id=1, source_target_pairs={{0,2},{1,3},{2,0},{3,1},{4,6},{5,7},{6,4},{7,5},{8,10},{9,11},{10,... | collective-permute-start | bytes 491528 | tf_op jit(solution)/shard_map/ppermute | solution.py:461
  34.5 1.3 %collective-permute-start.2 = (bf16[2,80,512]{2,1,0:T(8,128)(2,1)S(1)}, bf16[2,80,512]{2,1,0:T(8,128)(2,1)S(1)}, u32[]{:S(2)}, u32[]{:S(2)}) collective-permute-start(bf16[2,80,512]{2,1,0:T(8,128)(2,1)S(1)} %whiten.1.refs_0_.refs_7_), channel_id=1, source_target_pairs={{8,0},{16,8},{24,16},{9,1},{17,9},{25,17},{10,2},{18,10},{26,18},{... | collective-permute-start | bytes 491528 | tf_op jit(solution)/shard_map/ppermute | solution.py:446
  35.8 4.6 %collective-permute-start.1 = (bf16[2,80,512]{2,1,0:T(8,128)(2,1)S(1)}, bf16[2,80,512]{2,1,0:T(8,128)(2,1)S(1)}, u32[]{:S(2)}, u32[]{:S(2)}) collective-permute-start(bf16[2,80,512]{2,1,0:T(8,128)(2,1)S(1)} %whiten.1.refs_0_.refs_7_), channel_id=1, source_target_pairs={{0,8},{8,16},{16,24},{1,9},{9,17},{17,25},{2,10},{10,18},{18,26},{... | collective-permute-start | bytes 491528 | tf_op jit(solution)/shard_map/ppermute | solution.py:446
  40.3 1.3 %collective-permute-start.6 = (bf16[2,80,512]{2,1,0:T(8,128)(2,1)S(1)}, bf16[2,80,512]{2,1,0:T(8,128)(2,1)S(1)}, u32[]{:S(2)}, u32[]{:S(2)}) collective-permute-start(bf16[2,80,512]{2,1,0:T(8,128)(2,1)S(1)} %collective-permute-done.4.refs_4_), channel_id=1, source_target_pairs={{8,0},{16,8},{24,16},{9,1},{17,9},{25,17},{10,2},{18,10},{26,18},{... | collective-permute-start | bytes 491528 | tf_op jit(solution)/shard_map/ppermute | solution.py:446
  41.6 4.6 %collective-permute-start.5 = (bf16[2,80,512]{2,1,0:T(8,128)(2,1)S(1)}, bf16[2,80,512]{2,1,0:T(8,128)(2,1)S(1)}, u32[]{:S(2)}, u32[]{:S(2)}) collective-permute-start(bf16[2,80,512]{2,1,0:T(8,128)(2,1)S(1)} %collective-permute-done.3.refs_3_), channel_id=1, source_target_pairs={{0,8},{8,16},{16,24},{1,9},{9,17},{17,25},{2,10},{10,18},{18,26},{... | collective-permute-start | bytes 491528 | tf_op jit(solution)/shard_map/ppermute | solution.py:446
  46.2 1.3 %collective-permute-done.6.refs_6_ = bf16[2,80,512]{2,1,0:T(8,128)(2,1)S(1)} collective-permute-done((bf16[2,80,512]{2,1,0:T(8,128)(2,1)S(1)}, bf16[2,80,512]{2,1,0:T(8,128)(2,1)S(1)}, u32[]{:S(2)}, u32[]{:S(2)}) %collective-permute-start.6) | collective-permute-done | bytes 163872 | tf_op jit(solution)/shard_map/ppermute | solution.py:446
  47.5 1.5 %collective-permute-done.5.refs_5_ = bf16[2,80,512]{2,1,0:T(8,128)(2,1)S(1)} collective-permute-done((bf16[2,80,512]{2,1,0:T(8,128)(2,1)S(1)}, bf16[2,80,512]{2,1,0:T(8,128)(2,1)S(1)}, u32[]{:S(2)}, u32[]{:S(2)}) %collective-permute-start.5) | collective-permute-done | bytes 163872 | tf_op jit(solution)/shard_map/ppermute | solution.py:446
  49.8 1.1 %collective-permute-start.11 = (bf16[80,512]{1,0:T(8,128)(2,1)S(1)}, bf16[80,512]{1,0:T(8,128)(2,1)S(1)}, u32[]{:S(2)}, u32[]{:S(2)}) collective-permute-start(bf16[80,512]{1,0:T(8,128)(2,1)S(1)} %get-tuple-element.20), channel_id=1, source_target_pairs={{0,2},{1,3},{2,0},{3,1},{4,6},{5,7},{6,4},{7,5},{8,10},{9,11},{10,... | collective-permute-start | bytes 245768 | tf_op jit(solution)/shard_map/ppermute | solution.py:461
  51.2 2.0 %collective-permute-start.13 = (bf16[80,512]{1,0:T(8,128)(2,1)S(1)}, bf16[80,512]{1,0:T(8,128)(2,1)S(1)}, u32[]{:S(2)}, u32[]{:S(2)}) collective-permute-start(bf16[80,512]{1,0:T(8,128)(2,1)S(1)} %get-tuple-element.22), channel_id=1, source_target_pairs={{0,4},{1,5},{2,6},{3,7},{4,0},{5,1},{6,2},{7,3},{8,12},{9,13},{10,... | collective-permute-start | bytes 245768 | tf_op jit(solution)/shard_map/ppermute | solution.py:461
  53.6 1.0 %collective-permute-done.11.refs_2_ = bf16[80,512]{1,0:T(8,128)(2,1)S(1)} collective-permute-done((bf16[80,512]{1,0:T(8,128)(2,1)S(1)}, bf16[80,512]{1,0:T(8,128)(2,1)S(1)}, u32[]{:S(2)}, u32[]{:S(2)}) %collective-permute-start.11) | collective-permute-done | bytes 81952 | tf_op jit(solution)/shard_map/ppermute | solution.py:461
  54.6 1.7 %collective-permute-start.15 = (bf16[80,512]{1,0:T(8,128)(2,1)S(1)}, bf16[80,512]{1,0:T(8,128)(2,1)S(1)}, u32[]{:S(2)}, u32[]{:S(2)}) collective-permute-start(bf16[80,512]{1,0:T(8,128)(2,1)S(1)} %get-tuple-element.24), channel_id=1, source_target_pairs={{0,6},{1,7},{2,4},{3,5},{4,2},{5,3},{6,0},{7,1},{8,14},{9,15},{10,... | collective-permute-start | bytes 245768 | tf_op jit(solution)/shard_map/ppermute | solution.py:461
  56.3 1.5 %collective-permute-start.16 = (bf16[80,512]{1,0:T(8,128)(2,1)S(1)}, bf16[80,512]{1,0:T(8,128)(2,1)S(1)}, u32[]{:S(2)}, u32[]{:S(2)}) collective-permute-start(bf16[80,512]{1,0:T(8,128)(2,1)S(1)} %get-tuple-element.25), channel_id=1, source_target_pairs={{0,7},{1,6},{2,5},{3,4},{4,3},{5,2},{6,1},{7,0},{8,15},{9,14},{10,... | collective-permute-start | bytes 245768 | tf_op jit(solution)/shard_map/ppermute | solution.py:461
  57.7 1.0 %collective-permute-done.14.refs_5_ = bf16[80,512]{1,0:T(8,128)(2,1)S(1)} collective-permute-done((bf16[80,512]{1,0:T(8,128)(2,1)S(1)}, bf16[80,512]{1,0:T(8,128)(2,1)S(1)}, u32[]{:S(2)}, u32[]{:S(2)}) %collective-permute-start.14) | collective-permute-done | bytes 81952 | tf_op jit(solution)/shard_map/ppermute | solution.py:461
  58.7 1.3 %collective-permute-done.15.refs_6_ = bf16[80,512]{1,0:T(8,128)(2,1)S(1)} collective-permute-done((bf16[80,512]{1,0:T(8,128)(2,1)S(1)}, bf16[80,512]{1,0:T(8,128)(2,1)S(1)}, u32[]{:S(2)}, u32[]{:S(2)}) %collective-permute-start.15) | collective-permute-done | bytes 81952 | tf_op jit(solution)/shard_map/ppermute | solution.py:461
  60.0 1.9 %collective-permute-done.16.refs_7_ = bf16[80,512]{1,0:T(8,128)(2,1)S(1)} collective-permute-done((bf16[80,512]{1,0:T(8,128)(2,1)S(1)}, bf16[80,512]{1,0:T(8,128)(2,1)S(1)}, u32[]{:S(2)}, u32[]{:S(2)}) %collective-permute-start.16) | collective-permute-done | bytes 81952 | tf_op jit(solution)/shard_map/ppermute | solution.py:461
  61.9 16.2 %stack_products.1 = bf16[2,20,512,1024]{3,2,1,0:T(8,128)(2,1)} custom-call(bf16[80,512]{1,0:T(8,128)(2,1)S(1)} %get-tuple-element.18.refs_0_, bf16[80,512]{1,0:T(8,128)(2,1)S(1)} %collective-permute-done.10.refs_1_, bf16[80,512]{1,0:T(8,128)(2,1)S(1)} %collective-permute-done.11.refs_2_, bf16[80,512]{1,0:T(8,128)(2,1)S(1)} %collective-permute-done.12.refs_3_, ...), custom_call_target="tpu_custom_call" | custom-call | flops 5368709120 | bytes 41943040 | tf_op jit(solution)/shard_map/stack_products/pallas_call | solution.py:384
  (21 shorter events, 1.7 us)
Async XLA Ops:
  12.2 8.0 %copy-start.1 = (f32[88,1024]{1,0:T(8,128)S(1)}, f32[88,1024]{1,0:T(8,128)}, u32[]{:S(2)}) copy-start(f32[88,1024]{1,0:T(8,128)} %get-tuple-element.16.own_ref) | copy-start | bytes 1081348
  12.2 7.9 %collective-permute-start = (bf16[96,1024]{1,0:T(8,128)(2,1)}, bf16[96,1024]{1,0:T(8,128)(2,1)S(1)}, u32[]{:S(2)}, u32[]{:S(2)}) collective-permute-start(bf16[96,1024]{1,0:T(8,128)(2,1)} %get-tuple-element.17), channel_id=1, source_target_pairs={{1,0},{2,1},{3,2},{4,3},{5,4},{6,5},{7,6},{9,8},{10,9},{11,10},{12... | collective-permute-start | bytes 589832 | tf_op jit(solution)/shard_map/ppermute | solution.py:446
  20.2 1.0 %copy-start = (f32[88,1024]{1,0:T(8,128)S(1)}, f32[88,1024]{1,0:T(8,128)}, u32[]{:S(2)}) copy-start(f32[88,1024]{1,0:T(8,128)} %band_spectra_rest.1.rest_ref) | copy-start | bytes 1081348
  21.4 13.0 %collective-permute-start.9 = (bf16[2,80,512]{2,1,0:T(8,128)(2,1)S(1)}, bf16[2,80,512]{2,1,0:T(8,128)(2,1)S(1)}, u32[]{:S(2)}, u32[]{:S(2)}) collective-permute-start(bf16[2,80,512]{2,1,0:T(8,128)(2,1)S(1)} %whiten.1.refs_0_.refs_7_), channel_id=1, source_target_pairs={{0,6},{1,7},{2,4},{3,5},{4,2},{5,3},{6,0},{7,1},{8,14},{9,15},{10,... | collective-permute-start | bytes 491528 | tf_op jit(solution)/shard_map/ppermute | solution.py:461
  26.2 9.6 %collective-permute-start.8 = (bf16[2,80,512]{2,1,0:T(8,128)(2,1)S(1)}, bf16[2,80,512]{2,1,0:T(8,128)(2,1)S(1)}, u32[]{:S(2)}, u32[]{:S(2)}) collective-permute-start(bf16[2,80,512]{2,1,0:T(8,128)(2,1)S(1)} %whiten.1.refs_0_.refs_7_), channel_id=1, source_target_pairs={{0,4},{1,5},{2,6},{3,7},{4,0},{5,1},{6,2},{7,3},{8,12},{9,13},{10,... | collective-permute-start | bytes 491528 | tf_op jit(solution)/shard_map/ppermute | solution.py:461
  26.7 13.6 %collective-permute-start.4 = (bf16[2,80,512]{2,1,0:T(8,128)(2,1)S(1)}, bf16[2,80,512]{2,1,0:T(8,128)(2,1)S(1)}, u32[]{:S(2)}, u32[]{:S(2)}) collective-permute-start(bf16[2,80,512]{2,1,0:T(8,128)(2,1)S(1)} %whiten.1.refs_0_.refs_7_), channel_id=1, source_target_pairs={{16,0},{24,8},{17,1},{25,9},{18,2},{26,10},{19,3},{27,11},{20,4},{... | collective-permute-start | bytes 491528 | tf_op jit(solution)/shard_map/ppermute | solution.py:446
  28.0 13.6 %collective-permute-start.3 = (bf16[2,80,512]{2,1,0:T(8,128)(2,1)S(1)}, bf16[2,80,512]{2,1,0:T(8,128)(2,1)S(1)}, u32[]{:S(2)}, u32[]{:S(2)}) collective-permute-start(bf16[2,80,512]{2,1,0:T(8,128)(2,1)S(1)} %whiten.1.refs_0_.refs_7_), channel_id=1, source_target_pairs={{0,16},{8,24},{1,17},{9,25},{2,18},{10,26},{3,19},{11,27},{4,20},{... | collective-permute-start | bytes 491528 | tf_op jit(solution)/shard_map/ppermute | solution.py:446
  33.5 12.7 %collective-permute-start.7 = (bf16[2,80,512]{2,1,0:T(8,128)(2,1)S(1)}, bf16[2,80,512]{2,1,0:T(8,128)(2,1)S(1)}, u32[]{:S(2)}, u32[]{:S(2)}) collective-permute-start(bf16[2,80,512]{2,1,0:T(8,128)(2,1)S(1)} %whiten.1.refs_0_.refs_7_), channel_id=1, source_target_pairs={{0,2},{1,3},{2,0},{3,1},{4,6},{5,7},{6,4},{7,5},{8,10},{9,11},{10,... | collective-permute-start | bytes 491528 | tf_op jit(solution)/shard_map/ppermute | solution.py:461
  34.5 11.8 %collective-permute-start.2 = (bf16[2,80,512]{2,1,0:T(8,128)(2,1)S(1)}, bf16[2,80,512]{2,1,0:T(8,128)(2,1)S(1)}, u32[]{:S(2)}, u32[]{:S(2)}) collective-permute-start(bf16[2,80,512]{2,1,0:T(8,128)(2,1)S(1)} %whiten.1.refs_0_.refs_7_), channel_id=1, source_target_pairs={{8,0},{16,8},{24,16},{9,1},{17,9},{25,17},{10,2},{18,10},{26,18},{... | collective-permute-start | bytes 491528 | tf_op jit(solution)/shard_map/ppermute | solution.py:446
  35.8 10.5 %collective-permute-start.1 = (bf16[2,80,512]{2,1,0:T(8,128)(2,1)S(1)}, bf16[2,80,512]{2,1,0:T(8,128)(2,1)S(1)}, u32[]{:S(2)}, u32[]{:S(2)}) collective-permute-start(bf16[2,80,512]{2,1,0:T(8,128)(2,1)S(1)} %whiten.1.refs_0_.refs_7_), channel_id=1, source_target_pairs={{0,8},{8,16},{16,24},{1,9},{9,17},{17,25},{2,10},{10,18},{18,26},{... | collective-permute-start | bytes 491528 | tf_op jit(solution)/shard_map/ppermute | solution.py:446
  40.3 7.2 %collective-permute-start.6 = (bf16[2,80,512]{2,1,0:T(8,128)(2,1)S(1)}, bf16[2,80,512]{2,1,0:T(8,128)(2,1)S(1)}, u32[]{:S(2)}, u32[]{:S(2)}) collective-permute-start(bf16[2,80,512]{2,1,0:T(8,128)(2,1)S(1)} %collective-permute-done.4.refs_4_), channel_id=1, source_target_pairs={{8,0},{16,8},{24,16},{9,1},{17,9},{25,17},{10,2},{18,10},{26,18},{... | collective-permute-start | bytes 491528 | tf_op jit(solution)/shard_map/ppermute | solution.py:446
  41.6 7.4 %collective-permute-start.5 = (bf16[2,80,512]{2,1,0:T(8,128)(2,1)S(1)}, bf16[2,80,512]{2,1,0:T(8,128)(2,1)S(1)}, u32[]{:S(2)}, u32[]{:S(2)}) collective-permute-start(bf16[2,80,512]{2,1,0:T(8,128)(2,1)S(1)} %collective-permute-done.3.refs_3_), channel_id=1, source_target_pairs={{0,8},{8,16},{16,24},{1,9},{9,17},{17,25},{2,10},{10,18},{18,26},{... | collective-permute-start | bytes 491528 | tf_op jit(solution)/shard_map/ppermute | solution.py:446
  49.2 12.7 %collective-permute-start.17 = (bf16[4,2,80,512]{3,2,1,0:T(8,128)(2,1)S(1)}, bf16[4,2,80,512]{3,2,1,0:T(8,128)(2,1)S(1)}, u32[]{:S(2)}, u32[]{:S(2)}) collective-permute-start(bf16[4,2,80,512]{3,2,1,0:T(8,128)(2,1)S(1)} %get-tuple-element.26.refs_8_), channel_id=1, source_target_pairs={{0,1},{1,0},{2,3},{3,2},{4,5},{5,4},{6,7},{7,6},{8,9},{9,8},{10,11... | collective-permute-start | bytes 1966088 | tf_op jit(solution)/shard_map/ppermute | solution.py:461
  49.3 4.0 %collective-permute-start.10 = (bf16[80,512]{1,0:T(8,128)(2,1)S(1)}, bf16[80,512]{1,0:T(8,128)(2,1)S(1)}, u32[]{:S(2)}, u32[]{:S(2)}) collective-permute-start(bf16[80,512]{1,0:T(8,128)(2,1)S(1)} %get-tuple-element.19), channel_id=1, source_target_pairs={{0,1},{1,0},{2,3},{3,2},{4,5},{5,4},{6,7},{7,6},{8,9},{9,8},{10,11... | collective-permute-start | bytes 245768 | tf_op jit(solution)/shard_map/ppermute | solution.py:461
  49.8 4.8 %collective-permute-start.11 = (bf16[80,512]{1,0:T(8,128)(2,1)S(1)}, bf16[80,512]{1,0:T(8,128)(2,1)S(1)}, u32[]{:S(2)}, u32[]{:S(2)}) collective-permute-start(bf16[80,512]{1,0:T(8,128)(2,1)S(1)} %get-tuple-element.20), channel_id=1, source_target_pairs={{0,2},{1,3},{2,0},{3,1},{4,6},{5,7},{6,4},{7,5},{8,10},{9,11},{10,... | collective-permute-start | bytes 245768 | tf_op jit(solution)/shard_map/ppermute | solution.py:461
  50.9 5.4 %collective-permute-start.12 = (bf16[80,512]{1,0:T(8,128)(2,1)S(1)}, bf16[80,512]{1,0:T(8,128)(2,1)S(1)}, u32[]{:S(2)}, u32[]{:S(2)}) collective-permute-start(bf16[80,512]{1,0:T(8,128)(2,1)S(1)} %get-tuple-element.21), channel_id=1, source_target_pairs={{0,3},{1,2},{2,1},{3,0},{4,7},{5,6},{6,5},{7,4},{8,11},{9,10},{10,... | collective-permute-start | bytes 245768 | tf_op jit(solution)/shard_map/ppermute | solution.py:461
  51.2 6.5 %collective-permute-start.13 = (bf16[80,512]{1,0:T(8,128)(2,1)S(1)}, bf16[80,512]{1,0:T(8,128)(2,1)S(1)}, u32[]{:S(2)}, u32[]{:S(2)}) collective-permute-start(bf16[80,512]{1,0:T(8,128)(2,1)S(1)} %get-tuple-element.22), channel_id=1, source_target_pairs={{0,4},{1,5},{2,6},{3,7},{4,0},{5,1},{6,2},{7,3},{8,12},{9,13},{10,... | collective-permute-start | bytes 245768 | tf_op jit(solution)/shard_map/ppermute | solution.py:461
  53.2 5.5 %collective-permute-start.14 = (bf16[80,512]{1,0:T(8,128)(2,1)S(1)}, bf16[80,512]{1,0:T(8,128)(2,1)S(1)}, u32[]{:S(2)}, u32[]{:S(2)}) collective-permute-start(bf16[80,512]{1,0:T(8,128)(2,1)S(1)} %get-tuple-element.23), channel_id=1, source_target_pairs={{0,5},{1,4},{2,7},{3,6},{4,1},{5,0},{6,3},{7,2},{8,13},{9,12},{10,... | collective-permute-start | bytes 245768 | tf_op jit(solution)/shard_map/ppermute | solution.py:461
  54.6 5.4 %collective-permute-start.15 = (bf16[80,512]{1,0:T(8,128)(2,1)S(1)}, bf16[80,512]{1,0:T(8,128)(2,1)S(1)}, u32[]{:S(2)}, u32[]{:S(2)}) collective-permute-start(bf16[80,512]{1,0:T(8,128)(2,1)S(1)} %get-tuple-element.24), channel_id=1, source_target_pairs={{0,6},{1,7},{2,4},{3,5},{4,2},{5,3},{6,0},{7,1},{8,14},{9,15},{10,... | collective-permute-start | bytes 245768 | tf_op jit(solution)/shard_map/ppermute | solution.py:461
  56.3 5.6 %collective-permute-start.16 = (bf16[80,512]{1,0:T(8,128)(2,1)S(1)}, bf16[80,512]{1,0:T(8,128)(2,1)S(1)}, u32[]{:S(2)}, u32[]{:S(2)}) collective-permute-start(bf16[80,512]{1,0:T(8,128)(2,1)S(1)} %get-tuple-element.25), channel_id=1, source_target_pairs={{0,7},{1,6},{2,5},{3,4},{4,3},{5,2},{6,1},{7,0},{8,15},{9,14},{10,... | collective-permute-start | bytes 245768 | tf_op jit(solution)/shard_map/ppermute | solution.py:461

commit v8 on v7

--- a/solution.py
+++ b/solution.py
@@ -67,9 +67,10 @@
     ]
     for copy in small:
         copy.start()
+    x_copy(0).start()
     for copy in small:
         copy.wait()
-    for i in range(pl.cdiv(bulk, STEP)):
+    for i in range(1, pl.cdiv(bulk, STEP)):
         x_copy(i).start()
 
     tm = lax.axis_index("tm")
@@ -328,7 +329,8 @@
     channels = halves * span
     exact = math.frexp(scale)[0] == 0.5
 
-    cols = jnp.stack([ref[...].astype(F32) for ref in col_refs])
+    by_partner = dict(zip([0, *partners(devices)], col_refs))
+    cols = jnp.stack([by_partner[away][...].astype(F32) for away in range(devices)])
     if exact:
         cols = cols * scale
     head, tail = cols[:, :ROW_TILE // 2], cols[:, ROW_TILE // 2:]
@@ -403,41 +405,38 @@
             transcendentals=0,
         ),
         name="stack_products",
-    )(*col_blocks, *row_blocks)
-
-
-def pick_kernel(count, reach, row_count, *refs):
-    chan_refs, row_refs = refs[:len(reach)], refs[len(reach):len(reach) + row_count]
-    joined_ref, out_refs, held = refs[len(reach) + row_count], refs[-1 - count:-1], refs[-1]
+    )(*[col_blocks[away] for away in [0, *partners(devices)]], *row_blocks)
+
+
+def pick_kernel(count, chips, *refs):
+    row_refs, chan_refs = refs[:chips], refs[chips:-2 - count]
+    joined_ref, out_refs, held = refs[-2 - count], refs[-1 - count:-1], refs[-1]
     tm, mine = lax.axis_index("tm"), lax.axis_index("chan")
-    size = held.shape[0]
-    halves = chan_refs[0].shape[0]
-    for far, ref in zip(reach, chan_refs):
-        @pl.when(jnp.logical_and(mine + far >= 0, mine + far < size))
-        def _():
-            held[mine + far] = ref[...]
+    halves = row_refs[0].shape[0]
     for i, ref in enumerate(row_refs):
         joined_ref[i] = ref[...]
+    for away, ref in enumerate((row_refs[0], *chan_refs)):
+        held[jnp.bitwise_xor(mine, away)] = ref[...]
     for away, out_ref in enumerate(out_refs):
         wanted = jnp.bitwise_xor(tm, away)
         out_ref[...] = held[wanted // halves, wanted % halves]
 
 
-def picked(blocks, row_blocks, count, chan_count):
-    reach = list(blocks)
-    block = blocks[0]
+def picked(row_blocks, chan_blocks, count):
+    block = row_blocks[0]
     _, rows, width = block.shape
+    chips = len(row_blocks)
     whole = pl.BlockSpec(memory_space=pltpu.VMEM)
     joined, *picks = pl.pallas_call(
-        functools.partial(pick_kernel, count, reach, len(row_blocks)),
-        out_shape=[jax.ShapeDtypeStruct((len(row_blocks), *block.shape), block.dtype)]
+        functools.partial(pick_kernel, count, chips),
+        out_shape=[jax.ShapeDtypeStruct((chips, *block.shape), block.dtype)]
         + [jax.ShapeDtypeStruct((rows, width), block.dtype)] * count,
-        in_specs=[whole] * (len(blocks) + len(row_blocks)),
+        in_specs=[whole] * (chips + len(chan_blocks)),
         out_specs=[whole] * (1 + count),
-        scratch_shapes=[pltpu.VMEM((chan_count, *block.shape), block.dtype)],
+        scratch_shapes=[pltpu.VMEM((1 + len(chan_blocks), *block.shape), block.dtype)],
         compiler_params=pltpu.CompilerParams(vmem_limit_bytes=16 * 2**20),
         name="pick_blocks",
-    )(*blocks.values(), *row_blocks)
+    )(*row_blocks, *chan_blocks)
     return joined, picks
 
 
@@ -446,15 +445,8 @@
     return lax.ppermute(block, axis, [(i + far, i) for i in range(count) if 0 <= i + far < count])
 
 
-def chan_blocks(block):
-    blocks = {0: block}
-    for far in range(1, lax.axis_size("chan")):
-        for sign in (-1, 1):
-            if far < 3:
-                blocks[sign * far] = moved(block, "chan", sign * far)
-            else:
-                blocks[sign * far] = moved(blocks[sign * (far - 1)], "chan", sign)
-    return blocks
+def partners(count):
+    return [*range(2, count, 2), *range(3, count, 2), 1]
 
 
 def from_partner(block, axis, away):
@@ -473,10 +465,10 @@
     more = moved(back, "tm", 1)
     rest, = spectra_of(recording, offsets, band_bins, dead_flags, windows, cut, block_len, 1)
     white = whiten(own, rest, more, bins, windows, halves)
-    blocks = chan_blocks(white)
     row_blocks = [white] + [from_partner(white, "tm", away) for away in range(2, tm_count, 2)]
-    joined, col_blocks = picked(blocks, row_blocks, tm_count, chan_count)
-    for away in range(1, tm_count):
+    chan_blocks = [from_partner(white, "chan", away) for away in range(1, chan_count)]
+    joined, col_blocks = picked(row_blocks, chan_blocks, tm_count)
+    for away in partners(tm_count):
         col_blocks[away] = from_partner(col_blocks[away], "tm", away)
     return stacks_of(col_blocks, [joined, from_partner(joined, "tm", 1)], bins, windows)
 

time: 78.5 us -> 70.7 us (0.901)
  the two profiles are of different devices: /device:TPU:0 before, /device:TPU:19 now
where the time goes in v8:
time: 70.7 us; the launch traced here: 70.4 us
  Pallas kernels  35 us (50%)
  starting transfers between devices  19.2 us (27%)
  waiting for transfers between devices  15.1 us (21%)
  local copies, waits for them, and re-layouts  0.98 us (1%)
    pallas_call x2, Pallas kernels, spectra_of(): pl.pallas_call(functools.partial(spectra_kernel, bins, windows, block_len...  18.4 us
    ppermute x14, starting transfers between devices, from_partner(): lax.ppermute(block, axis, [(i, i ^ away) for i in range(lax.axis_size(axi...  16.5 us
    pallas_call x1, Pallas kernels, stacks_of(): pl.pallas_call(functools.partial(stack_kernel, windows, scale, devices),...  16.2 us
    ppermute x14, waiting for transfers between devices, from_partner(): lax.ppermute(block, axis, [(i, i ^ away) for i in range(lax.axis_size(axi...  15.1 us
    ppermute x1, starting transfers between devices, moved(): lax.ppermute(block, axis, [(i + far, i) for i in range(count) if 0 <= i +...  2.71 us
  transfers between devices with their start and end apart: 15, of which 5 were waited for; matrix products, arithmetic and copies ran while one was open for 0% of the time, Pallas kernels for 8%

profile of v8, /device:TPU:19, one launch (start us, length us, event | category | flops | bytes accessed | tf_op | source)
XLA Modules:
  0.0 70.4 jit_solution(7114720574377739223)
XLA Ops:
  0.0 12.4 %band_spectra.1 = (f32[88,1024]{1,0:T(8,128)}, bf16[96,1024]{1,0:T(8,128)(2,1)}) custom-call(s32[16]{0:T(128)} %offsets_hbm.3, s32[20]{0:T(128)} %bins_hbm.3, s32[1,1024]{1,0:T(1,128)} %bitcast.6, bf16[15000,1024]{1,0:T(8,128)(2,1)} %bitcast.2, bf16[15000,1024]{1,0:T(8,128)(2,1)} %bitcast.3), custom_call_target="tpu_custom_call" | custom-call | flops 3690987520 | bytes 23068672 | tf_op jit(solution)/shard_map/band_spectra/pallas_call | solution.py:254
  12.4 2.7 %collective-permute-start = (bf16[96,1024]{1,0:T(8,128)(2,1)}, bf16[96,1024]{1,0:T(8,128)(2,1)S(1)}, u32[]{:S(2)}, u32[]{:S(2)}) collective-permute-start(bf16[96,1024]{1,0:T(8,128)(2,1)} %get-tuple-element.17), channel_id=1, source_target_pairs={{1,0},{2,1},{3,2},{4,3},{5,4},{6,5},{7,6},{9,8},{10,9},{11,10},{12... | collective-permute-start | bytes 589832 | tf_op jit(solution)/shard_map/ppermute | solution.py:445
  15.1 6.0 %band_spectra_rest.1.rest_ref = f32[88,1024]{1,0:T(8,128)} custom-call(s32[16]{0:T(128)} %offsets_hbm.3, s32[20]{0:T(128)} %bins_hbm.3, s32[1,1024]{1,0:T(1,128)} %bitcast.7, bf16[15000,1024]{1,0:T(8,128)(2,1)} %bitcast.4, bf16[15000,1024]{1,0:T(8,128)(2,1)} %bitcast.5), custom_call_target="tpu_custom_call" | custom-call | flops 612106240 | bytes 7651328 | tf_op jit(solution)/shard_map/band_spectra_rest/pallas_call | solution.py:254
  21.1 1.0 %copy-done = f32[88,1024]{1,0:T(8,128)S(1)} copy-done((f32[88,1024]{1,0:T(8,128)S(1)}, f32[88,1024]{1,0:T(8,128)}, u32[]{:S(2)}) %copy-start) | copy-done | bytes 360472
  22.1 0.3 whiten.1.refs_0_
  22.4 0.2 collective-permute-start.6
  22.6 3.2 %collective-permute-start.5 = (bf16[2,80,512]{2,1,0:T(8,128)(2,1)S(1)}, bf16[2,80,512]{2,1,0:T(8,128)(2,1)S(1)}, u32[]{:S(2)}, u32[]{:S(2)}) collective-permute-start(bf16[2,80,512]{2,1,0:T(8,128)(2,1)S(1)} %whiten.1.refs_0_), channel_id=1, source_target_pairs={{0,16},{8,24},{16,0},{24,8},{1,17},{9,25},{17,1},{25,9},{2,18},{10... | collective-permute-start | bytes 491528 | tf_op jit(solution)/shard_map/ppermute | solution.py:453
  25.9 1.2 %collective-permute-start.3 = (bf16[2,80,512]{2,1,0:T(8,128)(2,1)S(1)}, bf16[2,80,512]{2,1,0:T(8,128)(2,1)S(1)}, u32[]{:S(2)}, u32[]{:S(2)}) collective-permute-start(bf16[2,80,512]{2,1,0:T(8,128)(2,1)S(1)} %whiten.1.refs_0_), channel_id=1, source_target_pairs={{0,6},{1,7},{2,4},{3,5},{4,2},{5,3},{6,0},{7,1},{8,14},{9,15},{10,... | collective-permute-start | bytes 491528 | tf_op jit(solution)/shard_map/ppermute | solution.py:453
  27.1 8.2 %collective-permute-done.6.refs_6_ = bf16[2,80,512]{2,1,0:T(8,128)(2,1)S(1)} collective-permute-done((bf16[2,80,512]{2,1,0:T(8,128)(2,1)S(1)}, bf16[2,80,512]{2,1,0:T(8,128)(2,1)S(1)}, u32[]{:S(2)}, u32[]{:S(2)}) %collective-permute-start.6) | collective-permute-done | bytes 163872 | tf_op jit(solution)/shard_map/ppermute | solution.py:453
  35.3 0.5 collective-permute-start.1
  35.8 1.0 %collective-permute-done.5.refs_5_ = bf16[2,80,512]{2,1,0:T(8,128)(2,1)S(1)} collective-permute-done((bf16[2,80,512]{2,1,0:T(8,128)(2,1)S(1)}, bf16[2,80,512]{2,1,0:T(8,128)(2,1)S(1)}, u32[]{:S(2)}, u32[]{:S(2)}) %collective-permute-start.5) | collective-permute-done | bytes 163872 | tf_op jit(solution)/shard_map/ppermute | solution.py:453
  36.8 3.0 %collective-permute-done.1.refs_1_ = bf16[2,80,512]{2,1,0:T(8,128)(2,1)S(1)} collective-permute-done((bf16[2,80,512]{2,1,0:T(8,128)(2,1)S(1)}, bf16[2,80,512]{2,1,0:T(8,128)(2,1)S(1)}, u32[]{:S(2)}, u32[]{:S(2)}) %collective-permute-start.1) | collective-permute-done | bytes 163872 | tf_op jit(solution)/shard_map/ppermute | solution.py:453
  39.8 0.1 pick_blocks.1
  40.0 2.2 %collective-permute-start.14 = (bf16[4,2,80,512]{3,2,1,0:T(8,128)(2,1)S(1)}, bf16[4,2,80,512]{3,2,1,0:T(8,128)(2,1)S(1)}, u32[]{:S(2)}, u32[]{:S(2)}) collective-permute-start(bf16[4,2,80,512]{3,2,1,0:T(8,128)(2,1)S(1)} %get-tuple-element.26.refs_8_), channel_id=1, source_target_pairs={{0,1},{1,0},{2,3},{3,2},{4,5},{5,4},{6,7},{7,6},{8,9},{9,8},{10,11... | collective-permute-start | bytes 1966088 | tf_op jit(solution)/shard_map/ppermute | solution.py:453
  42.1 0.5 collective-permute-start.7
  42.6 1.9 %collective-permute-start.8 = (bf16[80,512]{1,0:T(8,128)(2,1)S(1)}, bf16[80,512]{1,0:T(8,128)(2,1)S(1)}, u32[]{:S(2)}, u32[]{:S(2)}) collective-permute-start(bf16[80,512]{1,0:T(8,128)(2,1)S(1)} %get-tuple-element.20), channel_id=1, source_target_pairs={{0,4},{1,5},{2,6},{3,7},{4,0},{5,1},{6,2},{7,3},{8,12},{9,13},{10,... | collective-permute-start | bytes 245768 | tf_op jit(solution)/shard_map/ppermute | solution.py:453
  44.5 0.3 collective-permute-start.9
  44.8 1.4 %collective-permute-start.10 = (bf16[80,512]{1,0:T(8,128)(2,1)S(1)}, bf16[80,512]{1,0:T(8,128)(2,1)S(1)}, u32[]{:S(2)}, u32[]{:S(2)}) collective-permute-start(bf16[80,512]{1,0:T(8,128)(2,1)S(1)} %get-tuple-element.22), channel_id=1, source_target_pairs={{0,3},{1,2},{2,1},{3,0},{4,7},{5,6},{6,5},{7,4},{8,11},{9,10},{10,... | collective-permute-start | bytes 245768 | tf_op jit(solution)/shard_map/ppermute | solution.py:453
  46.2 1.9 %collective-permute-start.11 = (bf16[80,512]{1,0:T(8,128)(2,1)S(1)}, bf16[80,512]{1,0:T(8,128)(2,1)S(1)}, u32[]{:S(2)}, u32[]{:S(2)}) collective-permute-start(bf16[80,512]{1,0:T(8,128)(2,1)S(1)} %get-tuple-element.23), channel_id=1, source_target_pairs={{0,5},{1,4},{2,7},{3,6},{4,1},{5,0},{6,3},{7,2},{8,13},{9,12},{10,... | collective-permute-start | bytes 245768 | tf_op jit(solution)/shard_map/ppermute | solution.py:453
  48.2 2.8 %collective-permute-start.12 = (bf16[80,512]{1,0:T(8,128)(2,1)S(1)}, bf16[80,512]{1,0:T(8,128)(2,1)S(1)}, u32[]{:S(2)}, u32[]{:S(2)}) collective-permute-start(bf16[80,512]{1,0:T(8,128)(2,1)S(1)} %get-tuple-element.24), channel_id=1, source_target_pairs={{0,7},{1,6},{2,5},{3,4},{4,3},{5,2},{6,1},{7,0},{8,15},{9,14},{10,... | collective-permute-start | bytes 245768 | tf_op jit(solution)/shard_map/ppermute | solution.py:453
  51.0 0.3 collective-permute-start.13
  51.3 0.7 collective-permute-done.11.refs_5_
  52.0 2.2 %collective-permute-done.12.refs_6_ = bf16[80,512]{1,0:T(8,128)(2,1)S(1)} collective-permute-done((bf16[80,512]{1,0:T(8,128)(2,1)S(1)}, bf16[80,512]{1,0:T(8,128)(2,1)S(1)}, u32[]{:S(2)}, u32[]{:S(2)}) %collective-permute-start.12) | collective-permute-done | bytes 81952 | tf_op jit(solution)/shard_map/ppermute | solution.py:453
  54.2 16.2 %stack_products.1 = bf16[2,20,512,1024]{3,2,1,0:T(8,128)(2,1)} custom-call(bf16[80,512]{1,0:T(8,128)(2,1)S(1)} %get-tuple-element.18.refs_0_, bf16[80,512]{1,0:T(8,128)(2,1)S(1)} %collective-permute-done.7.refs_1_, bf16[80,512]{1,0:T(8,128)(2,1)S(1)} %collective-permute-done.8.refs_2_, bf16[80,512]{1,0:T(8,128)(2,1)S(1)} %collective-permute-done.9.refs_3_, ...), custom_call_target="tpu_custom_call" | custom-call | flops 5368709120 | bytes 41943040 | tf_op jit(solution)/shard_map/stack_products/pallas_call | solution.py:386
  (15 shorter events, 0.1 us)
Async XLA Ops:
  12.4 8.7 %copy-start.1 = (f32[88,1024]{1,0:T(8,128)S(1)}, f32[88,1024]{1,0:T(8,128)}, u32[]{:S(2)}) copy-start(f32[88,1024]{1,0:T(8,128)} %get-tuple-element.16.own_ref) | copy-start | bytes 1081348
  12.4 8.7 %collective-permute-start = (bf16[96,1024]{1,0:T(8,128)(2,1)}, bf16[96,1024]{1,0:T(8,128)(2,1)S(1)}, u32[]{:S(2)}, u32[]{:S(2)}) collective-permute-start(bf16[96,1024]{1,0:T(8,128)(2,1)} %get-tuple-element.17), channel_id=1, source_target_pairs={{1,0},{2,1},{3,2},{4,3},{5,4},{6,5},{7,6},{9,8},{10,9},{11,10},{12... | collective-permute-start | bytes 589832 | tf_op jit(solution)/shard_map/ppermute | solution.py:445
  21.1 1.0 %copy-start = (f32[88,1024]{1,0:T(8,128)S(1)}, f32[88,1024]{1,0:T(8,128)}, u32[]{:S(2)}) copy-start(f32[88,1024]{1,0:T(8,128)} %band_spectra_rest.1.rest_ref) | copy-start | bytes 1081348
  22.4 12.9 %collective-permute-start.6 = (bf16[2,80,512]{2,1,0:T(8,128)(2,1)S(1)}, bf16[2,80,512]{2,1,0:T(8,128)(2,1)S(1)}, u32[]{:S(2)}, u32[]{:S(2)}) collective-permute-start(bf16[2,80,512]{2,1,0:T(8,128)(2,1)S(1)} %whiten.1.refs_0_), channel_id=1, source_target_pairs={{0,24},{8,16},{16,8},{24,0},{1,25},{9,17},{17,9},{25,1},{2,26},{10... | collective-permute-start | bytes 491528 | tf_op jit(solution)/shard_map/ppermute | solution.py:453
  22.6 14.2 %collective-permute-start.5 = (bf16[2,80,512]{2,1,0:T(8,128)(2,1)S(1)}, bf16[2,80,512]{2,1,0:T(8,128)(2,1)S(1)}, u32[]{:S(2)}, u32[]{:S(2)}) collective-permute-start(bf16[2,80,512]{2,1,0:T(8,128)(2,1)S(1)} %whiten.1.refs_0_), channel_id=1, source_target_pairs={{0,16},{8,24},{16,0},{24,8},{1,17},{9,25},{17,1},{25,9},{2,18},{10... | collective-permute-start | bytes 491528 | tf_op jit(solution)/shard_map/ppermute | solution.py:453
  25.9 10.9 %collective-permute-start.4 = (bf16[2,80,512]{2,1,0:T(8,128)(2,1)S(1)}, bf16[2,80,512]{2,1,0:T(8,128)(2,1)S(1)}, u32[]{:S(2)}, u32[]{:S(2)}) collective-permute-start(bf16[2,80,512]{2,1,0:T(8,128)(2,1)S(1)} %whiten.1.refs_0_), channel_id=1, source_target_pairs={{0,8},{8,0},{16,24},{24,16},{1,9},{9,1},{17,25},{25,17},{2,10},{10... | collective-permute-start | bytes 491528 | tf_op jit(solution)/shard_map/ppermute | solution.py:453
  25.9 10.9 %collective-permute-start.3 = (bf16[2,80,512]{2,1,0:T(8,128)(2,1)S(1)}, bf16[2,80,512]{2,1,0:T(8,128)(2,1)S(1)}, u32[]{:S(2)}, u32[]{:S(2)}) collective-permute-start(bf16[2,80,512]{2,1,0:T(8,128)(2,1)S(1)} %whiten.1.refs_0_), channel_id=1, source_target_pairs={{0,6},{1,7},{2,4},{3,5},{4,2},{5,3},{6,0},{7,1},{8,14},{9,15},{10,... | collective-permute-start | bytes 491528 | tf_op jit(solution)/shard_map/ppermute | solution.py:453
  27.1 9.7 %collective-permute-start.2 = (bf16[2,80,512]{2,1,0:T(8,128)(2,1)S(1)}, bf16[2,80,512]{2,1,0:T(8,128)(2,1)S(1)}, u32[]{:S(2)}, u32[]{:S(2)}) collective-permute-start(bf16[2,80,512]{2,1,0:T(8,128)(2,1)S(1)} %whiten.1.refs_0_), channel_id=1, source_target_pairs={{0,4},{1,5},{2,6},{3,7},{4,0},{5,1},{6,2},{7,3},{8,12},{9,13},{10,... | collective-permute-start | bytes 491528 | tf_op jit(solution)/shard_map/ppermute | solution.py:453
  35.3 4.5 %collective-permute-start.1 = (bf16[2,80,512]{2,1,0:T(8,128)(2,1)S(1)}, bf16[2,80,512]{2,1,0:T(8,128)(2,1)S(1)}, u32[]{:S(2)}, u32[]{:S(2)}) collective-permute-start(bf16[2,80,512]{2,1,0:T(8,128)(2,1)S(1)} %whiten.1.refs_0_), channel_id=1, source_target_pairs={{0,2},{1,3},{2,0},{3,1},{4,6},{5,7},{6,4},{7,5},{8,10},{9,11},{10,... | collective-permute-start | bytes 491528 | tf_op jit(solution)/shard_map/ppermute | solution.py:453
  40.0 14.2 %collective-permute-start.14 = (bf16[4,2,80,512]{3,2,1,0:T(8,128)(2,1)S(1)}, bf16[4,2,80,512]{3,2,1,0:T(8,128)(2,1)S(1)}, u32[]{:S(2)}, u32[]{:S(2)}) collective-permute-start(bf16[4,2,80,512]{3,2,1,0:T(8,128)(2,1)S(1)} %get-tuple-element.26.refs_8_), channel_id=1, source_target_pairs={{0,1},{1,0},{2,3},{3,2},{4,5},{5,4},{6,7},{7,6},{8,9},{9,8},{10,11... | collective-permute-start | bytes 1966088 | tf_op jit(solution)/shard_map/ppermute | solution.py:453
  42.1 4.1 %collective-permute-start.7 = (bf16[80,512]{1,0:T(8,128)(2,1)S(1)}, bf16[80,512]{1,0:T(8,128)(2,1)S(1)}, u32[]{:S(2)}, u32[]{:S(2)}) collective-permute-start(bf16[80,512]{1,0:T(8,128)(2,1)S(1)} %get-tuple-element.19), channel_id=1, source_target_pairs={{0,2},{1,3},{2,0},{3,1},{4,6},{5,7},{6,4},{7,5},{8,10},{9,11},{10,... | collective-permute-start | bytes 245768 | tf_op jit(solution)/shard_map/ppermute | solution.py:453
  42.6 5.5 %collective-permute-start.8 = (bf16[80,512]{1,0:T(8,128)(2,1)S(1)}, bf16[80,512]{1,0:T(8,128)(2,1)S(1)}, u32[]{:S(2)}, u32[]{:S(2)}) collective-permute-start(bf16[80,512]{1,0:T(8,128)(2,1)S(1)} %get-tuple-element.20), channel_id=1, source_target_pairs={{0,4},{1,5},{2,6},{3,7},{4,0},{5,1},{6,2},{7,3},{8,12},{9,13},{10,... | collective-permute-start | bytes 245768 | tf_op jit(solution)/shard_map/ppermute | solution.py:453
  44.5 6.5 %collective-permute-start.9 = (bf16[80,512]{1,0:T(8,128)(2,1)S(1)}, bf16[80,512]{1,0:T(8,128)(2,1)S(1)}, u32[]{:S(2)}, u32[]{:S(2)}) collective-permute-start(bf16[80,512]{1,0:T(8,128)(2,1)S(1)} %get-tuple-element.21), channel_id=1, source_target_pairs={{0,6},{1,7},{2,4},{3,5},{4,2},{5,3},{6,0},{7,1},{8,14},{9,15},{10,... | collective-permute-start | bytes 245768 | tf_op jit(solution)/shard_map/ppermute | solution.py:453
  44.8 6.5 %collective-permute-start.10 = (bf16[80,512]{1,0:T(8,128)(2,1)S(1)}, bf16[80,512]{1,0:T(8,128)(2,1)S(1)}, u32[]{:S(2)}, u32[]{:S(2)}) collective-permute-start(bf16[80,512]{1,0:T(8,128)(2,1)S(1)} %get-tuple-element.22), channel_id=1, source_target_pairs={{0,3},{1,2},{2,1},{3,0},{4,7},{5,6},{6,5},{7,4},{8,11},{9,10},{10,... | collective-permute-start | bytes 245768 | tf_op jit(solution)/shard_map/ppermute | solution.py:453
  46.2 5.8 %collective-permute-start.11 = (bf16[80,512]{1,0:T(8,128)(2,1)S(1)}, bf16[80,512]{1,0:T(8,128)(2,1)S(1)}, u32[]{:S(2)}, u32[]{:S(2)}) collective-permute-start(bf16[80,512]{1,0:T(8,128)(2,1)S(1)} %get-tuple-element.23), channel_id=1, source_target_pairs={{0,5},{1,4},{2,7},{3,6},{4,1},{5,0},{6,3},{7,2},{8,13},{9,12},{10,... | collective-permute-start | bytes 245768 | tf_op jit(solution)/shard_map/ppermute | solution.py:453
  48.2 6.0 %collective-permute-start.12 = (bf16[80,512]{1,0:T(8,128)(2,1)S(1)}, bf16[80,512]{1,0:T(8,128)(2,1)S(1)}, u32[]{:S(2)}, u32[]{:S(2)}) collective-permute-start(bf16[80,512]{1,0:T(8,128)(2,1)S(1)} %get-tuple-element.24), channel_id=1, source_target_pairs={{0,7},{1,6},{2,5},{3,4},{4,3},{5,2},{6,1},{7,0},{8,15},{9,14},{10,... | collective-permute-start | bytes 245768 | tf_op jit(solution)/shard_map/ppermute | solution.py:453
  51.0 3.2 %collective-permute-start.13 = (bf16[80,512]{1,0:T(8,128)(2,1)S(1)}, bf16[80,512]{1,0:T(8,128)(2,1)S(1)}, u32[]{:S(2)}, u32[]{:S(2)}) collective-permute-start(bf16[80,512]{1,0:T(8,128)(2,1)S(1)} %get-tuple-element.25), channel_id=1, source_target_pairs={{0,1},{1,0},{2,3},{3,2},{4,5},{5,4},{6,7},{7,6},{8,9},{9,8},{10,11... | collective-permute-start | bytes 245768 | tf_op jit(solution)/shard_map/ppermute | solution.py:453

commit v9 on v8

--- a/solution.py
+++ b/solution.py
@@ -283,10 +283,12 @@
     )(offsets, band_bins, dead.reshape(1, channels), samples, samples)
 
 
-def whiten_kernel(bins, windows, own_ref, rest_ref, more_ref, white_ref):
+def whiten_kernel(bins, windows, own_ref, rest_ref, within_ref, across_ref, white_ref):
     rows = bins * windows * 2
-    raw = own_ref[:rows, :] + rest_ref[:rows, :] + more_ref[:rows, :].astype(F32)
-    extra = more_ref[rows:, :].astype(F32)
+    even = lax.axis_index("tm") % 2 == 0
+    more = jnp.where(even, within_ref[...].astype(F32), across_ref[...].astype(F32))
+    raw = own_ref[:rows, :] + rest_ref[:rows, :] + more[:rows]
+    extra = more[rows:]
     which = lax.broadcasted_iota(jnp.int32, (rows, 1), 0) % windows
     alive = own_ref[rows + windows:rows + windows + 1, :]
     scale = factor = None
@@ -308,14 +310,14 @@
         white_ref[h] = white[:, h * width:(h + 1) * width]
 
 
-def whiten(own, rest, more, bins, windows, halves):
+def whiten(own, rest, within, across, bins, windows, halves):
     channels = own.shape[1]
     return pl.pallas_call(
         functools.partial(whiten_kernel, bins, windows),
         out_shape=jax.ShapeDtypeStruct((halves, bins * windows * 2, channels // halves), BF16),
         compiler_params=pltpu.CompilerParams(vmem_limit_bytes=12 * 2**20),
         name="whiten",
-    )(own, rest, more)
+    )(own, rest, within, across)
 
 
 def stack_kernel(windows, scale, devices, *refs):
@@ -440,13 +442,24 @@
     return joined, picks
 
 
-def moved(block, axis, far):
+def earlier_share(block, axis):
     count = lax.axis_size(axis)
-    return lax.ppermute(block, axis, [(i + far, i) for i in range(count) if 0 <= i + far < count])
+    within = lax.ppermute(block, axis, [(i + 1, i) for i in range(0, count - 1, 2)])
+    across = lax.ppermute(block, axis, [(i + 1, i) for i in range(1, count - 1, 2)])
+    return within, across
 
 
 def partners(count):
     return [*range(2, count, 2), *range(3, count, 2), 1]
+
+
+def chan_blocks_of(block):
+    count = lax.axis_size("chan")
+    blocks = {0: block}
+    for away in range(1, count):
+        near = away & -away
+        blocks[away] = from_partner(blocks[away ^ near], "chan", near)
+    return [blocks[away] for away in range(1, count)]
 
 
 def from_partner(block, axis, away):
@@ -462,11 +475,11 @@
     rim = L // 2 + L // 4
     cut = min(pl.cdiv(rim, STEP) * STEP, block_len)
     own, back = spectra_of(recording, offsets, band_bins, dead_flags, windows, 0, cut, 2)
-    more = moved(back, "tm", 1)
+    more = earlier_share(back, "tm")
     rest, = spectra_of(recording, offsets, band_bins, dead_flags, windows, cut, block_len, 1)
-    white = whiten(own, rest, more, bins, windows, halves)
+    white = whiten(own, rest, *more, bins, windows, halves)
     row_blocks = [white] + [from_partner(white, "tm", away) for away in range(2, tm_count, 2)]
-    chan_blocks = [from_partner(white, "chan", away) for away in range(1, chan_count)]
+    chan_blocks = chan_blocks_of(white)
     joined, col_blocks = picked(row_blocks, chan_blocks, tm_count)
     for away in partners(tm_count):
         col_blocks[away] = from_partner(col_blocks[away], "tm", away)

time: 70.7 us -> 71.1 us (level)
  the two profiles are of different devices: /device:TPU:19 before, /device:TPU:0 now
where the time goes in v9:
time: 71.1 us; the launch traced here: 70.2 us
  Pallas kernels  34.8 us (49%)
  starting transfers between devices  24.4 us (34%)
  waiting for transfers between devices  9.87 us (14%)
  local copies, waits for them, and re-layouts  0.98 us (1%)
    ppermute x14, starting transfers between devices, from_partner(): lax.ppermute(block, axis, [(i, i ^ away) for i in range(lax.axis_size(axi...  22.3 us
    pallas_call x2, Pallas kernels, spectra_of(): pl.pallas_call(functools.partial(spectra_kernel, bins, windows, block_len...  18.2 us
    pallas_call x1, Pallas kernels, stacks_of(): pl.pallas_call(functools.partial(stack_kernel, windows, scale, devices),...  16.2 us
    ppermute x14, waiting for transfers between devices, from_partner(): lax.ppermute(block, axis, [(i, i ^ away) for i in range(lax.axis_size(axi...  9.87 us
  transfers between devices with their start and end apart: 16, of which 8 were waited for; matrix products, arithmetic and copies ran while one was open for 0% of the time, Pallas kernels for 8%

profile of v9, /device:TPU:0, one launch (start us, length us, event | category | flops | bytes accessed | tf_op | source)
XLA Modules:
  0.0 70.2 jit_solution(4986754252345858765)
XLA Ops:
  0.0 12.2 %band_spectra.1 = (f32[88,1024]{1,0:T(8,128)}, bf16[96,1024]{1,0:T(8,128)(2,1)}) custom-call(s32[16]{0:T(128)} %offsets_hbm.3, s32[20]{0:T(128)} %bins_hbm.3, s32[1,1024]{1,0:T(1,128)} %bitcast.6, bf16[15000,1024]{1,0:T(8,128)(2,1)} %bitcast.2, bf16[15000,1024]{1,0:T(8,128)(2,1)} %bitcast.3), custom_call_target="tpu_custom_call" | custom-call | flops 3690987520 | bytes 23068672 | tf_op jit(solution)/shard_map/band_spectra/pallas_call | solution.py:254
  12.2 0.8 %collective-permute-start.1 = (bf16[96,1024]{1,0:T(8,128)(2,1)}, bf16[96,1024]{1,0:T(8,128)(2,1)S(1)}, u32[]{:S(2)}, u32[]{:S(2)}) collective-permute-start(bf16[96,1024]{1,0:T(8,128)(2,1)} %get-tuple-element.17), channel_id=1, source_target_pairs={{2,1},{4,3},{6,5},{10,9},{12,11},{14,13},{18,17},{20,19},{22,21},{... | collective-permute-start | bytes 589832 | tf_op jit(solution)/shard_map/ppermute | solution.py:448
  13.0 1.3 %collective-permute-start = (bf16[96,1024]{1,0:T(8,128)(2,1)}, bf16[96,1024]{1,0:T(8,128)(2,1)S(1)}, u32[]{:S(2)}, u32[]{:S(2)}) collective-permute-start(bf16[96,1024]{1,0:T(8,128)(2,1)} %get-tuple-element.17), channel_id=1, source_target_pairs={{1,0},{3,2},{5,4},{7,6},{9,8},{11,10},{13,12},{15,14},{17,16},{19,... | collective-permute-start | bytes 589832 | tf_op jit(solution)/shard_map/ppermute | solution.py:447
  14.3 6.0 %band_spectra_rest.1.rest_ref = f32[88,1024]{1,0:T(8,128)} custom-call(s32[16]{0:T(128)} %offsets_hbm.3, s32[20]{0:T(128)} %bins_hbm.3, s32[1,1024]{1,0:T(1,128)} %bitcast.7, bf16[15000,1024]{1,0:T(8,128)(2,1)} %bitcast.4, bf16[15000,1024]{1,0:T(8,128)(2,1)} %bitcast.5), custom_call_target="tpu_custom_call" | custom-call | flops 612106240 | bytes 7651328 | tf_op jit(solution)/shard_map/band_spectra_rest/pallas_call | solution.py:254
  20.3 1.0 %copy-done = f32[88,1024]{1,0:T(8,128)S(1)} copy-done((f32[88,1024]{1,0:T(8,128)S(1)}, f32[88,1024]{1,0:T(8,128)}, u32[]{:S(2)}) %copy-start) | copy-done | bytes 360472
  21.6 4.1 %collective-permute-start.6 = (bf16[2,80,512]{2,1,0:T(8,128)(2,1)S(1)}, bf16[2,80,512]{2,1,0:T(8,128)(2,1)S(1)}, u32[]{:S(2)}, u32[]{:S(2)}) collective-permute-start(bf16[2,80,512]{2,1,0:T(8,128)(2,1)S(1)} %whiten.1.refs_0_), channel_id=1, source_target_pairs={{0,16},{8,24},{16,0},{24,8},{1,17},{9,25},{17,1},{25,9},{2,18},{10... | collective-permute-start | bytes 491528 | tf_op jit(solution)/shard_map/ppermute | solution.py:466
  25.7 1.6 %collective-permute-start.5 = (bf16[2,80,512]{2,1,0:T(8,128)(2,1)S(1)}, bf16[2,80,512]{2,1,0:T(8,128)(2,1)S(1)}, u32[]{:S(2)}, u32[]{:S(2)}) collective-permute-start(bf16[2,80,512]{2,1,0:T(8,128)(2,1)S(1)} %whiten.1.refs_0_), channel_id=1, source_target_pairs={{0,8},{8,0},{16,24},{24,16},{1,9},{9,1},{17,25},{25,17},{2,10},{10... | collective-permute-start | bytes 491528 | tf_op jit(solution)/shard_map/ppermute | solution.py:466
  27.3 3.7 %collective-permute-start.4 = (bf16[2,80,512]{2,1,0:T(8,128)(2,1)S(1)}, bf16[2,80,512]{2,1,0:T(8,128)(2,1)S(1)}, u32[]{:S(2)}, u32[]{:S(2)}) collective-permute-start(bf16[2,80,512]{2,1,0:T(8,128)(2,1)S(1)} %whiten.1.refs_0_), channel_id=1, source_target_pairs={{0,6},{1,7},{2,4},{3,5},{4,2},{5,3},{6,0},{7,1},{8,14},{9,15},{10,... | collective-permute-start | bytes 491528 | tf_op jit(solution)/shard_map/ppermute | solution.py:466
  31.0 0.6 collective-permute-start.3
  31.6 0.9 %collective-permute-start.2 = (bf16[2,80,512]{2,1,0:T(8,128)(2,1)S(1)}, bf16[2,80,512]{2,1,0:T(8,128)(2,1)S(1)}, u32[]{:S(2)}, u32[]{:S(2)}) collective-permute-start(bf16[2,80,512]{2,1,0:T(8,128)(2,1)S(1)} %whiten.1.refs_0_), channel_id=1, source_target_pairs={{0,2},{1,3},{2,0},{3,1},{4,6},{5,7},{6,4},{7,5},{8,10},{9,11},{10,... | collective-permute-start | bytes 491528 | tf_op jit(solution)/shard_map/ppermute | solution.py:466
  32.5 1.5 %collective-permute-done.6.refs_5_ = bf16[2,80,512]{2,1,0:T(8,128)(2,1)S(1)} collective-permute-done((bf16[2,80,512]{2,1,0:T(8,128)(2,1)S(1)}, bf16[2,80,512]{2,1,0:T(8,128)(2,1)S(1)}, u32[]{:S(2)}, u32[]{:S(2)}) %collective-permute-start.6) | collective-permute-done | bytes 163872 | tf_op jit(solution)/shard_map/ppermute | solution.py:466
  34.0 1.3 %collective-permute-start.7 = (bf16[2,80,512]{2,1,0:T(8,128)(2,1)S(1)}, bf16[2,80,512]{2,1,0:T(8,128)(2,1)S(1)}, u32[]{:S(2)}, u32[]{:S(2)}) collective-permute-start(bf16[2,80,512]{2,1,0:T(8,128)(2,1)S(1)} %collective-permute-done.6.refs_5_), channel_id=1, source_target_pairs={{0,8},{8,0},{16,24},{24,16},{1,9},{9,1},{17,25},{25,17},{2,10},{10... | collective-permute-start | bytes 491528 | tf_op jit(solution)/shard_map/ppermute | solution.py:466
  35.3 0.8 %collective-permute-done.4.refs_3_ = bf16[2,80,512]{2,1,0:T(8,128)(2,1)S(1)} collective-permute-done((bf16[2,80,512]{2,1,0:T(8,128)(2,1)S(1)}, bf16[2,80,512]{2,1,0:T(8,128)(2,1)S(1)}, u32[]{:S(2)}, u32[]{:S(2)}) %collective-permute-start.4) | collective-permute-done | bytes 163872 | tf_op jit(solution)/shard_map/ppermute | solution.py:466
  36.1 3.4 %collective-permute-done.3.refs_2_ = bf16[2,80,512]{2,1,0:T(8,128)(2,1)S(1)} collective-permute-done((bf16[2,80,512]{2,1,0:T(8,128)(2,1)S(1)}, bf16[2,80,512]{2,1,0:T(8,128)(2,1)S(1)}, u32[]{:S(2)}, u32[]{:S(2)}) %collective-permute-start.3) | collective-permute-done | bytes 163872 | tf_op jit(solution)/shard_map/ppermute | solution.py:466
  39.4 1.3 %collective-permute-done.2.refs_1_ = bf16[2,80,512]{2,1,0:T(8,128)(2,1)S(1)} collective-permute-done((bf16[2,80,512]{2,1,0:T(8,128)(2,1)S(1)}, bf16[2,80,512]{2,1,0:T(8,128)(2,1)S(1)}, u32[]{:S(2)}, u32[]{:S(2)}) %collective-permute-start.2) | collective-permute-done | bytes 163872 | tf_op jit(solution)/shard_map/ppermute | solution.py:466
  40.9 2.7 %collective-permute-start.8 = (bf16[80,512]{1,0:T(8,128)(2,1)S(1)}, bf16[80,512]{1,0:T(8,128)(2,1)S(1)}, u32[]{:S(2)}, u32[]{:S(2)}) collective-permute-start(bf16[80,512]{1,0:T(8,128)(2,1)S(1)} %get-tuple-element.19), channel_id=1, source_target_pairs={{0,2},{1,3},{2,0},{3,1},{4,6},{5,7},{6,4},{7,5},{8,10},{9,11},{10,... | collective-permute-start | bytes 245768 | tf_op jit(solution)/shard_map/ppermute | solution.py:466
  43.7 1.7 %collective-permute-start.9 = (bf16[80,512]{1,0:T(8,128)(2,1)S(1)}, bf16[80,512]{1,0:T(8,128)(2,1)S(1)}, u32[]{:S(2)}, u32[]{:S(2)}) collective-permute-start(bf16[80,512]{1,0:T(8,128)(2,1)S(1)} %get-tuple-element.20), channel_id=1, source_target_pairs={{0,4},{1,5},{2,6},{3,7},{4,0},{5,1},{6,2},{7,3},{8,12},{9,13},{10,... | collective-permute-start | bytes 245768 | tf_op jit(solution)/shard_map/ppermute | solution.py:466
  45.4 1.0 %collective-permute-start.10 = (bf16[80,512]{1,0:T(8,128)(2,1)S(1)}, bf16[80,512]{1,0:T(8,128)(2,1)S(1)}, u32[]{:S(2)}, u32[]{:S(2)}) collective-permute-start(bf16[80,512]{1,0:T(8,128)(2,1)S(1)} %get-tuple-element.21), channel_id=1, source_target_pairs={{0,6},{1,7},{2,4},{3,5},{4,2},{5,3},{6,0},{7,1},{8,14},{9,15},{10,... | collective-permute-start | bytes 245768 | tf_op jit(solution)/shard_map/ppermute | solution.py:466
  46.7 2.3 %collective-permute-start.12 = (bf16[80,512]{1,0:T(8,128)(2,1)S(1)}, bf16[80,512]{1,0:T(8,128)(2,1)S(1)}, u32[]{:S(2)}, u32[]{:S(2)}) collective-permute-start(bf16[80,512]{1,0:T(8,128)(2,1)S(1)} %get-tuple-element.23), channel_id=1, source_target_pairs={{0,5},{1,4},{2,7},{3,6},{4,1},{5,0},{6,3},{7,2},{8,13},{9,12},{10,... | collective-permute-start | bytes 245768 | tf_op jit(solution)/shard_map/ppermute | solution.py:466
  49.2 0.6 collective-permute-start.13
  49.8 1.1 %collective-permute-done.10.refs_3_ = bf16[80,512]{1,0:T(8,128)(2,1)S(1)} collective-permute-done((bf16[80,512]{1,0:T(8,128)(2,1)S(1)}, bf16[80,512]{1,0:T(8,128)(2,1)S(1)}, u32[]{:S(2)}, u32[]{:S(2)}) %collective-permute-start.10) | collective-permute-done | bytes 81952 | tf_op jit(solution)/shard_map/ppermute | solution.py:466
  51.0 1.8 %collective-permute-start.14 = (bf16[80,512]{1,0:T(8,128)(2,1)S(1)}, bf16[80,512]{1,0:T(8,128)(2,1)S(1)}, u32[]{:S(2)}, u32[]{:S(2)}) collective-permute-start(bf16[80,512]{1,0:T(8,128)(2,1)S(1)} %get-tuple-element.25), channel_id=1, source_target_pairs={{0,1},{1,0},{2,3},{3,2},{4,5},{5,4},{6,7},{7,6},{8,9},{9,8},{10,11... | collective-permute-start | bytes 245768 | tf_op jit(solution)/shard_map/ppermute | solution.py:466
  52.8 1.2 %collective-permute-done.13.refs_6_ = bf16[80,512]{1,0:T(8,128)(2,1)S(1)} collective-permute-done((bf16[80,512]{1,0:T(8,128)(2,1)S(1)}, bf16[80,512]{1,0:T(8,128)(2,1)S(1)}, u32[]{:S(2)}, u32[]{:S(2)}) %collective-permute-start.13) | collective-permute-done | bytes 81952 | tf_op jit(solution)/shard_map/ppermute | solution.py:466
  54.0 16.2 %stack_products.1 = bf16[2,20,512,1024]{3,2,1,0:T(8,128)(2,1)} custom-call(bf16[80,512]{1,0:T(8,128)(2,1)S(1)} %get-tuple-element.18.refs_0_, bf16[80,512]{1,0:T(8,128)(2,1)S(1)} %collective-permute-done.8.refs_1_, bf16[80,512]{1,0:T(8,128)(2,1)S(1)} %collective-permute-done.9.refs_2_, bf16[80,512]{1,0:T(8,128)(2,1)S(1)} %collective-permute-done.10.refs_3_, ...), custom_call_target="tpu_custom_call" | custom-call | flops 5368709120 | bytes 41943040 | tf_op jit(solution)/shard_map/stack_products/pallas_call | solution.py:388
  (17 shorter events, 1.1 us)
Async XLA Ops:
  12.2 8.1 %copy-start.1 = (f32[88,1024]{1,0:T(8,128)S(1)}, f32[88,1024]{1,0:T(8,128)}, u32[]{:S(2)}) copy-start(f32[88,1024]{1,0:T(8,128)} %get-tuple-element.16.own_ref) | copy-start | bytes 1081348
  12.2 8.1 %collective-permute-start.1 = (bf16[96,1024]{1,0:T(8,128)(2,1)}, bf16[96,1024]{1,0:T(8,128)(2,1)S(1)}, u32[]{:S(2)}, u32[]{:S(2)}) collective-permute-start(bf16[96,1024]{1,0:T(8,128)(2,1)} %get-tuple-element.17), channel_id=1, source_target_pairs={{2,1},{4,3},{6,5},{10,9},{12,11},{14,13},{18,17},{20,19},{22,21},{... | collective-permute-start | bytes 589832 | tf_op jit(solution)/shard_map/ppermute | solution.py:448
  13.0 7.3 %collective-permute-start = (bf16[96,1024]{1,0:T(8,128)(2,1)}, bf16[96,1024]{1,0:T(8,128)(2,1)S(1)}, u32[]{:S(2)}, u32[]{:S(2)}) collective-permute-start(bf16[96,1024]{1,0:T(8,128)(2,1)} %get-tuple-element.17), channel_id=1, source_target_pairs={{1,0},{3,2},{5,4},{7,6},{9,8},{11,10},{13,12},{15,14},{17,16},{19,... | collective-permute-start | bytes 589832 | tf_op jit(solution)/shard_map/ppermute | solution.py:447
  20.3 1.0 %copy-start = (f32[88,1024]{1,0:T(8,128)S(1)}, f32[88,1024]{1,0:T(8,128)}, u32[]{:S(2)}) copy-start(f32[88,1024]{1,0:T(8,128)} %band_spectra_rest.1.rest_ref) | copy-start | bytes 1081348
  21.6 12.4 %collective-permute-start.6 = (bf16[2,80,512]{2,1,0:T(8,128)(2,1)S(1)}, bf16[2,80,512]{2,1,0:T(8,128)(2,1)S(1)}, u32[]{:S(2)}, u32[]{:S(2)}) collective-permute-start(bf16[2,80,512]{2,1,0:T(8,128)(2,1)S(1)} %whiten.1.refs_0_), channel_id=1, source_target_pairs={{0,16},{8,24},{16,0},{24,8},{1,17},{9,25},{17,1},{25,9},{2,18},{10... | collective-permute-start | bytes 491528 | tf_op jit(solution)/shard_map/ppermute | solution.py:466
  25.7 9.6 %collective-permute-start.5 = (bf16[2,80,512]{2,1,0:T(8,128)(2,1)S(1)}, bf16[2,80,512]{2,1,0:T(8,128)(2,1)S(1)}, u32[]{:S(2)}, u32[]{:S(2)}) collective-permute-start(bf16[2,80,512]{2,1,0:T(8,128)(2,1)S(1)} %whiten.1.refs_0_), channel_id=1, source_target_pairs={{0,8},{8,0},{16,24},{24,16},{1,9},{9,1},{17,25},{25,17},{2,10},{10... | collective-permute-start | bytes 491528 | tf_op jit(solution)/shard_map/ppermute | solution.py:466
  27.3 8.8 %collective-permute-start.4 = (bf16[2,80,512]{2,1,0:T(8,128)(2,1)S(1)}, bf16[2,80,512]{2,1,0:T(8,128)(2,1)S(1)}, u32[]{:S(2)}, u32[]{:S(2)}) collective-permute-start(bf16[2,80,512]{2,1,0:T(8,128)(2,1)S(1)} %whiten.1.refs_0_), channel_id=1, source_target_pairs={{0,6},{1,7},{2,4},{3,5},{4,2},{5,3},{6,0},{7,1},{8,14},{9,15},{10,... | collective-permute-start | bytes 491528 | tf_op jit(solution)/shard_map/ppermute | solution.py:466
  31.0 8.4 %collective-permute-start.3 = (bf16[2,80,512]{2,1,0:T(8,128)(2,1)S(1)}, bf16[2,80,512]{2,1,0:T(8,128)(2,1)S(1)}, u32[]{:S(2)}, u32[]{:S(2)}) collective-permute-start(bf16[2,80,512]{2,1,0:T(8,128)(2,1)S(1)} %whiten.1.refs_0_), channel_id=1, source_target_pairs={{0,4},{1,5},{2,6},{3,7},{4,0},{5,1},{6,2},{7,3},{8,12},{9,13},{10,... | collective-permute-start | bytes 491528 | tf_op jit(solution)/shard_map/ppermute | solution.py:466
  31.6 9.1 %collective-permute-start.2 = (bf16[2,80,512]{2,1,0:T(8,128)(2,1)S(1)}, bf16[2,80,512]{2,1,0:T(8,128)(2,1)S(1)}, u32[]{:S(2)}, u32[]{:S(2)}) collective-permute-start(bf16[2,80,512]{2,1,0:T(8,128)(2,1)S(1)} %whiten.1.refs_0_), channel_id=1, source_target_pairs={{0,2},{1,3},{2,0},{3,1},{4,6},{5,7},{6,4},{7,5},{8,10},{9,11},{10,... | collective-permute-start | bytes 491528 | tf_op jit(solution)/shard_map/ppermute | solution.py:466
  34.0 6.7 %collective-permute-start.7 = (bf16[2,80,512]{2,1,0:T(8,128)(2,1)S(1)}, bf16[2,80,512]{2,1,0:T(8,128)(2,1)S(1)}, u32[]{:S(2)}, u32[]{:S(2)}) collective-permute-start(bf16[2,80,512]{2,1,0:T(8,128)(2,1)S(1)} %collective-permute-done.6.refs_5_), channel_id=1, source_target_pairs={{0,8},{8,0},{16,24},{24,16},{1,9},{9,1},{17,25},{25,17},{2,10},{10... | collective-permute-start | bytes 491528 | tf_op jit(solution)/shard_map/ppermute | solution.py:466
  40.8 13.1 %collective-permute-start.15 = (bf16[4,2,80,512]{3,2,1,0:T(8,128)(2,1)S(1)}, bf16[4,2,80,512]{3,2,1,0:T(8,128)(2,1)S(1)}, u32[]{:S(2)}, u32[]{:S(2)}) collective-permute-start(bf16[4,2,80,512]{3,2,1,0:T(8,128)(2,1)S(1)} %get-tuple-element.26.refs_8_), channel_id=1, source_target_pairs={{0,1},{1,0},{2,3},{3,2},{4,5},{5,4},{6,7},{7,6},{8,9},{9,8},{10,11... | collective-permute-start | bytes 1966088 | tf_op jit(solution)/shard_map/ppermute | solution.py:466
  40.9 5.8 %collective-permute-start.8 = (bf16[80,512]{1,0:T(8,128)(2,1)S(1)}, bf16[80,512]{1,0:T(8,128)(2,1)S(1)}, u32[]{:S(2)}, u32[]{:S(2)}) collective-permute-start(bf16[80,512]{1,0:T(8,128)(2,1)S(1)} %get-tuple-element.19), channel_id=1, source_target_pairs={{0,2},{1,3},{2,0},{3,1},{4,6},{5,7},{6,4},{7,5},{8,10},{9,11},{10,... | collective-permute-start | bytes 245768 | tf_op jit(solution)/shard_map/ppermute | solution.py:466
  43.7 5.5 %collective-permute-start.9 = (bf16[80,512]{1,0:T(8,128)(2,1)S(1)}, bf16[80,512]{1,0:T(8,128)(2,1)S(1)}, u32[]{:S(2)}, u32[]{:S(2)}) collective-permute-start(bf16[80,512]{1,0:T(8,128)(2,1)S(1)} %get-tuple-element.20), channel_id=1, source_target_pairs={{0,4},{1,5},{2,6},{3,7},{4,0},{5,1},{6,2},{7,3},{8,12},{9,13},{10,... | collective-permute-start | bytes 245768 | tf_op jit(solution)/shard_map/ppermute | solution.py:466
  45.4 5.6 %collective-permute-start.10 = (bf16[80,512]{1,0:T(8,128)(2,1)S(1)}, bf16[80,512]{1,0:T(8,128)(2,1)S(1)}, u32[]{:S(2)}, u32[]{:S(2)}) collective-permute-start(bf16[80,512]{1,0:T(8,128)(2,1)S(1)} %get-tuple-element.21), channel_id=1, source_target_pairs={{0,6},{1,7},{2,4},{3,5},{4,2},{5,3},{6,0},{7,1},{8,14},{9,15},{10,... | collective-permute-start | bytes 245768 | tf_op jit(solution)/shard_map/ppermute | solution.py:466
  46.4 6.4 %collective-permute-start.11 = (bf16[80,512]{1,0:T(8,128)(2,1)S(1)}, bf16[80,512]{1,0:T(8,128)(2,1)S(1)}, u32[]{:S(2)}, u32[]{:S(2)}) collective-permute-start(bf16[80,512]{1,0:T(8,128)(2,1)S(1)} %get-tuple-element.22), channel_id=1, source_target_pairs={{0,3},{1,2},{2,1},{3,0},{4,7},{5,6},{6,5},{7,4},{8,11},{9,10},{10,... | collective-permute-start | bytes 245768 | tf_op jit(solution)/shard_map/ppermute | solution.py:466
  46.7 6.1 %collective-permute-start.12 = (bf16[80,512]{1,0:T(8,128)(2,1)S(1)}, bf16[80,512]{1,0:T(8,128)(2,1)S(1)}, u32[]{:S(2)}, u32[]{:S(2)}) collective-permute-start(bf16[80,512]{1,0:T(8,128)(2,1)S(1)} %get-tuple-element.23), channel_id=1, source_target_pairs={{0,5},{1,4},{2,7},{3,6},{4,1},{5,0},{6,3},{7,2},{8,13},{9,12},{10,... | collective-permute-start | bytes 245768 | tf_op jit(solution)/shard_map/ppermute | solution.py:466
  49.2 4.8 %collective-permute-start.13 = (bf16[80,512]{1,0:T(8,128)(2,1)S(1)}, bf16[80,512]{1,0:T(8,128)(2,1)S(1)}, u32[]{:S(2)}, u32[]{:S(2)}) collective-permute-start(bf16[80,512]{1,0:T(8,128)(2,1)S(1)} %get-tuple-element.24), channel_id=1, source_target_pairs={{0,7},{1,6},{2,5},{3,4},{4,3},{5,2},{6,1},{7,0},{8,15},{9,14},{10,... | collective-permute-start | bytes 245768 | tf_op jit(solution)/shard_map/ppermute | solution.py:466
  51.0 3.0 %collective-permute-start.14 = (bf16[80,512]{1,0:T(8,128)(2,1)S(1)}, bf16[80,512]{1,0:T(8,128)(2,1)S(1)}, u32[]{:S(2)}, u32[]{:S(2)}) collective-permute-start(bf16[80,512]{1,0:T(8,128)(2,1)S(1)} %get-tuple-element.25), channel_id=1, source_target_pairs={{0,1},{1,0},{2,3},{3,2},{4,5},{5,4},{6,7},{7,6},{8,9},{9,8},{10,11... | collective-permute-start | bytes 245768 | tf_op jit(solution)/shard_map/ppermute | solution.py:466

commit v10 on v8

--- a/solution.py
+++ b/solution.py
@@ -119,11 +119,6 @@
             sin_now[at, :] = -sine * norm
             cos_turn[at, :], sin_turn[at, :] = cos_sin(tone * DEPTH, length)
             place[at, :] = start + (length - 1) - lane if side else lane - start
-
-    @pl.loop(0, padded // DEPTH)
-    def _(index):
-        make_table(index)
-
     acc[...] = jnp.zeros_like(acc)
     seg[...] = jnp.zeros_like(seg)
     if padded > bulk:
@@ -175,6 +170,8 @@
     @pl.loop(0, steps)
     def _(i):
         base = pl.multiple_of(i * STEP, STEP)
+        for j in range(STEP // DEPTH):
+            make_table(i * (STEP // DEPTH) + j)
         pltpu.make_async_copy(
             x_hbm.at[pl.ds(low_end + base, STEP)], x_ref.at[pl.ds(base, STEP)], x_sems.at[i]
         ).wait()
@@ -193,6 +190,8 @@
 
     done = steps * STEP
     if done < padded:
+        for j in range(done // DEPTH, padded // DEPTH):
+            make_table(jnp.int32(j))
         if done < bulk:
             x_copy(steps).wait()
         body(done, padded - done, False)
@@ -285,8 +284,9 @@
 
 def whiten_kernel(bins, windows, own_ref, rest_ref, more_ref, white_ref):
     rows = bins * windows * 2
-    raw = own_ref[:rows, :] + rest_ref[:rows, :] + more_ref[:rows, :].astype(F32)
-    extra = more_ref[rows:, :].astype(F32)
+    more = more_ref[...].astype(F32)
+    raw = own_ref[:rows, :] + rest_ref[:rows, :] + more[:rows]
+    extra = more[rows:]
     which = lax.broadcasted_iota(jnp.int32, (rows, 1), 0) % windows
     alive = own_ref[rows + windows:rows + windows + 1, :]
     scale = factor = None
@@ -449,6 +449,15 @@
     return [*range(2, count, 2), *range(3, count, 2), 1]
 
 
+def chan_blocks_of(block):
+    count = lax.axis_size("chan")
+    blocks = {0: block}
+    for away in range(1, count):
+        near = away & -away
+        blocks[away] = from_partner(blocks[away ^ near], "chan", near)
+    return [blocks[away] for away in range(1, count)]
+
+
 def from_partner(block, axis, away):
     return lax.ppermute(block, axis, [(i, i ^ away) for i in range(lax.axis_size(axis))])
 
@@ -466,7 +475,7 @@
     rest, = spectra_of(recording, offsets, band_bins, dead_flags, windows, cut, block_len, 1)
     white = whiten(own, rest, more, bins, windows, halves)
     row_blocks = [white] + [from_partner(white, "tm", away) for away in range(2, tm_count, 2)]
-    chan_blocks = [from_partner(white, "chan", away) for away in range(1, chan_count)]
+    chan_blocks = chan_blocks_of(white)
     joined, col_blocks = picked(row_blocks, chan_blocks, tm_count)
     for away in partners(tm_count):
         col_blocks[away] = from_partner(col_blocks[away], "tm", away)

time: 70.7 us -> 69 us (0.976)
  the two profiles are of different devices: /device:TPU:19 before, /device:TPU:0 now
where the time goes in v10:
time: 69 us; the launch traced here: 68.5 us
  Pallas kernels  35.3 us (51%)
  starting transfers between devices  20.7 us (30%)
  waiting for transfers between devices  11.4 us (17%)
  local copies, waits for them, and re-layouts  0.98 us (1%)
    ppermute x14, starting transfers between devices, from_partner(): lax.ppermute(block, axis, [(i, i ^ away) for i in range(lax.axis_size(axi...  19.3 us
    pallas_call x2, Pallas kernels, spectra_of(): pl.pallas_call(functools.partial(spectra_kernel, bins, windows, block_len...  18.7 us
    pallas_call x1, Pallas kernels, stacks_of(): pl.pallas_call(functools.partial(stack_kernel, windows, scale, devices),...  16.2 us
    ppermute x14, waiting for transfers between devices, from_partner(): lax.ppermute(block, axis, [(i, i ^ away) for i in range(lax.axis_size(axi...  11.4 us
    ppermute x1, starting transfers between devices, moved(): lax.ppermute(block, axis, [(i + far, i) for i in range(count) if 0 <= i +...  1.42 us
  transfers between devices with their start and end apart: 15, of which 10 were waited for; matrix products, arithmetic and copies ran while one was open for 0% of the time, Pallas kernels for 9%

profile of v10, /device:TPU:0, one launch (start us, length us, event | category | flops | bytes accessed | tf_op | source)
XLA Modules:
  0.0 68.5 jit_solution(1010974264060408471)
XLA Ops:
  0.0 12.6 %band_spectra.1 = (f32[88,1024]{1,0:T(8,128)}, bf16[96,1024]{1,0:T(8,128)(2,1)}) custom-call(s32[16]{0:T(128)} %offsets_hbm.3, s32[20]{0:T(128)} %bins_hbm.3, s32[1,1024]{1,0:T(1,128)} %bitcast.6, bf16[15000,1024]{1,0:T(8,128)(2,1)} %bitcast.2, bf16[15000,1024]{1,0:T(8,128)(2,1)} %bitcast.3), custom_call_target="tpu_custom_call" | custom-call | flops 3690987520 | bytes 23068672 | tf_op jit(solution)/shard_map/band_spectra/pallas_call | solution.py:253
  12.6 1.4 %collective-permute-start = (bf16[96,1024]{1,0:T(8,128)(2,1)}, bf16[96,1024]{1,0:T(8,128)(2,1)S(1)}, u32[]{:S(2)}, u32[]{:S(2)}) collective-permute-start(bf16[96,1024]{1,0:T(8,128)(2,1)} %get-tuple-element.17), channel_id=1, source_target_pairs={{1,0},{2,1},{3,2},{4,3},{5,4},{6,5},{7,6},{9,8},{10,9},{11,10},{12... | collective-permute-start | bytes 589832 | tf_op jit(solution)/shard_map/ppermute | solution.py:445
  14.1 6.1 %band_spectra_rest.1.rest_ref = f32[88,1024]{1,0:T(8,128)} custom-call(s32[16]{0:T(128)} %offsets_hbm.3, s32[20]{0:T(128)} %bins_hbm.3, s32[1,1024]{1,0:T(1,128)} %bitcast.7, bf16[15000,1024]{1,0:T(8,128)(2,1)} %bitcast.4, bf16[15000,1024]{1,0:T(8,128)(2,1)} %bitcast.5), custom_call_target="tpu_custom_call" | custom-call | flops 612106240 | bytes 7651328 | tf_op jit(solution)/shard_map/band_spectra_rest/pallas_call | solution.py:253
  20.2 1.0 %copy-done = f32[88,1024]{1,0:T(8,128)S(1)} copy-done((f32[88,1024]{1,0:T(8,128)S(1)}, f32[88,1024]{1,0:T(8,128)}, u32[]{:S(2)}) %copy-start) | copy-done | bytes 360472
  21.4 4.1 %collective-permute-start.5 = (bf16[2,80,512]{2,1,0:T(8,128)(2,1)S(1)}, bf16[2,80,512]{2,1,0:T(8,128)(2,1)S(1)}, u32[]{:S(2)}, u32[]{:S(2)}) collective-permute-start(bf16[2,80,512]{2,1,0:T(8,128)(2,1)S(1)} %whiten.1.refs_0_), channel_id=1, source_target_pairs={{0,16},{8,24},{16,0},{24,8},{1,17},{9,25},{17,1},{25,9},{2,18},{10... | collective-permute-start | bytes 491528 | tf_op jit(solution)/shard_map/ppermute | solution.py:462
  25.5 1.6 %collective-permute-start.4 = (bf16[2,80,512]{2,1,0:T(8,128)(2,1)S(1)}, bf16[2,80,512]{2,1,0:T(8,128)(2,1)S(1)}, u32[]{:S(2)}, u32[]{:S(2)}) collective-permute-start(bf16[2,80,512]{2,1,0:T(8,128)(2,1)S(1)} %whiten.1.refs_0_), channel_id=1, source_target_pairs={{0,8},{8,0},{16,24},{24,16},{1,9},{9,1},{17,25},{25,17},{2,10},{10... | collective-permute-start | bytes 491528 | tf_op jit(solution)/shard_map/ppermute | solution.py:462
  27.1 3.2 %collective-permute-start.3 = (bf16[2,80,512]{2,1,0:T(8,128)(2,1)S(1)}, bf16[2,80,512]{2,1,0:T(8,128)(2,1)S(1)}, u32[]{:S(2)}, u32[]{:S(2)}) collective-permute-start(bf16[2,80,512]{2,1,0:T(8,128)(2,1)S(1)} %whiten.1.refs_0_), channel_id=1, source_target_pairs={{0,6},{1,7},{2,4},{3,5},{4,2},{5,3},{6,0},{7,1},{8,14},{9,15},{10,... | collective-permute-start | bytes 491528 | tf_op jit(solution)/shard_map/ppermute | solution.py:462
  30.3 0.5 collective-permute-start.2
  30.8 0.9 %collective-permute-start.1 = (bf16[2,80,512]{2,1,0:T(8,128)(2,1)S(1)}, bf16[2,80,512]{2,1,0:T(8,128)(2,1)S(1)}, u32[]{:S(2)}, u32[]{:S(2)}) collective-permute-start(bf16[2,80,512]{2,1,0:T(8,128)(2,1)S(1)} %whiten.1.refs_0_), channel_id=1, source_target_pairs={{0,2},{1,3},{2,0},{3,1},{4,6},{5,7},{6,4},{7,5},{8,10},{9,11},{10,... | collective-permute-start | bytes 491528 | tf_op jit(solution)/shard_map/ppermute | solution.py:462
  31.8 2.1 %collective-permute-done.5.refs_5_ = bf16[2,80,512]{2,1,0:T(8,128)(2,1)S(1)} collective-permute-done((bf16[2,80,512]{2,1,0:T(8,128)(2,1)S(1)}, bf16[2,80,512]{2,1,0:T(8,128)(2,1)S(1)}, u32[]{:S(2)}, u32[]{:S(2)}) %collective-permute-start.5) | collective-permute-done | bytes 163872 | tf_op jit(solution)/shard_map/ppermute | solution.py:462
  33.8 1.2 %collective-permute-start.6 = (bf16[2,80,512]{2,1,0:T(8,128)(2,1)S(1)}, bf16[2,80,512]{2,1,0:T(8,128)(2,1)S(1)}, u32[]{:S(2)}, u32[]{:S(2)}) collective-permute-start(bf16[2,80,512]{2,1,0:T(8,128)(2,1)S(1)} %collective-permute-done.5.refs_5_), channel_id=1, source_target_pairs={{0,8},{8,0},{16,24},{24,16},{1,9},{9,1},{17,25},{25,17},{2,10},{10... | collective-permute-start | bytes 491528 | tf_op jit(solution)/shard_map/ppermute | solution.py:462
  35.3 2.8 %collective-permute-done.2.refs_2_ = bf16[2,80,512]{2,1,0:T(8,128)(2,1)S(1)} collective-permute-done((bf16[2,80,512]{2,1,0:T(8,128)(2,1)S(1)}, bf16[2,80,512]{2,1,0:T(8,128)(2,1)S(1)}, u32[]{:S(2)}, u32[]{:S(2)}) %collective-permute-start.2) | collective-permute-done | bytes 163872 | tf_op jit(solution)/shard_map/ppermute | solution.py:462
  38.5 1.9 %collective-permute-done.6.refs_6_ = bf16[2,80,512]{2,1,0:T(8,128)(2,1)S(1)} collective-permute-done((bf16[2,80,512]{2,1,0:T(8,128)(2,1)S(1)}, bf16[2,80,512]{2,1,0:T(8,128)(2,1)S(1)}, u32[]{:S(2)}, u32[]{:S(2)}) %collective-permute-start.6) | collective-permute-done | bytes 163872 | tf_op jit(solution)/shard_map/ppermute | solution.py:462
  40.6 1.7 %collective-permute-start.7 = (bf16[80,512]{1,0:T(8,128)(2,1)S(1)}, bf16[80,512]{1,0:T(8,128)(2,1)S(1)}, u32[]{:S(2)}, u32[]{:S(2)}) collective-permute-start(bf16[80,512]{1,0:T(8,128)(2,1)S(1)} %get-tuple-element.19), channel_id=1, source_target_pairs={{0,2},{1,3},{2,0},{3,1},{4,6},{5,7},{6,4},{7,5},{8,10},{9,11},{10,... | collective-permute-start | bytes 245768 | tf_op jit(solution)/shard_map/ppermute | solution.py:462
  42.3 1.2 %collective-permute-start.8 = (bf16[80,512]{1,0:T(8,128)(2,1)S(1)}, bf16[80,512]{1,0:T(8,128)(2,1)S(1)}, u32[]{:S(2)}, u32[]{:S(2)}) collective-permute-start(bf16[80,512]{1,0:T(8,128)(2,1)S(1)} %get-tuple-element.20), channel_id=1, source_target_pairs={{0,4},{1,5},{2,6},{3,7},{4,0},{5,1},{6,2},{7,3},{8,12},{9,13},{10,... | collective-permute-start | bytes 245768 | tf_op jit(solution)/shard_map/ppermute | solution.py:462
  43.6 0.6 collective-permute-start.9
  44.1 0.9 %collective-permute-start.10 = (bf16[80,512]{1,0:T(8,128)(2,1)S(1)}, bf16[80,512]{1,0:T(8,128)(2,1)S(1)}, u32[]{:S(2)}, u32[]{:S(2)}) collective-permute-start(bf16[80,512]{1,0:T(8,128)(2,1)S(1)} %get-tuple-element.22), channel_id=1, source_target_pairs={{0,3},{1,2},{2,1},{3,0},{4,7},{5,6},{6,5},{7,4},{8,11},{9,10},{10,... | collective-permute-start | bytes 245768 | tf_op jit(solution)/shard_map/ppermute | solution.py:462
  45.0 0.4 collective-permute-done.7.refs_1_
  45.4 1.3 %collective-permute-start.11 = (bf16[80,512]{1,0:T(8,128)(2,1)S(1)}, bf16[80,512]{1,0:T(8,128)(2,1)S(1)}, u32[]{:S(2)}, u32[]{:S(2)}) collective-permute-start(bf16[80,512]{1,0:T(8,128)(2,1)S(1)} %get-tuple-element.23), channel_id=1, source_target_pairs={{0,5},{1,4},{2,7},{3,6},{4,1},{5,0},{6,3},{7,2},{8,13},{9,12},{10,... | collective-permute-start | bytes 245768 | tf_op jit(solution)/shard_map/ppermute | solution.py:462
  46.8 1.9 %collective-permute-start.12 = (bf16[80,512]{1,0:T(8,128)(2,1)S(1)}, bf16[80,512]{1,0:T(8,128)(2,1)S(1)}, u32[]{:S(2)}, u32[]{:S(2)}) collective-permute-start(bf16[80,512]{1,0:T(8,128)(2,1)S(1)} %get-tuple-element.24), channel_id=1, source_target_pairs={{0,7},{1,6},{2,5},{3,4},{4,3},{5,2},{6,1},{7,0},{8,15},{9,14},{10,... | collective-permute-start | bytes 245768 | tf_op jit(solution)/shard_map/ppermute | solution.py:462
  48.7 1.0 %collective-permute-done.9.refs_3_ = bf16[80,512]{1,0:T(8,128)(2,1)S(1)} collective-permute-done((bf16[80,512]{1,0:T(8,128)(2,1)S(1)}, bf16[80,512]{1,0:T(8,128)(2,1)S(1)}, u32[]{:S(2)}, u32[]{:S(2)}) %collective-permute-start.9) | collective-permute-done | bytes 81952 | tf_op jit(solution)/shard_map/ppermute | solution.py:462
  49.8 0.8 %collective-permute-done.11.refs_5_ = bf16[80,512]{1,0:T(8,128)(2,1)S(1)} collective-permute-done((bf16[80,512]{1,0:T(8,128)(2,1)S(1)}, bf16[80,512]{1,0:T(8,128)(2,1)S(1)}, u32[]{:S(2)}, u32[]{:S(2)}) %collective-permute-start.11) | collective-permute-done | bytes 81952 | tf_op jit(solution)/shard_map/ppermute | solution.py:462
  50.5 1.8 %collective-permute-done.12.refs_6_ = bf16[80,512]{1,0:T(8,128)(2,1)S(1)} collective-permute-done((bf16[80,512]{1,0:T(8,128)(2,1)S(1)}, bf16[80,512]{1,0:T(8,128)(2,1)S(1)}, u32[]{:S(2)}, u32[]{:S(2)}) %collective-permute-start.12) | collective-permute-done | bytes 81952 | tf_op jit(solution)/shard_map/ppermute | solution.py:462
  52.3 16.2 %stack_products.1 = bf16[2,20,512,1024]{3,2,1,0:T(8,128)(2,1)} custom-call(bf16[80,512]{1,0:T(8,128)(2,1)S(1)} %get-tuple-element.18.refs_0_, bf16[80,512]{1,0:T(8,128)(2,1)S(1)} %collective-permute-done.7.refs_1_, bf16[80,512]{1,0:T(8,128)(2,1)S(1)} %collective-permute-done.8.refs_2_, bf16[80,512]{1,0:T(8,128)(2,1)S(1)} %collective-permute-done.9.refs_3_, ...), custom_call_target="tpu_custom_call" | custom-call | flops 5368709120 | bytes 41943040 | tf_op jit(solution)/shard_map/stack_products/pallas_call | solution.py:386
  (15 shorter events, 1.1 us)
Async XLA Ops:
  12.6 7.5 %copy-start.1 = (f32[88,1024]{1,0:T(8,128)S(1)}, f32[88,1024]{1,0:T(8,128)}, u32[]{:S(2)}) copy-start(f32[88,1024]{1,0:T(8,128)} %get-tuple-element.16.own_ref) | copy-start | bytes 1081348
  12.6 7.5 %collective-permute-start = (bf16[96,1024]{1,0:T(8,128)(2,1)}, bf16[96,1024]{1,0:T(8,128)(2,1)S(1)}, u32[]{:S(2)}, u32[]{:S(2)}) collective-permute-start(bf16[96,1024]{1,0:T(8,128)(2,1)} %get-tuple-element.17), channel_id=1, source_target_pairs={{1,0},{2,1},{3,2},{4,3},{5,4},{6,5},{7,6},{9,8},{10,9},{11,10},{12... | collective-permute-start | bytes 589832 | tf_op jit(solution)/shard_map/ppermute | solution.py:445
  20.2 1.0 %copy-start = (f32[88,1024]{1,0:T(8,128)S(1)}, f32[88,1024]{1,0:T(8,128)}, u32[]{:S(2)}) copy-start(f32[88,1024]{1,0:T(8,128)} %band_spectra_rest.1.rest_ref) | copy-start | bytes 1081348
  21.4 12.4 %collective-permute-start.5 = (bf16[2,80,512]{2,1,0:T(8,128)(2,1)S(1)}, bf16[2,80,512]{2,1,0:T(8,128)(2,1)S(1)}, u32[]{:S(2)}, u32[]{:S(2)}) collective-permute-start(bf16[2,80,512]{2,1,0:T(8,128)(2,1)S(1)} %whiten.1.refs_0_), channel_id=1, source_target_pairs={{0,16},{8,24},{16,0},{24,8},{1,17},{9,25},{17,1},{25,9},{2,18},{10... | collective-permute-start | bytes 491528 | tf_op jit(solution)/shard_map/ppermute | solution.py:462
  25.5 9.6 %collective-permute-start.4 = (bf16[2,80,512]{2,1,0:T(8,128)(2,1)S(1)}, bf16[2,80,512]{2,1,0:T(8,128)(2,1)S(1)}, u32[]{:S(2)}, u32[]{:S(2)}) collective-permute-start(bf16[2,80,512]{2,1,0:T(8,128)(2,1)S(1)} %whiten.1.refs_0_), channel_id=1, source_target_pairs={{0,8},{8,0},{16,24},{24,16},{1,9},{9,1},{17,25},{25,17},{2,10},{10... | collective-permute-start | bytes 491528 | tf_op jit(solution)/shard_map/ppermute | solution.py:462
  27.1 8.2 %collective-permute-start.3 = (bf16[2,80,512]{2,1,0:T(8,128)(2,1)S(1)}, bf16[2,80,512]{2,1,0:T(8,128)(2,1)S(1)}, u32[]{:S(2)}, u32[]{:S(2)}) collective-permute-start(bf16[2,80,512]{2,1,0:T(8,128)(2,1)S(1)} %whiten.1.refs_0_), channel_id=1, source_target_pairs={{0,6},{1,7},{2,4},{3,5},{4,2},{5,3},{6,0},{7,1},{8,14},{9,15},{10,... | collective-permute-start | bytes 491528 | tf_op jit(solution)/shard_map/ppermute | solution.py:462
  30.3 7.9 %collective-permute-start.2 = (bf16[2,80,512]{2,1,0:T(8,128)(2,1)S(1)}, bf16[2,80,512]{2,1,0:T(8,128)(2,1)S(1)}, u32[]{:S(2)}, u32[]{:S(2)}) collective-permute-start(bf16[2,80,512]{2,1,0:T(8,128)(2,1)S(1)} %whiten.1.refs_0_), channel_id=1, source_target_pairs={{0,4},{1,5},{2,6},{3,7},{4,0},{5,1},{6,2},{7,3},{8,12},{9,13},{10,... | collective-permute-start | bytes 491528 | tf_op jit(solution)/shard_map/ppermute | solution.py:462
  30.8 7.6 %collective-permute-start.1 = (bf16[2,80,512]{2,1,0:T(8,128)(2,1)S(1)}, bf16[2,80,512]{2,1,0:T(8,128)(2,1)S(1)}, u32[]{:S(2)}, u32[]{:S(2)}) collective-permute-start(bf16[2,80,512]{2,1,0:T(8,128)(2,1)S(1)} %whiten.1.refs_0_), channel_id=1, source_target_pairs={{0,2},{1,3},{2,0},{3,1},{4,6},{5,7},{6,4},{7,5},{8,10},{9,11},{10,... | collective-permute-start | bytes 491528 | tf_op jit(solution)/shard_map/ppermute | solution.py:462
  33.8 6.5 %collective-permute-start.6 = (bf16[2,80,512]{2,1,0:T(8,128)(2,1)S(1)}, bf16[2,80,512]{2,1,0:T(8,128)(2,1)S(1)}, u32[]{:S(2)}, u32[]{:S(2)}) collective-permute-start(bf16[2,80,512]{2,1,0:T(8,128)(2,1)S(1)} %collective-permute-done.5.refs_5_), channel_id=1, source_target_pairs={{0,8},{8,0},{16,24},{24,16},{1,9},{9,1},{17,25},{25,17},{2,10},{10... | collective-permute-start | bytes 491528 | tf_op jit(solution)/shard_map/ppermute | solution.py:462
  40.5 11.8 %collective-permute-start.14 = (bf16[4,2,80,512]{3,2,1,0:T(8,128)(2,1)S(1)}, bf16[4,2,80,512]{3,2,1,0:T(8,128)(2,1)S(1)}, u32[]{:S(2)}, u32[]{:S(2)}) collective-permute-start(bf16[4,2,80,512]{3,2,1,0:T(8,128)(2,1)S(1)} %get-tuple-element.26.refs_8_), channel_id=1, source_target_pairs={{0,1},{1,0},{2,3},{3,2},{4,5},{5,4},{6,7},{7,6},{8,9},{9,8},{10,11... | collective-permute-start | bytes 1966088 | tf_op jit(solution)/shard_map/ppermute | solution.py:462
  40.6 4.9 %collective-permute-start.7 = (bf16[80,512]{1,0:T(8,128)(2,1)S(1)}, bf16[80,512]{1,0:T(8,128)(2,1)S(1)}, u32[]{:S(2)}, u32[]{:S(2)}) collective-permute-start(bf16[80,512]{1,0:T(8,128)(2,1)S(1)} %get-tuple-element.19), channel_id=1, source_target_pairs={{0,2},{1,3},{2,0},{3,1},{4,6},{5,7},{6,4},{7,5},{8,10},{9,11},{10,... | collective-permute-start | bytes 245768 | tf_op jit(solution)/shard_map/ppermute | solution.py:462
  42.3 4.5 %collective-permute-start.8 = (bf16[80,512]{1,0:T(8,128)(2,1)S(1)}, bf16[80,512]{1,0:T(8,128)(2,1)S(1)}, u32[]{:S(2)}, u32[]{:S(2)}) collective-permute-start(bf16[80,512]{1,0:T(8,128)(2,1)S(1)} %get-tuple-element.20), channel_id=1, source_target_pairs={{0,4},{1,5},{2,6},{3,7},{4,0},{5,1},{6,2},{7,3},{8,12},{9,13},{10,... | collective-permute-start | bytes 245768 | tf_op jit(solution)/shard_map/ppermute | solution.py:462
  43.6 6.2 %collective-permute-start.9 = (bf16[80,512]{1,0:T(8,128)(2,1)S(1)}, bf16[80,512]{1,0:T(8,128)(2,1)S(1)}, u32[]{:S(2)}, u32[]{:S(2)}) collective-permute-start(bf16[80,512]{1,0:T(8,128)(2,1)S(1)} %get-tuple-element.21), channel_id=1, source_target_pairs={{0,6},{1,7},{2,4},{3,5},{4,2},{5,3},{6,0},{7,1},{8,14},{9,15},{10,... | collective-permute-start | bytes 245768 | tf_op jit(solution)/shard_map/ppermute | solution.py:462
  44.1 5.6 %collective-permute-start.10 = (bf16[80,512]{1,0:T(8,128)(2,1)S(1)}, bf16[80,512]{1,0:T(8,128)(2,1)S(1)}, u32[]{:S(2)}, u32[]{:S(2)}) collective-permute-start(bf16[80,512]{1,0:T(8,128)(2,1)S(1)} %get-tuple-element.22), channel_id=1, source_target_pairs={{0,3},{1,2},{2,1},{3,0},{4,7},{5,6},{6,5},{7,4},{8,11},{9,10},{10,... | collective-permute-start | bytes 245768 | tf_op jit(solution)/shard_map/ppermute | solution.py:462
  45.4 5.1 %collective-permute-start.11 = (bf16[80,512]{1,0:T(8,128)(2,1)S(1)}, bf16[80,512]{1,0:T(8,128)(2,1)S(1)}, u32[]{:S(2)}, u32[]{:S(2)}) collective-permute-start(bf16[80,512]{1,0:T(8,128)(2,1)S(1)} %get-tuple-element.23), channel_id=1, source_target_pairs={{0,5},{1,4},{2,7},{3,6},{4,1},{5,0},{6,3},{7,2},{8,13},{9,12},{10,... | collective-permute-start | bytes 245768 | tf_op jit(solution)/shard_map/ppermute | solution.py:462
  46.8 5.5 %collective-permute-start.12 = (bf16[80,512]{1,0:T(8,128)(2,1)S(1)}, bf16[80,512]{1,0:T(8,128)(2,1)S(1)}, u32[]{:S(2)}, u32[]{:S(2)}) collective-permute-start(bf16[80,512]{1,0:T(8,128)(2,1)S(1)} %get-tuple-element.24), channel_id=1, source_target_pairs={{0,7},{1,6},{2,5},{3,4},{4,3},{5,2},{6,1},{7,0},{8,15},{9,14},{10,... | collective-permute-start | bytes 245768 | tf_op jit(solution)/shard_map/ppermute | solution.py:462
  49.8 2.5 %collective-permute-start.13 = (bf16[80,512]{1,0:T(8,128)(2,1)S(1)}, bf16[80,512]{1,0:T(8,128)(2,1)S(1)}, u32[]{:S(2)}, u32[]{:S(2)}) collective-permute-start(bf16[80,512]{1,0:T(8,128)(2,1)S(1)} %get-tuple-element.25), channel_id=1, source_target_pairs={{0,1},{1,0},{2,3},{3,2},{4,5},{5,4},{6,7},{7,6},{8,9},{9,8},{10,11... | collective-permute-start | bytes 245768 | tf_op jit(solution)/shard_map/ppermute | solution.py:462

commit v11 on v10

--- a/solution.py
+++ b/solution.py
@@ -35,30 +35,78 @@
     return cos_sign * jnp.where(odd, sine, cosine), sin_sign * jnp.where(odd, cosine, sine)
 
 
+def load_samples(x_hbm, x_ref, x_sems, low_end, size):
+    return [
+        pltpu.make_async_copy(
+            x_hbm.at[pl.ds(low_end + i, min(STEP, size - i))], x_ref.at[pl.ds(i, min(STEP, size - i))],
+            x_sems.at[i // STEP],
+        )
+        for i in range(0, size, STEP)
+    ]
+
+
+def make_table(table, state, place, index, windows_rows):
+    rows = table.shape[0]
+    to_lanes = pl.ds(pl.multiple_of(index * DEPTH, DEPTH), DEPTH)
+    moved = (index * DEPTH).astype(F32)
+    for r in range(0, rows, ROW_TILE):
+        values = []
+        for at in (slice(r, r + 8), slice(r + 8, r + 16)):
+            u, v = state[0, at, :], state[1, at, :]
+            ct, st = state[2, at, :], state[3, at, :]
+            if place is not None:
+                limit = -moved if at.start < windows_rows else moved
+                values.append(jnp.where(place[at, :] >= limit, u, 0.0))
+            else:
+                values.append(u)
+            state[0, at, :] = u * ct - v * st
+            state[1, at, :] = v * ct + u * st
+        table[r:r + ROW_TILE, to_lanes] = jnp.concatenate(values, axis=0).astype(BF16)
+
+
+def add_products(table, x_ref, acc, base, size, row_range, energy_at):
+    view = x_ref.at[pl.ds(base, size)]
+    waves = table.at[:, pl.ds(base, size)]
+    low, high = row_range
+    channels = x_ref.shape[1]
+    for n in range(0, channels, DEPTH):
+        at = slice(n, min(n + DEPTH, channels))
+        if energy_at is not None:
+            total = squares(view, 0, at)
+            for t in range(1, size // ROW_TILE):
+                total = total + squares(view, t, at)
+        product = jnp.dot(waves[low:high, :], view[:, at], preferred_element_type=F32)
+        acc[low:high, at] += product
+        if energy_at is not None:
+            energy_at[:, at] = total
+
+
+def squares(view, t, at):
+    x = view[t * ROW_TILE:(t + 1) * ROW_TILE, at].astype(F32)
+    square = x * x
+    return square[:ROW_TILE // 2] + square[ROW_TILE // 2:]
+
+
+def mix_windows(out_ref, acc, first, windows, per_window, per_group):
+    for w in range(windows):
+        own_at = first + (windows - 1 - w) * per_window
+        for q in range(0, per_window, per_group):
+            to = q * windows + w * per_group
+            out_ref[to:to + per_group, :] = acc[own_at + q:own_at + q + per_group, :]
+
+
 def spectra_kernel(
-    bins, windows, block_len, low_end, high_end, sides,
-    offsets_hbm, bins_hbm, dead_hbm, x_hbm, tail_ref, own_ref, *refs,
+    bins, windows, block_len, high_end,
+    offsets_hbm, bins_hbm, dead_hbm, x_hbm, own_ref, back_ref, state_ref,
+    offsets, band_bins, dead, x_ref, acc, seg, part_seg, mixed, state, place, table, small_sems, x_sems,
 ):
-    back_ref = refs[0] if sides == 2 else None
-    offsets, band_bins, dead, x_ref, acc, seg, part_seg, cos_now, sin_now, cos_turn, sin_turn, place, table = refs[-15:-2]
-    small_sems, x_sems = refs[-2:]
     channels = x_ref.shape[1]
     length, hop = L, L // 2
-    rows = bins * windows * 2
+    per_window = 2 * bins
+    rows = windows * per_window
     half_tile = ROW_TILE // 2
     per_group = half_tile // windows
-    groups = rows // ROW_TILE
-    states = groups * half_tile
-    bulk = (high_end - low_end) // ROW_TILE * ROW_TILE
-    padded = x_ref.shape[0]
-    steps = padded // STEP
-    columns = [slice(n, min(n + DEPTH, channels)) for n in range(0, channels, DEPTH)]
-
-    def x_copy(i):
-        size = min(STEP, bulk - i * STEP)
-        return pltpu.make_async_copy(
-            x_hbm.at[pl.ds(low_end + i * STEP, size)], x_ref.at[pl.ds(i * STEP, size)], x_sems.at[i]
-        )
+    steps = high_end // STEP
 
     small = [
         pltpu.make_async_copy(offsets_hbm, offsets, small_sems.at[0]),
@@ -67,65 +115,51 @@
     ]
     for copy in small:
         copy.start()
-    x_copy(0).start()
+    loads = load_samples(x_hbm, x_ref, x_sems, 0, high_end)
+    loads[0].start()
     for copy in small:
         copy.wait()
-    for i in range(1, pl.cdiv(bulk, STEP)):
-        x_copy(i).start()
+    for copy in loads[1:]:
+        copy.start()
 
     tm = lax.axis_index("tm")
     ahead = [offsets[tm * windows + w] + w * hop for w in range(windows)]
     before = jnp.maximum(tm - 1, 0) * windows
     behind = [offsets[before + w] + w * hop + length - block_len for w in range(windows)]
     ends = []
-    for w in range(windows if sides == 2 else 0):
+    for w in range(windows):
         ends += [jnp.minimum(ahead[w], behind[w]), jnp.maximum(ahead[w], behind[w])]
     segments = len(ends) + 1
     trash = segments
 
-    def make_table(index):
-        moved = (index * DEPTH).astype(F32)
-        to_lanes = pl.ds(pl.multiple_of(index * DEPTH, DEPTH), DEPTH)
-        for side in range(sides):
-            limit = moved if side else -moved
-            for g in range(groups):
-                at = slice(side * states + g * half_tile, side * states + (g + 1) * half_tile)
-                to = side * rows + g * ROW_TILE
-                c, s = cos_now[at, :], sin_now[at, :]
-                inside = place[at, :] >= limit
-                wave = jnp.concatenate([jnp.where(inside, c, 0.0), jnp.where(inside, s, 0.0)], axis=0)
-                table[to:to + ROW_TILE, to_lanes] = wave.astype(BF16)
-                ct, st = cos_turn[at, :], sin_turn[at, :]
-                cos_now[at, :] = c * ct + s * st
-                sin_now[at, :] = s * ct - c * st
-
     shape = (half_tile, DEPTH)
-    row = lax.broadcasted_iota(jnp.int32, shape, 0)
-    lane = (lax.broadcasted_iota(jnp.int32, shape, 1) + low_end).astype(F32)
+    lane = lax.broadcasted_iota(jnp.int32, shape, 1).astype(F32)
     norm = 1.0 / math.sqrt(length)
-    for side in range(sides):
-        for g in range(groups):
-            at = slice(side * states + g * half_tile, side * states + (g + 1) * half_tile)
-            tone = jnp.zeros(shape, jnp.int32)
-            start = jnp.zeros(shape, jnp.int32)
-            for i in range(per_group):
-                tone = jnp.where(row // windows == i, band_bins[g * per_group + i], tone)
-            for w in range(windows):
-                here = behind[w] - length if side else ahead[w]
-                start = jnp.where(row % windows == w, here, start)
-            tone, start = tone.astype(F32), start.astype(F32)
-            cosine, sine = cos_sin((lane - start) * tone, length)
-            cos_now[at, :] = cosine * norm
-            sin_now[at, :] = -sine * norm
-            cos_turn[at, :], sin_turn[at, :] = cos_sin(tone * DEPTH, length)
-            place[at, :] = start + (length - 1) - lane if side else lane - start
+    for r in range(0, 2 * rows, half_tile):
+        at = slice(r, r + half_tile)
+        row = lax.broadcasted_iota(jnp.int32, shape, 0) + r
+        block, inner = row // per_window, row % per_window
+        part = inner // per_group % 2
+        bin_index = inner // (2 * per_group) * per_group + inner % per_group
+        tone = jnp.zeros(shape, jnp.int32)
+        for b in range(bins):
+            if r // per_window != (r + half_tile - 1) // per_window or (
+                r % per_window // (2 * per_group) * per_group <= b
+                < (r % per_window + half_tile - 1) // (2 * per_group) * per_group + per_group
+            ):
+                tone = jnp.where(bin_index == b, band_bins[b], tone)
+        start = jnp.zeros(shape, jnp.int32)
+        for w in range(windows):
+            start = jnp.where(block == windows - 1 - w, ahead[w], start)
+            start = jnp.where(block == 2 * windows - 1 - w, behind[w] - length, start)
+        tone, start = tone.astype(F32), start.astype(F32)
+        cosine, sine = cos_sin((lane - start) * tone, length)
+        state[0, at, :] = jnp.where(part == 1, -sine, cosine) * norm
+        state[1, at, :] = jnp.where(part == 1, cosine, sine) * norm
+        state[2, at, :], state[3, at, :] = cos_sin(tone * DEPTH, length)
+        place[at, :] = lane - start if r < rows else start + (length - 1) - lane
     acc[...] = jnp.zeros_like(acc)
     seg[...] = jnp.zeros_like(seg)
-    if padded > bulk:
-        x_ref[bulk:, :] = jnp.zeros((padded - bulk, channels), BF16)
-    if high_end - low_end > bulk:
-        inside = lax.broadcasted_iota(jnp.int32, (ROW_TILE, channels), 0) < high_end - low_end - bulk
-        x_ref[bulk:bulk + ROW_TILE, :] = jnp.where(inside, tail_ref[...].astype(F32), 0.0).astype(BF16)
 
     def segment_of(position):
         index = jnp.int32(0)
@@ -139,62 +173,60 @@
             found = jnp.logical_or(found, jnp.logical_and(end >= first, end < first + size))
         return found
 
-    def body(base, size, edge):
-        view = x_ref.at[pl.ds(base, size)]
-        waves = table.at[:, pl.ds(base, size)]
-        tiles = size // ROW_TILE
-
-        def squares(t, at):
-            x = view[t * ROW_TILE:(t + 1) * ROW_TILE, at].astype(F32)
-            square = x * x
-            return square[:half_tile] + square[half_tile:]
-
-        for at in columns:
-            if not edge:
-                total = squares(0, at)
-                for t in range(1, tiles):
-                    total = total + squares(t, at)
-            product = jnp.dot(waves[...], view[:, at], preferred_element_type=F32)
-            acc[:, at] += product
-            if not edge:
-                part_seg[:, at] = total
-        if edge:
-            for t in range(tiles):
-                first = base + t * ROW_TILE
-                target = jnp.where(has_end(first, ROW_TILE), trash, segment_of(first))
-                for at in columns:
-                    seg[target, :, at] += squares(t, at)
-        else:
+    def body(base, row_range, edge):
+        add_products(table, x_ref, acc, base, STEP, row_range, None if edge else part_seg)
+        if not edge:
             seg[segment_of(base)] += part_seg[...]
-
-    @pl.loop(0, steps)
-    def _(i):
-        base = pl.multiple_of(i * STEP, STEP)
-        for j in range(STEP // DEPTH):
-            make_table(i * (STEP // DEPTH) + j)
-        pltpu.make_async_copy(
-            x_hbm.at[pl.ds(low_end + base, STEP)], x_ref.at[pl.ds(base, STEP)], x_sems.at[i]
-        ).wait()
-        if not ends:
-            body(base, STEP, False)
             return
-        cut = has_end(base, STEP)
-
-        @pl.when(jnp.logical_not(cut))
-        def _():
-            body(base, STEP, False)
-
-        @pl.when(cut)
-        def _():
-            body(base, STEP, True)
-
-    done = steps * STEP
-    if done < padded:
-        for j in range(done // DEPTH, padded // DEPTH):
-            make_table(jnp.int32(j))
-        if done < bulk:
-            x_copy(steps).wait()
-        body(done, padded - done, False)
+        view = x_ref.at[pl.ds(base, STEP)]
+        for t in range(STEP // ROW_TILE):
+            first = base + t * ROW_TILE
+            target = jnp.where(has_end(first, ROW_TILE), trash, segment_of(first))
+            for n in range(0, channels, DEPTH):
+                at = slice(n, min(n + DEPTH, channels))
+                seg[target, :, at] += squares(view, t, at)
+
+    def reach(i):
+        low, high = i * STEP, (i + 1) * STEP
+        own = [w for w in range(windows) if w * hop < high]
+        back = [w for w in range(windows) if w * hop + hop // 2 + length - block_len > low]
+        first = (windows - 1 - max(own)) * per_window // ROW_TILE * ROW_TILE
+        last = (2 * windows - min(back, default=windows)) * per_window
+        edges = any(
+            w * hop + shift < high and w * hop + hop // 2 + shift > low
+            for w in range(windows) for shift in (0, length - block_len)
+        )
+        return (first, min(pl.cdiv(last, ROW_TILE) * ROW_TILE, 2 * rows)), edges
+
+    kinds = [reach(i) for i in range(steps)]
+    i = 0
+    while i < steps:
+        until = i
+        while until < steps and kinds[until] == kinds[i]:
+            until += 1
+        row_range, edges = kinds[i]
+
+        @pl.loop(i, until)
+        def _(step):
+            base = pl.multiple_of(step * STEP, STEP)
+            for j in range(STEP // DEPTH):
+                make_table(table, state, place, step * (STEP // DEPTH) + j, rows)
+            at = pl.ds(base, STEP)
+            pltpu.make_async_copy(x_hbm.at[at], x_ref.at[at], x_sems.at[step]).wait()
+            if not edges:
+                body(base, row_range, False)
+                return
+            cut = has_end(base, STEP)
+
+            @pl.when(jnp.logical_not(cut))
+            def _():
+                body(base, row_range, False)
+
+            @pl.when(cut)
+            def _():
+                body(base, row_range, True)
+
+        i = until
 
     for i, end in enumerate(ends):
         low = ends[i - 1] if i else jnp.int32(0)
@@ -210,76 +242,137 @@
             kept = jnp.where(where, square, 0.0)
             seg[index] += kept[:half_tile] + kept[half_tile:]
 
-    own_ref[:rows, :] = acc[:rows, :]
+    state_ref[...] = state[:, :rows, :]
+    mix_windows(own_ref, acc, 0, windows, per_window, per_group)
+    mix_windows(mixed, acc, rows, windows, per_window, per_group)
+    back_ref[:rows, :] = mixed[...].astype(BF16)
     parts = [seg[i] for i in range(segments)]
     row = lax.broadcasted_iota(jnp.int32, (half_tile, channels), 0)
     own_block = jnp.where(row == windows, (1 - dead[...]).astype(F32), 0.0)
-    for w in range(windows):
-        after = sum(parts[2 * w + 2:]) if ends else parts[0]
-        if ends:
-            after = after + jnp.where(ahead[w] <= behind[w], parts[2 * w + 1], 0.0)
-        own_block = jnp.where(row == w, jnp.sum(after, axis=0, keepdims=True), own_block)
-    own_ref[rows:, :] = own_block
-    if sides == 1:
-        return
-    back_ref[:rows, :] = acc[rows:, :].astype(BF16)
     back_block = jnp.zeros((ROW_TILE, channels), F32)
     back_row = lax.broadcasted_iota(jnp.int32, (ROW_TILE, channels), 0)
     for w in range(windows):
-        until = sum(parts[:2 * w + 1]) + jnp.where(ahead[w] <= behind[w], parts[2 * w + 1], 0.0)
-        rest = jnp.sum(until, axis=0, keepdims=True)
+        turn = jnp.where(ahead[w] <= behind[w], parts[2 * w + 1], 0.0)
+        own_energy = jnp.sum(sum(parts[2 * w + 2:]) + turn, axis=0, keepdims=True)
+        own_block = jnp.where(row == w, own_energy, own_block)
+        rest = jnp.sum(sum(parts[:2 * w + 1]) + turn, axis=0, keepdims=True)
         for term in range(3):
             piece_of = rest.astype(BF16).astype(F32)
             rest = rest - piece_of
             back_block = jnp.where(back_row == term * windows + w, piece_of, back_block)
+    own_ref[rows:, :] = own_block
     back_ref[rows:, :] = back_block.astype(BF16)
 
 
-def spectra_of(recording, offsets, band_bins, dead, windows, low_end, high_end, sides):
+def rest_kernel(
+    bins, windows, block_len, low_end, state_in, x_hbm, tail_ref, own_ref,
+    x_ref, acc, part_seg, total_seg, state, table, x_sems,
+):
+    channels = x_ref.shape[1]
+    per_window = 2 * bins
+    rows = windows * per_window
+    half_tile = ROW_TILE // 2
+    count = block_len - low_end
+    bulk = count // ROW_TILE * ROW_TILE
+    padded = x_ref.shape[0]
+    loads = load_samples(x_hbm, x_ref, x_sems, low_end, bulk)
+    for copy in loads:
+        copy.start()
+    state[...] = state_in[...]
+    acc[...] = jnp.zeros_like(acc)
+    total_seg[...] = jnp.zeros_like(total_seg)
+    if padded > bulk:
+        x_ref[bulk:, :] = jnp.zeros((padded - bulk, channels), BF16)
+    if count > bulk:
+        inside = lax.broadcasted_iota(jnp.int32, (ROW_TILE, channels), 0) < count - bulk
+        x_ref[bulk:bulk + ROW_TILE, :] = jnp.where(inside, tail_ref[...].astype(F32), 0.0).astype(BF16)
+    for i in range(0, padded, STEP):
+        size = min(STEP, padded - i)
+        for j in range(size // DEPTH):
+            make_table(table, state, None, jnp.int32(i // DEPTH + j), rows)
+        if i // STEP < len(loads):
+            loads[i // STEP].wait()
+        add_products(table, x_ref, acc, i, size, (0, rows), part_seg)
+        total_seg[...] += part_seg[...]
+    mix_windows(own_ref, acc, 0, windows, per_window, half_tile // windows)
+    energy = jnp.sum(total_seg[...], axis=0, keepdims=True)
+    row = lax.broadcasted_iota(jnp.int32, (half_tile, channels), 0)
+    own_ref[rows:, :] = jnp.where(row < windows, energy, 0.0)
+
+
+def spectra_of(recording, offsets, band_bins, dead, windows, high_end):
     channels, block_len = recording.shape
     bins = band_bins.shape[0]
     rows = bins * windows * 2
-    padded = pl.cdiv(high_end - low_end, DEPTH) * DEPTH
-    bulk = (high_end - low_end) // ROW_TILE * ROW_TILE
-    tail = min(low_end + bulk, block_len - 1) // ROW_TILE
     samples = recording.T
     hbm = pl.BlockSpec(memory_space=pltpu.HBM)
     whole = pl.BlockSpec(memory_space=pltpu.VMEM)
-    state = pltpu.VMEM((rows // 2 * sides, DEPTH), F32)
-    out_shape = [
-        jax.ShapeDtypeStruct((rows + ROW_TILE // 2, channels), F32),
-        jax.ShapeDtypeStruct((rows + ROW_TILE, channels), BF16),
-    ][:sides]
     return pl.pallas_call(
-        functools.partial(spectra_kernel, bins, windows, block_len, low_end, high_end, sides),
-        out_shape=out_shape,
-        grid=(1,),
-        in_specs=[
-            hbm, hbm, hbm, hbm,
-            pl.BlockSpec((ROW_TILE, channels), lambda i: (tail, 0)),
+        functools.partial(spectra_kernel, bins, windows, block_len, high_end),
+        out_shape=[
+            jax.ShapeDtypeStruct((rows + ROW_TILE // 2, channels), F32),
+            jax.ShapeDtypeStruct((rows + ROW_TILE, channels), BF16),
+            jax.ShapeDtypeStruct((4, rows, DEPTH), F32),
         ],
-        out_specs=[whole] * sides,
+        in_specs=[hbm, hbm, hbm, hbm],
+        out_specs=[whole] * 3,
         scratch_shapes=[
             pltpu.SMEM(offsets.shape, jnp.int32),
             pltpu.SMEM(band_bins.shape, jnp.int32),
             pltpu.VMEM((1, channels), jnp.int32),
-            pltpu.VMEM((padded, channels), BF16),
-            pltpu.VMEM((sides * rows, channels), F32),
+            pltpu.VMEM((high_end, channels), BF16),
+            pltpu.VMEM((2 * rows, channels), F32),
             pltpu.VMEM((2 * windows + 2, ROW_TILE // 2, channels), F32),
             pltpu.VMEM((ROW_TILE // 2, channels), F32),
-            state, state, state, state, state,
-            pltpu.VMEM((sides * rows, padded), BF16),
+            pltpu.VMEM((rows, channels), F32),
+            pltpu.VMEM((4, 2 * rows, DEPTH), F32),
+            pltpu.VMEM((2 * rows, DEPTH), F32),
+            pltpu.VMEM((2 * rows, high_end), BF16),
             pltpu.SemaphoreType.DMA((3,)),
-            pltpu.SemaphoreType.DMA((pl.cdiv(padded, STEP),)),
+            pltpu.SemaphoreType.DMA((high_end // STEP,)),
         ],
         compiler_params=pltpu.CompilerParams(vmem_limit_bytes=60 * 2**20),
         cost_estimate=pl.CostEstimate(
-            flops=2 * channels * (high_end - low_end) * sides * rows,
-            bytes_accessed=channels * (high_end - low_end) * 2,
-            transcendentals=0,
+            flops=2 * channels * high_end * 2 * rows, bytes_accessed=channels * high_end * 2, transcendentals=0
         ),
-        name="band_spectra" if sides == 2 else "band_spectra_rest",
-    )(offsets, band_bins, dead.reshape(1, channels), samples, samples)
+        name="band_spectra",
+    )(offsets, band_bins, dead.reshape(1, channels), samples)
+
+
+def rest_of(recording, state, bins, windows, low_end):
+    channels, block_len = recording.shape
+    rows = bins * windows * 2
+    count = block_len - low_end
+    padded = pl.cdiv(count, DEPTH) * DEPTH
+    bulk = count // ROW_TILE * ROW_TILE
+    tail = min(low_end + bulk, block_len - 1) // ROW_TILE
+    samples = recording.T
+    whole = pl.BlockSpec(memory_space=pltpu.VMEM)
+    return pl.pallas_call(
+        functools.partial(rest_kernel, bins, windows, block_len, low_end),
+        out_shape=jax.ShapeDtypeStruct((rows + ROW_TILE // 2, channels), F32),
+        grid=(1,),
+        in_specs=[
+            whole,
+            pl.BlockSpec(memory_space=pltpu.HBM),
+            pl.BlockSpec((ROW_TILE, channels), lambda i: (tail, 0)),
+        ],
+        out_specs=whole,
+        scratch_shapes=[
+            pltpu.VMEM((padded, channels), BF16),
+            pltpu.VMEM((rows, channels), F32),
+            pltpu.VMEM((ROW_TILE // 2, channels), F32),
+            pltpu.VMEM((ROW_TILE // 2, channels), F32),
+            pltpu.VMEM((4, rows, DEPTH), F32),
+            pltpu.VMEM((rows, padded), BF16),
+            pltpu.SemaphoreType.DMA((pl.cdiv(padded, STEP),)),
+        ],
+        compiler_params=pltpu.CompilerParams(vmem_limit_bytes=24 * 2**20),
+        cost_estimate=pl.CostEstimate(
+            flops=2 * channels * count * rows, bytes_accessed=channels * count * 2, transcendentals=0
+        ),
+        name="band_spectra_rest",
+    )(state, samples, samples)
 
 
 def whiten_kernel(bins, windows, own_ref, rest_ref, more_ref, white_ref):
@@ -287,7 +380,8 @@
     more = more_ref[...].astype(F32)
     raw = own_ref[:rows, :] + rest_ref[:rows, :] + more[:rows]
     extra = more[rows:]
-    which = lax.broadcasted_iota(jnp.int32, (rows, 1), 0) % windows
+    per_group = ROW_TILE // (2 * windows)
+    which = lax.broadcasted_iota(jnp.int32, (rows, 1), 0) // per_group % windows
     alive = own_ref[rows + windows:rows + windows + 1, :]
     scale = factor = None
     for w in range(windows):
@@ -347,7 +441,7 @@
         to = out_hbm.at[part, bin_index]
         return pltpu.make_async_copy(made.at[slot], to, sems.at[slot])
 
-    which = lax.broadcasted_iota(jnp.int32, (depth, 1), 0) % (ROW_TILE // 2) // windows
+    which = lax.broadcasted_iota(jnp.int32, (depth, 1), 0) % per_group
     for b in range(per_group):
         for part in range(2):
             slot = 2 * b + part
@@ -470,9 +564,11 @@
     halves = tm_count // chan_count
     rim = L // 2 + L // 4
     cut = min(pl.cdiv(rim, STEP) * STEP, block_len)
-    own, back = spectra_of(recording, offsets, band_bins, dead_flags, windows, 0, cut, 2)
+    rim = L // 2 + L // 4
+    cut = pl.cdiv(rim, STEP) * STEP
+    own, back, state = spectra_of(recording, offsets, band_bins, dead_flags, windows, cut)
     more = moved(back, "tm", 1)
-    rest, = spectra_of(recording, offsets, band_bins, dead_flags, windows, cut, block_len, 1)
+    rest = rest_of(recording, state, bins, windows, cut)
     white = whiten(own, rest, more, bins, windows, halves)
     row_blocks = [white] + [from_partner(white, "tm", away) for away in range(2, tm_count, 2)]
     chan_blocks = chan_blocks_of(white)

time: 69 us -> 67.8 us (0.983)
  Pallas kernels: 35.3 us -> 34.1 us
    pallas_call x2 -> x1, Pallas kernels: 18.7 us -> 12.7 us  [spectra_of(): pl.pallas_call(functools.partial(spectra_kernel, bins, windows, block_len...]
    pallas_call x0 -> x1, Pallas kernels: none -> 4.77 us  [rest_of(): pl.pallas_call(functools.partial(rest_kernel, bins, windows, block_len, l...]
  transfers between devices with their start and end apart: 15 -> 15, of which waited for: 10 -> 10; matrix products, arithmetic and copies ran while one was open for 0% -> 0% of each run, Pallas kernels for 9% -> 7%
where the time goes in v11:
time: 67.8 us; the launch traced here: 67.7 us
  Pallas kernels  34.1 us (50%)
  starting transfers between devices  20.8 us (31%)
  waiting for transfers between devices  11.8 us (17%)
  local copies, waits for them, and re-layouts  0.97 us (1%)
    ppermute x14, starting transfers between devices, from_partner(): lax.ppermute(block, axis, [(i, i ^ away) for i in range(lax.axis_size(axi...  19.3 us
    pallas_call x1, Pallas kernels, stacks_of(): pl.pallas_call(functools.partial(stack_kernel, windows, scale, devices),...  16.2 us
    pallas_call x1, Pallas kernels, spectra_of(): pl.pallas_call(functools.partial(spectra_kernel, bins, windows, block_len...  12.7 us
    ppermute x14, waiting for transfers between devices, from_partner(): lax.ppermute(block, axis, [(i, i ^ away) for i in range(lax.axis_size(axi...  11.8 us
    pallas_call x1, Pallas kernels, rest_of(): pl.pallas_call(functools.partial(rest_kernel, bins, windows, block_len, l...  4.77 us
    ppermute x1, starting transfers between devices, moved(): lax.ppermute(block, axis, [(i + far, i) for i in range(count) if 0 <= i +...  1.42 us
  transfers between devices with their start and end apart: 15, of which 10 were waited for; matrix products, arithmetic and copies ran while one was open for 0% of the time, Pallas kernels for 7%

profile of v11, /device:TPU:0, one launch (start us, length us, event | category | flops | bytes accessed | tf_op | source)
XLA Modules:
  0.0 67.7 jit_solution(15052500992415978208)
XLA Ops:
  0.0 12.7 %band_spectra.1 = (f32[88,1024]{1,0:T(8,128)}, bf16[96,1024]{1,0:T(8,128)(2,1)}, f32[4,80,256]{2,1,0:T(8,128)}) custom-call(s32[16]{0:T(128)} %offsets_hbm.1, s32[20]{0:T(128)} %bins_hbm.1, s32[1,1024]{1,0:T(1,128)} %bitcast.5, bf16[15000,1024]{1,0:T(8,128)(2,1)} %bitcast.2), custom_call_target="tpu_custom_call" | custom-call | flops 3690987520 | bytes 23068672 | tf_op jit(solution)/shard_map/band_spectra/pallas_call | solution.py:310
  12.7 1.4 %collective-permute-start = (bf16[96,1024]{1,0:T(8,128)(2,1)}, bf16[96,1024]{1,0:T(8,128)(2,1)S(1)}, u32[]{:S(2)}, u32[]{:S(2)}) collective-permute-start(bf16[96,1024]{1,0:T(8,128)(2,1)} %get-tuple-element.19), channel_id=1, source_target_pairs={{1,0},{2,1},{3,2},{4,3},{5,4},{6,5},{7,6},{9,8},{10,9},{11,10},{12... | collective-permute-start | bytes 589832 | tf_op jit(solution)/shard_map/ppermute | solution.py:539
  14.2 1.0 %copy-done.1 = f32[4,80,256]{2,1,0:T(8,128)S(1)} copy-done((f32[4,80,256]{2,1,0:T(8,128)S(1)}, f32[4,80,256]{2,1,0:T(8,128)}, u32[]{:S(2)}) %copy-start.1) | copy-done | bytes 327704
  15.1 4.8 %band_spectra_rest.1.rest_ref = f32[88,1024]{1,0:T(8,128)S(1)} custom-call(f32[4,80,256]{2,1,0:T(8,128)S(1)} %copy-done.1, bf16[15000,1024]{1,0:T(8,128)(2,1)} %bitcast.3, bf16[15000,1024]{1,0:T(8,128)(2,1)} %bitcast.4), custom_call_target="tpu_custom_call" | custom-call | flops 612106240 | bytes 7651328 | tf_op jit(solution)/shard_map/band_spectra_rest/pallas_call | solution.py:351
  20.2 4.1 %collective-permute-start.5 = (bf16[2,80,512]{2,1,0:T(8,128)(2,1)S(1)}, bf16[2,80,512]{2,1,0:T(8,128)(2,1)S(1)}, u32[]{:S(2)}, u32[]{:S(2)}) collective-permute-start(bf16[2,80,512]{2,1,0:T(8,128)(2,1)S(1)} %whiten.1.refs_0_), channel_id=1, source_target_pairs={{0,16},{8,24},{16,0},{24,8},{1,17},{9,25},{17,1},{25,9},{2,18},{10... | collective-permute-start | bytes 491528 | tf_op jit(solution)/shard_map/ppermute | solution.py:556
  24.3 1.6 %collective-permute-start.4 = (bf16[2,80,512]{2,1,0:T(8,128)(2,1)S(1)}, bf16[2,80,512]{2,1,0:T(8,128)(2,1)S(1)}, u32[]{:S(2)}, u32[]{:S(2)}) collective-permute-start(bf16[2,80,512]{2,1,0:T(8,128)(2,1)S(1)} %whiten.1.refs_0_), channel_id=1, source_target_pairs={{0,8},{8,0},{16,24},{24,16},{1,9},{9,1},{17,25},{25,17},{2,10},{10... | collective-permute-start | bytes 491528 | tf_op jit(solution)/shard_map/ppermute | solution.py:556
  25.9 3.4 %collective-permute-start.3 = (bf16[2,80,512]{2,1,0:T(8,128)(2,1)S(1)}, bf16[2,80,512]{2,1,0:T(8,128)(2,1)S(1)}, u32[]{:S(2)}, u32[]{:S(2)}) collective-permute-start(bf16[2,80,512]{2,1,0:T(8,128)(2,1)S(1)} %whiten.1.refs_0_), channel_id=1, source_target_pairs={{0,6},{1,7},{2,4},{3,5},{4,2},{5,3},{6,0},{7,1},{8,14},{9,15},{10,... | collective-permute-start | bytes 491528 | tf_op jit(solution)/shard_map/ppermute | solution.py:556
  29.2 0.5 collective-permute-start.2
  29.7 0.9 %collective-permute-start.1 = (bf16[2,80,512]{2,1,0:T(8,128)(2,1)S(1)}, bf16[2,80,512]{2,1,0:T(8,128)(2,1)S(1)}, u32[]{:S(2)}, u32[]{:S(2)}) collective-permute-start(bf16[2,80,512]{2,1,0:T(8,128)(2,1)S(1)} %whiten.1.refs_0_), channel_id=1, source_target_pairs={{0,2},{1,3},{2,0},{3,1},{4,6},{5,7},{6,4},{7,5},{8,10},{9,11},{10,... | collective-permute-start | bytes 491528 | tf_op jit(solution)/shard_map/ppermute | solution.py:556
  30.6 2.0 %collective-permute-done.5.refs_5_ = bf16[2,80,512]{2,1,0:T(8,128)(2,1)S(1)} collective-permute-done((bf16[2,80,512]{2,1,0:T(8,128)(2,1)S(1)}, bf16[2,80,512]{2,1,0:T(8,128)(2,1)S(1)}, u32[]{:S(2)}, u32[]{:S(2)}) %collective-permute-start.5) | collective-permute-done | bytes 163872 | tf_op jit(solution)/shard_map/ppermute | solution.py:556
  32.6 1.2 %collective-permute-start.6 = (bf16[2,80,512]{2,1,0:T(8,128)(2,1)S(1)}, bf16[2,80,512]{2,1,0:T(8,128)(2,1)S(1)}, u32[]{:S(2)}, u32[]{:S(2)}) collective-permute-start(bf16[2,80,512]{2,1,0:T(8,128)(2,1)S(1)} %collective-permute-done.5.refs_5_), channel_id=1, source_target_pairs={{0,8},{8,0},{16,24},{24,16},{1,9},{9,1},{17,25},{25,17},{2,10},{10... | collective-permute-start | bytes 491528 | tf_op jit(solution)/shard_map/ppermute | solution.py:556
  33.9 0.4 collective-permute-done.3.refs_3_
  34.2 2.8 %collective-permute-done.2.refs_2_ = bf16[2,80,512]{2,1,0:T(8,128)(2,1)S(1)} collective-permute-done((bf16[2,80,512]{2,1,0:T(8,128)(2,1)S(1)}, bf16[2,80,512]{2,1,0:T(8,128)(2,1)S(1)}, u32[]{:S(2)}, u32[]{:S(2)}) %collective-permute-start.2) | collective-permute-done | bytes 163872 | tf_op jit(solution)/shard_map/ppermute | solution.py:556
  37.2 2.0 %collective-permute-done.6.refs_6_ = bf16[2,80,512]{2,1,0:T(8,128)(2,1)S(1)} collective-permute-done((bf16[2,80,512]{2,1,0:T(8,128)(2,1)S(1)}, bf16[2,80,512]{2,1,0:T(8,128)(2,1)S(1)}, u32[]{:S(2)}, u32[]{:S(2)}) %collective-permute-start.6) | collective-permute-done | bytes 163872 | tf_op jit(solution)/shard_map/ppermute | solution.py:556
  39.4 1.8 %collective-permute-start.7 = (bf16[80,512]{1,0:T(8,128)(2,1)S(1)}, bf16[80,512]{1,0:T(8,128)(2,1)S(1)}, u32[]{:S(2)}, u32[]{:S(2)}) collective-permute-start(bf16[80,512]{1,0:T(8,128)(2,1)S(1)} %get-tuple-element.21), channel_id=1, source_target_pairs={{0,2},{1,3},{2,0},{3,1},{4,6},{5,7},{6,4},{7,5},{8,10},{9,11},{10,... | collective-permute-start | bytes 245768 | tf_op jit(solution)/shard_map/ppermute | solution.py:556
  41.1 1.7 %collective-permute-start.8 = (bf16[80,512]{1,0:T(8,128)(2,1)S(1)}, bf16[80,512]{1,0:T(8,128)(2,1)S(1)}, u32[]{:S(2)}, u32[]{:S(2)}) collective-permute-start(bf16[80,512]{1,0:T(8,128)(2,1)S(1)} %get-tuple-element.22), channel_id=1, source_target_pairs={{0,4},{1,5},{2,6},{3,7},{4,0},{5,1},{6,2},{7,3},{8,12},{9,13},{10,... | collective-permute-start | bytes 245768 | tf_op jit(solution)/shard_map/ppermute | solution.py:556
  42.9 0.9 %collective-permute-start.10 = (bf16[80,512]{1,0:T(8,128)(2,1)S(1)}, bf16[80,512]{1,0:T(8,128)(2,1)S(1)}, u32[]{:S(2)}, u32[]{:S(2)}) collective-permute-start(bf16[80,512]{1,0:T(8,128)(2,1)S(1)} %get-tuple-element.24), channel_id=1, source_target_pairs={{0,3},{1,2},{2,1},{3,0},{4,7},{5,6},{6,5},{7,4},{8,11},{9,10},{10,... | collective-permute-start | bytes 245768 | tf_op jit(solution)/shard_map/ppermute | solution.py:556
  43.8 0.4 collective-permute-done.7.refs_1_
  44.2 1.8 %collective-permute-start.11 = (bf16[80,512]{1,0:T(8,128)(2,1)S(1)}, bf16[80,512]{1,0:T(8,128)(2,1)S(1)}, u32[]{:S(2)}, u32[]{:S(2)}) collective-permute-start(bf16[80,512]{1,0:T(8,128)(2,1)S(1)} %get-tuple-element.25), channel_id=1, source_target_pairs={{0,5},{1,4},{2,7},{3,6},{4,1},{5,0},{6,3},{7,2},{8,13},{9,12},{10,... | collective-permute-start | bytes 245768 | tf_op jit(solution)/shard_map/ppermute | solution.py:556
  46.2 1.3 %collective-permute-start.12 = (bf16[80,512]{1,0:T(8,128)(2,1)S(1)}, bf16[80,512]{1,0:T(8,128)(2,1)S(1)}, u32[]{:S(2)}, u32[]{:S(2)}) collective-permute-start(bf16[80,512]{1,0:T(8,128)(2,1)S(1)} %get-tuple-element.26), channel_id=1, source_target_pairs={{0,7},{1,6},{2,5},{3,4},{4,3},{5,2},{6,1},{7,0},{8,15},{9,14},{10,... | collective-permute-start | bytes 245768 | tf_op jit(solution)/shard_map/ppermute | solution.py:556
  47.5 1.5 %collective-permute-done.9.refs_3_ = bf16[80,512]{1,0:T(8,128)(2,1)S(1)} collective-permute-done((bf16[80,512]{1,0:T(8,128)(2,1)S(1)}, bf16[80,512]{1,0:T(8,128)(2,1)S(1)}, u32[]{:S(2)}, u32[]{:S(2)}) %collective-permute-start.9) | collective-permute-done | bytes 81952 | tf_op jit(solution)/shard_map/ppermute | solution.py:556
  48.9 0.6 collective-permute-done.11.refs_5_
  49.6 1.9 %collective-permute-done.12.refs_6_ = bf16[80,512]{1,0:T(8,128)(2,1)S(1)} collective-permute-done((bf16[80,512]{1,0:T(8,128)(2,1)S(1)}, bf16[80,512]{1,0:T(8,128)(2,1)S(1)}, u32[]{:S(2)}, u32[]{:S(2)}) %collective-permute-start.12) | collective-permute-done | bytes 81952 | tf_op jit(solution)/shard_map/ppermute | solution.py:556
  51.5 16.2 %stack_products.1 = bf16[2,20,512,1024]{3,2,1,0:T(8,128)(2,1)} custom-call(bf16[80,512]{1,0:T(8,128)(2,1)S(1)} %get-tuple-element.20.refs_0_, bf16[80,512]{1,0:T(8,128)(2,1)S(1)} %collective-permute-done.7.refs_1_, bf16[80,512]{1,0:T(8,128)(2,1)S(1)} %collective-permute-done.8.refs_2_, bf16[80,512]{1,0:T(8,128)(2,1)S(1)} %collective-permute-done.9.refs_3_, ...), custom_call_target="tpu_custom_call" | custom-call | flops 5368709120 | bytes 41943040 | tf_op jit(solution)/shard_map/stack_products/pallas_call | solution.py:480
  (15 shorter events, 0.8 us)
Async XLA Ops:
  12.7 7.2 %copy-start = (f32[88,1024]{1,0:T(8,128)S(1)}, f32[88,1024]{1,0:T(8,128)}, u32[]{:S(2)}) copy-start(f32[88,1024]{1,0:T(8,128)} %get-tuple-element.17.own_ref) | copy-start | bytes 1081348
  12.7 7.2 %collective-permute-start = (bf16[96,1024]{1,0:T(8,128)(2,1)}, bf16[96,1024]{1,0:T(8,128)(2,1)S(1)}, u32[]{:S(2)}, u32[]{:S(2)}) collective-permute-start(bf16[96,1024]{1,0:T(8,128)(2,1)} %get-tuple-element.19), channel_id=1, source_target_pairs={{1,0},{2,1},{3,2},{4,3},{5,4},{6,5},{7,6},{9,8},{10,9},{11,10},{12... | collective-permute-start | bytes 589832 | tf_op jit(solution)/shard_map/ppermute | solution.py:539
  14.2 1.0 %copy-start.1 = (f32[4,80,256]{2,1,0:T(8,128)S(1)}, f32[4,80,256]{2,1,0:T(8,128)}, u32[]{:S(2)}) copy-start(f32[4,80,256]{2,1,0:T(8,128)} %get-tuple-element.18.state_in) | copy-start | bytes 983044
  20.2 12.4 %collective-permute-start.5 = (bf16[2,80,512]{2,1,0:T(8,128)(2,1)S(1)}, bf16[2,80,512]{2,1,0:T(8,128)(2,1)S(1)}, u32[]{:S(2)}, u32[]{:S(2)}) collective-permute-start(bf16[2,80,512]{2,1,0:T(8,128)(2,1)S(1)} %whiten.1.refs_0_), channel_id=1, source_target_pairs={{0,16},{8,24},{16,0},{24,8},{1,17},{9,25},{17,1},{25,9},{2,18},{10... | collective-permute-start | bytes 491528 | tf_op jit(solution)/shard_map/ppermute | solution.py:556
  24.3 9.6 %collective-permute-start.4 = (bf16[2,80,512]{2,1,0:T(8,128)(2,1)S(1)}, bf16[2,80,512]{2,1,0:T(8,128)(2,1)S(1)}, u32[]{:S(2)}, u32[]{:S(2)}) collective-permute-start(bf16[2,80,512]{2,1,0:T(8,128)(2,1)S(1)} %whiten.1.refs_0_), channel_id=1, source_target_pairs={{0,8},{8,0},{16,24},{24,16},{1,9},{9,1},{17,25},{25,17},{2,10},{10... | collective-permute-start | bytes 491528 | tf_op jit(solution)/shard_map/ppermute | solution.py:556
  25.9 8.4 %collective-permute-start.3 = (bf16[2,80,512]{2,1,0:T(8,128)(2,1)S(1)}, bf16[2,80,512]{2,1,0:T(8,128)(2,1)S(1)}, u32[]{:S(2)}, u32[]{:S(2)}) collective-permute-start(bf16[2,80,512]{2,1,0:T(8,128)(2,1)S(1)} %whiten.1.refs_0_), channel_id=1, source_target_pairs={{0,6},{1,7},{2,4},{3,5},{4,2},{5,3},{6,0},{7,1},{8,14},{9,15},{10,... | collective-permute-start | bytes 491528 | tf_op jit(solution)/shard_map/ppermute | solution.py:556
  29.2 7.8 %collective-permute-start.2 = (bf16[2,80,512]{2,1,0:T(8,128)(2,1)S(1)}, bf16[2,80,512]{2,1,0:T(8,128)(2,1)S(1)}, u32[]{:S(2)}, u32[]{:S(2)}) collective-permute-start(bf16[2,80,512]{2,1,0:T(8,128)(2,1)S(1)} %whiten.1.refs_0_), channel_id=1, source_target_pairs={{0,4},{1,5},{2,6},{3,7},{4,0},{5,1},{6,2},{7,3},{8,12},{9,13},{10,... | collective-permute-start | bytes 491528 | tf_op jit(solution)/shard_map/ppermute | solution.py:556
  29.7 7.5 %collective-permute-start.1 = (bf16[2,80,512]{2,1,0:T(8,128)(2,1)S(1)}, bf16[2,80,512]{2,1,0:T(8,128)(2,1)S(1)}, u32[]{:S(2)}, u32[]{:S(2)}) collective-permute-start(bf16[2,80,512]{2,1,0:T(8,128)(2,1)S(1)} %whiten.1.refs_0_), channel_id=1, source_target_pairs={{0,2},{1,3},{2,0},{3,1},{4,6},{5,7},{6,4},{7,5},{8,10},{9,11},{10,... | collective-permute-start | bytes 491528 | tf_op jit(solution)/shard_map/ppermute | solution.py:556
  32.6 6.5 %collective-permute-start.6 = (bf16[2,80,512]{2,1,0:T(8,128)(2,1)S(1)}, bf16[2,80,512]{2,1,0:T(8,128)(2,1)S(1)}, u32[]{:S(2)}, u32[]{:S(2)}) collective-permute-start(bf16[2,80,512]{2,1,0:T(8,128)(2,1)S(1)} %collective-permute-done.5.refs_5_), channel_id=1, source_target_pairs={{0,8},{8,0},{16,24},{24,16},{1,9},{9,1},{17,25},{25,17},{2,10},{10... | collective-permute-start | bytes 491528 | tf_op jit(solution)/shard_map/ppermute | solution.py:556
  39.3 12.2 %collective-permute-start.14 = (bf16[4,2,80,512]{3,2,1,0:T(8,128)(2,1)S(1)}, bf16[4,2,80,512]{3,2,1,0:T(8,128)(2,1)S(1)}, u32[]{:S(2)}, u32[]{:S(2)}) collective-permute-start(bf16[4,2,80,512]{3,2,1,0:T(8,128)(2,1)S(1)} %get-tuple-element.28.refs_8_), channel_id=1, source_target_pairs={{0,1},{1,0},{2,3},{3,2},{4,5},{5,4},{6,7},{7,6},{8,9},{9,8},{10,11... | collective-permute-start | bytes 1966088 | tf_op jit(solution)/shard_map/ppermute | solution.py:556
  39.4 4.9 %collective-permute-start.7 = (bf16[80,512]{1,0:T(8,128)(2,1)S(1)}, bf16[80,512]{1,0:T(8,128)(2,1)S(1)}, u32[]{:S(2)}, u32[]{:S(2)}) collective-permute-start(bf16[80,512]{1,0:T(8,128)(2,1)S(1)} %get-tuple-element.21), channel_id=1, source_target_pairs={{0,2},{1,3},{2,0},{3,1},{4,6},{5,7},{6,4},{7,5},{8,10},{9,11},{10,... | collective-permute-start | bytes 245768 | tf_op jit(solution)/shard_map/ppermute | solution.py:556
  41.1 5.0 %collective-permute-start.8 = (bf16[80,512]{1,0:T(8,128)(2,1)S(1)}, bf16[80,512]{1,0:T(8,128)(2,1)S(1)}, u32[]{:S(2)}, u32[]{:S(2)}) collective-permute-start(bf16[80,512]{1,0:T(8,128)(2,1)S(1)} %get-tuple-element.22), channel_id=1, source_target_pairs={{0,4},{1,5},{2,6},{3,7},{4,0},{5,1},{6,2},{7,3},{8,12},{9,13},{10,... | collective-permute-start | bytes 245768 | tf_op jit(solution)/shard_map/ppermute | solution.py:556
  42.8 6.1 %collective-permute-start.9 = (bf16[80,512]{1,0:T(8,128)(2,1)S(1)}, bf16[80,512]{1,0:T(8,128)(2,1)S(1)}, u32[]{:S(2)}, u32[]{:S(2)}) collective-permute-start(bf16[80,512]{1,0:T(8,128)(2,1)S(1)} %get-tuple-element.23), channel_id=1, source_target_pairs={{0,6},{1,7},{2,4},{3,5},{4,2},{5,3},{6,0},{7,1},{8,14},{9,15},{10,... | collective-permute-start | bytes 245768 | tf_op jit(solution)/shard_map/ppermute | solution.py:556
  42.9 6.0 %collective-permute-start.10 = (bf16[80,512]{1,0:T(8,128)(2,1)S(1)}, bf16[80,512]{1,0:T(8,128)(2,1)S(1)}, u32[]{:S(2)}, u32[]{:S(2)}) collective-permute-start(bf16[80,512]{1,0:T(8,128)(2,1)S(1)} %get-tuple-element.24), channel_id=1, source_target_pairs={{0,3},{1,2},{2,1},{3,0},{4,7},{5,6},{6,5},{7,4},{8,11},{9,10},{10,... | collective-permute-start | bytes 245768 | tf_op jit(solution)/shard_map/ppermute | solution.py:556
  44.2 5.4 %collective-permute-start.11 = (bf16[80,512]{1,0:T(8,128)(2,1)S(1)}, bf16[80,512]{1,0:T(8,128)(2,1)S(1)}, u32[]{:S(2)}, u32[]{:S(2)}) collective-permute-start(bf16[80,512]{1,0:T(8,128)(2,1)S(1)} %get-tuple-element.25), channel_id=1, source_target_pairs={{0,5},{1,4},{2,7},{3,6},{4,1},{5,0},{6,3},{7,2},{8,13},{9,12},{10,... | collective-permute-start | bytes 245768 | tf_op jit(solution)/shard_map/ppermute | solution.py:556
  46.2 5.4 %collective-permute-start.12 = (bf16[80,512]{1,0:T(8,128)(2,1)S(1)}, bf16[80,512]{1,0:T(8,128)(2,1)S(1)}, u32[]{:S(2)}, u32[]{:S(2)}) collective-permute-start(bf16[80,512]{1,0:T(8,128)(2,1)S(1)} %get-tuple-element.26), channel_id=1, source_target_pairs={{0,7},{1,6},{2,5},{3,4},{4,3},{5,2},{6,1},{7,0},{8,15},{9,14},{10,... | collective-permute-start | bytes 245768 | tf_op jit(solution)/shard_map/ppermute | solution.py:556
  48.9 2.6 %collective-permute-start.13 = (bf16[80,512]{1,0:T(8,128)(2,1)S(1)}, bf16[80,512]{1,0:T(8,128)(2,1)S(1)}, u32[]{:S(2)}, u32[]{:S(2)}) collective-permute-start(bf16[80,512]{1,0:T(8,128)(2,1)S(1)} %get-tuple-element.27), channel_id=1, source_target_pairs={{0,1},{1,0},{2,3},{3,2},{4,5},{5,4},{6,7},{7,6},{8,9},{9,8},{10,11... | collective-permute-start | bytes 245768 | tf_op jit(solution)/shard_map/ppermute | solution.py:556

commit v12 on v11

--- a/solution.py
+++ b/solution.py
@@ -45,23 +45,26 @@
     ]
 
 
-def make_table(table, state, place, index, windows_rows):
+def make_tables(table, state, place, first, count, windows_rows):
     rows = table.shape[0]
-    to_lanes = pl.ds(pl.multiple_of(index * DEPTH, DEPTH), DEPTH)
-    moved = (index * DEPTH).astype(F32)
     for r in range(0, rows, ROW_TILE):
-        values = []
-        for at in (slice(r, r + 8), slice(r + 8, r + 16)):
-            u, v = state[0, at, :], state[1, at, :]
-            ct, st = state[2, at, :], state[3, at, :]
+        halves = (slice(r, r + 8), slice(r + 8, r + 16))
+        now = [(state[0, at, :], state[1, at, :]) for at in halves]
+        turn = [(state[2, at, :], state[3, at, :]) for at in halves]
+        spot = None if place is None else [place[at, :] for at in halves]
+        for j in range(count):
+            moved = ((first + j) * DEPTH).astype(F32)
+            values = [u for u, _ in now]
             if place is not None:
-                limit = -moved if at.start < windows_rows else moved
-                values.append(jnp.where(place[at, :] >= limit, u, 0.0))
-            else:
-                values.append(u)
-            state[0, at, :] = u * ct - v * st
-            state[1, at, :] = v * ct + u * st
-        table[r:r + ROW_TILE, to_lanes] = jnp.concatenate(values, axis=0).astype(BF16)
+                values = [
+                    jnp.where(where >= (-moved if at.start < windows_rows else moved), u, 0.0)
+                    for at, where, u in zip(halves, spot, values)
+                ]
+            to_lanes = pl.ds(pl.multiple_of((first + j) * DEPTH, DEPTH), DEPTH)
+            table[r:r + ROW_TILE, to_lanes] = jnp.concatenate(values, axis=0).astype(BF16)
+            now = [(u * ct - v * st, v * ct + u * st) for (u, v), (ct, st) in zip(now, turn)]
+        for at, (u, v) in zip(halves, now):
+            state[0, at, :], state[1, at, :] = u, v
 
 
 def add_products(table, x_ref, acc, base, size, row_range, energy_at):
@@ -72,19 +75,22 @@
     for n in range(0, channels, DEPTH):
         at = slice(n, min(n + DEPTH, channels))
         if energy_at is not None:
-            total = squares(view, 0, at)
-            for t in range(1, size // ROW_TILE):
-                total = total + squares(view, t, at)
+            total = squares(view, 0, 2, at)
+            for t in range(2, size // ROW_TILE, 2):
+                total = total + squares(view, t, 2, at)
         product = jnp.dot(waves[low:high, :], view[:, at], preferred_element_type=F32)
         acc[low:high, at] += product
         if energy_at is not None:
             energy_at[:, at] = total
 
 
-def squares(view, t, at):
-    x = view[t * ROW_TILE:(t + 1) * ROW_TILE, at].astype(F32)
-    square = x * x
-    return square[:ROW_TILE // 2] + square[ROW_TILE // 2:]
+def squares(view, first, count, at):
+    total = None
+    for t in range(first, first + count):
+        x = view[t * ROW_TILE:(t + 1) * ROW_TILE, at]
+        total = x * x if total is None else total + x * x
+    total = total.astype(F32)
+    return total[:ROW_TILE // 2] + total[ROW_TILE // 2:]
 
 
 def mix_windows(out_ref, acc, first, windows, per_window, per_group):
@@ -184,7 +190,7 @@
             target = jnp.where(has_end(first, ROW_TILE), trash, segment_of(first))
             for n in range(0, channels, DEPTH):
                 at = slice(n, min(n + DEPTH, channels))
-                seg[target, :, at] += squares(view, t, at)
+                seg[target, :, at] += squares(view, t, 1, at)
 
     def reach(i):
         low, high = i * STEP, (i + 1) * STEP
@@ -209,8 +215,7 @@
         @pl.loop(i, until)
         def _(step):
             base = pl.multiple_of(step * STEP, STEP)
-            for j in range(STEP // DEPTH):
-                make_table(table, state, place, step * (STEP // DEPTH) + j, rows)
+            make_tables(table, state, place, step * (STEP // DEPTH), STEP // DEPTH, rows)
             at = pl.ds(base, STEP)
             pltpu.make_async_copy(x_hbm.at[at], x_ref.at[at], x_sems.at[step]).wait()
             if not edges:
@@ -288,8 +293,7 @@
         x_ref[bulk:bulk + ROW_TILE, :] = jnp.where(inside, tail_ref[...].astype(F32), 0.0).astype(BF16)
     for i in range(0, padded, STEP):
         size = min(STEP, padded - i)
-        for j in range(size // DEPTH):
-            make_table(table, state, None, jnp.int32(i // DEPTH + j), rows)
+        make_tables(table, state, None, jnp.int32(i // DEPTH), size // DEPTH, rows)
         if i // STEP < len(loads):
             loads[i // STEP].wait()
         add_products(table, x_ref, acc, i, size, (0, rows), part_seg)

time: 67.8 us -> 66.4 us (0.979)
  Pallas kernels: 34.1 us -> 32.6 us
    pallas_call x1, Pallas kernels: 12.7 us -> 11.5 us  [spectra_of(): pl.pallas_call(functools.partial(spectra_kernel, bins, windows, block_len...]
where the time goes in v12:
time: 66.4 us; the launch traced here: 66 us
  Pallas kernels  32.6 us (49%)
  starting transfers between devices  20.9 us (31%)
  waiting for transfers between devices  11.4 us (17%)
  local copies, waits for them, and re-layouts  0.97 us (1%)
    ppermute x14, starting transfers between devices, from_partner(): lax.ppermute(block, axis, [(i, i ^ away) for i in range(lax.axis_size(axi...  19.5 us
    pallas_call x1, Pallas kernels, stacks_of(): pl.pallas_call(functools.partial(stack_kernel, windows, scale, devices),...  16.2 us
    pallas_call x1, Pallas kernels, spectra_of(): pl.pallas_call(functools.partial(spectra_kernel, bins, windows, block_len...  11.5 us
    ppermute x14, waiting for transfers between devices, from_partner(): lax.ppermute(block, axis, [(i, i ^ away) for i in range(lax.axis_size(axi...  11.4 us
    pallas_call x1, Pallas kernels, rest_of(): pl.pallas_call(functools.partial(rest_kernel, bins, windows, block_len, l...  4.55 us
    ppermute x1, starting transfers between devices, moved(): lax.ppermute(block, axis, [(i + far, i) for i in range(count) if 0 <= i +...  1.42 us
  transfers between devices with their start and end apart: 15, of which 10 were waited for; matrix products, arithmetic and copies ran while one was open for 0% of the time, Pallas kernels for 7%

profile of v12, /device:TPU:0, one launch (start us, length us, event | category | flops | bytes accessed | tf_op | source)
XLA Modules:
  0.0 66.0 jit_solution(15458547169191178871)
XLA Ops:
  0.0 11.5 %band_spectra.1 = (f32[88,1024]{1,0:T(8,128)}, bf16[96,1024]{1,0:T(8,128)(2,1)}, f32[4,80,256]{2,1,0:T(8,128)}) custom-call(s32[16]{0:T(128)} %offsets_hbm.1, s32[20]{0:T(128)} %bins_hbm.1, s32[1,1024]{1,0:T(1,128)} %bitcast.5, bf16[15000,1024]{1,0:T(8,128)(2,1)} %bitcast.2), custom_call_target="tpu_custom_call" | custom-call | flops 3690987520 | bytes 23068672 | tf_op jit(solution)/shard_map/band_spectra/pallas_call | solution.py:314
  11.5 1.4 %collective-permute-start = (bf16[96,1024]{1,0:T(8,128)(2,1)}, bf16[96,1024]{1,0:T(8,128)(2,1)S(1)}, u32[]{:S(2)}, u32[]{:S(2)}) collective-permute-start(bf16[96,1024]{1,0:T(8,128)(2,1)} %get-tuple-element.19), channel_id=1, source_target_pairs={{1,0},{2,1},{3,2},{4,3},{5,4},{6,5},{7,6},{9,8},{10,9},{11,10},{12... | collective-permute-start | bytes 589832 | tf_op jit(solution)/shard_map/ppermute | solution.py:543
  12.9 1.0 %copy-done.1 = f32[4,80,256]{2,1,0:T(8,128)S(1)} copy-done((f32[4,80,256]{2,1,0:T(8,128)S(1)}, f32[4,80,256]{2,1,0:T(8,128)}, u32[]{:S(2)}) %copy-start.1) | copy-done | bytes 327704
  13.9 4.6 %band_spectra_rest.1.rest_ref = f32[88,1024]{1,0:T(8,128)S(1)} custom-call(f32[4,80,256]{2,1,0:T(8,128)S(1)} %copy-done.1, bf16[15000,1024]{1,0:T(8,128)(2,1)} %bitcast.3, bf16[15000,1024]{1,0:T(8,128)(2,1)} %bitcast.4), custom_call_target="tpu_custom_call" | custom-call | flops 612106240 | bytes 7651328 | tf_op jit(solution)/shard_map/band_spectra_rest/pallas_call | solution.py:355
  18.7 4.1 %collective-permute-start.5 = (bf16[2,80,512]{2,1,0:T(8,128)(2,1)S(1)}, bf16[2,80,512]{2,1,0:T(8,128)(2,1)S(1)}, u32[]{:S(2)}, u32[]{:S(2)}) collective-permute-start(bf16[2,80,512]{2,1,0:T(8,128)(2,1)S(1)} %whiten.1.refs_0_), channel_id=1, source_target_pairs={{0,16},{8,24},{16,0},{24,8},{1,17},{9,25},{17,1},{25,9},{2,18},{10... | collective-permute-start | bytes 491528 | tf_op jit(solution)/shard_map/ppermute | solution.py:560
  22.8 1.6 %collective-permute-start.4 = (bf16[2,80,512]{2,1,0:T(8,128)(2,1)S(1)}, bf16[2,80,512]{2,1,0:T(8,128)(2,1)S(1)}, u32[]{:S(2)}, u32[]{:S(2)}) collective-permute-start(bf16[2,80,512]{2,1,0:T(8,128)(2,1)S(1)} %whiten.1.refs_0_), channel_id=1, source_target_pairs={{0,8},{8,0},{16,24},{24,16},{1,9},{9,1},{17,25},{25,17},{2,10},{10... | collective-permute-start | bytes 491528 | tf_op jit(solution)/shard_map/ppermute | solution.py:560
  24.4 3.4 %collective-permute-start.3 = (bf16[2,80,512]{2,1,0:T(8,128)(2,1)S(1)}, bf16[2,80,512]{2,1,0:T(8,128)(2,1)S(1)}, u32[]{:S(2)}, u32[]{:S(2)}) collective-permute-start(bf16[2,80,512]{2,1,0:T(8,128)(2,1)S(1)} %whiten.1.refs_0_), channel_id=1, source_target_pairs={{0,6},{1,7},{2,4},{3,5},{4,2},{5,3},{6,0},{7,1},{8,14},{9,15},{10,... | collective-permute-start | bytes 491528 | tf_op jit(solution)/shard_map/ppermute | solution.py:560
  27.8 0.5 collective-permute-start.2
  28.3 0.7 %collective-permute-start.1 = (bf16[2,80,512]{2,1,0:T(8,128)(2,1)S(1)}, bf16[2,80,512]{2,1,0:T(8,128)(2,1)S(1)}, u32[]{:S(2)}, u32[]{:S(2)}) collective-permute-start(bf16[2,80,512]{2,1,0:T(8,128)(2,1)S(1)} %whiten.1.refs_0_), channel_id=1, source_target_pairs={{0,2},{1,3},{2,0},{3,1},{4,6},{5,7},{6,4},{7,5},{8,10},{9,11},{10,... | collective-permute-start | bytes 491528 | tf_op jit(solution)/shard_map/ppermute | solution.py:560
  29.0 2.1 %collective-permute-done.5.refs_5_ = bf16[2,80,512]{2,1,0:T(8,128)(2,1)S(1)} collective-permute-done((bf16[2,80,512]{2,1,0:T(8,128)(2,1)S(1)}, bf16[2,80,512]{2,1,0:T(8,128)(2,1)S(1)}, u32[]{:S(2)}, u32[]{:S(2)}) %collective-permute-start.5) | collective-permute-done | bytes 163872 | tf_op jit(solution)/shard_map/ppermute | solution.py:560
  31.1 1.2 %collective-permute-start.6 = (bf16[2,80,512]{2,1,0:T(8,128)(2,1)S(1)}, bf16[2,80,512]{2,1,0:T(8,128)(2,1)S(1)}, u32[]{:S(2)}, u32[]{:S(2)}) collective-permute-start(bf16[2,80,512]{2,1,0:T(8,128)(2,1)S(1)} %collective-permute-done.5.refs_5_), channel_id=1, source_target_pairs={{0,8},{8,0},{16,24},{24,16},{1,9},{9,1},{17,25},{25,17},{2,10},{10... | collective-permute-start | bytes 491528 | tf_op jit(solution)/shard_map/ppermute | solution.py:560
  32.4 0.5 collective-permute-done.3.refs_3_
  32.8 2.6 %collective-permute-done.2.refs_2_ = bf16[2,80,512]{2,1,0:T(8,128)(2,1)S(1)} collective-permute-done((bf16[2,80,512]{2,1,0:T(8,128)(2,1)S(1)}, bf16[2,80,512]{2,1,0:T(8,128)(2,1)S(1)}, u32[]{:S(2)}, u32[]{:S(2)}) %collective-permute-start.2) | collective-permute-done | bytes 163872 | tf_op jit(solution)/shard_map/ppermute | solution.py:560
  35.8 1.8 %collective-permute-done.6.refs_6_ = bf16[2,80,512]{2,1,0:T(8,128)(2,1)S(1)} collective-permute-done((bf16[2,80,512]{2,1,0:T(8,128)(2,1)S(1)}, bf16[2,80,512]{2,1,0:T(8,128)(2,1)S(1)}, u32[]{:S(2)}, u32[]{:S(2)}) %collective-permute-start.6) | collective-permute-done | bytes 163872 | tf_op jit(solution)/shard_map/ppermute | solution.py:560
  37.9 1.9 %collective-permute-start.7 = (bf16[80,512]{1,0:T(8,128)(2,1)S(1)}, bf16[80,512]{1,0:T(8,128)(2,1)S(1)}, u32[]{:S(2)}, u32[]{:S(2)}) collective-permute-start(bf16[80,512]{1,0:T(8,128)(2,1)S(1)} %get-tuple-element.21), channel_id=1, source_target_pairs={{0,2},{1,3},{2,0},{3,1},{4,6},{5,7},{6,4},{7,5},{8,10},{9,11},{10,... | collective-permute-start | bytes 245768 | tf_op jit(solution)/shard_map/ppermute | solution.py:560
  39.8 1.2 %collective-permute-start.8 = (bf16[80,512]{1,0:T(8,128)(2,1)S(1)}, bf16[80,512]{1,0:T(8,128)(2,1)S(1)}, u32[]{:S(2)}, u32[]{:S(2)}) collective-permute-start(bf16[80,512]{1,0:T(8,128)(2,1)S(1)} %get-tuple-element.22), channel_id=1, source_target_pairs={{0,4},{1,5},{2,6},{3,7},{4,0},{5,1},{6,2},{7,3},{8,12},{9,13},{10,... | collective-permute-start | bytes 245768 | tf_op jit(solution)/shard_map/ppermute | solution.py:560
  41.0 0.5 collective-permute-start.9
  41.4 1.1 %collective-permute-start.10 = (bf16[80,512]{1,0:T(8,128)(2,1)S(1)}, bf16[80,512]{1,0:T(8,128)(2,1)S(1)}, u32[]{:S(2)}, u32[]{:S(2)}) collective-permute-start(bf16[80,512]{1,0:T(8,128)(2,1)S(1)} %get-tuple-element.24), channel_id=1, source_target_pairs={{0,3},{1,2},{2,1},{3,0},{4,7},{5,6},{6,5},{7,4},{8,11},{9,10},{10,... | collective-permute-start | bytes 245768 | tf_op jit(solution)/shard_map/ppermute | solution.py:560
  42.8 1.3 %collective-permute-start.11 = (bf16[80,512]{1,0:T(8,128)(2,1)S(1)}, bf16[80,512]{1,0:T(8,128)(2,1)S(1)}, u32[]{:S(2)}, u32[]{:S(2)}) collective-permute-start(bf16[80,512]{1,0:T(8,128)(2,1)S(1)} %get-tuple-element.25), channel_id=1, source_target_pairs={{0,5},{1,4},{2,7},{3,6},{4,1},{5,0},{6,3},{7,2},{8,13},{9,12},{10,... | collective-permute-start | bytes 245768 | tf_op jit(solution)/shard_map/ppermute | solution.py:560
  44.3 1.9 %collective-permute-start.12 = (bf16[80,512]{1,0:T(8,128)(2,1)S(1)}, bf16[80,512]{1,0:T(8,128)(2,1)S(1)}, u32[]{:S(2)}, u32[]{:S(2)}) collective-permute-start(bf16[80,512]{1,0:T(8,128)(2,1)S(1)} %get-tuple-element.26), channel_id=1, source_target_pairs={{0,7},{1,6},{2,5},{3,4},{4,3},{5,2},{6,1},{7,0},{8,15},{9,14},{10,... | collective-permute-start | bytes 245768 | tf_op jit(solution)/shard_map/ppermute | solution.py:560
  46.2 1.0 %collective-permute-done.9.refs_3_ = bf16[80,512]{1,0:T(8,128)(2,1)S(1)} collective-permute-done((bf16[80,512]{1,0:T(8,128)(2,1)S(1)}, bf16[80,512]{1,0:T(8,128)(2,1)S(1)}, u32[]{:S(2)}, u32[]{:S(2)}) %collective-permute-start.9) | collective-permute-done | bytes 81952 | tf_op jit(solution)/shard_map/ppermute | solution.py:560
  47.2 0.7 %collective-permute-done.11.refs_5_ = bf16[80,512]{1,0:T(8,128)(2,1)S(1)} collective-permute-done((bf16[80,512]{1,0:T(8,128)(2,1)S(1)}, bf16[80,512]{1,0:T(8,128)(2,1)S(1)}, u32[]{:S(2)}, u32[]{:S(2)}) %collective-permute-start.11) | collective-permute-done | bytes 81952 | tf_op jit(solution)/shard_map/ppermute | solution.py:560
  47.9 1.9 %collective-permute-done.12.refs_6_ = bf16[80,512]{1,0:T(8,128)(2,1)S(1)} collective-permute-done((bf16[80,512]{1,0:T(8,128)(2,1)S(1)}, bf16[80,512]{1,0:T(8,128)(2,1)S(1)}, u32[]{:S(2)}, u32[]{:S(2)}) %collective-permute-start.12) | collective-permute-done | bytes 81952 | tf_op jit(solution)/shard_map/ppermute | solution.py:560
  49.8 16.2 %stack_products.1 = bf16[2,20,512,1024]{3,2,1,0:T(8,128)(2,1)} custom-call(bf16[80,512]{1,0:T(8,128)(2,1)S(1)} %get-tuple-element.20.refs_0_, bf16[80,512]{1,0:T(8,128)(2,1)S(1)} %collective-permute-done.7.refs_1_, bf16[80,512]{1,0:T(8,128)(2,1)S(1)} %collective-permute-done.8.refs_2_, bf16[80,512]{1,0:T(8,128)(2,1)S(1)} %collective-permute-done.9.refs_3_, ...), custom_call_target="tpu_custom_call" | custom-call | flops 5368709120 | bytes 41943040 | tf_op jit(solution)/shard_map/stack_products/pallas_call | solution.py:484
  (15 shorter events, 1.3 us)
Async XLA Ops:
  11.5 7.0 %copy-start = (f32[88,1024]{1,0:T(8,128)S(1)}, f32[88,1024]{1,0:T(8,128)}, u32[]{:S(2)}) copy-start(f32[88,1024]{1,0:T(8,128)} %get-tuple-element.17.own_ref) | copy-start | bytes 1081348
  11.5 7.0 %collective-permute-start = (bf16[96,1024]{1,0:T(8,128)(2,1)}, bf16[96,1024]{1,0:T(8,128)(2,1)S(1)}, u32[]{:S(2)}, u32[]{:S(2)}) collective-permute-start(bf16[96,1024]{1,0:T(8,128)(2,1)} %get-tuple-element.19), channel_id=1, source_target_pairs={{1,0},{2,1},{3,2},{4,3},{5,4},{6,5},{7,6},{9,8},{10,9},{11,10},{12... | collective-permute-start | bytes 589832 | tf_op jit(solution)/shard_map/ppermute | solution.py:543
  12.9 1.0 %copy-start.1 = (f32[4,80,256]{2,1,0:T(8,128)S(1)}, f32[4,80,256]{2,1,0:T(8,128)}, u32[]{:S(2)}) copy-start(f32[4,80,256]{2,1,0:T(8,128)} %get-tuple-element.18.state_in) | copy-start | bytes 983044
  18.7 12.4 %collective-permute-start.5 = (bf16[2,80,512]{2,1,0:T(8,128)(2,1)S(1)}, bf16[2,80,512]{2,1,0:T(8,128)(2,1)S(1)}, u32[]{:S(2)}, u32[]{:S(2)}) collective-permute-start(bf16[2,80,512]{2,1,0:T(8,128)(2,1)S(1)} %whiten.1.refs_0_), channel_id=1, source_target_pairs={{0,16},{8,24},{16,0},{24,8},{1,17},{9,25},{17,1},{25,9},{2,18},{10... | collective-permute-start | bytes 491528 | tf_op jit(solution)/shard_map/ppermute | solution.py:560
  22.8 9.6 %collective-permute-start.4 = (bf16[2,80,512]{2,1,0:T(8,128)(2,1)S(1)}, bf16[2,80,512]{2,1,0:T(8,128)(2,1)S(1)}, u32[]{:S(2)}, u32[]{:S(2)}) collective-permute-start(bf16[2,80,512]{2,1,0:T(8,128)(2,1)S(1)} %whiten.1.refs_0_), channel_id=1, source_target_pairs={{0,8},{8,0},{16,24},{24,16},{1,9},{9,1},{17,25},{25,17},{2,10},{10... | collective-permute-start | bytes 491528 | tf_op jit(solution)/shard_map/ppermute | solution.py:560
  24.4 8.4 %collective-permute-start.3 = (bf16[2,80,512]{2,1,0:T(8,128)(2,1)S(1)}, bf16[2,80,512]{2,1,0:T(8,128)(2,1)S(1)}, u32[]{:S(2)}, u32[]{:S(2)}) collective-permute-start(bf16[2,80,512]{2,1,0:T(8,128)(2,1)S(1)} %whiten.1.refs_0_), channel_id=1, source_target_pairs={{0,6},{1,7},{2,4},{3,5},{4,2},{5,3},{6,0},{7,1},{8,14},{9,15},{10,... | collective-permute-start | bytes 491528 | tf_op jit(solution)/shard_map/ppermute | solution.py:560
  27.8 7.7 %collective-permute-start.2 = (bf16[2,80,512]{2,1,0:T(8,128)(2,1)S(1)}, bf16[2,80,512]{2,1,0:T(8,128)(2,1)S(1)}, u32[]{:S(2)}, u32[]{:S(2)}) collective-permute-start(bf16[2,80,512]{2,1,0:T(8,128)(2,1)S(1)} %whiten.1.refs_0_), channel_id=1, source_target_pairs={{0,4},{1,5},{2,6},{3,7},{4,0},{5,1},{6,2},{7,3},{8,12},{9,13},{10,... | collective-permute-start | bytes 491528 | tf_op jit(solution)/shard_map/ppermute | solution.py:560
  28.3 7.5 %collective-permute-start.1 = (bf16[2,80,512]{2,1,0:T(8,128)(2,1)S(1)}, bf16[2,80,512]{2,1,0:T(8,128)(2,1)S(1)}, u32[]{:S(2)}, u32[]{:S(2)}) collective-permute-start(bf16[2,80,512]{2,1,0:T(8,128)(2,1)S(1)} %whiten.1.refs_0_), channel_id=1, source_target_pairs={{0,2},{1,3},{2,0},{3,1},{4,6},{5,7},{6,4},{7,5},{8,10},{9,11},{10,... | collective-permute-start | bytes 491528 | tf_op jit(solution)/shard_map/ppermute | solution.py:560
  31.1 6.5 %collective-permute-start.6 = (bf16[2,80,512]{2,1,0:T(8,128)(2,1)S(1)}, bf16[2,80,512]{2,1,0:T(8,128)(2,1)S(1)}, u32[]{:S(2)}, u32[]{:S(2)}) collective-permute-start(bf16[2,80,512]{2,1,0:T(8,128)(2,1)S(1)} %collective-permute-done.5.refs_5_), channel_id=1, source_target_pairs={{0,8},{8,0},{16,24},{24,16},{1,9},{9,1},{17,25},{25,17},{2,10},{10... | collective-permute-start | bytes 491528 | tf_op jit(solution)/shard_map/ppermute | solution.py:560
  37.8 12.0 %collective-permute-start.14 = (bf16[4,2,80,512]{3,2,1,0:T(8,128)(2,1)S(1)}, bf16[4,2,80,512]{3,2,1,0:T(8,128)(2,1)S(1)}, u32[]{:S(2)}, u32[]{:S(2)}) collective-permute-start(bf16[4,2,80,512]{3,2,1,0:T(8,128)(2,1)S(1)} %get-tuple-element.28.refs_8_), channel_id=1, source_target_pairs={{0,1},{1,0},{2,3},{3,2},{4,5},{5,4},{6,7},{7,6},{8,9},{9,8},{10,11... | collective-permute-start | bytes 1966088 | tf_op jit(solution)/shard_map/ppermute | solution.py:560
  37.9 5.0 %collective-permute-start.7 = (bf16[80,512]{1,0:T(8,128)(2,1)S(1)}, bf16[80,512]{1,0:T(8,128)(2,1)S(1)}, u32[]{:S(2)}, u32[]{:S(2)}) collective-permute-start(bf16[80,512]{1,0:T(8,128)(2,1)S(1)} %get-tuple-element.21), channel_id=1, source_target_pairs={{0,2},{1,3},{2,0},{3,1},{4,6},{5,7},{6,4},{7,5},{8,10},{9,11},{10,... | collective-permute-start | bytes 245768 | tf_op jit(solution)/shard_map/ppermute | solution.py:560
  39.8 4.5 %collective-permute-start.8 = (bf16[80,512]{1,0:T(8,128)(2,1)S(1)}, bf16[80,512]{1,0:T(8,128)(2,1)S(1)}, u32[]{:S(2)}, u32[]{:S(2)}) collective-permute-start(bf16[80,512]{1,0:T(8,128)(2,1)S(1)} %get-tuple-element.22), channel_id=1, source_target_pairs={{0,4},{1,5},{2,6},{3,7},{4,0},{5,1},{6,2},{7,3},{8,12},{9,13},{10,... | collective-permute-start | bytes 245768 | tf_op jit(solution)/shard_map/ppermute | solution.py:560
  41.0 6.2 %collective-permute-start.9 = (bf16[80,512]{1,0:T(8,128)(2,1)S(1)}, bf16[80,512]{1,0:T(8,128)(2,1)S(1)}, u32[]{:S(2)}, u32[]{:S(2)}) collective-permute-start(bf16[80,512]{1,0:T(8,128)(2,1)S(1)} %get-tuple-element.23), channel_id=1, source_target_pairs={{0,6},{1,7},{2,4},{3,5},{4,2},{5,3},{6,0},{7,1},{8,14},{9,15},{10,... | collective-permute-start | bytes 245768 | tf_op jit(solution)/shard_map/ppermute | solution.py:560
  41.4 5.8 %collective-permute-start.10 = (bf16[80,512]{1,0:T(8,128)(2,1)S(1)}, bf16[80,512]{1,0:T(8,128)(2,1)S(1)}, u32[]{:S(2)}, u32[]{:S(2)}) collective-permute-start(bf16[80,512]{1,0:T(8,128)(2,1)S(1)} %get-tuple-element.24), channel_id=1, source_target_pairs={{0,3},{1,2},{2,1},{3,0},{4,7},{5,6},{6,5},{7,4},{8,11},{9,10},{10,... | collective-permute-start | bytes 245768 | tf_op jit(solution)/shard_map/ppermute | solution.py:560
  42.8 5.1 %collective-permute-start.11 = (bf16[80,512]{1,0:T(8,128)(2,1)S(1)}, bf16[80,512]{1,0:T(8,128)(2,1)S(1)}, u32[]{:S(2)}, u32[]{:S(2)}) collective-permute-start(bf16[80,512]{1,0:T(8,128)(2,1)S(1)} %get-tuple-element.25), channel_id=1, source_target_pairs={{0,5},{1,4},{2,7},{3,6},{4,1},{5,0},{6,3},{7,2},{8,13},{9,12},{10,... | collective-permute-start | bytes 245768 | tf_op jit(solution)/shard_map/ppermute | solution.py:560
  44.3 5.5 %collective-permute-start.12 = (bf16[80,512]{1,0:T(8,128)(2,1)S(1)}, bf16[80,512]{1,0:T(8,128)(2,1)S(1)}, u32[]{:S(2)}, u32[]{:S(2)}) collective-permute-start(bf16[80,512]{1,0:T(8,128)(2,1)S(1)} %get-tuple-element.26), channel_id=1, source_target_pairs={{0,7},{1,6},{2,5},{3,4},{4,3},{5,2},{6,1},{7,0},{8,15},{9,14},{10,... | collective-permute-start | bytes 245768 | tf_op jit(solution)/shard_map/ppermute | solution.py:560
  47.2 2.6 %collective-permute-start.13 = (bf16[80,512]{1,0:T(8,128)(2,1)S(1)}, bf16[80,512]{1,0:T(8,128)(2,1)S(1)}, u32[]{:S(2)}, u32[]{:S(2)}) collective-permute-start(bf16[80,512]{1,0:T(8,128)(2,1)S(1)} %get-tuple-element.27), channel_id=1, source_target_pairs={{0,1},{1,0},{2,3},{3,2},{4,5},{5,4},{6,7},{7,6},{8,9},{9,8},{10,11... | collective-permute-start | bytes 245768 | tf_op jit(solution)/shard_map/ppermute | solution.py:560

commit v13 on v12

--- a/solution.py
+++ b/solution.py
@@ -434,18 +434,21 @@
     head, tail = cols[:, :ROW_TILE // 2], cols[:, ROW_TILE // 2:]
     straight = cols.reshape(depth, width)
     turned = jnp.concatenate([-tail, head], axis=1).reshape(depth, width)
-    lhs[:width, :] = straight.T.astype(BF16)
-    lhs[width:, :] = turned.T.astype(BF16)
+    bin_of = lax.broadcasted_iota(jnp.int32, (1, depth), 1) % per_group
+    for part, block in enumerate((straight, turned)):
+        turned_over = block.T
+        for b in range(per_group):
+            kept = jnp.where(bin_of == b, turned_over, 0.0).astype(BF16)
+            lhs[b, part * width:(part + 1) * width, :] = kept
     for away in range(devices):
         to = slice(away * ROW_TILE, (away + 1) * ROW_TILE)
         for h in range(halves):
-            held[to, h * span:(h + 1) * span] = row_refs[away % 2][away // 2, h].astype(F32)
+            held[to, h * span:(h + 1) * span] = row_refs[away % 2][away // 2, h]
 
     def out_copy(slot, part, bin_index):
         to = out_hbm.at[part, bin_index]
         return pltpu.make_async_copy(made.at[slot], to, sems.at[slot])
 
-    which = lax.broadcasted_iota(jnp.int32, (depth, 1), 0) % per_group
     for b in range(per_group):
         for part in range(2):
             slot = 2 * b + part
@@ -456,14 +459,11 @@
 
         for n in range(0, channels, DEPTH):
             at = slice(n, min(n + DEPTH, channels))
-            rhs = jnp.where(which == b, held[:, at], 0.0).astype(BF16)
+            product = jnp.dot(lhs[b], held[:, at], preferred_element_type=F32)
+            if not exact:
+                product = product * scale
             for part in range(2):
-                product = jnp.dot(
-                    lhs[part * width:(part + 1) * width, :], rhs, preferred_element_type=F32
-                )
-                if not exact:
-                    product = product * scale
-                made[2 * b + part, :, at] = product.astype(BF16)
+                made[2 * b + part, :, at] = product[part * width:(part + 1) * width].astype(BF16)
         for part in range(2):
             out_copy(2 * b + part, part, step * per_group + b).start()
 
@@ -489,8 +489,8 @@
         + [pl.BlockSpec((chips, halves, ROW_TILE, span), lambda i: (0, 0, i, 0))] * 2,
         out_specs=pl.BlockSpec(memory_space=pltpu.HBM),
         scratch_shapes=[
-            pltpu.VMEM((2 * width, devices * ROW_TILE), BF16),
-            pltpu.VMEM((devices * ROW_TILE, channels), F32),
+            pltpu.VMEM((per_group, 2 * width, devices * ROW_TILE), BF16),
+            pltpu.VMEM((devices * ROW_TILE, channels), BF16),
             pltpu.VMEM((2 * per_group, width, channels), BF16),
             pltpu.SemaphoreType.DMA((2 * per_group,)),
         ],
@@ -544,7 +544,7 @@
 
 
 def partners(count):
-    return [*range(2, count, 2), *range(3, count, 2), 1]
+    return sorted(range(1, count), key=lambda away: (-bin(away >> 1).count("1"), away % 2, away))
 
 
 def chan_blocks_of(block):

time: 66.4 us -> 67.2 us (1.012)
  waiting for transfers between devices: 11.4 us -> 12.1 us
    ppermute x14, waiting for transfers between devices: 11.4 us -> 12.1 us  [from_partner(): lax.ppermute(block, axis, [(i, i ^ away) for i in range(lax.axis_size(axi...]
where the time goes in v13:
time: 67.2 us; the launch traced here: 66.9 us
  Pallas kernels  33 us (49%)
  starting transfers between devices  20.7 us (31%)
  waiting for transfers between devices  12.1 us (18%)
  local copies, waits for them, and re-layouts  0.97 us (1%)
    ppermute x14, starting transfers between devices, from_partner(): lax.ppermute(block, axis, [(i, i ^ away) for i in range(lax.axis_size(axi...  19.3 us
    pallas_call x1, Pallas kernels, stacks_of(): pl.pallas_call(functools.partial(stack_kernel, windows, scale, devices),...  16.6 us
    ppermute x14, waiting for transfers between devices, from_partner(): lax.ppermute(block, axis, [(i, i ^ away) for i in range(lax.axis_size(axi...  12.1 us
    pallas_call x1, Pallas kernels, spectra_of(): pl.pallas_call(functools.partial(spectra_kernel, bins, windows, block_len...  11.4 us
    pallas_call x1, Pallas kernels, rest_of(): pl.pallas_call(functools.partial(rest_kernel, bins, windows, block_len, l...  4.55 us
    ppermute x1, starting transfers between devices, moved(): lax.ppermute(block, axis, [(i + far, i) for i in range(count) if 0 <= i +...  1.42 us
  transfers between devices with their start and end apart: 15, of which 10 were waited for; matrix products, arithmetic and copies ran while one was open for 0% of the time, Pallas kernels for 7%

profile of v13, /device:TPU:0, one launch (start us, length us, event | category | flops | bytes accessed | tf_op | source)
XLA Modules:
  0.0 66.9 jit_solution(3777587009928773938)
XLA Ops:
  0.0 11.4 %band_spectra.1 = (f32[88,1024]{1,0:T(8,128)}, bf16[96,1024]{1,0:T(8,128)(2,1)}, f32[4,80,256]{2,1,0:T(8,128)}) custom-call(s32[16]{0:T(128)} %offsets_hbm.1, s32[20]{0:T(128)} %bins_hbm.1, s32[1,1024]{1,0:T(1,128)} %bitcast.5, bf16[15000,1024]{1,0:T(8,128)(2,1)} %bitcast.2), custom_call_target="tpu_custom_call" | custom-call | flops 3690987520 | bytes 23068672 | tf_op jit(solution)/shard_map/band_spectra/pallas_call | solution.py:314
  11.5 1.4 %collective-permute-start = (bf16[96,1024]{1,0:T(8,128)(2,1)}, bf16[96,1024]{1,0:T(8,128)(2,1)S(1)}, u32[]{:S(2)}, u32[]{:S(2)}) collective-permute-start(bf16[96,1024]{1,0:T(8,128)(2,1)} %get-tuple-element.19), channel_id=1, source_target_pairs={{1,0},{2,1},{3,2},{4,3},{5,4},{6,5},{7,6},{9,8},{10,9},{11,10},{12... | collective-permute-start | bytes 589832 | tf_op jit(solution)/shard_map/ppermute | solution.py:543
  12.9 1.0 %copy-done.1 = f32[4,80,256]{2,1,0:T(8,128)S(1)} copy-done((f32[4,80,256]{2,1,0:T(8,128)S(1)}, f32[4,80,256]{2,1,0:T(8,128)}, u32[]{:S(2)}) %copy-start.1) | copy-done | bytes 327704
  13.9 4.6 %band_spectra_rest.1.rest_ref = f32[88,1024]{1,0:T(8,128)S(1)} custom-call(f32[4,80,256]{2,1,0:T(8,128)S(1)} %copy-done.1, bf16[15000,1024]{1,0:T(8,128)(2,1)} %bitcast.3, bf16[15000,1024]{1,0:T(8,128)(2,1)} %bitcast.4), custom_call_target="tpu_custom_call" | custom-call | flops 612106240 | bytes 7651328 | tf_op jit(solution)/shard_map/band_spectra_rest/pallas_call | solution.py:355
  18.7 4.1 %collective-permute-start.5 = (bf16[2,80,512]{2,1,0:T(8,128)(2,1)S(1)}, bf16[2,80,512]{2,1,0:T(8,128)(2,1)S(1)}, u32[]{:S(2)}, u32[]{:S(2)}) collective-permute-start(bf16[2,80,512]{2,1,0:T(8,128)(2,1)S(1)} %whiten.1.refs_0_), channel_id=1, source_target_pairs={{0,16},{8,24},{16,0},{24,8},{1,17},{9,25},{17,1},{25,9},{2,18},{10... | collective-permute-start | bytes 491528 | tf_op jit(solution)/shard_map/ppermute | solution.py:560
  22.8 1.6 %collective-permute-start.4 = (bf16[2,80,512]{2,1,0:T(8,128)(2,1)S(1)}, bf16[2,80,512]{2,1,0:T(8,128)(2,1)S(1)}, u32[]{:S(2)}, u32[]{:S(2)}) collective-permute-start(bf16[2,80,512]{2,1,0:T(8,128)(2,1)S(1)} %whiten.1.refs_0_), channel_id=1, source_target_pairs={{0,8},{8,0},{16,24},{24,16},{1,9},{9,1},{17,25},{25,17},{2,10},{10... | collective-permute-start | bytes 491528 | tf_op jit(solution)/shard_map/ppermute | solution.py:560
  24.4 3.3 %collective-permute-start.3 = (bf16[2,80,512]{2,1,0:T(8,128)(2,1)S(1)}, bf16[2,80,512]{2,1,0:T(8,128)(2,1)S(1)}, u32[]{:S(2)}, u32[]{:S(2)}) collective-permute-start(bf16[2,80,512]{2,1,0:T(8,128)(2,1)S(1)} %whiten.1.refs_0_), channel_id=1, source_target_pairs={{0,6},{1,7},{2,4},{3,5},{4,2},{5,3},{6,0},{7,1},{8,14},{9,15},{10,... | collective-permute-start | bytes 491528 | tf_op jit(solution)/shard_map/ppermute | solution.py:560
  27.7 0.5 collective-permute-start.2
  28.1 0.7 %collective-permute-start.1 = (bf16[2,80,512]{2,1,0:T(8,128)(2,1)S(1)}, bf16[2,80,512]{2,1,0:T(8,128)(2,1)S(1)}, u32[]{:S(2)}, u32[]{:S(2)}) collective-permute-start(bf16[2,80,512]{2,1,0:T(8,128)(2,1)S(1)} %whiten.1.refs_0_), channel_id=1, source_target_pairs={{0,2},{1,3},{2,0},{3,1},{4,6},{5,7},{6,4},{7,5},{8,10},{9,11},{10,... | collective-permute-start | bytes 491528 | tf_op jit(solution)/shard_map/ppermute | solution.py:560
  28.9 2.3 %collective-permute-done.5.refs_5_ = bf16[2,80,512]{2,1,0:T(8,128)(2,1)S(1)} collective-permute-done((bf16[2,80,512]{2,1,0:T(8,128)(2,1)S(1)}, bf16[2,80,512]{2,1,0:T(8,128)(2,1)S(1)}, u32[]{:S(2)}, u32[]{:S(2)}) %collective-permute-start.5) | collective-permute-done | bytes 163872 | tf_op jit(solution)/shard_map/ppermute | solution.py:560
  31.1 1.2 %collective-permute-start.6 = (bf16[2,80,512]{2,1,0:T(8,128)(2,1)S(1)}, bf16[2,80,512]{2,1,0:T(8,128)(2,1)S(1)}, u32[]{:S(2)}, u32[]{:S(2)}) collective-permute-start(bf16[2,80,512]{2,1,0:T(8,128)(2,1)S(1)} %collective-permute-done.5.refs_5_), channel_id=1, source_target_pairs={{0,8},{8,0},{16,24},{24,16},{1,9},{9,1},{17,25},{25,17},{2,10},{10... | collective-permute-start | bytes 491528 | tf_op jit(solution)/shard_map/ppermute | solution.py:560
  32.7 2.8 %collective-permute-done.2.refs_2_ = bf16[2,80,512]{2,1,0:T(8,128)(2,1)S(1)} collective-permute-done((bf16[2,80,512]{2,1,0:T(8,128)(2,1)S(1)}, bf16[2,80,512]{2,1,0:T(8,128)(2,1)S(1)}, u32[]{:S(2)}, u32[]{:S(2)}) %collective-permute-start.2) | collective-permute-done | bytes 163872 | tf_op jit(solution)/shard_map/ppermute | solution.py:560
  35.5 0.4 collective-permute-done.1.refs_1_
  35.9 1.8 %collective-permute-done.6.refs_6_ = bf16[2,80,512]{2,1,0:T(8,128)(2,1)S(1)} collective-permute-done((bf16[2,80,512]{2,1,0:T(8,128)(2,1)S(1)}, bf16[2,80,512]{2,1,0:T(8,128)(2,1)S(1)}, u32[]{:S(2)}, u32[]{:S(2)}) %collective-permute-start.6) | collective-permute-done | bytes 163872 | tf_op jit(solution)/shard_map/ppermute | solution.py:560
  37.9 2.8 %collective-permute-start.7 = (bf16[80,512]{1,0:T(8,128)(2,1)S(1)}, bf16[80,512]{1,0:T(8,128)(2,1)S(1)}, u32[]{:S(2)}, u32[]{:S(2)}) collective-permute-start(bf16[80,512]{1,0:T(8,128)(2,1)S(1)} %get-tuple-element.21), channel_id=1, source_target_pairs={{0,6},{1,7},{2,4},{3,5},{4,2},{5,3},{6,0},{7,1},{8,14},{9,15},{10,... | collective-permute-start | bytes 245768 | tf_op jit(solution)/shard_map/ppermute | solution.py:560
  40.8 1.6 %collective-permute-start.9 = (bf16[80,512]{1,0:T(8,128)(2,1)S(1)}, bf16[80,512]{1,0:T(8,128)(2,1)S(1)}, u32[]{:S(2)}, u32[]{:S(2)}) collective-permute-start(bf16[80,512]{1,0:T(8,128)(2,1)S(1)} %get-tuple-element.23), channel_id=1, source_target_pairs={{0,2},{1,3},{2,0},{3,1},{4,6},{5,7},{6,4},{7,5},{8,10},{9,11},{10,... | collective-permute-start | bytes 245768 | tf_op jit(solution)/shard_map/ppermute | solution.py:560
  42.4 1.6 %collective-permute-start.10 = (bf16[80,512]{1,0:T(8,128)(2,1)S(1)}, bf16[80,512]{1,0:T(8,128)(2,1)S(1)}, u32[]{:S(2)}, u32[]{:S(2)}) collective-permute-start(bf16[80,512]{1,0:T(8,128)(2,1)S(1)} %get-tuple-element.24), channel_id=1, source_target_pairs={{0,4},{1,5},{2,6},{3,7},{4,0},{5,1},{6,2},{7,3},{8,12},{9,13},{10,... | collective-permute-start | bytes 245768 | tf_op jit(solution)/shard_map/ppermute | solution.py:560
  43.9 0.7 %collective-permute-start.11 = (bf16[80,512]{1,0:T(8,128)(2,1)S(1)}, bf16[80,512]{1,0:T(8,128)(2,1)S(1)}, u32[]{:S(2)}, u32[]{:S(2)}) collective-permute-start(bf16[80,512]{1,0:T(8,128)(2,1)S(1)} %get-tuple-element.25), channel_id=1, source_target_pairs={{0,3},{1,2},{2,1},{3,0},{4,7},{5,6},{6,5},{7,4},{8,11},{9,10},{10,... | collective-permute-start | bytes 245768 | tf_op jit(solution)/shard_map/ppermute | solution.py:560
  44.6 1.5 %collective-permute-done.8.refs_2_ = bf16[80,512]{1,0:T(8,128)(2,1)S(1)} collective-permute-done((bf16[80,512]{1,0:T(8,128)(2,1)S(1)}, bf16[80,512]{1,0:T(8,128)(2,1)S(1)}, u32[]{:S(2)}, u32[]{:S(2)}) %collective-permute-start.8) | collective-permute-done | bytes 81952 | tf_op jit(solution)/shard_map/ppermute | solution.py:560
  46.1 1.1 %collective-permute-start.12 = (bf16[80,512]{1,0:T(8,128)(2,1)S(1)}, bf16[80,512]{1,0:T(8,128)(2,1)S(1)}, u32[]{:S(2)}, u32[]{:S(2)}) collective-permute-start(bf16[80,512]{1,0:T(8,128)(2,1)S(1)} %get-tuple-element.26), channel_id=1, source_target_pairs={{0,5},{1,4},{2,7},{3,6},{4,1},{5,0},{6,3},{7,2},{8,13},{9,12},{10,... | collective-permute-start | bytes 245768 | tf_op jit(solution)/shard_map/ppermute | solution.py:560
  47.3 0.7 %collective-permute-done.10.refs_4_ = bf16[80,512]{1,0:T(8,128)(2,1)S(1)} collective-permute-done((bf16[80,512]{1,0:T(8,128)(2,1)S(1)}, bf16[80,512]{1,0:T(8,128)(2,1)S(1)}, u32[]{:S(2)}, u32[]{:S(2)}) %collective-permute-start.10) | collective-permute-done | bytes 81952 | tf_op jit(solution)/shard_map/ppermute | solution.py:560
  48.1 0.6 collective-permute-done.11.refs_5_
  48.7 1.6 %collective-permute-done.12.refs_6_ = bf16[80,512]{1,0:T(8,128)(2,1)S(1)} collective-permute-done((bf16[80,512]{1,0:T(8,128)(2,1)S(1)}, bf16[80,512]{1,0:T(8,128)(2,1)S(1)}, u32[]{:S(2)}, u32[]{:S(2)}) %collective-permute-start.12) | collective-permute-done | bytes 81952 | tf_op jit(solution)/shard_map/ppermute | solution.py:560
  50.3 16.6 %stack_products.1 = bf16[2,20,512,1024]{3,2,1,0:T(8,128)(2,1)} custom-call(bf16[80,512]{1,0:T(8,128)(2,1)S(1)} %get-tuple-element.20.refs_0_, bf16[80,512]{1,0:T(8,128)(2,1)S(1)} %collective-permute-done.7.refs_1_, bf16[80,512]{1,0:T(8,128)(2,1)S(1)} %collective-permute-done.8.refs_2_, bf16[80,512]{1,0:T(8,128)(2,1)S(1)} %collective-permute-done.9.refs_3_, ...), custom_call_target="tpu_custom_call" | custom-call | flops 5368709120 | bytes 41943040 | tf_op jit(solution)/shard_map/stack_products/pallas_call | solution.py:484
  (15 shorter events, 1.0 us)
Async XLA Ops:
  11.5 7.0 %copy-start = (f32[88,1024]{1,0:T(8,128)S(1)}, f32[88,1024]{1,0:T(8,128)}, u32[]{:S(2)}) copy-start(f32[88,1024]{1,0:T(8,128)} %get-tuple-element.17.own_ref) | copy-start | bytes 1081348
  11.5 7.0 %collective-permute-start = (bf16[96,1024]{1,0:T(8,128)(2,1)}, bf16[96,1024]{1,0:T(8,128)(2,1)S(1)}, u32[]{:S(2)}, u32[]{:S(2)}) collective-permute-start(bf16[96,1024]{1,0:T(8,128)(2,1)} %get-tuple-element.19), channel_id=1, source_target_pairs={{1,0},{2,1},{3,2},{4,3},{5,4},{6,5},{7,6},{9,8},{10,9},{11,10},{12... | collective-permute-start | bytes 589832 | tf_op jit(solution)/shard_map/ppermute | solution.py:543
  12.9 1.0 %copy-start.1 = (f32[4,80,256]{2,1,0:T(8,128)S(1)}, f32[4,80,256]{2,1,0:T(8,128)}, u32[]{:S(2)}) copy-start(f32[4,80,256]{2,1,0:T(8,128)} %get-tuple-element.18.state_in) | copy-start | bytes 983044
  18.7 12.4 %collective-permute-start.5 = (bf16[2,80,512]{2,1,0:T(8,128)(2,1)S(1)}, bf16[2,80,512]{2,1,0:T(8,128)(2,1)S(1)}, u32[]{:S(2)}, u32[]{:S(2)}) collective-permute-start(bf16[2,80,512]{2,1,0:T(8,128)(2,1)S(1)} %whiten.1.refs_0_), channel_id=1, source_target_pairs={{0,16},{8,24},{16,0},{24,8},{1,17},{9,25},{17,1},{25,9},{2,18},{10... | collective-permute-start | bytes 491528 | tf_op jit(solution)/shard_map/ppermute | solution.py:560
  22.8 9.6 %collective-permute-start.4 = (bf16[2,80,512]{2,1,0:T(8,128)(2,1)S(1)}, bf16[2,80,512]{2,1,0:T(8,128)(2,1)S(1)}, u32[]{:S(2)}, u32[]{:S(2)}) collective-permute-start(bf16[2,80,512]{2,1,0:T(8,128)(2,1)S(1)} %whiten.1.refs_0_), channel_id=1, source_target_pairs={{0,8},{8,0},{16,24},{24,16},{1,9},{9,1},{17,25},{25,17},{2,10},{10... | collective-permute-start | bytes 491528 | tf_op jit(solution)/shard_map/ppermute | solution.py:560
  24.4 8.3 %collective-permute-start.3 = (bf16[2,80,512]{2,1,0:T(8,128)(2,1)S(1)}, bf16[2,80,512]{2,1,0:T(8,128)(2,1)S(1)}, u32[]{:S(2)}, u32[]{:S(2)}) collective-permute-start(bf16[2,80,512]{2,1,0:T(8,128)(2,1)S(1)} %whiten.1.refs_0_), channel_id=1, source_target_pairs={{0,6},{1,7},{2,4},{3,5},{4,2},{5,3},{6,0},{7,1},{8,14},{9,15},{10,... | collective-permute-start | bytes 491528 | tf_op jit(solution)/shard_map/ppermute | solution.py:560
  27.7 7.8 %collective-permute-start.2 = (bf16[2,80,512]{2,1,0:T(8,128)(2,1)S(1)}, bf16[2,80,512]{2,1,0:T(8,128)(2,1)S(1)}, u32[]{:S(2)}, u32[]{:S(2)}) collective-permute-start(bf16[2,80,512]{2,1,0:T(8,128)(2,1)S(1)} %whiten.1.refs_0_), channel_id=1, source_target_pairs={{0,4},{1,5},{2,6},{3,7},{4,0},{5,1},{6,2},{7,3},{8,12},{9,13},{10,... | collective-permute-start | bytes 491528 | tf_op jit(solution)/shard_map/ppermute | solution.py:560
  28.1 7.7 %collective-permute-start.1 = (bf16[2,80,512]{2,1,0:T(8,128)(2,1)S(1)}, bf16[2,80,512]{2,1,0:T(8,128)(2,1)S(1)}, u32[]{:S(2)}, u32[]{:S(2)}) collective-permute-start(bf16[2,80,512]{2,1,0:T(8,128)(2,1)S(1)} %whiten.1.refs_0_), channel_id=1, source_target_pairs={{0,2},{1,3},{2,0},{3,1},{4,6},{5,7},{6,4},{7,5},{8,10},{9,11},{10,... | collective-permute-start | bytes 491528 | tf_op jit(solution)/shard_map/ppermute | solution.py:560
  31.1 6.5 %collective-permute-start.6 = (bf16[2,80,512]{2,1,0:T(8,128)(2,1)S(1)}, bf16[2,80,512]{2,1,0:T(8,128)(2,1)S(1)}, u32[]{:S(2)}, u32[]{:S(2)}) collective-permute-start(bf16[2,80,512]{2,1,0:T(8,128)(2,1)S(1)} %collective-permute-done.5.refs_5_), channel_id=1, source_target_pairs={{0,8},{8,0},{16,24},{24,16},{1,9},{9,1},{17,25},{25,17},{2,10},{10... | collective-permute-start | bytes 491528 | tf_op jit(solution)/shard_map/ppermute | solution.py:560
  37.8 12.5 %collective-permute-start.14 = (bf16[4,2,80,512]{3,2,1,0:T(8,128)(2,1)S(1)}, bf16[4,2,80,512]{3,2,1,0:T(8,128)(2,1)S(1)}, u32[]{:S(2)}, u32[]{:S(2)}) collective-permute-start(bf16[4,2,80,512]{3,2,1,0:T(8,128)(2,1)S(1)} %get-tuple-element.28.refs_8_), channel_id=1, source_target_pairs={{0,1},{1,0},{2,3},{3,2},{4,5},{5,4},{6,7},{7,6},{8,9},{9,8},{10,11... | collective-permute-start | bytes 1966088 | tf_op jit(solution)/shard_map/ppermute | solution.py:560
  37.9 6.1 %collective-permute-start.7 = (bf16[80,512]{1,0:T(8,128)(2,1)S(1)}, bf16[80,512]{1,0:T(8,128)(2,1)S(1)}, u32[]{:S(2)}, u32[]{:S(2)}) collective-permute-start(bf16[80,512]{1,0:T(8,128)(2,1)S(1)} %get-tuple-element.21), channel_id=1, source_target_pairs={{0,6},{1,7},{2,4},{3,5},{4,2},{5,3},{6,0},{7,1},{8,14},{9,15},{10,... | collective-permute-start | bytes 245768 | tf_op jit(solution)/shard_map/ppermute | solution.py:560
  40.7 5.4 %collective-permute-start.8 = (bf16[80,512]{1,0:T(8,128)(2,1)S(1)}, bf16[80,512]{1,0:T(8,128)(2,1)S(1)}, u32[]{:S(2)}, u32[]{:S(2)}) collective-permute-start(bf16[80,512]{1,0:T(8,128)(2,1)S(1)} %get-tuple-element.22), channel_id=1, source_target_pairs={{0,7},{1,6},{2,5},{3,4},{4,3},{5,2},{6,1},{7,0},{8,15},{9,14},{10,... | collective-permute-start | bytes 245768 | tf_op jit(solution)/shard_map/ppermute | solution.py:560
  40.8 6.6 %collective-permute-start.9 = (bf16[80,512]{1,0:T(8,128)(2,1)S(1)}, bf16[80,512]{1,0:T(8,128)(2,1)S(1)}, u32[]{:S(2)}, u32[]{:S(2)}) collective-permute-start(bf16[80,512]{1,0:T(8,128)(2,1)S(1)} %get-tuple-element.23), channel_id=1, source_target_pairs={{0,2},{1,3},{2,0},{3,1},{4,6},{5,7},{6,4},{7,5},{8,10},{9,11},{10,... | collective-permute-start | bytes 245768 | tf_op jit(solution)/shard_map/ppermute | solution.py:560
  42.4 5.7 %collective-permute-start.10 = (bf16[80,512]{1,0:T(8,128)(2,1)S(1)}, bf16[80,512]{1,0:T(8,128)(2,1)S(1)}, u32[]{:S(2)}, u32[]{:S(2)}) collective-permute-start(bf16[80,512]{1,0:T(8,128)(2,1)S(1)} %get-tuple-element.24), channel_id=1, source_target_pairs={{0,4},{1,5},{2,6},{3,7},{4,0},{5,1},{6,2},{7,3},{8,12},{9,13},{10,... | collective-permute-start | bytes 245768 | tf_op jit(solution)/shard_map/ppermute | solution.py:560
  43.9 4.8 %collective-permute-start.11 = (bf16[80,512]{1,0:T(8,128)(2,1)S(1)}, bf16[80,512]{1,0:T(8,128)(2,1)S(1)}, u32[]{:S(2)}, u32[]{:S(2)}) collective-permute-start(bf16[80,512]{1,0:T(8,128)(2,1)S(1)} %get-tuple-element.25), channel_id=1, source_target_pairs={{0,3},{1,2},{2,1},{3,0},{4,7},{5,6},{6,5},{7,4},{8,11},{9,10},{10,... | collective-permute-start | bytes 245768 | tf_op jit(solution)/shard_map/ppermute | solution.py:560
  46.1 4.2 %collective-permute-start.12 = (bf16[80,512]{1,0:T(8,128)(2,1)S(1)}, bf16[80,512]{1,0:T(8,128)(2,1)S(1)}, u32[]{:S(2)}, u32[]{:S(2)}) collective-permute-start(bf16[80,512]{1,0:T(8,128)(2,1)S(1)} %get-tuple-element.26), channel_id=1, source_target_pairs={{0,5},{1,4},{2,7},{3,6},{4,1},{5,0},{6,3},{7,2},{8,13},{9,12},{10,... | collective-permute-start | bytes 245768 | tf_op jit(solution)/shard_map/ppermute | solution.py:560
  47.3 2.9 %collective-permute-start.13 = (bf16[80,512]{1,0:T(8,128)(2,1)S(1)}, bf16[80,512]{1,0:T(8,128)(2,1)S(1)}, u32[]{:S(2)}, u32[]{:S(2)}) collective-permute-start(bf16[80,512]{1,0:T(8,128)(2,1)S(1)} %get-tuple-element.27), channel_id=1, source_target_pairs={{0,1},{1,0},{2,3},{3,2},{4,5},{5,4},{6,7},{7,6},{8,9},{9,8},{10,11... | collective-permute-start | bytes 245768 | tf_op jit(solution)/shard_map/ppermute | solution.py:560

commit v14 on v12

--- a/solution.py
+++ b/solution.py
@@ -417,13 +417,13 @@
 
 
 def stack_kernel(windows, scale, devices, *refs):
-    col_refs, row_refs = refs[:devices], refs[devices:devices + 2]
-    out_hbm, lhs, held, made, sems = refs[devices + 2:]
+    col_refs, row_refs = refs[:devices], refs[devices:2 * devices]
+    out_hbm, lhs, held, made, sems = refs[2 * devices:]
     per_group = ROW_TILE // (2 * windows)
     step = pl.program_id(0)
     width = col_refs[0].shape[1]
     depth = devices * ROW_TILE
-    _, halves, _, span = row_refs[0].shape
+    halves, _, span = row_refs[0].shape
     channels = halves * span
     exact = math.frexp(scale)[0] == 0.5
 
@@ -439,7 +439,7 @@
     for away in range(devices):
         to = slice(away * ROW_TILE, (away + 1) * ROW_TILE)
         for h in range(halves):
-            held[to, h * span:(h + 1) * span] = row_refs[away % 2][away // 2, h].astype(F32)
+            held[to, h * span:(h + 1) * span] = row_refs[away][h].astype(F32)
 
     def out_copy(slot, part, bin_index):
         to = out_hbm.at[part, bin_index]
@@ -476,7 +476,7 @@
 
 def stacks_of(col_blocks, row_blocks, bins, windows):
     devices = len(col_blocks)
-    chips, halves, _, span = row_blocks[0].shape
+    halves, _, span = row_blocks[0].shape
     width = col_blocks[0].shape[1]
     per_group = ROW_TILE // (2 * windows)
     scale = 1.0 / math.sqrt(windows * devices)
@@ -486,7 +486,7 @@
         out_shape=jax.ShapeDtypeStruct((2, bins, width, channels), BF16),
         grid=(bins // per_group,),
         in_specs=[pl.BlockSpec((ROW_TILE, width), lambda i: (i, 0))] * devices
-        + [pl.BlockSpec((chips, halves, ROW_TILE, span), lambda i: (0, 0, i, 0))] * 2,
+        + [pl.BlockSpec((halves, ROW_TILE, span), lambda i: (0, i, 0))] * devices,
         out_specs=pl.BlockSpec(memory_space=pltpu.HBM),
         scratch_shapes=[
             pltpu.VMEM((2 * width, devices * ROW_TILE), BF16),
@@ -506,14 +506,11 @@
     )(*[col_blocks[away] for away in [0, *partners(devices)]], *row_blocks)
 
 
-def pick_kernel(count, chips, *refs):
-    row_refs, chan_refs = refs[:chips], refs[chips:-2 - count]
-    joined_ref, out_refs, held = refs[-2 - count], refs[-1 - count:-1], refs[-1]
+def pick_kernel(count, waits, *refs):
+    white_ref, chan_refs, out_refs, held = refs[0], refs[1 + waits:-1 - count], refs[-1 - count:-1], refs[-1]
     tm, mine = lax.axis_index("tm"), lax.axis_index("chan")
-    halves = row_refs[0].shape[0]
-    for i, ref in enumerate(row_refs):
-        joined_ref[i] = ref[...]
-    for away, ref in enumerate((row_refs[0], *chan_refs)):
+    halves = white_ref.shape[0]
+    for away, ref in enumerate((white_ref, *chan_refs)):
         held[jnp.bitwise_xor(mine, away)] = ref[...]
     for away, out_ref in enumerate(out_refs):
         wanted = jnp.bitwise_xor(tm, away)
@@ -523,19 +520,17 @@
 def picked(row_blocks, chan_blocks, count):
     block = row_blocks[0]
     _, rows, width = block.shape
-    chips = len(row_blocks)
     whole = pl.BlockSpec(memory_space=pltpu.VMEM)
-    joined, *picks = pl.pallas_call(
-        functools.partial(pick_kernel, count, chips),
-        out_shape=[jax.ShapeDtypeStruct((chips, *block.shape), block.dtype)]
-        + [jax.ShapeDtypeStruct((rows, width), block.dtype)] * count,
-        in_specs=[whole] * (chips + len(chan_blocks)),
-        out_specs=[whole] * (1 + count),
+    waits = len(row_blocks) - 1
+    return pl.pallas_call(
+        functools.partial(pick_kernel, count, waits),
+        out_shape=[jax.ShapeDtypeStruct((rows, width), block.dtype)] * count,
+        in_specs=[whole] + [pl.BlockSpec(memory_space=pl.ANY)] * waits + [whole] * len(chan_blocks),
+        out_specs=[whole] * count,
         scratch_shapes=[pltpu.VMEM((1 + len(chan_blocks), *block.shape), block.dtype)],
         compiler_params=pltpu.CompilerParams(vmem_limit_bytes=16 * 2**20),
         name="pick_blocks",
     )(*row_blocks, *chan_blocks)
-    return joined, picks
 
 
 def moved(block, axis, far):
@@ -576,10 +571,13 @@
     white = whiten(own, rest, more, bins, windows, halves)
     row_blocks = [white] + [from_partner(white, "tm", away) for away in range(2, tm_count, 2)]
     chan_blocks = chan_blocks_of(white)
-    joined, col_blocks = picked(row_blocks, chan_blocks, tm_count)
+    col_blocks = list(picked(row_blocks, chan_blocks, tm_count))
     for away in partners(tm_count):
         col_blocks[away] = from_partner(col_blocks[away], "tm", away)
-    return stacks_of(col_blocks, [joined, from_partner(joined, "tm", 1)], bins, windows)
+    all_rows = []
+    for block in row_blocks:
+        all_rows += [block, from_partner(block, "tm", 1)]
+    return stacks_of(col_blocks, all_rows, bins, windows)
 
 
 def solution(mesh):

time: 66.4 us -> 66.4 us (level)
    ppermute x14 -> x17, waiting for transfers between devices: 11.4 us -> 11.8 us  [from_partner(): lax.ppermute(block, axis, [(i, i ^ away) for i in range(lax.axis_size(axi...]
    ppermute x14 -> x17, starting transfers between devices: 19.5 us -> 19.2 us  [from_partner(): lax.ppermute(block, axis, [(i, i ^ away) for i in range(lax.axis_size(axi...]
  transfers between devices with their start and end apart: 15 -> 18, of which waited for: 10 -> 8; matrix products, arithmetic and copies ran while one was open for 0% -> 0% of each run, Pallas kernels for 7% -> 7%
where the time goes in v14:
time: 66.4 us; the launch traced here: 66.1 us
  Pallas kernels  32.6 us (49%)
  starting transfers between devices  20.6 us (31%)
  waiting for transfers between devices  11.8 us (18%)
  local copies, waits for them, and re-layouts  0.97 us (1%)
    ppermute x17, starting transfers between devices, from_partner(): lax.ppermute(block, axis, [(i, i ^ away) for i in range(lax.axis_size(axi...  19.2 us
    pallas_call x1, Pallas kernels, stacks_of(): pl.pallas_call(functools.partial(stack_kernel, windows, scale, devices),...  16.3 us
    ppermute x17, waiting for transfers between devices, from_partner(): lax.ppermute(block, axis, [(i, i ^ away) for i in range(lax.axis_size(axi...  11.8 us
    pallas_call x1, Pallas kernels, spectra_of(): pl.pallas_call(functools.partial(spectra_kernel, bins, windows, block_len...  11.5 us
    pallas_call x1, Pallas kernels, rest_of(): pl.pallas_call(functools.partial(rest_kernel, bins, windows, block_len, l...  4.55 us
    ppermute x1, starting transfers between devices, moved(): lax.ppermute(block, axis, [(i + far, i) for i in range(count) if 0 <= i +...  1.42 us
  transfers between devices with their start and end apart: 18, of which 8 were waited for; matrix products, arithmetic and copies ran while one was open for 0% of the time, Pallas kernels for 7%

profile of v14, /device:TPU:0, one launch (start us, length us, event | category | flops | bytes accessed | tf_op | source)
XLA Modules:
  0.0 66.1 jit_solution(9604277437307724158)
XLA Ops:
  0.0 11.5 %band_spectra.1 = (f32[88,1024]{1,0:T(8,128)}, bf16[96,1024]{1,0:T(8,128)(2,1)}, f32[4,80,256]{2,1,0:T(8,128)}) custom-call(s32[16]{0:T(128)} %offsets_hbm.1, s32[20]{0:T(128)} %bins_hbm.1, s32[1,1024]{1,0:T(1,128)} %bitcast.5, bf16[15000,1024]{1,0:T(8,128)(2,1)} %bitcast.2), custom_call_target="tpu_custom_call" | custom-call | flops 3690987520 | bytes 23068672 | tf_op jit(solution)/shard_map/band_spectra/pallas_call | solution.py:314
  11.5 1.4 %collective-permute-start = (bf16[96,1024]{1,0:T(8,128)(2,1)}, bf16[96,1024]{1,0:T(8,128)(2,1)S(1)}, u32[]{:S(2)}, u32[]{:S(2)}) collective-permute-start(bf16[96,1024]{1,0:T(8,128)(2,1)} %get-tuple-element.18), channel_id=1, source_target_pairs={{1,0},{2,1},{3,2},{4,3},{5,4},{6,5},{7,6},{9,8},{10,9},{11,10},{12... | collective-permute-start | bytes 589832 | tf_op jit(solution)/shard_map/ppermute | solution.py:538
  13.0 1.0 %copy-done.1 = f32[4,80,256]{2,1,0:T(8,128)S(1)} copy-done((f32[4,80,256]{2,1,0:T(8,128)S(1)}, f32[4,80,256]{2,1,0:T(8,128)}, u32[]{:S(2)}) %copy-start.1) | copy-done | bytes 327704
  13.9 4.6 %band_spectra_rest.1.rest_ref = f32[88,1024]{1,0:T(8,128)S(1)} custom-call(f32[4,80,256]{2,1,0:T(8,128)S(1)} %copy-done.1, bf16[15000,1024]{1,0:T(8,128)(2,1)} %bitcast.3, bf16[15000,1024]{1,0:T(8,128)(2,1)} %bitcast.4), custom_call_target="tpu_custom_call" | custom-call | flops 612106240 | bytes 7651328 | tf_op jit(solution)/shard_map/band_spectra_rest/pallas_call | solution.py:355
  18.5 0.2 whiten.1.refs_0_.refs_8_
  18.8 4.1 %collective-permute-start.5 = (bf16[2,80,512]{2,1,0:T(8,128)(2,1)S(1)}, bf16[2,80,512]{2,1,0:T(8,128)(2,1)S(1)}, u32[]{:S(2)}, u32[]{:S(2)}) collective-permute-start(bf16[2,80,512]{2,1,0:T(8,128)(2,1)S(1)} %whiten.1.refs_0_.refs_8_), channel_id=1, source_target_pairs={{0,16},{8,24},{16,0},{24,8},{1,17},{9,25},{17,1},{25,9},{2,18},{10... | collective-permute-start | bytes 491528 | tf_op jit(solution)/shard_map/ppermute | solution.py:555
  22.8 1.6 %collective-permute-start.4 = (bf16[2,80,512]{2,1,0:T(8,128)(2,1)S(1)}, bf16[2,80,512]{2,1,0:T(8,128)(2,1)S(1)}, u32[]{:S(2)}, u32[]{:S(2)}) collective-permute-start(bf16[2,80,512]{2,1,0:T(8,128)(2,1)S(1)} %whiten.1.refs_0_.refs_8_), channel_id=1, source_target_pairs={{0,8},{8,0},{16,24},{24,16},{1,9},{9,1},{17,25},{25,17},{2,10},{10... | collective-permute-start | bytes 491528 | tf_op jit(solution)/shard_map/ppermute | solution.py:555
  24.4 3.4 %collective-permute-start.3 = (bf16[2,80,512]{2,1,0:T(8,128)(2,1)S(1)}, bf16[2,80,512]{2,1,0:T(8,128)(2,1)S(1)}, u32[]{:S(2)}, u32[]{:S(2)}) collective-permute-start(bf16[2,80,512]{2,1,0:T(8,128)(2,1)S(1)} %whiten.1.refs_0_.refs_8_), channel_id=1, source_target_pairs={{0,6},{1,7},{2,4},{3,5},{4,2},{5,3},{6,0},{7,1},{8,14},{9,15},{10,... | collective-permute-start | bytes 491528 | tf_op jit(solution)/shard_map/ppermute | solution.py:555
  27.8 0.5 collective-permute-start.2
  28.3 0.7 %collective-permute-start.1 = (bf16[2,80,512]{2,1,0:T(8,128)(2,1)S(1)}, bf16[2,80,512]{2,1,0:T(8,128)(2,1)S(1)}, u32[]{:S(2)}, u32[]{:S(2)}) collective-permute-start(bf16[2,80,512]{2,1,0:T(8,128)(2,1)S(1)} %whiten.1.refs_0_.refs_8_), channel_id=1, source_target_pairs={{0,2},{1,3},{2,0},{3,1},{4,6},{5,7},{6,4},{7,5},{8,10},{9,11},{10,... | collective-permute-start | bytes 491528 | tf_op jit(solution)/shard_map/ppermute | solution.py:555
  29.1 2.1 %collective-permute-done.5.refs_5_ = bf16[2,80,512]{2,1,0:T(8,128)(2,1)S(1)} collective-permute-done((bf16[2,80,512]{2,1,0:T(8,128)(2,1)S(1)}, bf16[2,80,512]{2,1,0:T(8,128)(2,1)S(1)}, u32[]{:S(2)}, u32[]{:S(2)}) %collective-permute-start.5) | collective-permute-done | bytes 163872 | tf_op jit(solution)/shard_map/ppermute | solution.py:555
  31.2 1.2 %collective-permute-start.6 = (bf16[2,80,512]{2,1,0:T(8,128)(2,1)S(1)}, bf16[2,80,512]{2,1,0:T(8,128)(2,1)S(1)}, u32[]{:S(2)}, u32[]{:S(2)}) collective-permute-start(bf16[2,80,512]{2,1,0:T(8,128)(2,1)S(1)} %collective-permute-done.5.refs_5_), channel_id=1, source_target_pairs={{0,8},{8,0},{16,24},{24,16},{1,9},{9,1},{17,25},{25,17},{2,10},{10... | collective-permute-start | bytes 491528 | tf_op jit(solution)/shard_map/ppermute | solution.py:555
  32.4 0.4 collective-permute-done.3.refs_3_.refs_14_
  32.9 2.7 %collective-permute-done.2.refs_2_.refs_12_ = bf16[2,80,512]{2,1,0:T(8,128)(2,1)S(1)} collective-permute-done((bf16[2,80,512]{2,1,0:T(8,128)(2,1)S(1)}, bf16[2,80,512]{2,1,0:T(8,128)(2,1)S(1)}, u32[]{:S(2)}, u32[]{:S(2)}) %collective-permute-start.2) | collective-permute-done | bytes 163872 | tf_op jit(solution)/shard_map/ppermute | solution.py:555
  35.7 0.4 collective-permute-start.15
  36.2 1.5 %collective-permute-done.6.refs_6_ = bf16[2,80,512]{2,1,0:T(8,128)(2,1)S(1)} collective-permute-done((bf16[2,80,512]{2,1,0:T(8,128)(2,1)S(1)}, bf16[2,80,512]{2,1,0:T(8,128)(2,1)S(1)}, u32[]{:S(2)}, u32[]{:S(2)}) %collective-permute-start.6) | collective-permute-done | bytes 163872 | tf_op jit(solution)/shard_map/ppermute | solution.py:555
  37.8 2.0 %collective-permute-start.7 = (bf16[80,512]{1,0:T(8,128)(2,1)S(1)}, bf16[80,512]{1,0:T(8,128)(2,1)S(1)}, u32[]{:S(2)}, u32[]{:S(2)}) collective-permute-start(bf16[80,512]{1,0:T(8,128)(2,1)S(1)} %get-tuple-element.20), channel_id=1, source_target_pairs={{0,2},{1,3},{2,0},{3,1},{4,6},{5,7},{6,4},{7,5},{8,10},{9,11},{10,... | collective-permute-start | bytes 245768 | tf_op jit(solution)/shard_map/ppermute | solution.py:555
  39.8 1.5 %collective-permute-start.8 = (bf16[80,512]{1,0:T(8,128)(2,1)S(1)}, bf16[80,512]{1,0:T(8,128)(2,1)S(1)}, u32[]{:S(2)}, u32[]{:S(2)}) collective-permute-start(bf16[80,512]{1,0:T(8,128)(2,1)S(1)} %get-tuple-element.21), channel_id=1, source_target_pairs={{0,4},{1,5},{2,6},{3,7},{4,0},{5,1},{6,2},{7,3},{8,12},{9,13},{10,... | collective-permute-start | bytes 245768 | tf_op jit(solution)/shard_map/ppermute | solution.py:555
  41.4 3.1 %collective-permute-start.11 = (bf16[80,512]{1,0:T(8,128)(2,1)S(1)}, bf16[80,512]{1,0:T(8,128)(2,1)S(1)}, u32[]{:S(2)}, u32[]{:S(2)}) collective-permute-start(bf16[80,512]{1,0:T(8,128)(2,1)S(1)} %get-tuple-element.24), channel_id=1, source_target_pairs={{0,5},{1,4},{2,7},{3,6},{4,1},{5,0},{6,3},{7,2},{8,13},{9,12},{10,... | collective-permute-start | bytes 245768 | tf_op jit(solution)/shard_map/ppermute | solution.py:555
  44.5 0.4 collective-permute-done.8.refs_2_
  44.9 0.4 collective-permute-start.13
  45.3 1.8 %collective-permute-done.9.refs_3_ = bf16[80,512]{1,0:T(8,128)(2,1)S(1)} collective-permute-done((bf16[80,512]{1,0:T(8,128)(2,1)S(1)}, bf16[80,512]{1,0:T(8,128)(2,1)S(1)}, u32[]{:S(2)}, u32[]{:S(2)}) %collective-permute-start.9) | collective-permute-done | bytes 81952 | tf_op jit(solution)/shard_map/ppermute | solution.py:555
  47.1 2.8 %collective-permute-done.11.refs_5_ = bf16[80,512]{1,0:T(8,128)(2,1)S(1)} collective-permute-done((bf16[80,512]{1,0:T(8,128)(2,1)S(1)}, bf16[80,512]{1,0:T(8,128)(2,1)S(1)}, u32[]{:S(2)}, u32[]{:S(2)}) %collective-permute-start.11) | collective-permute-done | bytes 81952 | tf_op jit(solution)/shard_map/ppermute | solution.py:555
  49.8 16.3 %stack_products.1 = bf16[2,20,512,1024]{3,2,1,0:T(8,128)(2,1)} custom-call(bf16[80,512]{1,0:T(8,128)(2,1)S(1)} %get-tuple-element.19.refs_0_, bf16[80,512]{1,0:T(8,128)(2,1)S(1)} %collective-permute-done.7.refs_1_, bf16[80,512]{1,0:T(8,128)(2,1)S(1)} %collective-permute-done.8.refs_2_, bf16[80,512]{1,0:T(8,128)(2,1)S(1)} %collective-permute-done.9.refs_3_, ...), custom_call_target="tpu_custom_call" | custom-call | flops 5368709120 | bytes 41943040 | tf_op jit(solution)/shard_map/stack_products/pallas_call | solution.py:484
  (21 shorter events, 0.4 us)
Async XLA Ops:
  11.5 7.0 %copy-start = (f32[88,1024]{1,0:T(8,128)S(1)}, f32[88,1024]{1,0:T(8,128)}, u32[]{:S(2)}) copy-start(f32[88,1024]{1,0:T(8,128)} %get-tuple-element.16.own_ref) | copy-start | bytes 1081348
  11.5 7.0 %collective-permute-start = (bf16[96,1024]{1,0:T(8,128)(2,1)}, bf16[96,1024]{1,0:T(8,128)(2,1)S(1)}, u32[]{:S(2)}, u32[]{:S(2)}) collective-permute-start(bf16[96,1024]{1,0:T(8,128)(2,1)} %get-tuple-element.18), channel_id=1, source_target_pairs={{1,0},{2,1},{3,2},{4,3},{5,4},{6,5},{7,6},{9,8},{10,9},{11,10},{12... | collective-permute-start | bytes 589832 | tf_op jit(solution)/shard_map/ppermute | solution.py:538
  12.9 1.0 %copy-start.1 = (f32[4,80,256]{2,1,0:T(8,128)S(1)}, f32[4,80,256]{2,1,0:T(8,128)}, u32[]{:S(2)}) copy-start(f32[4,80,256]{2,1,0:T(8,128)} %get-tuple-element.17.state_in) | copy-start | bytes 983044
  18.8 12.4 %collective-permute-start.5 = (bf16[2,80,512]{2,1,0:T(8,128)(2,1)S(1)}, bf16[2,80,512]{2,1,0:T(8,128)(2,1)S(1)}, u32[]{:S(2)}, u32[]{:S(2)}) collective-permute-start(bf16[2,80,512]{2,1,0:T(8,128)(2,1)S(1)} %whiten.1.refs_0_.refs_8_), channel_id=1, source_target_pairs={{0,16},{8,24},{16,0},{24,8},{1,17},{9,25},{17,1},{25,9},{2,18},{10... | collective-permute-start | bytes 491528 | tf_op jit(solution)/shard_map/ppermute | solution.py:555
  22.8 9.6 %collective-permute-start.4 = (bf16[2,80,512]{2,1,0:T(8,128)(2,1)S(1)}, bf16[2,80,512]{2,1,0:T(8,128)(2,1)S(1)}, u32[]{:S(2)}, u32[]{:S(2)}) collective-permute-start(bf16[2,80,512]{2,1,0:T(8,128)(2,1)S(1)} %whiten.1.refs_0_.refs_8_), channel_id=1, source_target_pairs={{0,8},{8,0},{16,24},{24,16},{1,9},{9,1},{17,25},{25,17},{2,10},{10... | collective-permute-start | bytes 491528 | tf_op jit(solution)/shard_map/ppermute | solution.py:555
  24.4 8.4 %collective-permute-start.3 = (bf16[2,80,512]{2,1,0:T(8,128)(2,1)S(1)}, bf16[2,80,512]{2,1,0:T(8,128)(2,1)S(1)}, u32[]{:S(2)}, u32[]{:S(2)}) collective-permute-start(bf16[2,80,512]{2,1,0:T(8,128)(2,1)S(1)} %whiten.1.refs_0_.refs_8_), channel_id=1, source_target_pairs={{0,6},{1,7},{2,4},{3,5},{4,2},{5,3},{6,0},{7,1},{8,14},{9,15},{10,... | collective-permute-start | bytes 491528 | tf_op jit(solution)/shard_map/ppermute | solution.py:555
  27.8 7.8 %collective-permute-start.2 = (bf16[2,80,512]{2,1,0:T(8,128)(2,1)S(1)}, bf16[2,80,512]{2,1,0:T(8,128)(2,1)S(1)}, u32[]{:S(2)}, u32[]{:S(2)}) collective-permute-start(bf16[2,80,512]{2,1,0:T(8,128)(2,1)S(1)} %whiten.1.refs_0_.refs_8_), channel_id=1, source_target_pairs={{0,4},{1,5},{2,6},{3,7},{4,0},{5,1},{6,2},{7,3},{8,12},{9,13},{10,... | collective-permute-start | bytes 491528 | tf_op jit(solution)/shard_map/ppermute | solution.py:555
  28.3 7.4 %collective-permute-start.1 = (bf16[2,80,512]{2,1,0:T(8,128)(2,1)S(1)}, bf16[2,80,512]{2,1,0:T(8,128)(2,1)S(1)}, u32[]{:S(2)}, u32[]{:S(2)}) collective-permute-start(bf16[2,80,512]{2,1,0:T(8,128)(2,1)S(1)} %whiten.1.refs_0_.refs_8_), channel_id=1, source_target_pairs={{0,2},{1,3},{2,0},{3,1},{4,6},{5,7},{6,4},{7,5},{8,10},{9,11},{10,... | collective-permute-start | bytes 491528 | tf_op jit(solution)/shard_map/ppermute | solution.py:555
  31.2 6.5 %collective-permute-start.6 = (bf16[2,80,512]{2,1,0:T(8,128)(2,1)S(1)}, bf16[2,80,512]{2,1,0:T(8,128)(2,1)S(1)}, u32[]{:S(2)}, u32[]{:S(2)}) collective-permute-start(bf16[2,80,512]{2,1,0:T(8,128)(2,1)S(1)} %collective-permute-done.5.refs_5_), channel_id=1, source_target_pairs={{0,8},{8,0},{16,24},{24,16},{1,9},{9,1},{17,25},{25,17},{2,10},{10... | collective-permute-start | bytes 491528 | tf_op jit(solution)/shard_map/ppermute | solution.py:555
  32.4 7.4 %collective-permute-start.14 = (bf16[2,80,512]{2,1,0:T(8,128)(2,1)S(1)}, bf16[2,80,512]{2,1,0:T(8,128)(2,1)S(1)}, u32[]{:S(2)}, u32[]{:S(2)}) collective-permute-start(bf16[2,80,512]{2,1,0:T(8,128)(2,1)S(1)} %whiten.1.refs_0_.refs_8_), channel_id=1, source_target_pairs={{0,1},{1,0},{2,3},{3,2},{4,5},{5,4},{6,7},{7,6},{8,9},{9,8},{10,11... | collective-permute-start | bytes 491528 | tf_op jit(solution)/shard_map/ppermute | solution.py:555
  32.8 8.5 %collective-permute-start.17 = (bf16[2,80,512]{2,1,0:T(8,128)(2,1)S(1)}, bf16[2,80,512]{2,1,0:T(8,128)(2,1)S(1)}, u32[]{:S(2)}, u32[]{:S(2)}) collective-permute-start(bf16[2,80,512]{2,1,0:T(8,128)(2,1)S(1)} %collective-permute-done.3.refs_3_.refs_14_), channel_id=1, source_target_pairs={{0,1},{1,0},{2,3},{3,2},{4,5},{5,4},{6,7},{7,6},{8,9},{9,8},{10,11... | collective-permute-start | bytes 491528 | tf_op jit(solution)/shard_map/ppermute | solution.py:555
  35.7 5.7 %collective-permute-start.16 = (bf16[2,80,512]{2,1,0:T(8,128)(2,1)S(1)}, bf16[2,80,512]{2,1,0:T(8,128)(2,1)S(1)}, u32[]{:S(2)}, u32[]{:S(2)}) collective-permute-start(bf16[2,80,512]{2,1,0:T(8,128)(2,1)S(1)} %collective-permute-done.2.refs_2_.refs_12_), channel_id=1, source_target_pairs={{0,1},{1,0},{2,3},{3,2},{4,5},{5,4},{6,7},{7,6},{8,9},{9,8},{10,11... | collective-permute-start | bytes 491528 | tf_op jit(solution)/shard_map/ppermute | solution.py:555
  35.7 5.7 %collective-permute-start.15 = (bf16[2,80,512]{2,1,0:T(8,128)(2,1)S(1)}, bf16[2,80,512]{2,1,0:T(8,128)(2,1)S(1)}, u32[]{:S(2)}, u32[]{:S(2)}) collective-permute-start(bf16[2,80,512]{2,1,0:T(8,128)(2,1)S(1)} %collective-permute-done.1.refs_1_.refs_10_), channel_id=1, source_target_pairs={{0,1},{1,0},{2,3},{3,2},{4,5},{5,4},{6,7},{7,6},{8,9},{9,8},{10,11... | collective-permute-start | bytes 491528 | tf_op jit(solution)/shard_map/ppermute | solution.py:555
  37.8 6.7 %collective-permute-start.7 = (bf16[80,512]{1,0:T(8,128)(2,1)S(1)}, bf16[80,512]{1,0:T(8,128)(2,1)S(1)}, u32[]{:S(2)}, u32[]{:S(2)}) collective-permute-start(bf16[80,512]{1,0:T(8,128)(2,1)S(1)} %get-tuple-element.20), channel_id=1, source_target_pairs={{0,2},{1,3},{2,0},{3,1},{4,6},{5,7},{6,4},{7,5},{8,10},{9,11},{10,... | collective-permute-start | bytes 245768 | tf_op jit(solution)/shard_map/ppermute | solution.py:555
  39.8 5.1 %collective-permute-start.8 = (bf16[80,512]{1,0:T(8,128)(2,1)S(1)}, bf16[80,512]{1,0:T(8,128)(2,1)S(1)}, u32[]{:S(2)}, u32[]{:S(2)}) collective-permute-start(bf16[80,512]{1,0:T(8,128)(2,1)S(1)} %get-tuple-element.21), channel_id=1, source_target_pairs={{0,4},{1,5},{2,6},{3,7},{4,0},{5,1},{6,2},{7,3},{8,12},{9,13},{10,... | collective-permute-start | bytes 245768 | tf_op jit(solution)/shard_map/ppermute | solution.py:555
  41.3 5.8 %collective-permute-start.9 = (bf16[80,512]{1,0:T(8,128)(2,1)S(1)}, bf16[80,512]{1,0:T(8,128)(2,1)S(1)}, u32[]{:S(2)}, u32[]{:S(2)}) collective-permute-start(bf16[80,512]{1,0:T(8,128)(2,1)S(1)} %get-tuple-element.22), channel_id=1, source_target_pairs={{0,6},{1,7},{2,4},{3,5},{4,2},{5,3},{6,0},{7,1},{8,14},{9,15},{10,... | collective-permute-start | bytes 245768 | tf_op jit(solution)/shard_map/ppermute | solution.py:555
  41.4 5.7 %collective-permute-start.10 = (bf16[80,512]{1,0:T(8,128)(2,1)S(1)}, bf16[80,512]{1,0:T(8,128)(2,1)S(1)}, u32[]{:S(2)}, u32[]{:S(2)}) collective-permute-start(bf16[80,512]{1,0:T(8,128)(2,1)S(1)} %get-tuple-element.23), channel_id=1, source_target_pairs={{0,3},{1,2},{2,1},{3,0},{4,7},{5,6},{6,5},{7,4},{8,11},{9,10},{10,... | collective-permute-start | bytes 245768 | tf_op jit(solution)/shard_map/ppermute | solution.py:555
  41.4 8.4 %collective-permute-start.11 = (bf16[80,512]{1,0:T(8,128)(2,1)S(1)}, bf16[80,512]{1,0:T(8,128)(2,1)S(1)}, u32[]{:S(2)}, u32[]{:S(2)}) collective-permute-start(bf16[80,512]{1,0:T(8,128)(2,1)S(1)} %get-tuple-element.24), channel_id=1, source_target_pairs={{0,5},{1,4},{2,7},{3,6},{4,1},{5,0},{6,3},{7,2},{8,13},{9,12},{10,... | collective-permute-start | bytes 245768 | tf_op jit(solution)/shard_map/ppermute | solution.py:555
  44.5 5.3 %collective-permute-start.12 = (bf16[80,512]{1,0:T(8,128)(2,1)S(1)}, bf16[80,512]{1,0:T(8,128)(2,1)S(1)}, u32[]{:S(2)}, u32[]{:S(2)}) collective-permute-start(bf16[80,512]{1,0:T(8,128)(2,1)S(1)} %get-tuple-element.25), channel_id=1, source_target_pairs={{0,7},{1,6},{2,5},{3,4},{4,3},{5,2},{6,1},{7,0},{8,15},{9,14},{10,... | collective-permute-start | bytes 245768 | tf_op jit(solution)/shard_map/ppermute | solution.py:555
  44.9 4.9 %collective-permute-start.13 = (bf16[80,512]{1,0:T(8,128)(2,1)S(1)}, bf16[80,512]{1,0:T(8,128)(2,1)S(1)}, u32[]{:S(2)}, u32[]{:S(2)}) collective-permute-start(bf16[80,512]{1,0:T(8,128)(2,1)S(1)} %get-tuple-element.26), channel_id=1, source_target_pairs={{0,1},{1,0},{2,3},{3,2},{4,5},{5,4},{6,7},{7,6},{8,9},{9,8},{10,11... | collective-permute-start | bytes 245768 | tf_op jit(solution)/shard_map/ppermute | solution.py:555

commit v15 on v14

--- a/solution.py
+++ b/solution.py
@@ -417,18 +417,17 @@
 
 
 def stack_kernel(windows, scale, devices, *refs):
-    col_refs, row_refs = refs[:devices], refs[devices:2 * devices]
-    out_hbm, lhs, held, made, sems = refs[2 * devices:]
+    col_refs, row_refs = refs[:2], refs[2:2 + devices]
+    out_hbm, lhs, held, made, sems = refs[2 + devices:]
     per_group = ROW_TILE // (2 * windows)
     step = pl.program_id(0)
-    width = col_refs[0].shape[1]
+    width = col_refs[0].shape[2]
     depth = devices * ROW_TILE
     halves, _, span = row_refs[0].shape
     channels = halves * span
     exact = math.frexp(scale)[0] == 0.5
 
-    by_partner = dict(zip([0, *partners(devices)], col_refs))
-    cols = jnp.stack([by_partner[away][...].astype(F32) for away in range(devices)])
+    cols = jnp.stack([col_refs[away % 2][away // 2].astype(F32) for away in range(devices)])
     if exact:
         cols = cols * scale
     head, tail = cols[:, :ROW_TILE // 2], cols[:, ROW_TILE // 2:]
@@ -475,9 +474,9 @@
 
 
 def stacks_of(col_blocks, row_blocks, bins, windows):
-    devices = len(col_blocks)
+    devices = len(row_blocks)
     halves, _, span = row_blocks[0].shape
-    width = col_blocks[0].shape[1]
+    chips, _, width = col_blocks[0].shape
     per_group = ROW_TILE // (2 * windows)
     scale = 1.0 / math.sqrt(windows * devices)
     channels = halves * span
@@ -485,7 +484,7 @@
         functools.partial(stack_kernel, windows, scale, devices),
         out_shape=jax.ShapeDtypeStruct((2, bins, width, channels), BF16),
         grid=(bins // per_group,),
-        in_specs=[pl.BlockSpec((ROW_TILE, width), lambda i: (i, 0))] * devices
+        in_specs=[pl.BlockSpec((chips, ROW_TILE, width), lambda i: (0, i, 0))] * 2
         + [pl.BlockSpec((halves, ROW_TILE, span), lambda i: (0, i, 0))] * devices,
         out_specs=pl.BlockSpec(memory_space=pltpu.HBM),
         scratch_shapes=[
@@ -503,7 +502,7 @@
             transcendentals=0,
         ),
         name="stack_products",
-    )(*[col_blocks[away] for away in [0, *partners(devices)]], *row_blocks)
+    )(*col_blocks, *row_blocks)
 
 
 def pick_kernel(count, waits, *refs):
@@ -513,18 +512,16 @@
     for away, ref in enumerate((white_ref, *chan_refs)):
         held[jnp.bitwise_xor(mine, away)] = ref[...]
     for away, out_ref in enumerate(out_refs):
-        wanted = jnp.bitwise_xor(tm, away)
-        out_ref[...] = held[wanted // halves, wanted % halves]
+        out_ref[...] = held[jnp.bitwise_xor(tm // halves, away)]
 
 
 def picked(row_blocks, chan_blocks, count):
     block = row_blocks[0]
-    _, rows, width = block.shape
     whole = pl.BlockSpec(memory_space=pltpu.VMEM)
     waits = len(row_blocks) - 1
     return pl.pallas_call(
         functools.partial(pick_kernel, count, waits),
-        out_shape=[jax.ShapeDtypeStruct((rows, width), block.dtype)] * count,
+        out_shape=[jax.ShapeDtypeStruct(block.shape, block.dtype)] * count,
         in_specs=[whole] + [pl.BlockSpec(memory_space=pl.ANY)] * waits + [whole] * len(chan_blocks),
         out_specs=[whole] * count,
         scratch_shapes=[pltpu.VMEM((1 + len(chan_blocks), *block.shape), block.dtype)],
@@ -533,13 +530,31 @@
     )(*row_blocks, *chan_blocks)
 
 
+def part_kernel(count, *refs):
+    blocks, (mine_ref, other_ref) = refs[:count], refs[-2:]
+    halves = blocks[0].shape[0]
+    core = lax.axis_index("tm") % halves
+    for i, block in enumerate(blocks):
+        mine_ref[i] = block[core]
+        other_ref[i] = block[halves - 1 - core]
+
+
+def parted(blocks, others):
+    whole = pl.BlockSpec(memory_space=pltpu.VMEM)
+    shape = jax.ShapeDtypeStruct((len(blocks), *blocks[0].shape[1:]), blocks[0].dtype)
+    return pl.pallas_call(
+        functools.partial(part_kernel, len(blocks)),
+        out_shape=[shape] * 2,
+        in_specs=[whole] * len(blocks) + [pl.BlockSpec(memory_space=pl.ANY)] * len(others),
+        out_specs=[whole] * 2,
+        compiler_params=pltpu.CompilerParams(vmem_limit_bytes=8 * 2**20),
+        name="part_blocks",
+    )(*blocks, *others)
+
+
 def moved(block, axis, far):
     count = lax.axis_size(axis)
     return lax.ppermute(block, axis, [(i + far, i) for i in range(count) if 0 <= i + far < count])
-
-
-def partners(count):
-    return [*range(2, count, 2), *range(3, count, 2), 1]
 
 
 def chan_blocks_of(block):
@@ -571,12 +586,16 @@
     white = whiten(own, rest, more, bins, windows, halves)
     row_blocks = [white] + [from_partner(white, "tm", away) for away in range(2, tm_count, 2)]
     chan_blocks = chan_blocks_of(white)
-    col_blocks = list(picked(row_blocks, chan_blocks, tm_count))
-    for away in partners(tm_count):
-        col_blocks[away] = from_partner(col_blocks[away], "tm", away)
+    chips = len(row_blocks)
+    chip_blocks = list(picked(row_blocks, chan_blocks, chips))
+    for away in range(1, chips):
+        chip_blocks[away] = from_partner(chip_blocks[away], "tm", 2 * away)
+    rows_there = [from_partner(block, "tm", 1) for block in row_blocks]
+    mine, other = parted(chip_blocks, rows_there)
+    col_blocks = [mine, from_partner(other, "tm", 1)]
     all_rows = []
-    for block in row_blocks:
-        all_rows += [block, from_partner(block, "tm", 1)]
+    for here, there in zip(row_blocks, rows_there):
+        all_rows += [here, there]
     return stacks_of(col_blocks, all_rows, bins, windows)
 
 

time: 66.4 us -> 66.8 us (level)
  waiting for transfers between devices: 11.8 us -> 15.4 us
  starting transfers between devices: 20.6 us -> 17.1 us
    ppermute x17 -> x14, waiting for transfers between devices: 11.8 us -> 15.4 us  [from_partner(): lax.ppermute(block, axis, [(i, i ^ away) for i in range(lax.axis_size(axi...]
    ppermute x17 -> x14, starting transfers between devices: 19.2 us -> 15.7 us  [from_partner(): lax.ppermute(block, axis, [(i, i ^ away) for i in range(lax.axis_size(axi...]
  transfers between devices with their start and end apart: 18 -> 15, of which waited for: 8 -> 8; matrix products, arithmetic and copies ran while one was open for 0% -> 0% of each run, Pallas kernels for 7% -> 7%
where the time goes in v15:
time: 66.8 us; the launch traced here: 66.5 us
  Pallas kernels  32.9 us (49%)
  starting transfers between devices  17.1 us (26%)
  waiting for transfers between devices  15.4 us (23%)
  local copies, waits for them, and re-layouts  0.97 us (1%)
    pallas_call x1, Pallas kernels, stacks_of(): pl.pallas_call(functools.partial(stack_kernel, windows, scale, devices),...  16.4 us
    ppermute x14, starting transfers between devices, from_partner(): lax.ppermute(block, axis, [(i, i ^ away) for i in range(lax.axis_size(axi...  15.7 us
    ppermute x14, waiting for transfers between devices, from_partner(): lax.ppermute(block, axis, [(i, i ^ away) for i in range(lax.axis_size(axi...  15.4 us
    pallas_call x1, Pallas kernels, spectra_of(): pl.pallas_call(functools.partial(spectra_kernel, bins, windows, block_len...  11.5 us
    pallas_call x1, Pallas kernels, rest_of(): pl.pallas_call(functools.partial(rest_kernel, bins, windows, block_len, l...  4.55 us
    ppermute x1, starting transfers between devices, moved(): lax.ppermute(block, axis, [(i + far, i) for i in range(count) if 0 <= i +...  1.42 us
  transfers between devices with their start and end apart: 15, of which 8 were waited for; matrix products, arithmetic and copies ran while one was open for 0% of the time, Pallas kernels for 7%

profile of v15, /device:TPU:0, one launch (start us, length us, event | category | flops | bytes accessed | tf_op | source)
XLA Modules:
  0.0 66.5 jit_solution(16057622854502723736)
XLA Ops:
  0.0 11.5 %band_spectra.1 = (f32[88,1024]{1,0:T(8,128)}, bf16[96,1024]{1,0:T(8,128)(2,1)}, f32[4,80,256]{2,1,0:T(8,128)}) custom-call(s32[16]{0:T(128)} %offsets_hbm.1, s32[20]{0:T(128)} %bins_hbm.1, s32[1,1024]{1,0:T(1,128)} %bitcast.5, bf16[15000,1024]{1,0:T(8,128)(2,1)} %bitcast.2), custom_call_target="tpu_custom_call" | custom-call | flops 3690987520 | bytes 23068672 | tf_op jit(solution)/shard_map/band_spectra/pallas_call | solution.py:314
  11.5 1.4 %collective-permute-start = (bf16[96,1024]{1,0:T(8,128)(2,1)}, bf16[96,1024]{1,0:T(8,128)(2,1)S(1)}, u32[]{:S(2)}, u32[]{:S(2)}) collective-permute-start(bf16[96,1024]{1,0:T(8,128)(2,1)} %get-tuple-element.16), channel_id=1, source_target_pairs={{1,0},{2,1},{3,2},{4,3},{5,4},{6,5},{7,6},{9,8},{10,9},{11,10},{12... | collective-permute-start | bytes 589832 | tf_op jit(solution)/shard_map/ppermute | solution.py:557
  13.0 1.0 %copy-done.1 = f32[4,80,256]{2,1,0:T(8,128)S(1)} copy-done((f32[4,80,256]{2,1,0:T(8,128)S(1)}, f32[4,80,256]{2,1,0:T(8,128)}, u32[]{:S(2)}) %copy-start.1) | copy-done | bytes 327704
  13.9 4.6 %band_spectra_rest.1.rest_ref = f32[88,1024]{1,0:T(8,128)S(1)} custom-call(f32[4,80,256]{2,1,0:T(8,128)S(1)} %copy-done.1, bf16[15000,1024]{1,0:T(8,128)(2,1)} %bitcast.3, bf16[15000,1024]{1,0:T(8,128)(2,1)} %bitcast.4), custom_call_target="tpu_custom_call" | custom-call | flops 612106240 | bytes 7651328 | tf_op jit(solution)/shard_map/band_spectra_rest/pallas_call | solution.py:355
  18.5 0.2 whiten.1.refs_0_.refs_2_
  18.8 4.1 %collective-permute-start.5 = (bf16[2,80,512]{2,1,0:T(8,128)(2,1)S(1)}, bf16[2,80,512]{2,1,0:T(8,128)(2,1)S(1)}, u32[]{:S(2)}, u32[]{:S(2)}) collective-permute-start(bf16[2,80,512]{2,1,0:T(8,128)(2,1)S(1)} %whiten.1.refs_0_.refs_2_), channel_id=1, source_target_pairs={{0,16},{8,24},{16,0},{24,8},{1,17},{9,25},{17,1},{25,9},{2,18},{10... | collective-permute-start | bytes 491528 | tf_op jit(solution)/shard_map/ppermute | solution.py:570
  22.9 1.6 %collective-permute-start.4 = (bf16[2,80,512]{2,1,0:T(8,128)(2,1)S(1)}, bf16[2,80,512]{2,1,0:T(8,128)(2,1)S(1)}, u32[]{:S(2)}, u32[]{:S(2)}) collective-permute-start(bf16[2,80,512]{2,1,0:T(8,128)(2,1)S(1)} %whiten.1.refs_0_.refs_2_), channel_id=1, source_target_pairs={{0,8},{8,0},{16,24},{24,16},{1,9},{9,1},{17,25},{25,17},{2,10},{10... | collective-permute-start | bytes 491528 | tf_op jit(solution)/shard_map/ppermute | solution.py:570
  24.4 3.3 %collective-permute-start.3 = (bf16[2,80,512]{2,1,0:T(8,128)(2,1)S(1)}, bf16[2,80,512]{2,1,0:T(8,128)(2,1)S(1)}, u32[]{:S(2)}, u32[]{:S(2)}) collective-permute-start(bf16[2,80,512]{2,1,0:T(8,128)(2,1)S(1)} %whiten.1.refs_0_.refs_2_), channel_id=1, source_target_pairs={{0,6},{1,7},{2,4},{3,5},{4,2},{5,3},{6,0},{7,1},{8,14},{9,15},{10,... | collective-permute-start | bytes 491528 | tf_op jit(solution)/shard_map/ppermute | solution.py:570
  27.8 0.5 collective-permute-start.2
  28.3 0.9 %collective-permute-start.1 = (bf16[2,80,512]{2,1,0:T(8,128)(2,1)S(1)}, bf16[2,80,512]{2,1,0:T(8,128)(2,1)S(1)}, u32[]{:S(2)}, u32[]{:S(2)}) collective-permute-start(bf16[2,80,512]{2,1,0:T(8,128)(2,1)S(1)} %whiten.1.refs_0_.refs_2_), channel_id=1, source_target_pairs={{0,2},{1,3},{2,0},{3,1},{4,6},{5,7},{6,4},{7,5},{8,10},{9,11},{10,... | collective-permute-start | bytes 491528 | tf_op jit(solution)/shard_map/ppermute | solution.py:570
  29.2 2.0 %collective-permute-done.5.refs_5_ = bf16[2,80,512]{2,1,0:T(8,128)(2,1)S(1)} collective-permute-done((bf16[2,80,512]{2,1,0:T(8,128)(2,1)S(1)}, bf16[2,80,512]{2,1,0:T(8,128)(2,1)S(1)}, u32[]{:S(2)}, u32[]{:S(2)}) %collective-permute-start.5) | collective-permute-done | bytes 163872 | tf_op jit(solution)/shard_map/ppermute | solution.py:570
  31.2 1.2 %collective-permute-start.6 = (bf16[2,80,512]{2,1,0:T(8,128)(2,1)S(1)}, bf16[2,80,512]{2,1,0:T(8,128)(2,1)S(1)}, u32[]{:S(2)}, u32[]{:S(2)}) collective-permute-start(bf16[2,80,512]{2,1,0:T(8,128)(2,1)S(1)} %collective-permute-done.5.refs_5_), channel_id=1, source_target_pairs={{0,8},{8,0},{16,24},{24,16},{1,9},{9,1},{17,25},{25,17},{2,10},{10... | collective-permute-start | bytes 491528 | tf_op jit(solution)/shard_map/ppermute | solution.py:570
  32.4 0.4 collective-permute-done.3.refs_3_.refs_8_
  32.8 0.1 collective-permute-start.13
  32.9 2.7 %collective-permute-done.2.refs_2_.refs_6_ = bf16[2,80,512]{2,1,0:T(8,128)(2,1)S(1)} collective-permute-done((bf16[2,80,512]{2,1,0:T(8,128)(2,1)S(1)}, bf16[2,80,512]{2,1,0:T(8,128)(2,1)S(1)}, u32[]{:S(2)}, u32[]{:S(2)}) %collective-permute-start.2) | collective-permute-done | bytes 163872 | tf_op jit(solution)/shard_map/ppermute | solution.py:570
  35.6 0.2 collective-permute-done.1.refs_1_.refs_4_
  35.8 0.3 collective-permute-start.11
  36.1 1.6 %collective-permute-done.6.refs_6_ = bf16[2,80,512]{2,1,0:T(8,128)(2,1)S(1)} collective-permute-done((bf16[2,80,512]{2,1,0:T(8,128)(2,1)S(1)}, bf16[2,80,512]{2,1,0:T(8,128)(2,1)S(1)}, u32[]{:S(2)}, u32[]{:S(2)}) %collective-permute-start.6) | collective-permute-done | bytes 163872 | tf_op jit(solution)/shard_map/ppermute | solution.py:570
  37.8 1.9 %collective-permute-start.7 = (bf16[2,80,512]{2,1,0:T(8,128)(2,1)S(1)}, bf16[2,80,512]{2,1,0:T(8,128)(2,1)S(1)}, u32[]{:S(2)}, u32[]{:S(2)}) collective-permute-start(bf16[2,80,512]{2,1,0:T(8,128)(2,1)S(1)} %get-tuple-element.18), channel_id=1, source_target_pairs={{0,2},{1,3},{2,0},{3,1},{4,6},{5,7},{6,4},{7,5},{8,10},{9,11},{10,... | collective-permute-start | bytes 491528 | tf_op jit(solution)/shard_map/ppermute | solution.py:570
  39.7 1.5 %collective-permute-start.8 = (bf16[2,80,512]{2,1,0:T(8,128)(2,1)S(1)}, bf16[2,80,512]{2,1,0:T(8,128)(2,1)S(1)}, u32[]{:S(2)}, u32[]{:S(2)}) collective-permute-start(bf16[2,80,512]{2,1,0:T(8,128)(2,1)S(1)} %get-tuple-element.19), channel_id=1, source_target_pairs={{0,4},{1,5},{2,6},{3,7},{4,0},{5,1},{6,2},{7,3},{8,12},{9,13},{10,... | collective-permute-start | bytes 491528 | tf_op jit(solution)/shard_map/ppermute | solution.py:570
  41.4 3.6 %collective-permute-done.7.refs_1_ = bf16[2,80,512]{2,1,0:T(8,128)(2,1)S(1)} collective-permute-done((bf16[2,80,512]{2,1,0:T(8,128)(2,1)S(1)}, bf16[2,80,512]{2,1,0:T(8,128)(2,1)S(1)}, u32[]{:S(2)}, u32[]{:S(2)}) %collective-permute-start.7) | collective-permute-done | bytes 163872 | tf_op jit(solution)/shard_map/ppermute | solution.py:570
  45.0 3.4 %collective-permute-done.8.refs_2_ = bf16[2,80,512]{2,1,0:T(8,128)(2,1)S(1)} collective-permute-done((bf16[2,80,512]{2,1,0:T(8,128)(2,1)S(1)}, bf16[2,80,512]{2,1,0:T(8,128)(2,1)S(1)}, u32[]{:S(2)}, u32[]{:S(2)}) %collective-permute-start.8) | collective-permute-done | bytes 163872 | tf_op jit(solution)/shard_map/ppermute | solution.py:570
  48.5 1.6 %collective-permute-done.14.refs_1_ = bf16[4,80,512]{2,1,0:T(8,128)(2,1)S(1)} collective-permute-done((bf16[4,80,512]{2,1,0:T(8,128)(2,1)S(1)}, bf16[4,80,512]{2,1,0:T(8,128)(2,1)S(1)}, u32[]{:S(2)}, u32[]{:S(2)}) %collective-permute-start.14) | collective-permute-done | bytes 327712 | tf_op jit(solution)/shard_map/ppermute | solution.py:570
  50.1 16.4 %stack_products.1 = bf16[2,20,512,1024]{3,2,1,0:T(8,128)(2,1)} custom-call(bf16[4,80,512]{2,1,0:T(8,128)(2,1)S(1)} %get-tuple-element.21.refs_0_, bf16[4,80,512]{2,1,0:T(8,128)(2,1)S(1)} %collective-permute-done.14.refs_1_, bf16[2,80,512]{2,1,0:T(8,128)(2,1)S(1)} %whiten.1.refs_0_.refs_2_, bf16[2,80,512]{2,1,0:T(8,128)(2,1)S(1)} %collective-permute-done.10.refs_4_.refs_3_, ...), custom_call_target="tpu_custom_call" | custom-call | flops 5368709120 | bytes 41943040 | tf_op jit(solution)/shard_map/stack_products/pallas_call | solution.py:483
  (16 shorter events, 0.4 us)
Async XLA Ops:
  11.5 7.0 %copy-start = (f32[88,1024]{1,0:T(8,128)S(1)}, f32[88,1024]{1,0:T(8,128)}, u32[]{:S(2)}) copy-start(f32[88,1024]{1,0:T(8,128)} %get-tuple-element.14.own_ref) | copy-start | bytes 1081348
  11.5 7.0 %collective-permute-start = (bf16[96,1024]{1,0:T(8,128)(2,1)}, bf16[96,1024]{1,0:T(8,128)(2,1)S(1)}, u32[]{:S(2)}, u32[]{:S(2)}) collective-permute-start(bf16[96,1024]{1,0:T(8,128)(2,1)} %get-tuple-element.16), channel_id=1, source_target_pairs={{1,0},{2,1},{3,2},{4,3},{5,4},{6,5},{7,6},{9,8},{10,9},{11,10},{12... | collective-permute-start | bytes 589832 | tf_op jit(solution)/shard_map/ppermute | solution.py:557
  12.9 1.0 %copy-start.1 = (f32[4,80,256]{2,1,0:T(8,128)S(1)}, f32[4,80,256]{2,1,0:T(8,128)}, u32[]{:S(2)}) copy-start(f32[4,80,256]{2,1,0:T(8,128)} %get-tuple-element.15.state_in) | copy-start | bytes 983044
  18.8 12.4 %collective-permute-start.5 = (bf16[2,80,512]{2,1,0:T(8,128)(2,1)S(1)}, bf16[2,80,512]{2,1,0:T(8,128)(2,1)S(1)}, u32[]{:S(2)}, u32[]{:S(2)}) collective-permute-start(bf16[2,80,512]{2,1,0:T(8,128)(2,1)S(1)} %whiten.1.refs_0_.refs_2_), channel_id=1, source_target_pairs={{0,16},{8,24},{16,0},{24,8},{1,17},{9,25},{17,1},{25,9},{2,18},{10... | collective-permute-start | bytes 491528 | tf_op jit(solution)/shard_map/ppermute | solution.py:570
  22.9 9.6 %collective-permute-start.4 = (bf16[2,80,512]{2,1,0:T(8,128)(2,1)S(1)}, bf16[2,80,512]{2,1,0:T(8,128)(2,1)S(1)}, u32[]{:S(2)}, u32[]{:S(2)}) collective-permute-start(bf16[2,80,512]{2,1,0:T(8,128)(2,1)S(1)} %whiten.1.refs_0_.refs_2_), channel_id=1, source_target_pairs={{0,8},{8,0},{16,24},{24,16},{1,9},{9,1},{17,25},{25,17},{2,10},{10... | collective-permute-start | bytes 491528 | tf_op jit(solution)/shard_map/ppermute | solution.py:570
  24.4 8.4 %collective-permute-start.3 = (bf16[2,80,512]{2,1,0:T(8,128)(2,1)S(1)}, bf16[2,80,512]{2,1,0:T(8,128)(2,1)S(1)}, u32[]{:S(2)}, u32[]{:S(2)}) collective-permute-start(bf16[2,80,512]{2,1,0:T(8,128)(2,1)S(1)} %whiten.1.refs_0_.refs_2_), channel_id=1, source_target_pairs={{0,6},{1,7},{2,4},{3,5},{4,2},{5,3},{6,0},{7,1},{8,14},{9,15},{10,... | collective-permute-start | bytes 491528 | tf_op jit(solution)/shard_map/ppermute | solution.py:570
  27.8 7.8 %collective-permute-start.2 = (bf16[2,80,512]{2,1,0:T(8,128)(2,1)S(1)}, bf16[2,80,512]{2,1,0:T(8,128)(2,1)S(1)}, u32[]{:S(2)}, u32[]{:S(2)}) collective-permute-start(bf16[2,80,512]{2,1,0:T(8,128)(2,1)S(1)} %whiten.1.refs_0_.refs_2_), channel_id=1, source_target_pairs={{0,4},{1,5},{2,6},{3,7},{4,0},{5,1},{6,2},{7,3},{8,12},{9,13},{10,... | collective-permute-start | bytes 491528 | tf_op jit(solution)/shard_map/ppermute | solution.py:570
  28.3 7.5 %collective-permute-start.1 = (bf16[2,80,512]{2,1,0:T(8,128)(2,1)S(1)}, bf16[2,80,512]{2,1,0:T(8,128)(2,1)S(1)}, u32[]{:S(2)}, u32[]{:S(2)}) collective-permute-start(bf16[2,80,512]{2,1,0:T(8,128)(2,1)S(1)} %whiten.1.refs_0_.refs_2_), channel_id=1, source_target_pairs={{0,2},{1,3},{2,0},{3,1},{4,6},{5,7},{6,4},{7,5},{8,10},{9,11},{10,... | collective-permute-start | bytes 491528 | tf_op jit(solution)/shard_map/ppermute | solution.py:570
  31.2 6.5 %collective-permute-start.6 = (bf16[2,80,512]{2,1,0:T(8,128)(2,1)S(1)}, bf16[2,80,512]{2,1,0:T(8,128)(2,1)S(1)}, u32[]{:S(2)}, u32[]{:S(2)}) collective-permute-start(bf16[2,80,512]{2,1,0:T(8,128)(2,1)S(1)} %collective-permute-done.5.refs_5_), channel_id=1, source_target_pairs={{0,8},{8,0},{16,24},{24,16},{1,9},{9,1},{17,25},{25,17},{2,10},{10... | collective-permute-start | bytes 491528 | tf_op jit(solution)/shard_map/ppermute | solution.py:570
  32.4 7.3 %collective-permute-start.10 = (bf16[2,80,512]{2,1,0:T(8,128)(2,1)S(1)}, bf16[2,80,512]{2,1,0:T(8,128)(2,1)S(1)}, u32[]{:S(2)}, u32[]{:S(2)}) collective-permute-start(bf16[2,80,512]{2,1,0:T(8,128)(2,1)S(1)} %whiten.1.refs_0_.refs_2_), channel_id=1, source_target_pairs={{0,1},{1,0},{2,3},{3,2},{4,5},{5,4},{6,7},{7,6},{8,9},{9,8},{10,11... | collective-permute-start | bytes 491528 | tf_op jit(solution)/shard_map/ppermute | solution.py:570
  32.8 8.4 %collective-permute-start.13 = (bf16[2,80,512]{2,1,0:T(8,128)(2,1)S(1)}, bf16[2,80,512]{2,1,0:T(8,128)(2,1)S(1)}, u32[]{:S(2)}, u32[]{:S(2)}) collective-permute-start(bf16[2,80,512]{2,1,0:T(8,128)(2,1)S(1)} %collective-permute-done.3.refs_3_.refs_8_), channel_id=1, source_target_pairs={{0,1},{1,0},{2,3},{3,2},{4,5},{5,4},{6,7},{7,6},{8,9},{9,8},{10,11... | collective-permute-start | bytes 491528 | tf_op jit(solution)/shard_map/ppermute | solution.py:570
  35.6 5.8 %collective-permute-start.12 = (bf16[2,80,512]{2,1,0:T(8,128)(2,1)S(1)}, bf16[2,80,512]{2,1,0:T(8,128)(2,1)S(1)}, u32[]{:S(2)}, u32[]{:S(2)}) collective-permute-start(bf16[2,80,512]{2,1,0:T(8,128)(2,1)S(1)} %collective-permute-done.2.refs_2_.refs_6_), channel_id=1, source_target_pairs={{0,1},{1,0},{2,3},{3,2},{4,5},{5,4},{6,7},{7,6},{8,9},{9,8},{10,11... | collective-permute-start | bytes 491528 | tf_op jit(solution)/shard_map/ppermute | solution.py:570
  35.8 5.5 %collective-permute-start.11 = (bf16[2,80,512]{2,1,0:T(8,128)(2,1)S(1)}, bf16[2,80,512]{2,1,0:T(8,128)(2,1)S(1)}, u32[]{:S(2)}, u32[]{:S(2)}) collective-permute-start(bf16[2,80,512]{2,1,0:T(8,128)(2,1)S(1)} %collective-permute-done.1.refs_1_.refs_4_), channel_id=1, source_target_pairs={{0,1},{1,0},{2,3},{3,2},{4,5},{5,4},{6,7},{7,6},{8,9},{9,8},{10,11... | collective-permute-start | bytes 491528 | tf_op jit(solution)/shard_map/ppermute | solution.py:570
  37.8 7.2 %collective-permute-start.7 = (bf16[2,80,512]{2,1,0:T(8,128)(2,1)S(1)}, bf16[2,80,512]{2,1,0:T(8,128)(2,1)S(1)}, u32[]{:S(2)}, u32[]{:S(2)}) collective-permute-start(bf16[2,80,512]{2,1,0:T(8,128)(2,1)S(1)} %get-tuple-element.18), channel_id=1, source_target_pairs={{0,2},{1,3},{2,0},{3,1},{4,6},{5,7},{6,4},{7,5},{8,10},{9,11},{10,... | collective-permute-start | bytes 491528 | tf_op jit(solution)/shard_map/ppermute | solution.py:570
  39.7 8.6 %collective-permute-start.8 = (bf16[2,80,512]{2,1,0:T(8,128)(2,1)S(1)}, bf16[2,80,512]{2,1,0:T(8,128)(2,1)S(1)}, u32[]{:S(2)}, u32[]{:S(2)}) collective-permute-start(bf16[2,80,512]{2,1,0:T(8,128)(2,1)S(1)} %get-tuple-element.19), channel_id=1, source_target_pairs={{0,4},{1,5},{2,6},{3,7},{4,0},{5,1},{6,2},{7,3},{8,12},{9,13},{10,... | collective-permute-start | bytes 491528 | tf_op jit(solution)/shard_map/ppermute | solution.py:570
  41.2 7.1 %collective-permute-start.9 = (bf16[2,80,512]{2,1,0:T(8,128)(2,1)S(1)}, bf16[2,80,512]{2,1,0:T(8,128)(2,1)S(1)}, u32[]{:S(2)}, u32[]{:S(2)}) collective-permute-start(bf16[2,80,512]{2,1,0:T(8,128)(2,1)S(1)} %get-tuple-element.20), channel_id=1, source_target_pairs={{0,6},{1,7},{2,4},{3,5},{4,2},{5,3},{6,0},{7,1},{8,14},{9,15},{10,... | collective-permute-start | bytes 491528 | tf_op jit(solution)/shard_map/ppermute | solution.py:570
  48.4 1.7 %collective-permute-start.14 = (bf16[4,80,512]{2,1,0:T(8,128)(2,1)S(1)}, bf16[4,80,512]{2,1,0:T(8,128)(2,1)S(1)}, u32[]{:S(2)}, u32[]{:S(2)}) collective-permute-start(bf16[4,80,512]{2,1,0:T(8,128)(2,1)S(1)} %get-tuple-element.22), channel_id=1, source_target_pairs={{0,1},{1,0},{2,3},{3,2},{4,5},{5,4},{6,7},{7,6},{8,9},{9,8},{10,11... | collective-permute-start | bytes 983048 | tf_op jit(solution)/shard_map/ppermute | solution.py:570
